TPU v7x, 32 devices: a whole 2x2x4 slice. The times are simulated.
32 devices in a mesh: rep: 4 (over x, core), fsdp: 8 (over z, y).
Axes of the slice: x: 2, y: 2, z: 4, core: 2. Of those that a mesh axis runs over, the one named last changes fastest.
Arguments:
- block_in: bfloat16 [32, 1024, 1152], P(('rep', 'fsdp')), may hold values from -6 to 6
- condition: bfloat16 [32, 8, 1152], P(('rep', 'fsdp')), may hold values from -6 to 6
- item_lengths: int32 [32, 8], P(('rep', 'fsdp')), may hold values from 1 to 256, 1024 in all within a row
- item_widths: int32 [32, 8], P(('rep', 'fsdp')), may hold values from 2 to 32
- ada_weight: bfloat16 [1152, 6912], P('fsdp'), may hold values from -0.1875 to 0.1875
- ada_bias: bfloat16 [6912], P('fsdp'), may hold values from -3 to 3
- qkv_weight: bfloat16 [1152, 3456], P('fsdp'), may hold values from -0.1875 to 0.1875
- query_gain: bfloat16 [72], replicated, may hold values from 0.099609375 to 1.8984375
- key_gain: bfloat16 [72], replicated, may hold values from 0.099609375 to 1.8984375
- proj_weight: bfloat16 [1152, 1152], P('fsdp'), may hold values from -1.5 to 1.5
- gate_up_weight: bfloat16 [1152, 6144], P('fsdp'), may hold values from -0.1875 to 0.1875
- down_weight: bfloat16 [3072, 1152], P('fsdp'), may hold values from -0.109375 to 0.109375
- out_grad: bfloat16 [32, 1024, 1152], P(('rep', 'fsdp')), may hold values from -6 to 6
Outputs:
- block_out: bfloat16 [32, 1024, 1152], P(('rep', 'fsdp'))
- grad_input: float32 [32, 1024, 1152], P(('rep', 'fsdp'))
- grad_condition: float32 [32, 8, 1152], P(('rep', 'fsdp'))
- grad_ada_weight: float32 [1152, 6912], P('fsdp')
- grad_ada_bias: float32 [6912], P('fsdp')
- grad_qkv: float32 [1152, 3456], P('fsdp')
- grad_query_gain: float32 [72], replicated
- grad_key_gain: float32 [72], replicated
- grad_proj: float32 [1152, 1152], P('fsdp')
- grad_gate_up: float32 [1152, 6144], P('fsdp')
- grad_down: float32 [3072, 1152], P('fsdp')
Inputs may be any that keep to these rules, and one draw needn't show every extreme that they name: `item_lengths`: each row: the lengths of 7 items and last that of the padding, summing to 1024.
All inputs are finite; a program needn't handle non-finite values.
Results may differ from a plain program's by a relative error of at most 0.019.
Values may be sent and summed in bfloat16 or wider, within the bound.
No kernel may reach another device: no remote copies, remote signals or barrier semaphores. Data moves between devices by JAX's collectives and lax.ppermute only.
A program may use at most 448 MiB of HBM per device.

v0:
```python
from functools import partial

import jax
import jax.numpy as jnp
from jax import lax
from jax.sharding import PartitionSpec as P

HIGHEST_PRECISION = lax.Precision.HIGHEST
EPSILON = 1e-06


def matmul(left, right):
    return jnp.dot(left, right, preferred_element_type=jnp.float32)


def matmul_left(left, right):
    return lax.dot_general(
        left, right, (((0,), (0,)), ((), ())), preferred_element_type=jnp.float32
    )


def matmul_right(left, right):
    return lax.dot_general(
        left, right, (((1,), (1,)), ((), ())), preferred_element_type=jnp.float32
    )


def layer_norm(values):
    centred = values - jnp.mean(values, axis=-1, keepdims=True)
    return centred * lax.rsqrt(jnp.mean(centred * centred, axis=-1, keepdims=True) + EPSILON)


def modulated(values, shift_part, scale_part):
    return layer_norm(values) * (1.0 + scale_part) + shift_part


def rms_norm(values, gain_part):
    return (
        values * lax.rsqrt(jnp.mean(values * values, axis=-1, keepdims=True) + EPSILON) * gain_part
    )


def turn_pairs(values, angle_part):
    quarter = values.shape[-1] // 2
    leading = values[..., :quarter]
    trailing = values[..., quarter:]
    cosine = jnp.cos(angle_part)[:, None, :]
    sine_part = jnp.sin(angle_part)[:, None, :]
    return jnp.concatenate(
        [leading * cosine - trailing * sine_part, leading * sine_part + trailing * cosine], axis=-1
    )


def rotate(values, row_angle, column_angle):
    half_dim = values.shape[-1] // 2
    return jnp.concatenate(
        [
            turn_pairs(values[..., :half_dim], row_angle),
            turn_pairs(values[..., half_dim:], column_angle),
        ],
        axis=-1,
    )


def prepared(raw_part, gain_part, row_angle, column_angle, head_count):
    shaped = raw_part.reshape(raw_part.shape[0], head_count, -1)
    return rotate(rms_norm(shaped, gain_part), row_angle, column_angle)


def swiglu(paired):
    gate_part, up_part = jnp.split(paired, 2, axis=1)
    return jax.nn.silu(gate_part) * up_part


def angles(row_place, column_place, head_dim):
    quarter = head_dim // 4
    inverse = 10000.0 ** (-jnp.arange(quarter, dtype=jnp.float32) / quarter)
    return (
        row_place.astype(jnp.float32)[:, None] * inverse[None, :],
        column_place.astype(jnp.float32)[:, None] * inverse[None, :],
    )


def layout(lengths_row, widths_row, length):
    seg_count = lengths_row.shape[0]
    item_ends = jnp.cumsum(lengths_row)
    item_starts = item_ends - lengths_row
    token_place = jnp.arange(length, dtype=jnp.int32)[:, None]
    member = ((token_place >= item_starts[None, :]) & (token_place < item_ends[None, :])).astype(
        jnp.int32
    )
    segment = jnp.sum(member * jnp.arange(seg_count, dtype=jnp.int32)[None, :], axis=1)
    offset = token_place[:, 0] - jnp.sum(member * item_starts[None, :], axis=1)
    across = jnp.sum(member * widths_row[None, :], axis=1)
    return (member, segment, offset // across, offset % across)


def regroup(operand, groups, shards):
    leading_shape = operand.shape[:-1]
    piece_size = operand.shape[-1] // (groups * shards)
    shaped = operand.reshape(leading_shape + (shards, groups, piece_size))
    return jnp.swapaxes(shaped, -3, -2).reshape(leading_shape + (operand.shape[-1],))


def local(
    block_in,
    condition,
    item_lengths,
    item_widths,
    ada_weight,
    ada_bias,
    qkv_weight,
    query_gain,
    key_gain,
    proj_weight,
    gate_up_weight,
    down_weight,
    out_grad,
):
    seq_count, seq_len, model_width = block_in.shape
    seg_count = item_lengths.shape[1]
    head_dim = query_gain.shape[0]
    head_count = model_width // head_dim
    row_count = seq_count * seq_len
    query_block = min(512, seq_len)
    score_scale = float(head_dim) ** (-0.5)
    replicas = lax.axis_size("rep")
    shards = lax.axis_size("fsdp")
    arrange = partial(regroup, groups=1, shards=1)
    member, segment, row_place, column_place = jax.vmap(partial(layout, length=seq_len))(
        item_lengths, item_widths
    )
    keep_mask = (segment < seg_count - 1).astype(jnp.float32).reshape(row_count, 1)
    member_float = member.astype(jnp.float32)
    row_angle, column_angle = angles(row_place.reshape(-1), column_place.reshape(-1), head_dim)
    gathered = (
        lax.all_gather(ada_weight, "fsdp", axis=0, tiled=True),
        lax.all_gather(ada_bias, "fsdp", axis=0, tiled=True),
        lax.all_gather(qkv_weight, "fsdp", axis=0, tiled=True),
        lax.all_gather(proj_weight, "fsdp", axis=0, tiled=True),
        lax.all_gather(gate_up_weight, "fsdp", axis=0, tiled=True),
        lax.all_gather(down_weight, "fsdp", axis=0, tiled=True),
    )
    ada_full, bias_full, qkv_full, proj_full, gate_up_full, down_full = gathered
    cond_float = condition.astype(jnp.float32).reshape(seq_count * seg_count, model_width)
    cond_silu, silu_pull = jax.vjp(jax.nn.silu, cond_float)
    cond_act = cond_silu.astype(jnp.bfloat16)
    modulation = (matmul(cond_act, ada_full) + bias_full.astype(jnp.float32)).reshape(
        seq_count, seg_count, -1
    )
    token_mod = jnp.einsum(
        "nts,nsf->ntf", member_float, modulation, precision=HIGHEST_PRECISION
    ).reshape(row_count, -1)
    shift_a, scale_a, gate_a, shift_b, scale_b, gate_b = jnp.split(token_mod, 6, axis=1)
    inputs = block_in.astype(jnp.float32).reshape(row_count, model_width)
    normed_float, norm_pull_a = jax.vjp(modulated, inputs, shift_a, scale_a)
    normed_a = normed_float.astype(jnp.bfloat16)
    joint = matmul(normed_a, qkv_full)
    query_raw, key_raw, value_raw = jnp.split(joint, 3, axis=1)
    head_prep = partial(
        prepared, row_angle=row_angle, column_angle=column_angle, head_count=head_count
    )
    query_float, query_pull = jax.vjp(head_prep, query_raw, query_gain.astype(jnp.float32))
    key_float, key_pull = jax.vjp(head_prep, key_raw, key_gain.astype(jnp.float32))
    queries = query_float.astype(jnp.bfloat16)
    keys_low = key_float.astype(jnp.bfloat16)
    values_low = value_raw.reshape(row_count, head_count, head_dim).astype(jnp.bfloat16)
    mixed_parts = []
    log_totals = []
    sequence = 0
    first_row = sequence * seq_len
    segment_seq = segment[sequence]
    for offset_row in range(0, seq_len, query_block):
        query_part = queries[first_row + offset_row : first_row + offset_row + query_block]
        allowed = (
            segment_seq[offset_row : offset_row + query_block][:, None] == segment_seq[None, :]
        )
        scores = (
            jnp.einsum("qhd,khd->hqk", query_part, keys_low, preferred_element_type=jnp.float32)
            * score_scale
        )
        scores = jnp.where(allowed[None], scores, -1e30)
        row_peak = jnp.max(scores, axis=-1, keepdims=True)
        exponent = jnp.exp(scores - row_peak)
        totals = jnp.sum(exponent, axis=-1, keepdims=True)
        probs_low = (exponent / totals).astype(jnp.bfloat16)
        mixed_parts.append(
            jnp.einsum("hqk,khd->qhd", probs_low, values_low, preferred_element_type=jnp.float32)
        )
        log_totals.append(row_peak + jnp.log(totals))
    mixed = (
        jnp.concatenate(mixed_parts, axis=0).astype(jnp.bfloat16).reshape(row_count, model_width)
    )
    attended = matmul(mixed, proj_full)
    middle = inputs + keep_mask * gate_a * attended
    normed_b_float, norm_pull_b = jax.vjp(modulated, middle, shift_b, scale_b)
    normed_b = normed_b_float.astype(jnp.bfloat16)
    hidden = matmul(normed_b, gate_up_full)
    inner_float, swiglu_pull = jax.vjp(swiglu, hidden)
    inner = inner_float.astype(jnp.bfloat16)
    returned = matmul(inner, down_full)
    block_out = (
        (middle + keep_mask * gate_b * returned)
        .astype(jnp.bfloat16)
        .reshape(seq_count, seq_len, model_width)
    )
    ada_back, qkv_back, proj_back, gate_up_back, down_back = (
        lax.all_gather(ada_weight, "fsdp", axis=0, tiled=True),
        lax.all_gather(qkv_weight, "fsdp", axis=0, tiled=True),
        lax.all_gather(proj_weight, "fsdp", axis=0, tiled=True),
        lax.all_gather(gate_up_weight, "fsdp", axis=0, tiled=True),
        lax.all_gather(down_weight, "fsdp", axis=0, tiled=True),
    )
    upstream = out_grad.astype(jnp.float32).reshape(row_count, model_width)
    grad_gate_b = upstream * keep_mask * returned
    grad_returned = (upstream * keep_mask * gate_b).astype(jnp.bfloat16)
    grad_down = matmul_left(arrange(inner), grad_returned)
    grad_inner = matmul_right(grad_returned, down_back)
    grad_hidden = swiglu_pull(grad_inner)[0].astype(jnp.bfloat16)
    grad_gate_up = matmul_left(arrange(normed_b), grad_hidden)
    grad_normed_b = matmul_right(grad_hidden, gate_up_back)
    grad_middle_part, grad_shift_b, grad_scale_b = norm_pull_b(grad_normed_b)
    grad_middle = upstream + grad_middle_part
    grad_gate_a = grad_middle * keep_mask * attended
    grad_attended = (grad_middle * keep_mask * gate_a).astype(jnp.bfloat16)
    grad_proj = matmul_left(arrange(mixed), grad_attended)
    grad_mixed = (
        matmul_right(grad_attended, proj_back)
        .astype(jnp.bfloat16)
        .reshape(row_count, head_count, head_dim)
    )
    grad_query_parts = []
    block_number = 0
    sequence = 0
    first_row = sequence * seq_len
    segment_seq = segment[sequence]
    grad_key_seq = jnp.zeros((seq_len, head_count, head_dim), jnp.float32)
    grad_value_seq = jnp.zeros((seq_len, head_count, head_dim), jnp.float32)
    for offset_row in range(0, seq_len, query_block):
        query_part = queries[first_row + offset_row : first_row + offset_row + query_block]
        grad_out_part = grad_mixed[first_row + offset_row : first_row + offset_row + query_block]
        allowed = (
            segment_seq[offset_row : offset_row + query_block][:, None] == segment_seq[None, :]
        )
        scores = (
            jnp.einsum("qhd,khd->hqk", query_part, keys_low, preferred_element_type=jnp.float32)
            * score_scale
        )
        scores = jnp.where(allowed[None], scores, -1e30)
        probs_float = jnp.exp(scores - log_totals[block_number])
        block_number = block_number + 1
        probs_low = probs_float.astype(jnp.bfloat16)
        grad_value_seq = grad_value_seq + jnp.einsum(
            "hqk,qhd->khd", probs_low, grad_out_part, preferred_element_type=jnp.float32
        )
        grad_probs = jnp.einsum(
            "qhd,khd->hqk", grad_out_part, values_low, preferred_element_type=jnp.float32
        )
        row_delta = jnp.sum(grad_probs * probs_float, axis=-1, keepdims=True)
        grad_scores = (probs_float * (grad_probs - row_delta)).astype(jnp.bfloat16)
        grad_query_parts.append(
            jnp.einsum("hqk,khd->qhd", grad_scores, keys_low, preferred_element_type=jnp.float32)
            * score_scale
        )
        grad_key_seq = (
            grad_key_seq
            + jnp.einsum(
                "hqk,qhd->khd", grad_scores, query_part, preferred_element_type=jnp.float32
            )
            * score_scale
        )
    grad_query_raw, grad_query_gain = query_pull(jnp.concatenate(grad_query_parts, axis=0))
    grad_key_raw, grad_key_gain = key_pull(grad_key_seq)
    grad_value = grad_value_seq.reshape(row_count, model_width)
    grad_joint = jnp.concatenate([grad_query_raw, grad_key_raw, grad_value], axis=1).astype(
        jnp.bfloat16
    )
    grad_qkv = matmul_left(arrange(normed_a), grad_joint)
    grad_normed_a = matmul_right(grad_joint, qkv_back)
    grad_input_part, grad_shift_a, grad_scale_a = norm_pull_a(grad_normed_a)
    grad_input = (grad_middle + grad_input_part).reshape(seq_count, seq_len, model_width)
    grad_token_mod = jnp.concatenate(
        [grad_shift_a, grad_scale_a, grad_gate_a, grad_shift_b, grad_scale_b, grad_gate_b], axis=1
    ).reshape(seq_count, seq_len, -1)
    grad_modulation = jnp.einsum(
        "nts,ntf->nsf", member_float, grad_token_mod, precision=HIGHEST_PRECISION
    ).reshape(seq_count * seg_count, -1)
    grad_bias = arrange(jnp.sum(grad_modulation, axis=0))
    grad_mod_low = grad_modulation.astype(jnp.bfloat16)
    grad_ada = matmul_left(arrange(cond_act), grad_mod_low)
    grad_cond_act = matmul_right(grad_mod_low, ada_back)
    grad_condition = silu_pull(grad_cond_act)[0].reshape(seq_count, seg_count, model_width)
    gain_grads = jnp.concatenate([grad_query_gain, grad_key_gain], axis=0)
    tiled = jnp.broadcast_to(gain_grads[None, :], (replicas * shards, 2 * head_dim))
    summed = (
        lax.psum_scatter(
            grad_ada.astype(jnp.bfloat16), "fsdp", scatter_dimension=0, tiled=True
        ).astype(jnp.float32),
        lax.psum_scatter(
            grad_bias.astype(jnp.bfloat16), "fsdp", scatter_dimension=0, tiled=True
        ).astype(jnp.float32),
        lax.psum_scatter(
            grad_qkv.astype(jnp.bfloat16), "fsdp", scatter_dimension=0, tiled=True
        ).astype(jnp.float32),
        lax.psum_scatter(
            grad_proj.astype(jnp.bfloat16), "fsdp", scatter_dimension=0, tiled=True
        ).astype(jnp.float32),
        lax.psum_scatter(
            grad_gate_up.astype(jnp.bfloat16), "fsdp", scatter_dimension=0, tiled=True
        ).astype(jnp.float32),
        lax.psum_scatter(
            grad_down.astype(jnp.bfloat16), "fsdp", scatter_dimension=0, tiled=True
        ).astype(jnp.float32),
        lax.psum_scatter(
            tiled.astype(jnp.bfloat16), "fsdp", scatter_dimension=0, tiled=True
        ).astype(jnp.float32),
    )
    summed = (
        lax.psum_scatter(
            summed[0].astype(jnp.bfloat16), "rep", scatter_dimension=0, tiled=True
        ).astype(jnp.float32),
        lax.psum_scatter(
            summed[1].astype(jnp.bfloat16), "rep", scatter_dimension=0, tiled=True
        ).astype(jnp.float32),
        lax.psum_scatter(
            summed[2].astype(jnp.bfloat16), "rep", scatter_dimension=0, tiled=True
        ).astype(jnp.float32),
        lax.psum_scatter(
            summed[3].astype(jnp.bfloat16), "rep", scatter_dimension=0, tiled=True
        ).astype(jnp.float32),
        lax.psum_scatter(
            summed[4].astype(jnp.bfloat16), "rep", scatter_dimension=0, tiled=True
        ).astype(jnp.float32),
        lax.psum_scatter(
            summed[5].astype(jnp.bfloat16), "rep", scatter_dimension=0, tiled=True
        ).astype(jnp.float32),
        lax.psum_scatter(
            summed[6].astype(jnp.bfloat16), "rep", scatter_dimension=0, tiled=True
        ).astype(jnp.float32),
    )
    summed = (
        lax.all_gather(summed[0].astype(jnp.bfloat16), "rep", axis=0, tiled=True).astype(
            jnp.float32
        ),
        lax.all_gather(summed[1].astype(jnp.bfloat16), "rep", axis=0, tiled=True).astype(
            jnp.float32
        ),
        lax.all_gather(summed[2].astype(jnp.bfloat16), "rep", axis=0, tiled=True).astype(
            jnp.float32
        ),
        lax.all_gather(summed[3].astype(jnp.bfloat16), "rep", axis=0, tiled=True).astype(
            jnp.float32
        ),
        lax.all_gather(summed[4].astype(jnp.bfloat16), "rep", axis=0, tiled=True).astype(
            jnp.float32
        ),
        lax.all_gather(summed[5].astype(jnp.bfloat16), "rep", axis=0, tiled=True).astype(
            jnp.float32
        ),
        lax.all_gather(summed[6].astype(jnp.bfloat16), "rep", axis=0, tiled=True).astype(
            jnp.float32
        ),
    )
    shard_ada, shard_bias, shard_qkv, shard_proj, shard_gate_up, shard_down, gain_rows = summed
    return (
        block_out,
        grad_input,
        grad_condition,
        shard_ada,
        shard_bias,
        shard_qkv,
        gain_rows[0, :head_dim],
        gain_rows[0, head_dim:],
        shard_proj,
        shard_gate_up,
        shard_down,
    )


def solution(mesh):
    return jax.shard_map(
        local,
        mesh=mesh,
        in_specs=(
            P(("rep", "fsdp"), None, None),
            P(("rep", "fsdp"), None, None),
            P(("rep", "fsdp"), None),
            P(("rep", "fsdp"), None),
            P("fsdp", None),
            P("fsdp"),
            P("fsdp", None),
            P(),
            P(),
            P("fsdp", None),
            P("fsdp", None),
            P("fsdp", None),
            P(("rep", "fsdp"), None, None),
        ),
        out_specs=(
            P(("rep", "fsdp"), None, None),
            P(("rep", "fsdp"), None, None),
            P(("rep", "fsdp"), None, None),
            P("fsdp", None),
            P("fsdp"),
            P("fsdp", None),
            P(),
            P(),
            P("fsdp", None),
            P("fsdp", None),
            P("fsdp", None),
        ),
        check_vma=False,
    )
```

profile of v0, /device:TPU:1, one launch (start us, length us, event | category | flops | bytes accessed | tf_op | source)
XLA Modules:
  0.0 1886.0 jit_solution(2041193907524399454)
XLA Ops:
  14.5 32.1 %all-reduce.12 = bf16[6912]{0:T(1024)(128)(2,1)S(1)} all-reduce(bf16[6912]{0:T(1024)(128)(2,1)S(1)} %dynamic-update-slice), channel_id=1, replica_groups=mesh['rep'=4,'fsdp'=8] {'fsdp'}, use_global_device_ids=true, to_apply=%add.12 | all-reduce | flops 6912 | bytes 27648
  49.1 180.5 %all-gather.13.cloned.1.call-done = bf16[1152,6912]{1,0:T(8,128)(2,1)} async-done(((bf16[144,6912]{1,0:T(8,128)(2,1)}), bf16[1152,6912]{1,0:T(8,128)(2,1)}) %all-gather.13.cloned.1.call-update) | async-done | bytes 15925264 | tf_op jit(solution)/shard_map/all_gather | solution.py:137
  229.7 7.7 convolution_add_fusion
  237.4 22.8 %fusion.60 = f32[1024,6912]{1,0:T(8,128)S(1)} fusion(f32[8,6912]{1,0:T(8,128)S(1)} %convolution_add_fusion, s32[8]{0:T(128)S(1)} %bitcast.188, s32[8]{0:T(128)S(1)} %subtract_bitcast_fusion), kind=kOutput, calls=%fused_computation.143 | convolution fusion | flops 679518208 | bytes 28532800 | tf_op jit(solution)/shard_map/nts,nsf->ntf/dot_general | solution.py:151
  260.2 9.4 copy-done
  272.3 77.3 %all-gather.15.cloned.1.call-done = bf16[1152,3456]{1,0:T(8,128)(2,1)} async-done(((bf16[144,3456]{1,0:T(8,128)(2,1)}), bf16[1152,3456]{1,0:T(8,128)(2,1)}) %all-gather.15.cloned.1.call-update) | async-done | bytes 7962640 | tf_op jit(solution)/shard_map/all_gather | solution.py:139
  349.6 13.0 fusion.112
  364.3 4.4 fusion.104
  368.7 6.1 copy.50
  377.6 4.0 multiply_reduce_fusion.8
  382.2 6.5 copy.49
  403.0 17.8 fusion.109
  420.9 16.5 fusion.110
  437.4 14.4 fusion.5
  451.8 13.8 fusion.50
  465.6 14.4 fusion.4
  480.0 16.2 fusion.51
  496.3 13.2 fusion.102
  511.8 4.4 fusion.40
  516.3 85.0 %all-gather.19.cloned.1.call-done = bf16[1152,6144]{1,0:T(8,128)(2,1)} async-done(((bf16[144,6144]{1,0:T(8,128)(2,1)}), bf16[1152,6144]{1,0:T(8,128)(2,1)}) %all-gather.19.cloned.1.call-update) | async-done | bytes 14155792 | tf_op jit(solution)/shard_map/all_gather | solution.py:141
  601.3 22.4 %fusion.113 = f32[1024,6144]{1,0:T(8,128)} fusion(bf16[1024,1152]{1,0:T(8,128)(2,1)S(1)} %fusion.40, bf16[1152,6144]{1,0:T(8,128)(2,1)} %all-gather.19.cloned.1.call-done), kind=kOutput, calls=%fused_computation.237 | convolution fusion | flops 14495514624 | bytes 41680896 | tf_op jit(solution)/shard_map/dot_general | solution.py:13
  623.7 86.7 %all-gather.21.cloned.1.call-done = bf16[3072,1152]{1,0:T(8,128)(2,1)} async-done(((bf16[384,1152]{1,0:T(8,128)(2,1)}), bf16[3072,1152]{1,0:T(8,128)(2,1)}) %all-gather.21.cloned.1.call-update) | async-done | bytes 7077904 | tf_op jit(solution)/shard_map/all_gather | solution.py:142
  710.4 26.4 %fusion.18 = (bf16[1024,3072]{1,0:T(8,128)(2,1)}, bf16[1024,3072]{1,0:T(8,128)(2,1)}, bf16[1024,3072]{1,0:T(8,128)(2,1)}) fusion(f32[1024,6144]{1,0:T(8,128)} %fusion.113, bf16[1024,1152]{1,0:T(8,128)(2,1)} %get-tuple-element.39, bf16[3072,1152]{1,0:T(8,128)(2,1)} %all-gather.21.cloned.1.call-done), kind=kOutput, calls=%fused_computation.28 | convolution fusion | flops 7298088960 | bytes 53477376 | tf_op jit(solution)/shard_map/dot_general | solution.py:23
  736.9 25.4 %multiply_reduce_fusion.6 = (f32[1024]{0:T(1024)S(1)}, f32[1024,1152]{1,0:T(8,128)}) fusion(f32[1024,1152]{1,0:T(8,128)} %copy-done.1, f32[1024]{0:T(1024)S(1)} %broadcast_multiply_fusion, f32[1024,6912]{1,0:T(8,128)} %copy-done, bf16[1152,6144]{1,0:T(8,128)(2,1)} %all-gather.19.cloned.1.call-done, bf16[1024,3072]{1,0:T(8,128)(2,1)} %get-tuple-element.37, ...), kind=kOutput, calls=%fused_computation.89 | convolution fusion | flops 14526577664 | bytes 40902656 | tf_op jit(solution)/shard_map/dot_general | solution.py:23
  762.3 12.3 convolution_convert_fusion.3
  774.7 11.7 fusion.114
  786.4 10.9 fusion.101
  798.0 4.2 multiply_convert_fusion.4
  802.3 3.7 convolution_convert_fusion.5
  812.2 23.1 %multiply_reduce_fusion.1 = (f32[16,512]{1,0:T(8,128)}, f32[16,512,1024]{2,1,0:T(8,128)}) fusion(f32[16,512,1024]{2,1,0:T(8,128)} %get-tuple-element.95, f32[16,512]{1,0:T(8,128)} %log_add_fusion.1, bf16[512,16,72]{0,2,1:T(8,128)(2,1)S(1)} %bitcast.176, bf16[1024,16,72]{0,2,1:T(8,128)(2,1)S(1)} %bitcast.172), kind=kOutput, calls=%fused_computation.4 | convolution fusion | flops 1233117184 | bytes 70713344 | tf_op jit(solution)/shard_map/qhd,khd->hqk/dot_general | solution.py:256
  835.3 28.7 %multiply_convert_fusion.1 = bf16[16,512,1024]{2,1,0:T(8,128)(2,1)} fusion(f32[16,512,1024]{2,1,0:T(8,128)} %get-tuple-element.100, f32[16,512,1024]{2,1,0:T(8,128)} %get-tuple-element.95, f32[16,512]{1,0:T(8,128)} %get-tuple-element.99, f32[16,512]{1,0:T(8,128)} %log_add_fusion.1), kind=kLoop, calls=%fused_computation.3 | loop fusion | flops 33554432 | bytes 83951616 | tf_op jit(solution)/shard_map/convert_element_type | solution.py:260
  864.0 11.4 fusion.55
  875.4 23.1 %multiply_reduce_fusion = (f32[16,512]{1,0:T(8,128)}, f32[16,512,1024]{2,1,0:T(8,128)}) fusion(f32[16,512,1024]{2,1,0:T(8,128)} %get-tuple-element.93, f32[16,512]{1,0:T(8,128)S(1)} %copy-done.34, bf16[512,16,72]{0,2,1:T(8,128)(2,1)S(1)} %bitcast.178, bf16[1024,16,72]{0,2,1:T(8,128)(2,1)S(1)} %bitcast.173), kind=kOutput, calls=%fused_computation.1 | convolution fusion | flops 1233117184 | bytes 70713344 | tf_op jit(solution)/shard_map/qhd,khd->hqk/dot_general | solution.py:256
  898.5 28.0 %multiply_convert_fusion = bf16[16,512,1024]{2,1,0:T(8,128)(2,1)} fusion(f32[16,512,1024]{2,1,0:T(8,128)} %get-tuple-element.102, f32[16,512,1024]{2,1,0:T(8,128)} %get-tuple-element.93, f32[16,512]{1,0:T(8,128)} %get-tuple-element.101, f32[16,512]{1,0:T(8,128)} %log_add_fusion), kind=kLoop, calls=%fused_computation | loop fusion | flops 33554432 | bytes 83951616 | tf_op jit(solution)/shard_map/convert_element_type | solution.py:260
  926.6 10.3 multiply_bitcast_fusion
  938.9 4.5 multiply_reduce_fusion.2
  946.7 4.9 convolution_convert_fusion.4
  951.7 10.7 multiply_bitcast_fusion.2
  962.4 10.4 multiply_bitcast_fusion.1
  972.9 6.2 multiply_add_fusion.7
  985.0 16.1 fusion.8
  1001.0 15.1 add_convert_fusion
  1017.5 14.4 convolution_convert_fusion.2
  1033.6 22.4 %convolution_convert_fusion.1 = bf16[1152,6144]{1,0:T(8,128)(2,1)} fusion(bf16[1024,1152]{1,0:T(8,128)(2,1)S(1)} %copy-done.30, bf16[1024,3072]{1,0:T(8,128)(2,1)} %get-tuple-element.37, bf16[1024,3072]{1,0:T(8,128)(2,1)} %get-tuple-element.36), kind=kOutput, calls=%fused_computation.17 | convolution fusion | flops 14527758336 | bytes 29097984 | tf_op jit(solution)/shard_map/dot_general | solution.py:17
  1056.1 16.8 constant_dynamic-update-slice_fusion.1
  1072.9 6.3 fusion.33
  1079.7 4.2 fusion.100
  1084.0 7.1 multiply_dynamic-update-slice_fusion.1
  1099.3 17.1 fusion.111
  1116.4 8.0 convolution_convert_fusion
  1125.2 62.5 %reduce-scatter.17.cloned.1.call-done = bf16[144,3456]{1,0:T(8,128)(2,1)} async-done(((bf16[1152,3456]{1,0:T(8,128)(2,1)}), bf16[144,3456]{1,0:T(8,128)(2,1)}) %reduce-scatter.17.cloned.1.call-update) | async-done | bytes 995344 | tf_op jit(solution)/shard_map/reduce_scatter | solution.py:302
  1187.8 232.0 %reduce-scatter.21.cloned.1.call-done = bf16[144,6144]{1,0:T(8,128)(2,1)} async-done(((bf16[1152,6144]{1,0:T(8,128)(2,1)}), bf16[144,6144]{1,0:T(8,128)(2,1)}) %reduce-scatter.21.cloned.1.call-update) | async-done | bytes 1769488 | tf_op jit(solution)/shard_map/reduce_scatter | solution.py:308
  1419.8 272.2 %reduce-scatter.15.cloned.1.call-done = bf16[144,6912]{1,0:T(8,128)(2,1)} async-done(((bf16[1152,6912]{1,0:T(8,128)(2,1)}), bf16[144,6912]{1,0:T(8,128)(2,1)}) %reduce-scatter.15.cloned.1.call-update) | async-done | bytes 1990672 | tf_op jit(solution)/shard_map/reduce_scatter | solution.py:296
  1692.0 58.0 %fusion.99 = (bf16[40,6912]{1,0:T(8,128)(2,1)S(1)}, bf16[48,3456]{1,0:T(8,128)(2,1)S(1)}, bf16[48,1152]{1,0:T(8,128)(2,1)S(1)}, bf16[40,6144]{1,0:T(8,128)(2,1)S(1)}) fusion(bf16[144,6912]{1,0:T(8,128)(2,1)} %reduce-scatter.15.cloned.1.call-done, bf16[144,3456]{1,0:T(8,128)(2,1)} %reduce-scatter.17.cloned.1.call-done, ...), kind=kCustom, calls=%all-reduce-scatter.4 | all-reduce-scatter fusion | flops 2973698 | bytes 6574592
  1750.0 4.4 collective-permute-start.3
  1758.7 4.4 collective-permute-start
  1770.4 27.9 %all-reduce.26 = (bf16[6912]{0:T(1024)(128)(2,1)S(1)}, bf16[32,144]{1,0:T(8,128)(2,1)S(1)}) all-reduce(bf16[6912]{0:T(1024)(128)(2,1)S(1)} %get-tuple-element.105, bf16[32,144]{1,0:T(8,128)(2,1)S(1)} %broadcast_in_dim.57), channel_id=4, replica_groups=mesh['rep'=4,'fsdp'=8] {'fsdp'}, use_global_device_ids=true, to_apply=%region_25.26.clone | all-reduce | flops 11520 | bytes 46080
  1798.4 13.1 all-reduce.16
  1811.7 5.8 all-reduce.27
  1818.6 6.5 all-gather.2
  1825.8 10.4 fusion.78
  1838.6 9.5 all_gather.56
  1851.9 6.4 all-gather.3
  1860.4 10.6 all-gather.1
  (329 shorter events, 90.1 us)
Async XLA Ops:
  7.2 222.4 %all-gather.13.cloned.1.call-start = ((), (), s32[]{:S(2)}) async-start(), calls=%async_computation.6 | async-start | bytes 17915904 | tf_op jit(solution)/shard_map/all_gather | solution.py:137
  8.0 341.6 %all-gather.15.cloned.1.call-start = ((), (), s32[]{:S(2)}) async-start(), calls=%async_computation.7 | async-start | bytes 8957952 | tf_op jit(solution)/shard_map/all_gather | solution.py:139
  8.8 220.9 %copy-start.51 = (bf16[1,8,1152]{2,1,0:T(8,128)(2,1)S(1)}, bf16[1,8,1152]{2,1,0:T(8,128)(2,1)}, u32[]{:S(2)}) copy-start(bf16[1,8,1152]{2,1,0:T(8,128)(2,1)} %param.14) | copy-start | bytes 55300
  8.8 487.5 %all-gather.17.cloned.1.call-start = ((), (), s32[]{:S(2)}) async-start(), calls=%async_computation.8 | async-start | bytes 2985984 | tf_op jit(solution)/shard_map/all_gather | solution.py:140
  9.5 591.8 %all-gather.19.cloned.1.call-start = ((), (), s32[]{:S(2)}) async-start(), calls=%async_computation.9 | async-start | bytes 15925248 | tf_op jit(solution)/shard_map/all_gather | solution.py:141
  10.1 700.4 %all-gather.21.cloned.1.call-start = ((), (), s32[]{:S(2)}) async-start(), calls=%async_computation.10 | async-start | bytes 7962624 | tf_op jit(solution)/shard_map/all_gather | solution.py:142
  10.7 1113.8 %reduce-scatter.23.cloned.1.call-start = ((), (), s32[]{:S(2)}) async-start(), calls=%async_computation.15 | async-start | bytes 7962624 | tf_op jit(solution)/shard_map/reduce_scatter | solution.py:311
  10.8 385.0 %copy-start.72 = (f32[72]{0:T(128)}, f32[72]{0:T(128)S(1)}, u32[]{:S(2)}) copy-start(f32[72]{0:T(128)S(1)} %convert_element_type.193) | copy-start | bytes 868
  10.8 381.7 %copy-start.74 = (f32[72]{0:T(128)}, f32[72]{0:T(128)S(1)}, u32[]{:S(2)}) copy-start(f32[72]{0:T(128)S(1)} %convert_element_type.196) | copy-start | bytes 868
  11.0 226.4 %copy-start.67 = (s32[1,8]{1,0:T(1,128)}, s32[1,8]{1,0:T(1,128)S(1)}, u32[]{:S(2)}) copy-start(s32[1,8]{1,0:T(1,128)S(1)} %reduce_window_sum.11) | copy-start | bytes 100
  11.0 226.3 %copy-start.69 = (s32[8]{0:T(128)}, s32[8]{0:T(128)S(1)}, u32[]{:S(2)}) copy-start(s32[8]{0:T(128)S(1)} %subtract_bitcast_fusion) | copy-start | bytes 100
  11.4 248.8 %copy-start.57 = (f32[1024]{0:T(1024)}, f32[1024]{0:T(1024)S(1)}, u32[]{:S(2)}) copy-start(f32[1024]{0:T(1024)S(1)} %broadcast_multiply_fusion.1) | copy-start | bytes 12292
  12.2 248.0 %copy-start.61 = (f32[1024]{0:T(1024)}, f32[1024]{0:T(1024)S(1)}, u32[]{:S(2)}) copy-start(f32[1024]{0:T(1024)S(1)} %fusion.89) | copy-start | bytes 12292
  49.1 350.3 %copy-start.17 = (f32[1024,18]{0,1:T(8,128)}, f32[1024,18]{0,1:T(8,128)S(1)}, u32[]{:S(2)}) copy-start(f32[1024,18]{0,1:T(8,128)S(1)} %get-tuple-element.75) | copy-start | bytes 221188
  49.1 350.3 %copy-start.20 = (f32[1024,18]{0,1:T(8,128)}, f32[1024,18]{0,1:T(8,128)S(1)}, u32[]{:S(2)}) copy-start(f32[1024,18]{0,1:T(8,128)S(1)} %get-tuple-element.76) | copy-start | bytes 221188
  49.1 350.2 %copy-start.23 = (f32[1024,18]{0,1:T(8,128)}, f32[1024,18]{0,1:T(8,128)S(1)}, u32[]{:S(2)}) copy-start(f32[1024,18]{0,1:T(8,128)S(1)} %get-tuple-element.90) | copy-start | bytes 221188
  49.1 350.2 %copy-start.26 = (f32[1024,18]{0,1:T(8,128)}, f32[1024,18]{0,1:T(8,128)S(1)}, u32[]{:S(2)}) copy-start(f32[1024,18]{0,1:T(8,128)S(1)} %get-tuple-element.91) | copy-start | bytes 221188
  377.6 74.2 %copy-start.6 = (bf16[1024,1152]{0,1:T(8,128)(2,1)}, bf16[1024,1152]{0,1:T(8,128)(2,1)S(1)}, u32[]{:S(2)}) copy-start(bf16[1024,1152]{0,1:T(8,128)(2,1)S(1)} %copy.48) | copy-start | bytes 7077892
  382.2 10.3 copy-start.38
  399.4 21.5 %copy-start.40 = (bf16[1024,16,18]{0,2,1:T(8,128)(2,1)}, bf16[1024,16,18]{0,2,1:T(8,128)(2,1)S(1)}, u32[]{:S(2)}) copy-start(bf16[1024,16,18]{0,2,1:T(8,128)(2,1)S(1)} %get-tuple-element.55) | copy-start | bytes 1769476
  399.4 21.5 %copy-start.42 = (bf16[1024,16,18]{0,2,1:T(8,128)(2,1)}, bf16[1024,16,18]{0,2,1:T(8,128)(2,1)S(1)}, u32[]{:S(2)}) copy-start(bf16[1024,16,18]{0,2,1:T(8,128)(2,1)S(1)} %get-tuple-element.56) | copy-start | bytes 1769476
  399.4 21.5 %copy-start.44 = (bf16[1024,16,18]{0,2,1:T(8,128)(2,1)}, bf16[1024,16,18]{0,2,1:T(8,128)(2,1)S(1)}, u32[]{:S(2)}) copy-start(bf16[1024,16,18]{0,2,1:T(8,128)(2,1)S(1)} %get-tuple-element.67) | copy-start | bytes 1769476
  465.6 14.4 copy-start.7
  480.0 16.3 copy-start.3
  480.0 16.3 copy-start.53
  509.5 276.9 %copy-start.55 = (f32[1024]{0:T(1024)}, f32[1024]{0:T(1024)S(1)}, u32[]{:S(2)}) copy-start(f32[1024]{0:T(1024)S(1)} %broadcast_multiply_fusion) | copy-start | bytes 12292
  510.1 276.3 %copy-start.59 = (f32[1024]{0:T(1024)}, f32[1024]{0:T(1024)S(1)}, u32[]{:S(2)}) copy-start(f32[1024]{0:T(1024)S(1)} %fusion.90) | copy-start | bytes 12292
  516.3 107.5 %copy-start.29 = (bf16[1024,1152]{1,0:T(8,128)(2,1)}, bf16[1024,1152]{1,0:T(8,128)(2,1)S(1)}, u32[]{:S(2)}) copy-start(bf16[1024,1152]{1,0:T(8,128)(2,1)S(1)} %fusion.40) | copy-start | bytes 7077892
  736.8 25.4 %copy-start.86 = (bf16[1024,1152]{1,0:T(8,128)(2,1)S(1)}, bf16[1024,1152]{1,0:T(8,128)(2,1)}, u32[]{:S(2)}) copy-start(bf16[1024,1152]{1,0:T(8,128)(2,1)} %get-tuple-element.39) | copy-start | bytes 7077892
  774.6 350.6 %reduce-scatter.19.cloned.1.call-start = ((), (), s32[]{:S(2)}) async-start(), calls=%async_computation.13 | async-start | bytes 2985984 | tf_op jit(solution)/shard_map/reduce_scatter | solution.py:305
  786.4 10.9 copy-start.11
  786.4 11.6 copy-start.9
  809.3 26.0 %copy-start.13 = (bf16[512,1152]{0,1:T(8,128)(2,1)}, bf16[512,1152]{0,1:T(8,128)(2,1)S(1)}, u32[]{:S(2)}) copy-start(bf16[512,1152]{0,1:T(8,128)(2,1)S(1)} %copy.51) | copy-start | bytes 3538948
  864.0 11.4 copy-start.15
  864.0 11.4 copy-start.34
  898.5 28.0 %copy-start.16 = (bf16[1024,16,72]{0,2,1:T(8,128)(2,1)S(1)}, bf16[1024,16,72]{0,2,1:T(8,128)(2,1)}, u32[]{:S(2)}) copy-start(bf16[1024,16,72]{0,2,1:T(8,128)(2,1)} %pad_maximum_fusion.6) | copy-start | bytes 7077892
  926.5 10.3 copy-start.18
  926.5 10.3 copy-start.21
  926.5 10.3 copy-start.24
  951.7 10.7 copy-start.45
  951.7 10.7 copy-start.46
  962.4 10.5 copy-start.19
  962.4 10.5 copy-start.22
  962.4 10.5 copy-start.25
  962.4 10.5 copy-start.28
  972.8 215.0 %reduce-scatter.17.cloned.1.call-start = ((), (), s32[]{:S(2)}) async-start(), calls=%async_computation.12 | async-start | bytes 8957952 | tf_op jit(solution)/shard_map/reduce_scatter | solution.py:302
  985.0 16.1 copy-start.14
  1031.9 387.8 %reduce-scatter.21.cloned.1.call-start = ((), (), s32[]{:S(2)}) async-start(), calls=%async_computation.14 | async-start | bytes 15925248 | tf_op jit(solution)/shard_map/reduce_scatter | solution.py:308
  1056.0 16.8 copy-start.4
  1056.0 16.8 copy-start.58
  1056.0 16.8 copy-start.62
  1056.0 636.0 %reduce-scatter.15.cloned.1.call-start = ((), (), s32[]{:S(2)}) async-start(), calls=%async_computation.11 | async-start | bytes 17915904 | tf_op jit(solution)/shard_map/reduce_scatter | solution.py:296
  1072.9 11.0 slice-start.8
  1079.7 11.4 slice-start.10
  1079.7 14.2 slice-start.6
  1099.3 17.1 copy-start.52
  1124.4 714.2 %reduce-scatter.25.cloned.1.call-start = ((), (), s32[]{:S(2)}) async-start(), calls=%async_computation.16 | async-start | bytes 1105920 | tf_op jit(solution)/shard_map/reduce_scatter | solution.py:334
  1125.1 747.3 %all-gather.25.cloned.1.call-start = ((), (), s32[]{:S(2)}) async-start(), calls=%async_computation.18 | async-start | bytes 2457600 | tf_op jit(solution)/shard_map/all_gather | solution.py:354
  1750.0 20.3 %copy-start.79 = (bf16[72]{0:T(256)(128)(2,1)S(1)}, bf16[72]{0:T(256)(128)(2,1)}, u32[]{:S(2)}) copy-start(bf16[72]{0:T(256)(128)(2,1)} %get-tuple-element.13) | copy-start | bytes 436
  1750.0 7.0 collective-permute-start.3
  1758.6 117.0 %all-gather.23.cloned.1.call-start = ((), (), s32[]{:S(2)}) async-start(), calls=%async_computation.17 | async-start | bytes 2764800 | tf_op jit(solution)/shard_map/all_gather | solution.py:342
  1758.7 7.6 collective-permute-start
  1836.2 15.4 collective-permute-start.2
  1849.5 9.8 collective-permute-start.1
  (54 other events, 213.1 us)
Sparse Core Ops, SparseCore 0:
  10.2 219.3 all-gather.12
  231.8 117.7 all-gather.14
  351.8 52.3 all-gather.16
  406.3 195.0 all-gather.18
  603.4 107.0 all-gather.20
  774.8 126.6 reduce-scatter.22
  972.9 68.1 reduce-scatter.18
  1044.7 143.0 reduce-scatter.16
  1191.4 228.3 reduce-scatter.20
  1423.5 268.4 reduce-scatter.14
  1694.5 28.0 reduce-scatter.24
  1758.8 22.1 all-gather.24
  1783.1 23.1 all-gather.22
where the time goes:
time: 1900 us; the launch traced here: 1890 us
  waiting for transfers between devices  1000 us (53%)
  matrix products  437 us (23%)
  other arithmetic  178 us (9%)
  blocking collectives  170 us (9%)
  local copies, waits for them, and re-layouts  64.2 us (3%)
  between operations  20.5 us (1%)
    reduce_scatter x1, waiting for transfers between devices, local(): lax.psum_scatter(grad_ada.astype(jnp.bfloat16), 'fsdp', scatter_dimension...  272 us
    reduce_scatter x1, waiting for transfers between devices, local(): lax.psum_scatter(grad_gate_up.astype(jnp.bfloat16), 'fsdp', scatter_dimen...  232 us
    all_gather x1, waiting for transfers between devices, local(): lax.all_gather(ada_weight, 'fsdp', axis=0, tiled=True)  181 us
    unnamed x5, blocking collectives  137 us
    all_gather x1, waiting for transfers between devices, local(): lax.all_gather(down_weight, 'fsdp', axis=0, tiled=True)  86.7 us
    all_gather x1, waiting for transfers between devices, local(): lax.all_gather(gate_up_weight, 'fsdp', axis=0, tiled=True)  85 us
    dot_general x5, matrix products, matmul_right(): lax.dot_general(left, right, (((1,), (1,)), ((), ())), preferred_element_...  82.7 us
    all_gather x1, waiting for transfers between devices, local(): lax.all_gather(qkv_weight, 'fsdp', axis=0, tiled=True)  77.3 us
  transfers between devices with their start and end apart: 17, of which 8 were waited for; matrix products, arithmetic and copies ran while one was open for 35% of the time, Pallas kernels for 0%

commit v1 on v0

--- a/solution.py
+++ b/solution.py
@@ -3,6 +3,8 @@
 import jax
 import jax.numpy as jnp
 from jax import lax
+from jax.experimental import pallas as pl
+from jax.experimental.pallas import tpu as pltpu
 from jax.sharding import PartitionSpec as P
 
 HIGHEST_PRECISION = lax.Precision.HIGHEST
@@ -95,11 +97,160 @@
     return (member, segment, offset // across, offset % across)
 
 
-def regroup(operand, groups, shards):
-    leading_shape = operand.shape[:-1]
-    piece_size = operand.shape[-1] // (groups * shards)
-    shaped = operand.reshape(leading_shape + (shards, groups, piece_size))
-    return jnp.swapaxes(shaped, -3, -2).reshape(leading_shape + (operand.shape[-1],))
+AXES = ("rep", "fsdp")
+HIGH_Z = 4
+PARTS = 3
+
+
+def device_index(x, core, z, y):
+    return (x * 2 + core) * 8 + z * 2 + y
+
+
+PLACES = [(x, c, z, y) for x in range(2) for c in range(2) for z in range(4) for y in range(2)]
+TO_CORE = [(device_index(x, c, z, y), device_index(x, 1 - c, z, y)) for x, c, z, y in PLACES]
+TO_X = [(device_index(x, c, z, y), device_index(1 - x, c, z, y)) for x, c, z, y in PLACES]
+TO_Y = [(device_index(x, c, z, y), device_index(x, c, z, 1 - y)) for x, c, z, y in PLACES]
+Z_GROUPS = [[0, 2, 4, 6], [1, 3, 5, 7]]
+
+
+def coordinates():
+    replica = lax.axis_index("rep")
+    shard = lax.axis_index("fsdp")
+    return replica // 2, replica % 2, shard // 2, shard % 2
+
+
+def pick(operand, index, axis):
+    return lax.dynamic_index_in_dim(operand, index, axis, keepdims=False)
+
+
+def place_kernel(where, a0, a1, ax, b0, b1, bx, out, sems):
+    x, core, y = where[0], where[1], where[2]
+    copies = []
+    for p0, p1, px, c in ((a0, a1, ax, core), (b0, b1, bx, 1 - core)):
+        for q in range(HIGH_Z):
+            for source, target in (
+                (p0.at[q, 0], out.at[q, y, c, x]),
+                (p0.at[q, 1], out.at[q, y, c, 2]),
+                (p1.at[q, 0], out.at[q, 1 - y, c, x]),
+                (p1.at[q, 1], out.at[q, 1 - y, c, 2]),
+                (px.at[q, 0], out.at[q, y, c, 1 - x]),
+                (px.at[q, 1], out.at[q, 1 - y, c, 1 - x]),
+            ):
+                copy = pltpu.make_async_copy(source, target, sems.at[len(copies)])
+                copy.start()
+                copies.append(copy)
+    for copy in copies:
+        copy.wait()
+
+
+def gather_fast(weight):
+    x, core, z, y = coordinates()
+    rows, width = weight.shape
+    h = rows // 6
+    mine = pick(weight.reshape(2, PARTS, h, width), core, 0)
+    base = jnp.stack([pick(mine, x, 0), mine[2]], 0)
+    own = lax.all_to_all(
+        jnp.broadcast_to(base, (HIGH_Z, 2, h, width)), "fsdp", 0, 0, axis_index_groups=Z_GROUPS
+    )
+    over_y = lax.ppermute(own, AXES, TO_Y)
+    over_x = lax.ppermute(jnp.stack([own[:, 0], over_y[:, 0]], 1), AXES, TO_X)
+    pieces = (own, over_y, over_x)
+    others = tuple(lax.ppermute(piece, AXES, TO_CORE) for piece in pieces)
+    where = jnp.stack([x, core, y]).astype(jnp.int32)
+    full = pl.pallas_call(
+        place_kernel,
+        out_shape=jax.ShapeDtypeStruct((HIGH_Z, 2, 2, PARTS, h, width), weight.dtype),
+        in_specs=[pl.BlockSpec(memory_space=pltpu.SMEM)] + [pl.BlockSpec(memory_space=pl.ANY)] * 6,
+        out_specs=pl.BlockSpec(memory_space=pltpu.VMEM),
+        scratch_shapes=[pltpu.SemaphoreType.DMA((48,))],
+        compiler_params=pltpu.CompilerParams(vmem_limit_bytes=40 * 2**20),
+        cost_estimate=pl.CostEstimate(
+            flops=0, bytes_accessed=2 * 48 * h * width * 2, transcendentals=0
+        ),
+        name="place",
+    )(where, *pieces, *others)
+    return full.reshape(8 * rows, width)
+
+
+def scatter_fast(grad):
+    x, core, z, y = coordinates()
+    total, width = grad.shape
+    h = total // 48
+    low = jnp.bfloat16
+    wide = jnp.float32
+    views = grad.reshape(HIGH_Z, 2, 2, PARTS, h, width)
+    kept = pick(views, core, 2)
+    got = lax.ppermute(pick(views, 1 - core, 2), AXES, TO_CORE)
+
+    def pair(t):
+        first = pick(kept, t, 2) if not isinstance(t, int) else kept[:, :, t]
+        second = pick(got, t, 2) if not isinstance(t, int) else got[:, :, t]
+        return first.astype(wide) + second.astype(wide)
+
+    from_x = lax.ppermute(pair(1 - x).astype(low), AXES, TO_X)
+    own = (pair(x) + from_x.astype(wide)).astype(low)
+    both = pair(2).astype(low)
+    halves = jnp.stack([own, both], 2)
+    from_y = lax.ppermute(pick(halves, 1 - y, 1), AXES, TO_Y)
+    line = (pick(halves, y, 1).astype(wide) + from_y.astype(wide)).astype(low)
+    spread = lax.all_to_all(line, "fsdp", 0, 0, axis_index_groups=Z_GROUPS)
+    part = jnp.sum(spread.astype(wide), axis=0).astype(low)
+    other = lax.ppermute(part, AXES, TO_X)
+    shared = (part[1].astype(wide) + other[1].astype(wide)).astype(low)
+    first = jnp.where(x == 0, part[0], other[0])
+    second = jnp.where(x == 0, other[0], part[0])
+    done = jnp.stack([first, second, shared], 0)
+    twin = lax.ppermute(done, AXES, TO_CORE)
+    whole = jnp.stack([jnp.where(core == 0, done, twin), jnp.where(core == 0, twin, done)], 0)
+    return whole.reshape(total // 8, width).astype(wide)
+
+
+def is_fast():
+    return lax.axis_size("rep") == 4 and lax.axis_size("fsdp") == 8
+
+
+def gather_weight(weight):
+    if is_fast() and weight.shape[0] % 48 == 0:
+        return gather_fast(weight)
+    return lax.all_gather(weight, "fsdp", axis=0, tiled=True)
+
+
+def scatter_grad(grad):
+    shards = lax.axis_size("fsdp")
+    replicas = lax.axis_size("rep")
+    if is_fast() and grad.shape[0] % 384 == 0:
+        return scatter_fast(grad)
+    part = lax.psum_scatter(grad, "fsdp", scatter_dimension=0, tiled=True)
+    return lax.psum(part, "rep").astype(jnp.float32)
+
+
+def gather_rows(rows):
+    shards = lax.axis_size("fsdp")
+    count, width = rows.shape
+    group = lax.all_to_all(jnp.broadcast_to(rows, (shards, count, width)), "fsdp", 0, 0)
+    group = group.reshape(shards * count, width)
+    if not is_fast():
+        return group, lax.all_gather(group, "rep", axis=0, tiled=True)
+    x, core, z, y = coordinates()
+    twin = lax.ppermute(group, AXES, TO_CORE)
+    chip = jnp.stack([jnp.where(core == 0, group, twin), jnp.where(core == 0, twin, group)], 0)
+    far = lax.ppermute(chip, AXES, TO_X)
+    every = jnp.stack([jnp.where(x == 0, chip, far), jnp.where(x == 0, far, chip)], 0)
+    return group, every.reshape(4 * shards * count, width)
+
+
+def exchange(rows):
+    shards = lax.axis_size("fsdp")
+    count, width = rows.shape
+    shaped = rows.reshape(count, shards, width // shards).swapaxes(0, 1)
+    return lax.all_to_all(shaped, "fsdp", 0, 0).reshape(shards * count, width // shards)
+
+
+def sum_back(partial_rows, count):
+    shards = lax.axis_size("fsdp")
+    shaped = partial_rows.astype(jnp.bfloat16).reshape(shards, count, -1)
+    got = lax.all_to_all(shaped, "fsdp", 0, 0)
+    return jnp.sum(got.astype(jnp.float32), axis=0)
 
 
 def local(
@@ -124,33 +275,44 @@
     row_count = seq_count * seq_len
     query_block = min(512, seq_len)
     score_scale = float(head_dim) ** (-0.5)
-    replicas = lax.axis_size("rep")
     shards = lax.axis_size("fsdp")
-    arrange = partial(regroup, groups=1, shards=1)
     member, segment, row_place, column_place = jax.vmap(partial(layout, length=seq_len))(
         item_lengths, item_widths
     )
     keep_mask = (segment < seg_count - 1).astype(jnp.float32).reshape(row_count, 1)
-    member_float = member.astype(jnp.float32)
     row_angle, column_angle = angles(row_place.reshape(-1), column_place.reshape(-1), head_dim)
-    gathered = (
-        lax.all_gather(ada_weight, "fsdp", axis=0, tiled=True),
-        lax.all_gather(ada_bias, "fsdp", axis=0, tiled=True),
-        lax.all_gather(qkv_weight, "fsdp", axis=0, tiled=True),
-        lax.all_gather(proj_weight, "fsdp", axis=0, tiled=True),
-        lax.all_gather(gate_up_weight, "fsdp", axis=0, tiled=True),
-        lax.all_gather(down_weight, "fsdp", axis=0, tiled=True),
-    )
-    ada_full, bias_full, qkv_full, proj_full, gate_up_full, down_full = gathered
+    qkv_full = gather_weight(qkv_weight)
+    proj_full = gather_weight(proj_weight)
+    gate_up_full = gather_weight(gate_up_weight)
+    down_full = gather_weight(down_weight)
     cond_float = condition.astype(jnp.float32).reshape(seq_count * seg_count, model_width)
     cond_silu, silu_pull = jax.vjp(jax.nn.silu, cond_float)
     cond_act = cond_silu.astype(jnp.bfloat16)
-    modulation = (matmul(cond_act, ada_full) + bias_full.astype(jnp.float32)).reshape(
-        seq_count, seg_count, -1
-    )
-    token_mod = jnp.einsum(
-        "nts,nsf->ntf", member_float, modulation, precision=HIGHEST_PRECISION
-    ).reshape(row_count, -1)
+    mod_width = ada_weight.shape[1]
+    item_count = seq_count * seg_count
+    fsdp_place = lax.axis_index("fsdp")
+    group_act = exchange(cond_act)
+    bias_row = lax.dynamic_update_slice(
+        jnp.zeros((mod_width,), jnp.float32),
+        ada_bias.astype(jnp.float32),
+        (fsdp_place * ada_bias.shape[0],),
+    )
+    mod_part = matmul(group_act, ada_weight) + bias_row[None, :]
+    early = 2 * model_width
+    modulation = jnp.concatenate(
+        [
+            sum_back(mod_part[:, :early], item_count),
+            sum_back(mod_part[:, early:], item_count),
+        ],
+        axis=1,
+    )
+    mod_high = modulation.astype(jnp.bfloat16)
+    mod_rest = (modulation - mod_high.astype(jnp.float32)).astype(jnp.bfloat16)
+    member_low = member.astype(jnp.bfloat16).reshape(row_count, seg_count)
+    token_mod = matmul(
+        jnp.concatenate([member_low, member_low], axis=1),
+        jnp.concatenate([mod_high, mod_rest], axis=0),
+    )
     shift_a, scale_a, gate_a, shift_b, scale_b, gate_b = jnp.split(token_mod, 6, axis=1)
     inputs = block_in.astype(jnp.float32).reshape(row_count, model_width)
     normed_float, norm_pull_a = jax.vjp(modulated, inputs, shift_a, scale_a)
@@ -204,28 +366,21 @@
         .astype(jnp.bfloat16)
         .reshape(seq_count, seq_len, model_width)
     )
-    ada_back, qkv_back, proj_back, gate_up_back, down_back = (
-        lax.all_gather(ada_weight, "fsdp", axis=0, tiled=True),
-        lax.all_gather(qkv_weight, "fsdp", axis=0, tiled=True),
-        lax.all_gather(proj_weight, "fsdp", axis=0, tiled=True),
-        lax.all_gather(gate_up_weight, "fsdp", axis=0, tiled=True),
-        lax.all_gather(down_weight, "fsdp", axis=0, tiled=True),
-    )
     upstream = out_grad.astype(jnp.float32).reshape(row_count, model_width)
     grad_gate_b = upstream * keep_mask * returned
     grad_returned = (upstream * keep_mask * gate_b).astype(jnp.bfloat16)
-    grad_down = matmul_left(arrange(inner), grad_returned)
-    grad_inner = matmul_right(grad_returned, down_back)
+    grad_down = matmul_left(inner, grad_returned)
+    grad_inner = matmul_right(grad_returned, down_full)
     grad_hidden = swiglu_pull(grad_inner)[0].astype(jnp.bfloat16)
-    grad_gate_up = matmul_left(arrange(normed_b), grad_hidden)
-    grad_normed_b = matmul_right(grad_hidden, gate_up_back)
+    grad_gate_up = matmul_left(normed_b, grad_hidden)
+    grad_normed_b = matmul_right(grad_hidden, gate_up_full)
     grad_middle_part, grad_shift_b, grad_scale_b = norm_pull_b(grad_normed_b)
     grad_middle = upstream + grad_middle_part
     grad_gate_a = grad_middle * keep_mask * attended
     grad_attended = (grad_middle * keep_mask * gate_a).astype(jnp.bfloat16)
-    grad_proj = matmul_left(arrange(mixed), grad_attended)
+    grad_proj = matmul_left(mixed, grad_attended)
     grad_mixed = (
-        matmul_right(grad_attended, proj_back)
+        matmul_right(grad_attended, proj_full)
         .astype(jnp.bfloat16)
         .reshape(row_count, head_count, head_dim)
     )
@@ -275,93 +430,68 @@
     grad_joint = jnp.concatenate([grad_query_raw, grad_key_raw, grad_value], axis=1).astype(
         jnp.bfloat16
     )
-    grad_qkv = matmul_left(arrange(normed_a), grad_joint)
-    grad_normed_a = matmul_right(grad_joint, qkv_back)
+    grad_qkv = matmul_left(normed_a, grad_joint)
+    grad_normed_a = matmul_right(grad_joint, qkv_full)
     grad_input_part, grad_shift_a, grad_scale_a = norm_pull_a(grad_normed_a)
     grad_input = (grad_middle + grad_input_part).reshape(seq_count, seq_len, model_width)
-    grad_token_mod = jnp.concatenate(
-        [grad_shift_a, grad_scale_a, grad_gate_a, grad_shift_b, grad_scale_b, grad_gate_b], axis=1
-    ).reshape(seq_count, seq_len, -1)
-    grad_modulation = jnp.einsum(
-        "nts,ntf->nsf", member_float, grad_token_mod, precision=HIGHEST_PRECISION
-    ).reshape(seq_count * seg_count, -1)
-    grad_bias = arrange(jnp.sum(grad_modulation, axis=0))
-    grad_mod_low = grad_modulation.astype(jnp.bfloat16)
-    grad_ada = matmul_left(arrange(cond_act), grad_mod_low)
-    grad_cond_act = matmul_right(grad_mod_low, ada_back)
+    def segment_sums(parts):
+        stacked = jnp.concatenate([part.astype(jnp.bfloat16) for part in parts], axis=1)
+        return matmul_left(member_low, stacked)
+
+    late_sums = segment_sums([grad_gate_a, grad_shift_b, grad_scale_b, grad_gate_b])
+    early_sums = segment_sums([grad_shift_a, grad_scale_a])
+    gain_row = jnp.concatenate([grad_query_gain, grad_key_gain], axis=0)
+    gain_high = gain_row.astype(jnp.bfloat16).astype(jnp.float32)
+    gain_block = jnp.zeros((item_count, 256), jnp.float32)
+    gain_block = gain_block.at[0, : 2 * head_dim].set(gain_high)
+    gain_block = gain_block.at[1, : 2 * head_dim].set(gain_row - gain_high)
+    ada_group = []
+    ada_every = []
+    for block in (late_sums, jnp.concatenate([early_sums, gain_block], axis=1)):
+        group_rows, every_rows = gather_rows(block.astype(jnp.bfloat16))
+        ada_group.append(group_rows)
+        ada_every.append(every_rows)
+    if is_fast():
+        x, core, _, _ = coordinates()
+        twin = lax.ppermute(group_act, AXES, TO_CORE)
+        chip = jnp.stack(
+            [jnp.where(core == 0, group_act, twin), jnp.where(core == 0, twin, group_act)], 0
+        )
+        far = lax.ppermute(chip, AXES, TO_X)
+        every_act = jnp.stack([jnp.where(x == 0, chip, far), jnp.where(x == 0, far, chip)], 0)
+        every_act = every_act.reshape(-1, group_act.shape[1])
+    else:
+        every_act = lax.all_gather(group_act, "rep", axis=0, tiled=True)
+    early_every = ada_every[1][:, :early]
+    early_group = ada_group[1][:, :early]
+    shard_ada = jnp.concatenate(
+        [matmul_left(every_act, early_every), matmul_left(every_act, ada_every[0])], axis=1
+    )
+    bias_sums = jnp.concatenate(
+        [
+            jnp.sum(early_every.astype(jnp.float32), axis=0),
+            jnp.sum(ada_every[0].astype(jnp.float32), axis=0),
+        ],
+        axis=0,
+    )
+    shard_bias = lax.dynamic_slice(
+        bias_sums, (fsdp_place * ada_bias.shape[0],), (ada_bias.shape[0],)
+    )
+    gain_sums = jnp.sum(ada_every[1][:, early:].astype(jnp.float32), axis=0)[: 2 * head_dim]
+    cond_part = matmul_right(early_group, ada_weight[:, :early]) + matmul_right(
+        ada_group[0], ada_weight[:, early:]
+    )
+    cond_back = lax.all_to_all(
+        cond_part.astype(jnp.bfloat16).reshape(shards, item_count, -1), "fsdp", 0, 0
+    )
+    grad_cond_act = (
+        cond_back.swapaxes(0, 1).reshape(item_count, model_width).astype(jnp.float32)
+    )
     grad_condition = silu_pull(grad_cond_act)[0].reshape(seq_count, seg_count, model_width)
-    gain_grads = jnp.concatenate([grad_query_gain, grad_key_gain], axis=0)
-    tiled = jnp.broadcast_to(gain_grads[None, :], (replicas * shards, 2 * head_dim))
-    summed = (
-        lax.psum_scatter(
-            grad_ada.astype(jnp.bfloat16), "fsdp", scatter_dimension=0, tiled=True
-        ).astype(jnp.float32),
-        lax.psum_scatter(
-            grad_bias.astype(jnp.bfloat16), "fsdp", scatter_dimension=0, tiled=True
-        ).astype(jnp.float32),
-        lax.psum_scatter(
-            grad_qkv.astype(jnp.bfloat16), "fsdp", scatter_dimension=0, tiled=True
-        ).astype(jnp.float32),
-        lax.psum_scatter(
-            grad_proj.astype(jnp.bfloat16), "fsdp", scatter_dimension=0, tiled=True
-        ).astype(jnp.float32),
-        lax.psum_scatter(
-            grad_gate_up.astype(jnp.bfloat16), "fsdp", scatter_dimension=0, tiled=True
-        ).astype(jnp.float32),
-        lax.psum_scatter(
-            grad_down.astype(jnp.bfloat16), "fsdp", scatter_dimension=0, tiled=True
-        ).astype(jnp.float32),
-        lax.psum_scatter(
-            tiled.astype(jnp.bfloat16), "fsdp", scatter_dimension=0, tiled=True
-        ).astype(jnp.float32),
-    )
-    summed = (
-        lax.psum_scatter(
-            summed[0].astype(jnp.bfloat16), "rep", scatter_dimension=0, tiled=True
-        ).astype(jnp.float32),
-        lax.psum_scatter(
-            summed[1].astype(jnp.bfloat16), "rep", scatter_dimension=0, tiled=True
-        ).astype(jnp.float32),
-        lax.psum_scatter(
-            summed[2].astype(jnp.bfloat16), "rep", scatter_dimension=0, tiled=True
-        ).astype(jnp.float32),
-        lax.psum_scatter(
-            summed[3].astype(jnp.bfloat16), "rep", scatter_dimension=0, tiled=True
-        ).astype(jnp.float32),
-        lax.psum_scatter(
-            summed[4].astype(jnp.bfloat16), "rep", scatter_dimension=0, tiled=True
-        ).astype(jnp.float32),
-        lax.psum_scatter(
-            summed[5].astype(jnp.bfloat16), "rep", scatter_dimension=0, tiled=True
-        ).astype(jnp.float32),
-        lax.psum_scatter(
-            summed[6].astype(jnp.bfloat16), "rep", scatter_dimension=0, tiled=True
-        ).astype(jnp.float32),
-    )
-    summed = (
-        lax.all_gather(summed[0].astype(jnp.bfloat16), "rep", axis=0, tiled=True).astype(
-            jnp.float32
-        ),
-        lax.all_gather(summed[1].astype(jnp.bfloat16), "rep", axis=0, tiled=True).astype(
-            jnp.float32
-        ),
-        lax.all_gather(summed[2].astype(jnp.bfloat16), "rep", axis=0, tiled=True).astype(
-            jnp.float32
-        ),
-        lax.all_gather(summed[3].astype(jnp.bfloat16), "rep", axis=0, tiled=True).astype(
-            jnp.float32
-        ),
-        lax.all_gather(summed[4].astype(jnp.bfloat16), "rep", axis=0, tiled=True).astype(
-            jnp.float32
-        ),
-        lax.all_gather(summed[5].astype(jnp.bfloat16), "rep", axis=0, tiled=True).astype(
-            jnp.float32
-        ),
-        lax.all_gather(summed[6].astype(jnp.bfloat16), "rep", axis=0, tiled=True).astype(
-            jnp.float32
-        ),
-    )
-    shard_ada, shard_bias, shard_qkv, shard_proj, shard_gate_up, shard_down, gain_rows = summed
+    shard_qkv = scatter_grad(grad_qkv.astype(jnp.bfloat16))
+    shard_proj = scatter_grad(grad_proj.astype(jnp.bfloat16))
+    shard_gate_up = scatter_grad(grad_gate_up.astype(jnp.bfloat16))
+    shard_down = scatter_grad(grad_down.astype(jnp.bfloat16))
     return (
         block_out,
         grad_input,
@@ -369,8 +499,8 @@
         shard_ada,
         shard_bias,
         shard_qkv,
-        gain_rows[0, :head_dim],
-        gain_rows[0, head_dim:],
+        gain_sums[:head_dim],
+        gain_sums[head_dim:],
         shard_proj,
         shard_gate_up,
         shard_down,

time: 1900 us -> 1240 us (0.65)
  waiting for transfers between devices: 1000 us -> 362 us
  blocking collectives: 170 us -> 0 us
  starting transfers between devices: 13.8 us -> 117 us
  other arithmetic: 178 us -> 239 us
  matrix products: 437 us -> 386 us
  Pallas kernels: 0 us -> 38.1 us
  local copies, waits for them, and re-layouts: 64.2 us -> 89.3 us
    reduce_scatter x6 -> x0, waiting for transfers between devices: 567 us -> none  [the longest x1 272 us: local(): lax.psum_scatter(grad_ada.astype(jnp.bfloat16), 'fsdp', scatter_dimension...]
    all_gather x7 -> x0, waiting for transfers between devices: 430 us -> none  [the longest x1 181 us: local(): lax.all_gather(ada_weight, 'fsdp', axis=0, tiled=True)]
    ppermute x0 -> x46, waiting for transfers between devices: none -> 206 us  [the longest x4 83.7 us: scatter_fast(): from_x = lax.ppermute(pair(1 - x).astype(low), AXES, TO_X)]
    all_to_all x0 -> x14, waiting for transfers between devices: none -> 156 us  [the longest x4 64.5 us: scatter_fast(): spread = lax.all_to_all(line, 'fsdp', 0, 0, axis_index_groups=Z_GROUPS)]
    unnamed x5 -> x0, blocking collectives: 137 us -> none
    all_to_all x0 -> x14, starting transfers between devices: none -> 64.6 us  [the longest x4 16.6 us: scatter_fast(): spread = lax.all_to_all(line, 'fsdp', 0, 0, axis_index_groups=Z_GROUPS)]
    ppermute x0 -> x46, starting transfers between devices: none -> 52.7 us  [the longest x12 14 us: gather_fast(): others = tuple((lax.ppermute(piece, AXES, TO_CORE) for piece in pieces))]
    dot_general x2 -> x0, matrix products: 39.9 us -> none  [the longest x1 22.8 us: local(): jnp.einsum('nts,nsf->ntf', member_float, modulation, precision=HIGHEST_PR...]
  transfers between devices with their start and end apart: 17 -> 60, of which waited for: 8 -> 30; matrix products, arithmetic and copies ran while one was open for 35% -> 25% of each run, Pallas kernels for 0% -> 2%
where the time goes in v1:
time: 1240 us
  matrix products  386 us (31%)
  waiting for transfers between devices  362 us (29%)
  other arithmetic  239 us (19%)
  starting transfers between devices  117 us (9%)
  local copies, waits for them, and re-layouts  89.3 us (7%)
  Pallas kernels  38.1 us (3%)
    ppermute x4, waiting for transfers between devices, scatter_fast(): from_x = lax.ppermute(pair(1 - x).astype(low), AXES, TO_X)  83.7 us
    dot_general x6, matrix products, matmul_right(): lax.dot_general(left, right, (((1,), (1,)), ((), ())), preferred_element_...  74.6 us
    dot_general x6, matrix products, matmul(): return jnp.dot(left, right, preferred_element_type=jnp.float32)  73.7 us
    all_to_all x4, waiting for transfers between devices, scatter_fast(): spread = lax.all_to_all(line, 'fsdp', 0, 0, axis_index_groups=Z_GROUPS)  64.5 us
    all_to_all x4, waiting for transfers between devices, gather_fast(): lax.all_to_all(jnp.broadcast_to(base, (HIGH_Z, 2, h, width)), 'fsdp', 0,...  59.2 us
    dot_general x8, matrix products, matmul_left(): lax.dot_general(left, right, (((0,), (0,)), ((), ())), preferred_element_...  57.8 us
    convert_element_type x2, other arithmetic, local(): grad_scores = (probs_float * (grad_probs - row_delta)).astype(jnp.bfloat16)  55.7 us
    dot_general x2, matrix products, local(): jnp.einsum('qhd,khd->hqk', grad_out_part, values_low, preferred_element_t...  45.8 us
  transfers between devices with their start and end apart: 60, of which 30 were waited for; matrix products, arithmetic and copies ran while one was open for 25% of the time, Pallas kernels for 2%

profile of v1, /device:TPU:1, one launch (start us, length us, event | category | flops | bytes accessed | tf_op | source)
XLA Modules:
  0.0 1235.1 jit_solution(440292935503949863)
XLA Ops:
  2.1 6.4 all-to-all-start
  22.4 6.2 all-to-all-done.1
  35.4 7.9 all-to-all-done.4.a0
  43.3 5.4 all-to-all-start.2
  50.3 12.7 %all-to-all-done.2 = bf16[8,8,4608]{2,1,0:T(8,128)(2,1)S(1)} async-done(((bf16[8,8,4608]{2,1,0:T(8,128)(2,1)}), bf16[8,8,4608]{2,1,0:T(8,128)(2,1)S(1)}, u32[]{:S(2)}, u32[]{:S(2)}) %all-to-all-start.2) | async-done | bytes 589856 | tf_op jit(solution)/shard_map/all_to_all | solution.py:252
  69.7 26.1 %all-to-all-done.6.a0 = bf16[4,2,64,1152]{3,2,1,0:T(8,128)(2,1)S(1)} async-done(((bf16[4,2,64,1152]{3,2,1,0:T(8,128)(2,1)}), bf16[4,2,64,1152]{3,2,1,0:T(8,128)(2,1)S(1)}, u32[]{:S(2)}, u32[]{:S(2)}) %all-to-all-start.6) | async-done | bytes 1179680 | tf_op jit(solution)/shard_map/all_to_all | solution.py:152
  106.3 25.3 %all-to-all-done.3.a0 = bf16[4,2,24,3456]{3,2,1,0:T(8,128)(2,1)S(1)} async-done(((bf16[4,2,24,3456]{3,2,1,0:T(8,128)(2,1)}), bf16[4,2,24,3456]{3,2,1,0:T(8,128)(2,1)S(1)}, u32[]{:S(2)}, u32[]{:S(2)}) %all-to-all-start.3) | async-done | bytes 1327136 | tf_op jit(solution)/shard_map/all_to_all | solution.py:152
  160.2 5.6 collective-permute-done.6.ax
  169.3 12.2 collective-permute-done.15.a1
  184.0 26.1 %collective-permute-done.a1 = bf16[4,2,24,3456]{3,2,1,0:T(8,128)(2,1)S(1)} collective-permute-done((bf16[4,2,24,3456]{3,2,1,0:T(8,128)(2,1)S(1)}, bf16[4,2,24,3456]{3,2,1,0:T(8,128)(2,1)S(1)}, u32[]{:S(2)}, u32[]{:S(2)}) %collective-permute-start) | collective-permute-done | bytes 1327136 | tf_op jit(solution)/shard_map/ppermute | solution.py:155
  218.2 12.2 fusion.129
  230.9 11.1 collective-permute-done.1.ax
  244.3 5.4 fusion.40
  256.5 9.6 place.7
  273.0 13.2 %place.4 = bf16[4,2,2,3,24,3456]{5,4,3,2,1,0:T(8,128)(2,1)} custom-call(s32[3]{0:T(128)S(1)} %pad_add_fusion.6.where, bf16[4,2,24,3456]{3,2,1,0:T(8,128)(2,1)S(1)} %all-to-all-done.3.a0, bf16[4,2,24,3456]{3,2,1,0:T(8,128)(2,1)S(1)} %copy-done.2, bf16[4,2,24,3456]{3,2,1,0:T(8,128)(2,1)} %collective-permute-done.1.ax, ...), custom_call_target="tpu_custom_call" | custom-call | bytes 15925248 | tf_op jit(solution)/shard_map/place/pallas_call | solution.py:160
  286.2 13.2 %fusion.175 = f32[1024,3456]{1,0:T(8,128)S(1)} fusion(bf16[1024,1152]{1,0:T(8,128)(2,1)} %fusion.40, bf16[1152,3456]{1,0:T(8,128)(2,1)} %bitcast.414), kind=kOutput, calls=%fused_computation.419 | convolution fusion | flops 8153726976 | bytes 24477696 | tf_op jit(solution)/shard_map/dot_general | solution.py:15
  305.4 6.1 copy.109
  318.3 6.1 copy.108
  338.7 16.8 %fusion.173 = (f32[16,512]{1,0:T(8,128)S(1)}, f32[16,512,1024]{2,1,0:T(8,128)}) fusion(bf16[1024,16,18]{0,2,1:T(8,128)(2,1)} %get-tuple-element.90, bf16[1024,16,18]{0,2,1:T(8,128)(2,1)} %get-tuple-element.91, bf16[1024,16,18]{0,2,1:T(8,128)(2,1)S(1)} %get-tuple-element.74, bf16[1024,16,18]{0,2,1:T(8,128)(2,1)S(1)} %get-tuple-element.73, ...), kind=kOutput, calls=%fused_computation.417 | convolution fusion | flops 1242554368 | bytes 38043648 | tf_op jit(solution)/shard_map/qhd,khd->hqk/dot_general | solution.py:341
  355.5 16.4 %fusion.174 = (f32[16,512]{1,0:T(8,128)S(1)}, f32[16,512,1024]{2,1,0:T(8,128)}) fusion(bf16[1024,16,18]{0,2,1:T(8,128)(2,1)} %get-tuple-element.90, bf16[1024,16,18]{0,2,1:T(8,128)(2,1)} %get-tuple-element.91, bf16[1024,16,18]{0,2,1:T(8,128)(2,1)S(1)} %get-tuple-element.74, bf16[1024,16,18]{0,2,1:T(8,128)(2,1)S(1)} %get-tuple-element.73, ...), kind=kOutput, calls=%fused_computation.418 | convolution fusion | flops 1242554368 | bytes 38043648 | tf_op jit(solution)/shard_map/qhd,khd->hqk/dot_general | solution.py:341
  371.9 14.3 %fusion.1 = f32[16,512]{1,0:T(8,128)S(1)} fusion(f32[16,512,1024]{2,1,0:T(8,128)} %get-tuple-element.151, f32[16,512]{1,0:T(8,128)S(1)} %get-tuple-element.150), kind=kLoop, calls=%fused_computation.13 | loop fusion | flops 16769024 | bytes 33619968 | tf_op jit(solution)/shard_map/reduce_sum | solution.py:347
  386.2 12.9 %fusion.85 = bf16[16,72,512]{2,1,0:T(8,128)(2,1)S(1)} fusion(bf16[1024,16,72]{0,2,1:T(8,128)(2,1)S(1)} %bitcast.392, f32[16,512,1024]{2,1,0:T(8,128)} %get-tuple-element.151, f32[16,512]{1,0:T(8,128)S(1)} %fusion.1, f32[16,512]{1,0:T(8,128)S(1)} %get-tuple-element.150), kind=kOutput, calls=%fused_computation.203 | convolution fusion | flops 1233715200 | bytes 37158912 | tf_op jit(solution)/shard_map/hqk,khd->qhd/dot_general | solution.py:350
  399.2 14.7 %fusion = f32[16,512]{1,0:T(8,128)S(1)} fusion(f32[16,512,1024]{2,1,0:T(8,128)} %get-tuple-element.153, f32[16,512]{1,0:T(8,128)S(1)} %get-tuple-element.152), kind=kLoop, calls=%fused_computation.12 | loop fusion | flops 16769024 | bytes 33619968 | tf_op jit(solution)/shard_map/reduce_sum | solution.py:347
  414.0 14.1 %fusion.86 = bf16[16,72,512]{2,1,0:T(8,128)(2,1)S(1)} fusion(bf16[1024,16,72]{0,2,1:T(8,128)(2,1)S(1)} %bitcast.393, f32[16,512,1024]{2,1,0:T(8,128)} %get-tuple-element.153, f32[16,512]{1,0:T(8,128)S(1)} %fusion, f32[16,512]{1,0:T(8,128)S(1)} %get-tuple-element.152), kind=kOutput, calls=%fused_computation.204 | convolution fusion | flops 1233715200 | bytes 37158912 | tf_op jit(solution)/shard_map/hqk,khd->qhd/dot_general | solution.py:350
  428.2 9.7 fusion.165
  444.9 11.5 place.6
  456.4 22.6 %fusion.176 = f32[1024,6144]{1,0:T(8,128)} fusion(bf16[1024,1152]{1,0:T(8,128)(2,1)S(1)} %fusion.48, bf16[1152,6144]{1,0:T(8,128)(2,1)} %bitcast.406), kind=kOutput, calls=%fused_computation.420 | convolution fusion | flops 14495514624 | bytes 41680896 | tf_op jit(solution)/shard_map/dot_general | solution.py:15
  479.0 22.2 %fusion.14 = (bf16[1024,3072]{1,0:T(8,128)(2,1)}, bf16[1024,3072]{1,0:T(8,128)(2,1)}, bf16[1024,3072]{1,0:T(8,128)(2,1)}) fusion(f32[1024,6144]{1,0:T(8,128)} %fusion.176, bf16[1024,1152]{1,0:T(8,128)(2,1)} %get-tuple-element.51, bf16[3072,1152]{1,0:T(8,128)(2,1)S(1)} %bitcast.373), kind=kOutput, calls=%fused_computation.27 | convolution fusion | flops 7298088960 | bytes 53477376 | tf_op jit(solution)/shard_map/dot_general | solution.py:25
  501.2 27.0 %fusion.168 = (bf16[1024,1152]{1,0:T(8,128)(2,1)}, f32[1024]{0:T(1024)S(1)}, f32[1024,1152]{1,0:T(8,128)S(1)}) fusion(f32[1024,6912]{1,0:T(8,128)} %fusion.129, f32[1024,1152]{1,0:T(8,128)} %copy-done.11, f32[1024]{0:T(1024)S(1)} %broadcast_multiply_fusion, bf16[1152,6144]{1,0:T(8,128)(2,1)} %bitcast.407, bf16[1024,3072]{1,0:T(8,128)(2,1)} %get-tuple-element.49, ...), kind=kOutput, calls=%fused_computation.412 | convolution fusion | flops 14527757312 | bytes 43261952 | tf_op jit(solution)/shard_map/dot_general | solution.py:25
  528.2 22.9 %convolution_convert_fusion = bf16[1152,6144]{1,0:T(8,128)(2,1)} fusion(bf16[1024,1152]{1,0:T(8,128)(2,1)} %copy-done.38, bf16[1024,3072]{1,0:T(8,128)(2,1)} %get-tuple-element.49, bf16[1024,3072]{1,0:T(8,128)(2,1)} %get-tuple-element.48), kind=kOutput, calls=%fused_computation.16 | convolution fusion | flops 14527758336 | bytes 29097984 | tf_op jit(solution)/shard_map/dot_general | solution.py:19
  551.2 14.0 %fusion.177 = f32[1024,1152]{1,0:T(8,128)} fusion(bf16[1024,3072]{1,0:T(8,128)(2,1)} %get-tuple-element.52, bf16[3072,1152]{1,0:T(8,128)(2,1)} %bitcast.370), kind=kOutput, calls=%fused_computation.421 | convolution fusion | flops 7247757312 | bytes 18087936 | tf_op jit(solution)/shard_map/dot_general | solution.py:15
  565.3 8.7 fusion.164
  574.0 7.2 multiply_convert_fusion.5
  589.9 10.5 convolution_convert_fusion.2
  603.6 22.8 %multiply_reduce_fusion.1 = (f32[16,512]{1,0:T(8,128)}, f32[16,512,1024]{2,1,0:T(8,128)}) fusion(f32[16,512,1024]{2,1,0:T(8,128)} %get-tuple-element.153, f32[16,512]{1,0:T(8,128)} %log_add_fusion.1, bf16[512,16,72]{0,2,1:T(8,128)(2,1)S(1)} %bitcast.399, bf16[1024,16,72]{0,2,1:T(8,128)(2,1)S(1)} %bitcast.394), kind=kOutput, calls=%fused_computation.4 | convolution fusion | flops 1233117184 | bytes 70713344 | tf_op jit(solution)/shard_map/qhd,khd->hqk/dot_general | solution.py:411
  626.4 27.8 %multiply_convert_fusion.1 = bf16[16,512,1024]{2,1,0:T(8,128)(2,1)} fusion(f32[16,512,1024]{2,1,0:T(8,128)} %get-tuple-element.157, f32[16,512,1024]{2,1,0:T(8,128)} %get-tuple-element.153, f32[16,512]{1,0:T(8,128)} %get-tuple-element.156, f32[16,512]{1,0:T(8,128)} %log_add_fusion.1), kind=kLoop, calls=%fused_computation.3 | loop fusion | flops 33554432 | bytes 83951616 | tf_op jit(solution)/shard_map/convert_element_type | solution.py:415
  654.2 11.3 multiply_bitcast_fusion.2
  665.5 10.9 fusion.113
  678.8 15.9 %fusion.4 = f32[16,72,1024]{2,1,0:T(8,128)} fusion(bf16[512,16,72]{0,2,1:T(8,128)(2,1)} %bitcast.401, f32[16,512,1024]{2,1,0:T(8,128)} %get-tuple-element.151, f32[16,512]{1,0:T(8,128)} %log_add_fusion), kind=kOutput, calls=%fused_computation.18 | convolution fusion | flops 1224736768 | bytes 39485440 | tf_op jit(solution)/shard_map/hqk,qhd->khd/dot_general | solution.py:408
  694.7 23.0 %multiply_reduce_fusion = (f32[16,512]{1,0:T(8,128)}, f32[16,512,1024]{2,1,0:T(8,128)}) fusion(f32[16,512,1024]{2,1,0:T(8,128)} %get-tuple-element.151, f32[16,512]{1,0:T(8,128)S(1)} %copy-done.44, bf16[512,16,72]{0,2,1:T(8,128)(2,1)S(1)} %bitcast.402, bf16[1024,16,72]{0,2,1:T(8,128)(2,1)S(1)} %bitcast.395), kind=kOutput, calls=%fused_computation.1 | convolution fusion | flops 1233117184 | bytes 70713344 | tf_op jit(solution)/shard_map/qhd,khd->hqk/dot_general | solution.py:411
  717.7 16.1 %add_convert_fusion = bf16[16,72,1024]{2,1,0:T(8,128)(2,1)} fusion(f32[16,72,1024]{2,1,0:T(8,128)} %fusion.4, bf16[512,16,72]{0,2,1:T(8,128)(2,1)S(1)} %bitcast.400, f32[16,512,1024]{2,1,0:T(8,128)} %get-tuple-element.153, f32[16,512]{1,0:T(8,128)} %log_add_fusion.1), kind=kOutput, calls=%fused_computation.113 | convolution fusion | flops 1227096064 | bytes 41844736 | tf_op jit(solution)/shard_map/hqk,qhd->khd/dot_general | solution.py:408
  733.8 28.0 %multiply_convert_fusion = bf16[16,512,1024]{2,1,0:T(8,128)(2,1)} fusion(f32[16,512,1024]{2,1,0:T(8,128)} %get-tuple-element.159, f32[16,512,1024]{2,1,0:T(8,128)} %get-tuple-element.151, f32[16,512]{1,0:T(8,128)} %get-tuple-element.158, f32[16,512]{1,0:T(8,128)S(1)} %copy-done.45), kind=kLoop, calls=%fused_computation | loop fusion | flops 33554432 | bytes 83951616 | tf_op jit(solution)/shard_map/convert_element_type | solution.py:415
  761.8 9.4 multiply_bitcast_fusion.1
  771.3 10.4 multiply_bitcast_fusion
  798.6 17.5 %fusion.169 = (bf16[1024,1152]{1,0:T(8,128)(2,1)}, f32[1024]{0:T(1024)S(1)}, f32[1024,1152]{1,0:T(8,128)}) fusion(f32[1024,6912]{1,0:T(8,128)} %fusion.129, f32[1024]{0:T(1024)S(1)} %copy-done.71, bf16[1,1024,1152]{2,1,0:T(8,128)(2,1)S(1)} %copy-done.15, bf16[1152,3456]{1,0:T(8,128)(2,1)} %bitcast.415, bf16[1024,1152]{0,1:T(8,128)(2,1)} %bitcast.420, ...), kind=kOutput, calls=%fused_computation.413 | convolution fusion | flops 8183217152 | bytes 29204480 | tf_op jit(solution)/shard_map/dot_general | solution.py:25
  816.1 14.5 %convolution_convert_fusion.1 = bf16[1152,3456]{1,0:T(8,128)(2,1)} fusion(bf16[1024,1152]{1,0:T(8,128)(2,1)} %fusion.40, bf16[1024,1152]{0,1:T(8,128)(2,1)} %bitcast.421, bf16[1024,1152]{0,1:T(8,128)(2,1)} %bitcast.426, bf16[1024,1152]{0,1:T(8,128)(2,1)} %bitcast.424), kind=kOutput, calls=%fused_computation.24 | convolution fusion | flops 8178941952 | bytes 17399808 | tf_op jit(solution)/shard_map/dot_general | solution.py:19
  833.2 5.5 dynamic-slice_bitcast_fusion.2
  841.2 8.3 dynamic-slice_bitcast_fusion
  853.1 6.5 fusion.163
  861.3 5.7 all-to-all-start.7
  867.0 5.8 dynamic-slice_bitcast_fusion.1
  881.9 5.7 all-to-all-start.8
  888.8 6.8 add_bitcast_fusion
  928.9 6.5 collective-permute-done.32
  938.2 6.1 collective-permute-done.33
  949.2 11.6 collective-permute-done.25
  978.7 16.2 %collective-permute-done.42 = bf16[4,2,64,1152]{3,2,1,0:T(8,128)(2,1)S(1)} collective-permute-done((bf16[4,2,64,1152]{3,2,1,0:T(8,128)(2,1)S(1)}, bf16[4,2,64,1152]{3,2,1,0:T(8,128)(2,1)S(1)}, u32[]{:S(2)}, u32[]{:S(2)}) %collective-permute-start.42) | collective-permute-done | bytes 1179680 | tf_op jit(solution)/shard_map/ppermute | solution.py:190
  997.7 25.6 %collective-permute-done.27 = bf16[4,2,24,3456]{3,2,1,0:T(8,128)(2,1)S(1)} collective-permute-done((bf16[4,2,24,3456]{3,2,1,0:T(8,128)(2,1)S(1)}, bf16[4,2,24,3456]{3,2,1,0:T(8,128)(2,1)S(1)}, u32[]{:S(2)}, u32[]{:S(2)}) %collective-permute-start.27) | collective-permute-done | bytes 1327136 | tf_op jit(solution)/shard_map/ppermute | solution.py:190
  1043.0 10.0 collective-permute-done.28
  1058.9 35.4 %collective-permute-done.37 = bf16[4,2,24,6144]{3,2,1,0:T(8,128)(2,1)S(1)} collective-permute-done((bf16[4,2,24,6144]{3,2,1,0:T(8,128)(2,1)S(1)}, bf16[4,2,24,6144]{3,2,1,0:T(8,128)(2,1)S(1)}, u32[]{:S(2)}, u32[]{:S(2)}) %collective-permute-start.37) | collective-permute-done | bytes 2359328 | tf_op jit(solution)/shard_map/ppermute | solution.py:190
  1117.2 19.3 %all-to-all-done.10 = bf16[4,2,24,3456]{3,2,1,0:T(8,128)(2,1)} async-done(((bf16[4,2,24,3456]{3,2,1,0:T(8,128)(2,1)}), bf16[4,2,24,3456]{3,2,1,0:T(8,128)(2,1)}, u32[]{:S(2)}, u32[]{:S(2)}) %all-to-all-start.10) | async-done | bytes 1327136 | tf_op jit(solution)/shard_map/all_to_all | solution.py:196
  1139.3 12.6 %collective-permute-done.38 = bf16[4,2,24,6144]{3,2,1,0:T(8,128)(2,1)} collective-permute-done((bf16[4,2,24,6144]{3,2,1,0:T(8,128)(2,1)}, bf16[4,2,24,6144]{3,2,1,0:T(8,128)(2,1)}, u32[]{:S(2)}, u32[]{:S(2)}) %collective-permute-start.38) | collective-permute-done | bytes 2359328 | tf_op jit(solution)/shard_map/ppermute | solution.py:194
  1168.1 45.2 %all-to-all-done.12 = bf16[4,2,24,6144]{3,2,1,0:T(8,128)(2,1)S(1)} async-done(((bf16[4,2,24,6144]{3,2,1,0:T(8,128)(2,1)}), bf16[4,2,24,6144]{3,2,1,0:T(8,128)(2,1)S(1)}, u32[]{:S(2)}, u32[]{:S(2)}) %all-to-all-start.12) | async-done | bytes 2359328 | tf_op jit(solution)/shard_map/all_to_all | solution.py:196
  1216.4 10.9 collective-permute-done.39
  (506 shorter events, 324.6 us)
Async XLA Ops:
  2.1 11.9 all-to-all-start
  17.7 10.8 all-to-all-start.1
  29.4 13.9 %all-to-all-start.4 = ((bf16[4,2,24,1152]{3,2,1,0:T(8,128)(2,1)}), bf16[4,2,24,1152]{3,2,1,0:T(8,128)(2,1)S(1)}, u32[]{:S(2)}, u32[]{:S(2)}) async-start(bf16[4,2,24,1152]{3,2,1,0:T(8,128)(2,1)} %broadcast_in_dim.62), calls=%async_computation.4 | async-start | bytes 884736 | tf_op jit(solution)/shard_map/all_to_all | solution.py:152
  43.3 19.7 %all-to-all-start.2 = ((bf16[8,8,4608]{2,1,0:T(8,128)(2,1)}), bf16[8,8,4608]{2,1,0:T(8,128)(2,1)S(1)}, u32[]{:S(2)}, u32[]{:S(2)}) async-start(bf16[8,8,4608]{2,1,0:T(8,128)(2,1)} %slice_bitcast_fusion.3), calls=%async_computation.2 | async-start | bytes 1179648 | tf_op jit(solution)/shard_map/all_to_all | solution.py:252
  64.2 31.5 %all-to-all-start.6 = ((bf16[4,2,64,1152]{3,2,1,0:T(8,128)(2,1)}), bf16[4,2,64,1152]{3,2,1,0:T(8,128)(2,1)S(1)}, u32[]{:S(2)}, u32[]{:S(2)}) async-start(bf16[4,2,64,1152]{3,2,1,0:T(8,128)(2,1)} %broadcast_in_dim.64), calls=%async_computation.6 | async-start | bytes 2359296 | tf_op jit(solution)/shard_map/all_to_all | solution.py:152
  67.8 176.5 %copy-start.70 = (f32[1024]{0:T(1024)}, f32[1024]{0:T(1024)S(1)}, u32[]{:S(2)}) copy-start(f32[1024]{0:T(1024)S(1)} %broadcast_multiply_fusion.1) | copy-start | bytes 12292
  96.9 34.7 %all-to-all-start.3 = ((bf16[4,2,24,3456]{3,2,1,0:T(8,128)(2,1)}), bf16[4,2,24,3456]{3,2,1,0:T(8,128)(2,1)S(1)}, u32[]{:S(2)}, u32[]{:S(2)}) async-start(bf16[4,2,24,3456]{3,2,1,0:T(8,128)(2,1)} %broadcast_in_dim.57), calls=%async_computation.3 | async-start | bytes 2654208 | tf_op jit(solution)/shard_map/all_to_all | solution.py:152
  101.9 233.1 %copy-start.27 = (f32[1024,18]{0,1:T(8,128)}, f32[1024,18]{0,1:T(8,128)S(1)}, u32[]{:S(2)}) copy-start(f32[1024,18]{0,1:T(8,128)S(1)} %get-tuple-element.136) | copy-start | bytes 221188
  134.3 79.1 %all-to-all-start.5 = ((bf16[4,2,24,6144]{3,2,1,0:T(8,128)(2,1)}), bf16[4,2,24,6144]{3,2,1,0:T(8,128)(2,1)}, u32[]{:S(2)}, u32[]{:S(2)}) async-start(bf16[4,2,24,6144]{3,2,1,0:T(8,128)(2,1)} %broadcast_in_dim.63), calls=%async_computation.5 | async-start | bytes 4718592 | tf_op jit(solution)/shard_map/all_to_all | solution.py:152
  140.7 2.3 collective-permute-start.20
  143.7 3.7 collective-permute-start.21
  145.0 185.7 %copy-start.86 = (f32[72]{0:T(128)}, f32[72]{0:T(128)S(1)}, u32[]{:S(2)}) copy-start(f32[72]{0:T(128)S(1)} %convert_element_type.528) | copy-start | bytes 868
  145.1 182.3 %copy-start.84 = (f32[72]{0:T(128)}, f32[72]{0:T(128)S(1)}, u32[]{:S(2)}) copy-start(f32[72]{0:T(128)S(1)} %convert_element_type.531) | copy-start | bytes 868
  145.1 11.3 collective-permute-start.5
  149.0 32.5 %collective-permute-start.15 = (bf16[4,2,64,1152]{3,2,1,0:T(8,128)(2,1)S(1)}, bf16[4,2,64,1152]{3,2,1,0:T(8,128)(2,1)S(1)}, u32[]{:S(2)}, u32[]{:S(2)}) collective-permute-start(bf16[4,2,64,1152]{3,2,1,0:T(8,128)(2,1)S(1)} %all-to-all-done.6.a0), channel_id=1, source_target_pairs={{0,1},{1,0},{2,3},{3,2},{4,5},{5,4},{6,7},{7,6},{8,9},{9,8},{10,11... | collective-permute-start | bytes 3538952 | tf_op jit(solution)/shard_map/ppermute | solution.py:155
  151.3 61.4 %collective-permute-start.7 = (bf16[4,2,24,1152]{3,2,1,0:T(8,128)(2,1)S(1)}, bf16[4,2,24,1152]{3,2,1,0:T(8,128)(2,1)S(1)}, u32[]{:S(2)}, u32[]{:S(2)}) collective-permute-start(bf16[4,2,24,1152]{3,2,1,0:T(8,128)(2,1)S(1)} %all-to-all-done.4.a0), channel_id=1, source_target_pairs={{0,8},{1,9},{2,10},{3,11},{4,12},{5,13},{6,14},{7,15},{8,0},{9,1},... | collective-permute-start | bytes 1327112 | tf_op jit(solution)/shard_map/ppermute | solution.py:158
  152.9 57.2 %collective-permute-start = (bf16[4,2,24,3456]{3,2,1,0:T(8,128)(2,1)S(1)}, bf16[4,2,24,3456]{3,2,1,0:T(8,128)(2,1)S(1)}, u32[]{:S(2)}, u32[]{:S(2)}) collective-permute-start(bf16[4,2,24,3456]{3,2,1,0:T(8,128)(2,1)S(1)} %all-to-all-done.3.a0), channel_id=1, source_target_pairs={{0,1},{1,0},{2,3},{3,2},{4,5},{5,4},{6,7},{7,6},{8,9},{9,8},{10,11... | collective-permute-start | bytes 3981320 | tf_op jit(solution)/shard_map/ppermute | solution.py:155
  156.5 9.3 collective-permute-start.6
  157.4 58.2 %collective-permute-start.8 = (bf16[4,2,24,1152]{3,2,1,0:T(8,128)(2,1)S(1)}, bf16[4,2,24,1152]{3,2,1,0:T(8,128)(2,1)}, u32[]{:S(2)}, u32[]{:S(2)}) collective-permute-start(bf16[4,2,24,1152]{3,2,1,0:T(8,128)(2,1)S(1)} %collective-permute-done.5.a1), channel_id=1, source_target_pairs={{0,8},{1,9},{2,10},{3,11},{4,12},{5,13},{6,14},{7,15},{8,0},{9,1},... | collective-permute-start | bytes 1327112 | tf_op jit(solution)/shard_map/ppermute | solution.py:158
  165.8 51.9 %collective-permute-start.9 = (bf16[4,2,24,1152]{3,2,1,0:T(8,128)(2,1)}, bf16[4,2,24,1152]{3,2,1,0:T(8,128)(2,1)}, u32[]{:S(2)}, u32[]{:S(2)}) collective-permute-start(bf16[4,2,24,1152]{3,2,1,0:T(8,128)(2,1)} %collective-permute-done.6.ax), channel_id=1, source_target_pairs={{0,8},{1,9},{2,10},{3,11},{4,12},{5,13},{6,14},{7,15},{8,0},{9,1},... | collective-permute-start | bytes 1327112 | tf_op jit(solution)/shard_map/ppermute | solution.py:158
  183.8 34.0 %collective-permute-start.16 = (bf16[4,2,64,1152]{3,2,1,0:T(8,128)(2,1)}, bf16[4,2,64,1152]{3,2,1,0:T(8,128)(2,1)}, u32[]{:S(2)}, u32[]{:S(2)}) collective-permute-start(bf16[4,2,64,1152]{3,2,1,0:T(8,128)(2,1)} %pad_maximum_fusion.19), channel_id=1, source_target_pairs={{0,16},{1,17},{2,18},{3,19},{4,20},{5,21},{6,22},{7,23},{8,24},{9,... | collective-permute-start | bytes 3538952 | tf_op jit(solution)/shard_map/ppermute | solution.py:156
  212.4 29.5 %collective-permute-start.1 = (bf16[4,2,24,3456]{3,2,1,0:T(8,128)(2,1)}, bf16[4,2,24,3456]{3,2,1,0:T(8,128)(2,1)}, u32[]{:S(2)}, u32[]{:S(2)}) collective-permute-start(bf16[4,2,24,3456]{3,2,1,0:T(8,128)(2,1)} %pad_maximum_fusion.17), channel_id=1, source_target_pairs={{0,16},{1,17},{2,18},{3,19},{4,20},{5,21},{6,22},{7,23},{8,24},{9,... | collective-permute-start | bytes 3981320 | tf_op jit(solution)/shard_map/ppermute | solution.py:156
  213.4 55.6 %collective-permute-start.10 = (bf16[4,2,24,6144]{3,2,1,0:T(8,128)(2,1)}, bf16[4,2,24,6144]{3,2,1,0:T(8,128)(2,1)}, u32[]{:S(2)}, u32[]{:S(2)}) collective-permute-start(bf16[4,2,24,6144]{3,2,1,0:T(8,128)(2,1)} %all-to-all-done.5.a0), channel_id=1, source_target_pairs={{0,1},{1,0},{2,3},{3,2},{4,5},{5,4},{6,7},{7,6},{8,9},{9,8},{10,11... | collective-permute-start | bytes 7077896 | tf_op jit(solution)/shard_map/ppermute | solution.py:155
  215.7 14.7 %collective-permute-start.17 = (bf16[4,2,64,1152]{3,2,1,0:T(8,128)(2,1)S(1)}, bf16[4,2,64,1152]{3,2,1,0:T(8,128)(2,1)S(1)}, u32[]{:S(2)}, u32[]{:S(2)}) collective-permute-start(bf16[4,2,64,1152]{3,2,1,0:T(8,128)(2,1)S(1)} %all-to-all-done.6.a0), channel_id=1, source_target_pairs={{0,8},{1,9},{2,10},{3,11},{4,12},{5,13},{6,14},{7,15},{8,0},{9,1},... | collective-permute-start | bytes 3538952 | tf_op jit(solution)/shard_map/ppermute | solution.py:158
  217.7 13.1 %collective-permute-start.18 = (bf16[4,2,64,1152]{3,2,1,0:T(8,128)(2,1)}, bf16[4,2,64,1152]{3,2,1,0:T(8,128)(2,1)S(1)}, u32[]{:S(2)}, u32[]{:S(2)}) collective-permute-start(bf16[4,2,64,1152]{3,2,1,0:T(8,128)(2,1)} %copy-done.6), channel_id=1, source_target_pairs={{0,8},{1,9},{2,10},{3,11},{4,12},{5,13},{6,14},{7,15},{8,0},{9,1},... | collective-permute-start | bytes 3538952 | tf_op jit(solution)/shard_map/ppermute | solution.py:158
  217.8 38.6 %collective-permute-start.19 = (bf16[4,2,64,1152]{3,2,1,0:T(8,128)(2,1)}, bf16[4,2,64,1152]{3,2,1,0:T(8,128)(2,1)S(1)}, u32[]{:S(2)}, u32[]{:S(2)}) collective-permute-start(bf16[4,2,64,1152]{3,2,1,0:T(8,128)(2,1)} %collective-permute-done.16.ax), channel_id=1, source_target_pairs={{0,8},{1,9},{2,10},{3,11},{4,12},{5,13},{6,14},{7,15},{8,0},{9,1},... | collective-permute-start | bytes 3538952 | tf_op jit(solution)/shard_map/ppermute | solution.py:158
  230.4 41.9 %collective-permute-start.2 = (bf16[4,2,24,3456]{3,2,1,0:T(8,128)(2,1)S(1)}, bf16[4,2,24,3456]{3,2,1,0:T(8,128)(2,1)S(1)}, u32[]{:S(2)}, u32[]{:S(2)}) collective-permute-start(bf16[4,2,24,3456]{3,2,1,0:T(8,128)(2,1)S(1)} %all-to-all-done.3.a0), channel_id=1, source_target_pairs={{0,8},{1,9},{2,10},{3,11},{4,12},{5,13},{6,14},{7,15},{8,0},{9,1},... | collective-permute-start | bytes 3981320 | tf_op jit(solution)/shard_map/ppermute | solution.py:158
  230.8 42.2 %collective-permute-start.3 = (bf16[4,2,24,3456]{3,2,1,0:T(8,128)(2,1)S(1)}, bf16[4,2,24,3456]{3,2,1,0:T(8,128)(2,1)S(1)}, u32[]{:S(2)}, u32[]{:S(2)}) collective-permute-start(bf16[4,2,24,3456]{3,2,1,0:T(8,128)(2,1)S(1)} %copy-done.2), channel_id=1, source_target_pairs={{0,8},{1,9},{2,10},{3,11},{4,12},{5,13},{6,14},{7,15},{8,0},{9,1},... | collective-permute-start | bytes 3981320 | tf_op jit(solution)/shard_map/ppermute | solution.py:158
  241.9 31.1 %collective-permute-start.4 = (bf16[4,2,24,3456]{3,2,1,0:T(8,128)(2,1)}, bf16[4,2,24,3456]{3,2,1,0:T(8,128)(2,1)S(1)}, u32[]{:S(2)}, u32[]{:S(2)}) collective-permute-start(bf16[4,2,24,3456]{3,2,1,0:T(8,128)(2,1)} %collective-permute-done.1.ax), channel_id=1, source_target_pairs={{0,8},{1,9},{2,10},{3,11},{4,12},{5,13},{6,14},{7,15},{8,0},{9,1},... | collective-permute-start | bytes 3981320 | tf_op jit(solution)/shard_map/ppermute | solution.py:158
  256.4 188.5 %collective-permute-start.12 = (bf16[4,2,24,6144]{3,2,1,0:T(8,128)(2,1)}, bf16[4,2,24,6144]{3,2,1,0:T(8,128)(2,1)}, u32[]{:S(2)}, u32[]{:S(2)}) collective-permute-start(bf16[4,2,24,6144]{3,2,1,0:T(8,128)(2,1)} %all-to-all-done.5.a0), channel_id=1, source_target_pairs={{0,8},{1,9},{2,10},{3,11},{4,12},{5,13},{6,14},{7,15},{8,0},{9,1},... | collective-permute-start | bytes 7077896 | tf_op jit(solution)/shard_map/ppermute | solution.py:158
  272.0 156.1 %collective-permute-start.11 = (bf16[4,2,24,6144]{3,2,1,0:T(8,128)(2,1)}, bf16[4,2,24,6144]{3,2,1,0:T(8,128)(2,1)}, u32[]{:S(2)}, u32[]{:S(2)}) collective-permute-start(bf16[4,2,24,6144]{3,2,1,0:T(8,128)(2,1)} %pad_maximum_fusion.10), channel_id=1, source_target_pairs={{0,16},{1,17},{2,18},{3,19},{4,20},{5,21},{6,22},{7,23},{8,24},{9,... | collective-permute-start | bytes 7077896 | tf_op jit(solution)/shard_map/ppermute | solution.py:156
  272.3 172.6 %collective-permute-start.13 = (bf16[4,2,24,6144]{3,2,1,0:T(8,128)(2,1)}, bf16[4,2,24,6144]{3,2,1,0:T(8,128)(2,1)}, u32[]{:S(2)}, u32[]{:S(2)}) collective-permute-start(bf16[4,2,24,6144]{3,2,1,0:T(8,128)(2,1)} %collective-permute-done.10.a1), channel_id=1, source_target_pairs={{0,8},{1,9},{2,10},{3,11},{4,12},{5,13},{6,14},{7,15},{8,0},{9,1},... | collective-permute-start | bytes 7077896 | tf_op jit(solution)/shard_map/ppermute | solution.py:158
  428.1 16.8 %collective-permute-start.14 = (bf16[4,2,24,6144]{3,2,1,0:T(8,128)(2,1)}, bf16[4,2,24,6144]{3,2,1,0:T(8,128)(2,1)S(1)}, u32[]{:S(2)}, u32[]{:S(2)}) collective-permute-start(bf16[4,2,24,6144]{3,2,1,0:T(8,128)(2,1)} %collective-permute-done.11.ax), channel_id=1, source_target_pairs={{0,8},{1,9},{2,10},{3,11},{4,12},{5,13},{6,14},{7,15},{8,0},{9,1},... | collective-permute-start | bytes 7077896 | tf_op jit(solution)/shard_map/ppermute | solution.py:158
  833.0 83.1 %collective-permute-start.31 = (bf16[4,2,3,24,1152]{4,3,1,0,2:T(8,128)(2,1)}, bf16[4,2,3,24,1152]{4,3,1,0,2:T(8,128)(2,1)}, u32[]{:S(2)}, u32[]{:S(2)}) collective-permute-start(bf16[4,2,3,24,1152]{4,3,1,0,2:T(8,128)(2,1)} %bitcast.369), channel_id=1, source_target_pairs={{0,8},{1,9},{2,10},{3,11},{4,12},{5,13},{6,14},{7,15},{8,0},{9,1},... | collective-permute-start | bytes 3981320 | tf_op jit(solution)/shard_map/ppermute | solution.py:183
  840.9 128.3 %collective-permute-start.41 = (bf16[4,2,3,64,1152]{4,3,1,0,2:T(8,128)(2,1)}, bf16[4,2,3,64,1152]{4,3,1,0,2:T(8,128)(2,1)}, u32[]{:S(2)}, u32[]{:S(2)}) collective-permute-start(bf16[4,2,3,64,1152]{4,3,1,0,2:T(8,128)(2,1)} %bitcast.368), channel_id=1, source_target_pairs={{0,8},{1,9},{2,10},{3,11},{4,12},{5,13},{6,14},{7,15},{8,0},{9,1},... | collective-permute-start | bytes 10616840 | tf_op jit(solution)/shard_map/ppermute | solution.py:183
  852.8 185.7 %collective-permute-start.36 = (bf16[4,2,3,24,6144]{4,3,1,0,2:T(8,128)(2,1)}, bf16[4,2,3,24,6144]{4,3,1,0,2:T(8,128)(2,1)}, u32[]{:S(2)}, u32[]{:S(2)}) collective-permute-start(bf16[4,2,3,24,6144]{4,3,1,0,2:T(8,128)(2,1)} %bitcast.416), channel_id=1, source_target_pairs={{0,8},{1,9},{2,10},{3,11},{4,12},{5,13},{6,14},{7,15},{8,0},{9,1},... | collective-permute-start | bytes 21233672 | tf_op jit(solution)/shard_map/ppermute | solution.py:183
  861.3 19.7 %all-to-all-start.7 = ((bf16[8,8,2560]{2,1,0:T(8,128)(2,1)}), bf16[8,8,2560]{2,1,0:T(8,128)(2,1)S(1)}, u32[]{:S(2)}, u32[]{:S(2)}) async-start(bf16[8,8,2560]{2,1,0:T(8,128)(2,1)} %broadcast_in_dim.128), calls=%async_computation.7 | async-start | bytes 655360 | tf_op jit(solution)/shard_map/all_to_all | solution.py:230
  875.1 99.2 %collective-permute-start.26 = (bf16[4,2,3,24,3456]{4,3,1,0,2:T(8,128)(2,1)}, bf16[4,2,3,24,3456]{4,3,1,0,2:T(8,128)(2,1)}, u32[]{:S(2)}, u32[]{:S(2)}) collective-permute-start(bf16[4,2,3,24,3456]{4,3,1,0,2:T(8,128)(2,1)} %bitcast.367), channel_id=1, source_target_pairs={{0,8},{1,9},{2,10},{3,11},{4,12},{5,13},{6,14},{7,15},{8,0},{9,1},... | collective-permute-start | bytes 11943944 | tf_op jit(solution)/shard_map/ppermute | solution.py:183
  881.9 20.1 %all-to-all-start.8 = ((bf16[8,8,4608]{2,1,0:T(8,128)(2,1)}), bf16[8,8,4608]{2,1,0:T(8,128)(2,1)S(1)}, u32[]{:S(2)}, u32[]{:S(2)}) async-start(bf16[8,8,4608]{2,1,0:T(8,128)(2,1)} %broadcast_in_dim.129), calls=%async_computation.8 | async-start | bytes 1179648 | tf_op jit(solution)/shard_map/all_to_all | solution.py:230
  887.6 9.5 collective-permute-start.22
  904.5 10.8 all-to-all-start.9
  909.8 15.5 %collective-permute-start.23 = (bf16[2,64,2560]{2,1,0:T(8,128)(2,1)S(1)}, bf16[2,64,2560]{2,1,0:T(8,128)(2,1)S(1)}, u32[]{:S(2)}, u32[]{:S(2)}) collective-permute-start(bf16[2,64,2560]{2,1,0:T(8,128)(2,1)S(1)} %pad_maximum_fusion.24), channel_id=1, source_target_pairs={{0,16},{1,17},{2,18},{3,19},{4,20},{5,21},{6,22},{7,23},{8,24},{9,... | collective-permute-start | bytes 1966088 | tf_op jit(solution)/shard_map/ppermute | solution.py:237
  916.1 11.4 collective-permute-start.24
  925.4 10.0 collective-permute-start.32
  928.7 32.1 %collective-permute-start.25 = (bf16[2,64,4608]{2,1,0:T(8,128)(2,1)}, bf16[2,64,4608]{2,1,0:T(8,128)(2,1)}, u32[]{:S(2)}, u32[]{:S(2)}) collective-permute-start(bf16[2,64,4608]{2,1,0:T(8,128)(2,1)} %pad_maximum_fusion.20), channel_id=1, source_target_pairs={{0,16},{1,17},{2,18},{3,19},{4,20},{5,21},{6,22},{7,23},{8,24},{9,... | collective-permute-start | bytes 3538952 | tf_op jit(solution)/shard_map/ppermute | solution.py:237
  936.8 7.6 collective-permute-start.33
  945.3 20.1 %all-to-all-start.11 = ((bf16[4,2,24,1152]{3,2,1,0:T(8,128)(2,1)}), bf16[4,2,24,1152]{3,2,1,0:T(8,128)(2,1)S(1)}, u32[]{:S(2)}, u32[]{:S(2)}) async-start(bf16[4,2,24,1152]{3,2,1,0:T(8,128)(2,1)} %fusion.116), calls=%async_computation.11 | async-start | bytes 884736 | tf_op jit(solution)/shard_map/all_to_all | solution.py:196
  965.4 3.7 collective-permute-start.34
  971.1 23.8 %collective-permute-start.42 = (bf16[4,2,64,1152]{3,2,1,0:T(8,128)(2,1)S(1)}, bf16[4,2,64,1152]{3,2,1,0:T(8,128)(2,1)S(1)}, u32[]{:S(2)}, u32[]{:S(2)}) collective-permute-start(bf16[4,2,64,1152]{3,2,1,0:T(8,128)(2,1)S(1)} %fusion.77), channel_id=1, source_target_pairs={{0,16},{1,17},{2,18},{3,19},{4,20},{5,21},{6,22},{7,23},{8,24},{9,... | collective-permute-start | bytes 3538952 | tf_op jit(solution)/shard_map/ppermute | solution.py:190
  976.3 47.0 %collective-permute-start.27 = (bf16[4,2,24,3456]{3,2,1,0:T(8,128)(2,1)S(1)}, bf16[4,2,24,3456]{3,2,1,0:T(8,128)(2,1)S(1)}, u32[]{:S(2)}, u32[]{:S(2)}) collective-permute-start(bf16[4,2,24,3456]{3,2,1,0:T(8,128)(2,1)S(1)} %fusion.66), channel_id=1, source_target_pairs={{0,16},{1,17},{2,18},{3,19},{4,20},{5,21},{6,22},{7,23},{8,24},{9,... | collective-permute-start | bytes 3981320 | tf_op jit(solution)/shard_map/ppermute | solution.py:190
  997.1 35.6 %collective-permute-start.43 = (bf16[4,2,64,1152]{3,2,1,0:T(8,128)(2,1)S(1)}, bf16[4,2,64,1152]{3,2,1,0:T(8,128)(2,1)S(1)}, u32[]{:S(2)}, u32[]{:S(2)}) collective-permute-start(bf16[4,2,64,1152]{3,2,1,0:T(8,128)(2,1)S(1)} %fusion.97), channel_id=1, source_target_pairs={{0,1},{1,0},{2,3},{3,2},{4,5},{5,4},{6,7},{7,6},{8,9},{9,8},{10,11... | collective-permute-start | bytes 3538952 | tf_op jit(solution)/shard_map/ppermute | solution.py:194
  1026.8 26.3 %collective-permute-start.28 = (bf16[4,2,24,3456]{3,2,1,0:T(8,128)(2,1)}, bf16[4,2,24,3456]{3,2,1,0:T(8,128)(2,1)}, u32[]{:S(2)}, u32[]{:S(2)}) collective-permute-start(bf16[4,2,24,3456]{3,2,1,0:T(8,128)(2,1)} %fusion.90), channel_id=1, source_target_pairs={{0,1},{1,0},{2,3},{3,2},{4,5},{5,4},{6,7},{7,6},{8,9},{9,8},{10,11... | collective-permute-start | bytes 3981320 | tf_op jit(solution)/shard_map/ppermute | solution.py:194
  1027.3 77.9 %collective-permute-start.35 = (bf16[3,24,1152]{2,1,0:T(8,128)(2,1)S(1)}, bf16[3,24,1152]{2,1,0:T(8,128)(2,1)S(1)}, u32[]{:S(2)}, u32[]{:S(2)}) collective-permute-start(bf16[3,24,1152]{2,1,0:T(8,128)(2,1)S(1)} %pad_maximum_fusion.33), channel_id=1, source_target_pairs={{0,8},{1,9},{2,10},{3,11},{4,12},{5,13},{6,14},{7,15},{8,0},{9,1},... | collective-permute-start | bytes 497672 | tf_op jit(solution)/shard_map/ppermute | solution.py:203
  1034.0 67.0 %all-to-all-start.13 = ((bf16[4,2,64,1152]{3,2,1,0:T(8,128)(2,1)}), bf16[4,2,64,1152]{3,2,1,0:T(8,128)(2,1)}, u32[]{:S(2)}, u32[]{:S(2)}) async-start(bf16[4,2,64,1152]{3,2,1,0:T(8,128)(2,1)} %fusion.75), calls=%async_computation.13 | async-start | bytes 2359296 | tf_op jit(solution)/shard_map/all_to_all | solution.py:196
  1041.7 52.6 %collective-permute-start.37 = (bf16[4,2,24,6144]{3,2,1,0:T(8,128)(2,1)S(1)}, bf16[4,2,24,6144]{3,2,1,0:T(8,128)(2,1)S(1)}, u32[]{:S(2)}, u32[]{:S(2)}) collective-permute-start(bf16[4,2,24,6144]{3,2,1,0:T(8,128)(2,1)S(1)} %fusion.55), channel_id=1, source_target_pairs={{0,16},{1,17},{2,18},{3,19},{4,20},{5,21},{6,22},{7,23},{8,24},{9,... | collective-permute-start | bytes 7077896 | tf_op jit(solution)/shard_map/ppermute | solution.py:190
  1100.0 51.9 %collective-permute-start.38 = (bf16[4,2,24,6144]{3,2,1,0:T(8,128)(2,1)}, bf16[4,2,24,6144]{3,2,1,0:T(8,128)(2,1)}, u32[]{:S(2)}, u32[]{:S(2)}) collective-permute-start(bf16[4,2,24,6144]{3,2,1,0:T(8,128)(2,1)} %fusion.72), channel_id=1, source_target_pairs={{0,1},{1,0},{2,3},{3,2},{4,5},{5,4},{6,7},{7,6},{8,9},{9,8},{10,11... | collective-permute-start | bytes 7077896 | tf_op jit(solution)/shard_map/ppermute | solution.py:194
  1100.9 35.6 %all-to-all-start.10 = ((bf16[4,2,24,3456]{3,2,1,0:T(8,128)(2,1)}), bf16[4,2,24,3456]{3,2,1,0:T(8,128)(2,1)}, u32[]{:S(2)}, u32[]{:S(2)}) async-start(bf16[4,2,24,3456]{3,2,1,0:T(8,128)(2,1)} %fusion.64), calls=%async_computation.10 | async-start | bytes 2654208 | tf_op jit(solution)/shard_map/all_to_all | solution.py:196
  1106.8 7.1 collective-permute-start.44
  1114.9 45.1 %collective-permute-start.45 = (bf16[3,64,1152]{2,1,0:T(8,128)(2,1)}, bf16[3,64,1152]{2,1,0:T(8,128)(2,1)}, u32[]{:S(2)}, u32[]{:S(2)}) collective-permute-start(bf16[3,64,1152]{2,1,0:T(8,128)(2,1)} %pad_maximum_fusion.28), channel_id=1, source_target_pairs={{0,8},{1,9},{2,10},{3,11},{4,12},{5,13},{6,14},{7,15},{8,0},{9,1},... | collective-permute-start | bytes 1327112 | tf_op jit(solution)/shard_map/ppermute | solution.py:203
  1138.1 23.2 %collective-permute-start.29 = (bf16[2,24,3456]{2,1,0:T(8,128)(2,1)S(1)}, bf16[2,24,3456]{2,1,0:T(8,128)(2,1)}, u32[]{:S(2)}, u32[]{:S(2)}) collective-permute-start(bf16[2,24,3456]{2,1,0:T(8,128)(2,1)S(1)} %reduce_sum.342), channel_id=1, source_target_pairs={{0,16},{1,17},{2,18},{3,19},{4,20},{5,21},{6,22},{7,23},{8,24},{9,... | collective-permute-start | bytes 995336 | tf_op jit(solution)/shard_map/ppermute | solution.py:198
  1156.1 57.2 %all-to-all-start.12 = ((bf16[4,2,24,6144]{3,2,1,0:T(8,128)(2,1)}), bf16[4,2,24,6144]{3,2,1,0:T(8,128)(2,1)S(1)}, u32[]{:S(2)}, u32[]{:S(2)}) async-start(bf16[4,2,24,6144]{3,2,1,0:T(8,128)(2,1)} %fusion.53), calls=%async_computation.12 | async-start | bytes 4718592 | tf_op jit(solution)/shard_map/all_to_all | solution.py:196
  1164.1 51.1 %collective-permute-start.30 = (bf16[3,24,3456]{2,1,0:T(8,128)(2,1)}, bf16[3,24,3456]{2,1,0:T(8,128)(2,1)}, u32[]{:S(2)}, u32[]{:S(2)}) collective-permute-start(bf16[3,24,3456]{2,1,0:T(8,128)(2,1)} %pad_maximum_fusion.26), channel_id=1, source_target_pairs={{0,8},{1,9},{2,10},{3,11},{4,12},{5,13},{6,14},{7,15},{8,0},{9,1},... | collective-permute-start | bytes 1493000 | tf_op jit(solution)/shard_map/ppermute | solution.py:203
  1213.9 13.4 %collective-permute-start.39 = (bf16[2,24,6144]{2,1,0:T(8,128)(2,1)S(1)}, bf16[2,24,6144]{2,1,0:T(8,128)(2,1)S(1)}, u32[]{:S(2)}, u32[]{:S(2)}) collective-permute-start(bf16[2,24,6144]{2,1,0:T(8,128)(2,1)S(1)} %reduce_sum.345), channel_id=1, source_target_pairs={{0,16},{1,17},{2,18},{3,19},{4,20},{5,21},{6,22},{7,23},{8,24},{9,... | collective-permute-start | bytes 1769480 | tf_op jit(solution)/shard_map/ppermute | solution.py:198
  1227.5 4.5 collective-permute-start.40
  (110 other events, 1421.4 us)

commit v2 on v0

v2 whole, which is shorter than its diff:
```python
import functools
from functools import partial

import jax
import jax.numpy as jnp
from jax import lax
from jax.experimental import pallas as pl
from jax.experimental.pallas import tpu as pltpu
from jax.sharding import PartitionSpec as P

EPSILON = 1e-06
WIDE = jnp.float32
LOW = jnp.bfloat16
AXES = ("rep", "fsdp")
HIGH_Z = 4
PARTS = 3
BLOCK = 256
LANES = 128
GROUP = 4
MASK = 4096.0
MIB = 2**20


def dot(left, right):
    return jnp.dot(left, right, preferred_element_type=WIDE)


def dot_left(left, right):
    return lax.dot_general(left, right, (((0,), (0,)), ((), ())), preferred_element_type=WIDE)


def dot_right(left, right):
    return lax.dot_general(left, right, (((1,), (1,)), ((), ())), preferred_element_type=WIDE)


def layer_norm(values):
    centred = values - jnp.mean(values, axis=-1, keepdims=True)
    return centred * lax.rsqrt(jnp.mean(centred * centred, axis=-1, keepdims=True) + EPSILON)


def modulated(values, shift_part, scale_part):
    return layer_norm(values) * (1.0 + scale_part) + shift_part


def layout(lengths_row, widths_row, length):
    seg_count = lengths_row.shape[0]
    item_ends = jnp.cumsum(lengths_row)
    item_starts = item_ends - lengths_row
    token_place = jnp.arange(length, dtype=jnp.int32)[:, None]
    member = ((token_place >= item_starts[None, :]) & (token_place < item_ends[None, :])).astype(
        jnp.int32
    )
    segment = jnp.sum(member * jnp.arange(seg_count, dtype=jnp.int32)[None, :], axis=1)
    offset = token_place[:, 0] - jnp.sum(member * item_starts[None, :], axis=1)
    across = jnp.sum(member * widths_row[None, :], axis=1)
    return (member, segment, offset // across, offset % across)


def device_index(x, core, z, y):
    return (x * 2 + core) * 8 + z * 2 + y


PLACES = [(x, c, z, y) for x in range(2) for c in range(2) for z in range(4) for y in range(2)]
TO_CORE = [(device_index(x, c, z, y), device_index(x, 1 - c, z, y)) for x, c, z, y in PLACES]
TO_X = [(device_index(x, c, z, y), device_index(1 - x, c, z, y)) for x, c, z, y in PLACES]
TO_Y = [(device_index(x, c, z, y), device_index(x, c, z, 1 - y)) for x, c, z, y in PLACES]
Z_GROUPS = [[0, 2, 4, 6], [1, 3, 5, 7]]


def coordinates():
    replica = lax.axis_index("rep")
    shard = lax.axis_index("fsdp")
    return replica // 2, replica % 2, shard // 2, shard % 2


def is_fast():
    return lax.axis_size("rep") == 4 and lax.axis_size("fsdp") == 8


def pick(operand, index, axis):
    return lax.dynamic_index_in_dim(operand, index, axis, keepdims=False)


def over_z(operand):
    return lax.all_to_all(operand, "fsdp", 0, 0, axis_index_groups=Z_GROUPS)


def hold(plans, values):
    flat, tree = jax.tree.flatten(([plan.live for plan in plans], values))
    flat = lax.optimization_barrier(flat)
    lives, values = jax.tree.unflatten(tree, flat)
    for plan, live in zip(plans, lives):
        plan.live = live
    return values


def place_kernel(rows, half, where, a0, a1, ax, b0, b1, bx, out, sems):
    x, core, y = where[0], where[1], where[2]
    h = rows // PARTS
    copies = []
    for p0, p1, px, c in ((a0, a1, ax, core), (b0, b1, bx, 1 - core)):
        for q in range(HIGH_Z):
            for source, yy, third in (
                (p0.at[q, 0], y, x),
                (p0.at[q, 1], y, 2),
                (p1.at[q, 0], 1 - y, x),
                (p1.at[q, 1], 1 - y, 2),
                (px.at[q, 0], y, 1 - x),
                (px.at[q, 1], 1 - y, 1 - x),
            ):
                row = pl.multiple_of((2 * q + yy) * rows + third * h, 16)
                column = pl.multiple_of(c * half, LANES)
                target = out.at[pl.ds(row, h), pl.ds(column, half)]
                copy = pltpu.make_async_copy(source, target, sems.at[len(copies)])
                copy.start()
                copies.append(copy)
    for copy in copies:
        copy.wait()


class Gather:
    def __init__(self, weight):
        self.rows, self.width = weight.shape
        self.live = {"weight": weight}
        self.fast = is_fast() and self.rows % 48 == 0

    def z(self):
        if not self.fast:
            return
        x, core, _, _ = coordinates()
        h, half = self.rows // PARTS, self.width // 2
        weight = self.live.pop("weight")
        mine = lax.dynamic_slice_in_dim(weight, core * half, half, 1).reshape(PARTS, h, half)
        base = jnp.stack([pick(mine, x, 0), mine[2]], 0)
        self.live["own"] = over_z(jnp.broadcast_to(base, (HIGH_Z, 2, h, half)))

    def y(self):
        if self.fast:
            self.live["far"] = lax.ppermute(self.live["own"], AXES, TO_Y)

    def x(self, early=False, late=False):
        if not self.fast:
            return
        own = None if late else self.live["own"][:, 0]
        far = None if early else self.live["far"][:, 0]
        if early:
            self.live["side"] = lax.ppermute(own, AXES, TO_X)
        elif late:
            self.live["side_far"] = lax.ppermute(far, AXES, TO_X)
        else:
            self.live["both"] = lax.ppermute(jnp.stack([own, far], 1), AXES, TO_X)

    def core(self, *names):
        if self.fast:
            for name in names:
                self.live["twin_" + name] = lax.ppermute(self.live[name], AXES, TO_CORE)

    def whole(self):
        if not self.fast:
            return lax.all_gather(self.live["weight"], "fsdp", axis=0, tiled=True)
        x, core, _, y = coordinates()
        live = self.live
        if "both" not in live:
            live["both"] = jnp.stack([live["side"], live["side_far"]], 1)
            live["twin_both"] = jnp.stack([live["twin_side"], live["twin_side_far"]], 1)
        where = jnp.stack([x, core, y]).astype(jnp.int32)
        any_space = pl.BlockSpec(memory_space=pl.ANY)
        shape = (8 * self.rows, self.width)
        return pl.pallas_call(
            partial(place_kernel, self.rows, self.width // 2),
            out_shape=jax.ShapeDtypeStruct(shape, LOW),
            in_specs=[pl.BlockSpec(memory_space=pltpu.SMEM)] + [any_space] * 6,
            out_specs=pl.BlockSpec(memory_space=pltpu.VMEM),
            scratch_shapes=[pltpu.SemaphoreType.DMA((48,))],
            compiler_params=pltpu.CompilerParams(vmem_limit_bytes=40 * MIB),
            cost_estimate=pl.CostEstimate(
                flops=0, bytes_accessed=4 * shape[0] * shape[1], transcendentals=0
            ),
            name="place",
        )(
            where,
            live["own"],
            live["far"],
            live["both"],
            live["twin_own"],
            live["twin_far"],
            live["twin_both"],
        )


class Scatter:
    def __init__(self, left, send, keep):
        self.left, self.fast = None, is_fast() and left.shape[1] % 384 == 0
        self.live = {"left": left, "send": send, "keep": keep}

    def first(self):
        live = self.live
        if self.fast:
            live["out"] = dot_left(live["left"], live.pop("send")).astype(LOW)

    def core(self):
        if self.fast:
            self.live["got"] = lax.ppermute(self.live.pop("out"), AXES, TO_CORE)

    def second(self):
        live = self.live
        if self.fast:
            product = dot_left(live.pop("left"), live.pop("keep"))
            live["kept"] = (product + live.pop("got").astype(WIDE)).astype(LOW)

    def view(self):
        rows, half = self.live["kept"].shape
        return self.live["kept"].reshape(HIGH_Z, 2, PARTS, rows // 24, half)

    def x(self):
        if self.fast:
            x, _, _, _ = coordinates()
            self.live["side"] = lax.ppermute(pick(self.view(), 1 - x, 2), AXES, TO_X)

    def row(self, index):
        x, _, _, _ = coordinates()
        view = pick(self.view(), index, 1)
        own = pick(view, x, 1).astype(WIDE) + pick(self.live["side"], index, 1).astype(WIDE)
        return jnp.stack([own.astype(LOW), view[:, 2]], 1)

    def y(self):
        if self.fast:
            _, _, _, y = coordinates()
            self.live["far"] = lax.ppermute(self.row(1 - y), AXES, TO_Y)

    def z(self):
        if self.fast:
            _, _, _, y = coordinates()
            line = self.row(y).astype(WIDE) + self.live["far"].astype(WIDE)
            self.live = {"line": over_z(line.astype(LOW))}

    def last_x(self):
        if self.fast:
            part = jnp.sum(self.live["line"].astype(WIDE), axis=0).astype(LOW)
            self.live = {"part": part, "other": lax.ppermute(part, AXES, TO_X)}

    def last_core(self):
        if self.fast:
            x, _, _, _ = coordinates()
            part, other = self.live["part"], self.live["other"]
            shared = (part[1].astype(WIDE) + other[1].astype(WIDE)).astype(LOW)
            first = jnp.where(x == 0, part[0], other[0])
            second = jnp.where(x == 0, other[0], part[0])
            done = jnp.concatenate([first, second, shared], 0)
            self.live = {"done": done, "twin": lax.ppermute(done, AXES, TO_CORE)}

    def halves(self):
        if self.fast:
            _, core, _, _ = coordinates()
            done, twin = self.live["done"], self.live["twin"]
            first = jnp.where(core == 0, done, twin)
            second = jnp.where(core == 0, twin, done)
            return first.astype(WIDE), second.astype(WIDE)
        _, core, _, _ = coordinates()
        left = self.live["left"]
        keep, send = self.live["keep"], self.live["send"]
        first = jnp.where(core == 0, keep, send)
        second = jnp.where(core == 0, send, keep)
        sums = []
        for columns in (first, second):
            grad = dot_left(left, columns).astype(LOW)
            part = lax.psum_scatter(grad, "fsdp", scatter_dimension=0, tiled=True)
            sums.append(lax.psum(part, "rep").astype(WIDE))
        return sums[0], sums[1]


def mine_and_other(first, second):
    _, core, _, _ = coordinates()
    return jnp.where(core == 0, second, first), jnp.where(core == 0, first, second)


def column_halves(array):
    _, core, _, _ = coordinates()
    half = array.shape[1] // 2
    send = lax.dynamic_slice_in_dim(array, (1 - core) * half, half, 1)
    keep = lax.dynamic_slice_in_dim(array, core * half, half, 1)
    return send, keep


def across_replicas(rows):
    if not is_fast():
        return lax.all_gather(rows, "rep", axis=0, tiled=True)
    x, core, _, _ = coordinates()
    count, width = rows.shape
    twin = lax.ppermute(rows, AXES, TO_CORE)
    chip = jnp.stack([jnp.where(core == 0, rows, twin), jnp.where(core == 0, twin, rows)], 0)
    far = lax.ppermute(chip, AXES, TO_X)
    every = jnp.stack([jnp.where(x == 0, chip, far), jnp.where(x == 0, far, chip)], 0)
    return every.reshape(4 * count, width)


def gather_rows(rows):
    shards = lax.axis_size("fsdp")
    count, width = rows.shape
    group = lax.all_to_all(jnp.broadcast_to(rows, (shards, count, width)), "fsdp", 0, 0)
    return group.reshape(shards * count, width)


def exchange(rows):
    shards = lax.axis_size("fsdp")
    count, width = rows.shape
    shaped = rows.reshape(count, shards, width // shards).swapaxes(0, 1)
    return lax.all_to_all(shaped, "fsdp", 0, 0).reshape(shards * count, width // shards)


def sum_back(partial_rows, count):
    shards = lax.axis_size("fsdp")
    shaped = partial_rows.astype(LOW).reshape(shards, count, -1)
    got = lax.all_to_all(shaped, "fsdp", 0, 0)
    return jnp.sum(got.astype(WIDE), axis=0)


def whole_block(array):
    return pl.BlockSpec(
        array.shape, lambda i: (0,) * array.ndim, pipeline_mode=pl.Buffered(1)
    )


def part_width(hd):
    return -(-3 * GROUP * hd // LANES) * LANES


def prepare_kernel(
    heads, hd, x_ref, hot_ref, mod_ref, w_ref, gq_ref, gk_ref, rot_ref, qt_ref, kt_ref, vt_ref,
    normed_ref, q_ref, k_ref, v_ref, rq_ref, rk_ref, wide_ref,
):
    width = heads * hd
    step = part_width(hd)
    x = x_ref[...].astype(WIDE)
    hot = hot_ref[...]
    shift = dot(hot, mod_ref[:, :width])
    scale = dot(hot, mod_ref[:, width:])
    mean = jnp.mean(x, axis=-1, keepdims=True)
    centred = x - mean
    var = jnp.mean(centred * centred, axis=-1, keepdims=True)
    normed = (centred * lax.rsqrt(var + EPSILON) * (1.0 + scale) + shift).astype(LOW)
    normed_ref[...] = normed
    cosine, plus, minus = rot_ref[0], rot_ref[1], rot_ref[2]
    lane = lax.broadcasted_iota(jnp.int32, (BLOCK, LANES), 1)
    inside = lane < hd
    ones = jnp.full((LANES, LANES), 1.0, LOW)
    wide_ref[:, step:] = jnp.zeros((BLOCK, LANES), WIDE)
    for part in range(heads // GROUP):
        wide_ref[:, :step] = dot(normed, w_ref[:, part * step : (part + 1) * step])
        for kind, (g_ref, t_ref, o_ref, r_ref) in enumerate(
            (
                (gq_ref, qt_ref, q_ref, rq_ref),
                (gk_ref, kt_ref, k_ref, rk_ref),
                (None, vt_ref, v_ref, None),
            )
        ):
            tail = t_ref[...]
            for g in range(GROUP):
                h = part * GROUP + g
                at = (kind * GROUP + g) * hd
                raw = jnp.where(inside, wide_ref[:, at : at + LANES], 0.0)
                if kind < 2:
                    r_ref[h] = raw.astype(LOW)
                    total = dot((raw * raw).astype(LOW), ones)
                    u = raw * lax.rsqrt(total * (1.0 / hd) + EPSILON) * g_ref[...]
                    up = pltpu.roll(u, LANES - hd // 4, 1)
                    down = pltpu.roll(u, hd // 4, 1)
                    raw = u * cosine + up * plus + down * minus
                o_ref[h] = raw.astype(LOW) + tail


def prepare(x, hot, mod, w, gq, gk, rot, qt, kt, vt, heads, hd):
    n = x.shape[0]
    width = heads * hd
    rows = pl.BlockSpec((BLOCK, width), lambda i: (i, 0))
    head_spec = pl.BlockSpec((heads, BLOCK, LANES), lambda i: (0, i, 0))
    tail = pl.BlockSpec((BLOCK, LANES), lambda i: (i, 0))
    return pl.pallas_call(
        partial(prepare_kernel, heads, hd),
        grid=(n // BLOCK,),
        in_specs=[
            rows,
            pl.BlockSpec((BLOCK, hot.shape[1]), lambda i: (i, 0)),
            whole_block(mod),
            whole_block(w),
            whole_block(gq),
            whole_block(gk),
            pl.BlockSpec((3, BLOCK, LANES), lambda i: (0, i, 0)),
            tail,
            tail,
            pl.BlockSpec((1, LANES), lambda i: (0, 0)),
        ],
        out_specs=[rows] + [head_spec] * 5,
        out_shape=[jax.ShapeDtypeStruct((n, width), LOW)]
        + [jax.ShapeDtypeStruct((heads, n, LANES), LOW)] * 5,
        scratch_shapes=[pltpu.VMEM((BLOCK, part_width(hd) + LANES), WIDE)],
        compiler_params=pltpu.CompilerParams(vmem_limit_bytes=56 * MIB),
        cost_estimate=pl.CostEstimate(
            flops=2 * n * width * w.shape[1], bytes_accessed=40 * MIB, transcendentals=0
        ),
        name="prepare",
    )(x, hot, mod, w, gq, gk, rot, qt, kt, vt)


def near_blocks(run):
    i = pl.program_id(0)
    n = pl.num_programs(0)

    @pl.when(i == 0)
    def _():
        run((0, 1))

    @pl.when(i == n - 1)
    def _():
        run((-1, 0))

    @pl.when((i > 0) & (i < n - 1))
    def _():
        run((-1, 0, 1))


def attend_kernel(hd, c, q_ref, k_ref, v_ref, mix_ref, q2_ref):
    i = pl.program_id(0)
    heads = q_ref.shape[0]
    lane = lax.broadcasted_iota(jnp.int32, (BLOCK, LANES), 1)

    def run(blocks):
        for h in range(heads):
            q = q_ref[h]
            total = None
            for j in blocks:
                at = pl.ds(pl.multiple_of((i + j) * BLOCK, BLOCK), BLOCK)
                p = jnp.exp2(dot_right(q, k_ref[h, at]) * c).astype(LOW)
                term = dot(p, v_ref[h, at])
                total = term if total is None else total + term
            norm = total[:, hd : hd + 1]
            out = (total * (1.0 / norm)).astype(LOW)
            mix_ref[:, hd * h : hd * (h + 1)] = out[:, :hd]
            rest = jnp.log2(norm) * (1.0 / c)
            first = rest.astype(LOW).astype(WIDE)
            rest = rest - first
            second = rest.astype(LOW).astype(WIDE)
            third = rest - second
            logs = jnp.where(lane == hd + 8, first, jnp.where(lane == hd + 9, second, third))
            q2_ref[h] = jnp.where((lane >= hd + 8) & (lane < hd + 11), logs.astype(LOW), q)

    near_blocks(run)


def attend(q, k, v, hd, c):
    heads, n, _ = q.shape
    full = pl.BlockSpec((heads, n, LANES), lambda i: (0, 0, 0), pipeline_mode=pl.Buffered(1))
    block = pl.BlockSpec((heads, BLOCK, LANES), lambda i: (0, i, 0))
    return pl.pallas_call(
        partial(attend_kernel, hd, c),
        grid=(n // BLOCK,),
        in_specs=[block, full, full],
        out_specs=[pl.BlockSpec((BLOCK, heads * hd), lambda i: (i, 0)), block],
        out_shape=[
            jax.ShapeDtypeStruct((n, heads * hd), LOW),
            jax.ShapeDtypeStruct((heads, n, LANES), LOW),
        ],
        compiler_params=pltpu.CompilerParams(vmem_limit_bytes=56 * MIB),
        cost_estimate=pl.CostEstimate(
            flops=4 * n * 640 * LANES * heads,
            bytes_accessed=20 * MIB,
            transcendentals=heads * n * 640,
        ),
        name="attend",
    )(q, k, v)


def spread_kernel(heads, hd, ga_ref, w_ref, mix_ref, out_ref, grad_scr, mix_scr):
    width = heads * hd
    grad_scr[:, width:] = jnp.zeros((BLOCK, LANES), WIDE)
    mix_scr[:, width:] = jnp.zeros((BLOCK, LANES), WIDE)
    grad_scr[:, :width] = dot_right(ga_ref[...], w_ref[:, :width]).astype(LOW).astype(WIDE)
    mix_scr[:, :width] = mix_ref[...].astype(WIDE)
    lane = lax.broadcasted_iota(jnp.int32, (BLOCK, LANES), 1)
    ones = jnp.full((LANES, LANES), 1.0, LOW)
    for h in range(heads):
        at = hd * h
        grad = jnp.where(lane < hd, grad_scr[:, at : at + LANES], 0.0)
        product = grad * mix_scr[:, at : at + LANES]
        high = product.astype(LOW)
        rest = (product - high.astype(WIDE)).astype(LOW)
        delta = -(dot(high, ones) + dot(rest, ones))
        first = delta.astype(LOW)
        second = (delta - first.astype(WIDE)).astype(LOW)
        out_ref[h] = jnp.where(
            lane == hd, first, jnp.where(lane == hd + 1, second, grad.astype(LOW))
        )


def spread(ga, w, mix, heads, hd):
    n = ga.shape[0]
    width = heads * hd
    row = pl.BlockSpec((BLOCK, width), lambda i: (i, 0))
    return pl.pallas_call(
        partial(spread_kernel, heads, hd),
        grid=(n // BLOCK,),
        in_specs=[row, whole_block(w), row],
        out_specs=pl.BlockSpec((heads, BLOCK, LANES), lambda i: (0, i, 0)),
        out_shape=jax.ShapeDtypeStruct((heads, n, LANES), LOW),
        scratch_shapes=[
            pltpu.VMEM((BLOCK, width + LANES), WIDE),
            pltpu.VMEM((BLOCK, width + LANES), WIDE),
        ],
        compiler_params=pltpu.CompilerParams(vmem_limit_bytes=56 * MIB),
        cost_estimate=pl.CostEstimate(
            flops=2 * n * width * width, bytes_accessed=12 * MIB, transcendentals=0
        ),
        name="spread",
    )(ga, w, mix)


def back_kernel(
    hd, c, score_scale, q_ref, k_ref, v_ref, do_ref, rq_ref, rk_ref, rot_ref, gq_ref, gk_ref,
    joint_ref, gain_ref, dq_scr, dk_scr, dv_scr, gain_scr,
):
    i = pl.program_id(0)
    n = pl.num_programs(0)
    heads = q_ref.shape[0]
    tail = joint_ref.shape[1] - 3 * heads * hd

    @pl.when(i == 0)
    def _():
        dq_scr[...] = jnp.zeros(dq_scr.shape, WIDE)
        gain_scr[...] = jnp.zeros(gain_scr.shape, WIDE)

    ones = jnp.full((LANES, LANES), 1.0, LOW)

    def run(blocks):
        def body(h, carry):
            kk = k_ref[h]
            vv = v_ref[h]
            dk = dv = None
            for j in blocks:
                at = pl.ds(pl.multiple_of((i + j) * BLOCK, BLOCK), BLOCK)
                q = q_ref[h, at]
                do = do_ref[h, at]
                p = jnp.exp2(dot_right(kk, q) * c)
                term = dot(p.astype(LOW), do)
                dv = term if dv is None else dv + term
                ds = (p * dot_right(vv, do)).astype(LOW)
                term = dot(ds, q)
                dk = term if dk is None else dk + term
                dq_scr[h, at] += dot_left(ds, kk)
            dk_scr[h] = dk
            dv_scr[h] = dv
            return carry

        lax.fori_loop(0, heads, body, 0, unroll=2)

    near_blocks(run)

    def finish(dy, raw, rot, gain, row):
        raw = raw.astype(WIDE)
        dy = dy * score_scale
        up = pltpu.roll(dy, LANES - hd // 4, 1)
        down = pltpu.roll(dy, hd // 4, 1)
        d = dy * rot[0] - up * rot[1] - down * rot[2]
        r = lax.rsqrt(dot((raw * raw).astype(LOW), ones) * (1.0 / hd) + EPSILON)
        u = raw * r
        ud = u * d
        gain_scr[row] += jnp.sum(ud.reshape(BLOCK // 8, 8, LANES), axis=0)
        m = dot((ud * gain).astype(LOW), ones) * (1.0 / hd)
        return (r * (gain * d - u * m)).astype(LOW)

    here = pl.ds(pl.multiple_of(i * BLOCK, BLOCK), BLOCK)
    rot = [rot_ref[t, here] for t in range(3)]
    width = heads * hd
    joint_ref[here, 3 * width :] = jnp.zeros((BLOCK, tail), LOW)
    for h in range(heads):
        grad = finish(dk_scr[h], rk_ref[h], rot, gk_ref[...], 1)
        joint_ref[here, width + hd * h : width + hd * (h + 1)] = grad[:, :hd]
        value = dv_scr[h].astype(LOW)
        joint_ref[here, 2 * width + hd * h : 2 * width + hd * (h + 1)] = value[:, :hd]

    @pl.when(i == n - 1)
    def _():
        def rows(b, carry):
            at = pl.ds(pl.multiple_of(b * BLOCK, BLOCK), BLOCK)
            turn = [rot_ref[t, at] for t in range(3)]
            for h in range(heads):
                grad = finish(dq_scr[h, at], rq_ref[h, at], turn, gq_ref[...], 0)
                joint_ref[at, hd * h : hd * (h + 1)] = grad[:, :hd]
            return carry

        lax.fori_loop(0, n, rows, 0)
        gain_ref[...] = gain_scr[...]


def attend_back(part, q2, k, v, do, rq, rk, rot, gq, gk, hd, c, score_scale):
    _, n, _ = q2.shape
    one = pl.Buffered(1)
    full = pl.BlockSpec((GROUP, n, LANES), lambda i: (part, 0, 0), pipeline_mode=one)
    block = pl.BlockSpec((GROUP, BLOCK, LANES), lambda i: (part, i, 0))
    small = pl.BlockSpec((1, LANES), lambda i: (0, 0))
    width = part_width(hd)
    return pl.pallas_call(
        partial(back_kernel, hd, c, score_scale),
        grid=(n // BLOCK,),
        in_specs=[full, block, block, full, full, block, whole_block(rot), small, small],
        out_specs=[
            pl.BlockSpec((n, width), lambda i: (0, 0), pipeline_mode=one),
            pl.BlockSpec((2, 8, LANES), lambda i: (0, 0, 0)),
        ],
        out_shape=[
            jax.ShapeDtypeStruct((n, width), LOW),
            jax.ShapeDtypeStruct((2, 8, LANES), WIDE),
        ],
        scratch_shapes=[
            pltpu.VMEM((GROUP, n, LANES), WIDE),
            pltpu.VMEM((GROUP, BLOCK, LANES), WIDE),
            pltpu.VMEM((GROUP, BLOCK, LANES), WIDE),
            pltpu.VMEM((2, 8, LANES), WIDE),
        ],
        compiler_params=pltpu.CompilerParams(vmem_limit_bytes=56 * MIB),
        cost_estimate=pl.CostEstimate(
            flops=10 * n * 640 * LANES * GROUP,
            bytes_accessed=10 * MIB,
            transcendentals=GROUP * n * 640,
        ),
        name="attend_back",
    )(q2, k, v, do, rq, rk, rot, gq, gk)


def turn_tables(row_place, column_place, hd):
    quarter = hd // 4
    inverse = 10000.0 ** (-jnp.arange(quarter, dtype=WIDE) / quarter)
    row_angle = row_place.astype(WIDE)[:, None] * inverse[None, :]
    column_angle = column_place.astype(WIDE)[:, None] * inverse[None, :]
    rest = jnp.zeros((row_place.shape[0], LANES - hd), WIDE)
    none = jnp.zeros_like(row_angle)
    rc, rs = jnp.cos(row_angle), jnp.sin(row_angle)
    cc, cs = jnp.cos(column_angle), jnp.sin(column_angle)
    return jnp.stack(
        [
            jnp.concatenate([rc, rc, cc, cc, rest], 1),
            jnp.concatenate([-rs, none, -cs, none, rest], 1),
            jnp.concatenate([none, rs, none, cs, rest], 1),
        ],
        0,
    )


def pad_columns(array, width):
    return jnp.pad(array, ((0, 0), (0, width - array.shape[1])))


def to_parts(array, heads, hd):
    rows = array.shape[0]
    shaped = array.reshape(rows, 3, heads // GROUP, GROUP * hd).swapaxes(1, 2)
    shaped = shaped.reshape(rows, heads // GROUP, 3 * GROUP * hd)
    padded = jnp.pad(shaped, ((0, 0), (0, 0), (0, part_width(hd) - 3 * GROUP * hd)))
    return padded.reshape(rows, -1)


def from_parts(array, heads, hd):
    rows = array.shape[0]
    shaped = array.reshape(rows, heads // GROUP, -1)[:, :, : 3 * GROUP * hd]
    shaped = shaped.reshape(rows, heads // GROUP, 3, GROUP * hd).swapaxes(1, 2)
    return shaped.reshape(rows, -1)


def local(
    block_in,
    condition,
    item_lengths,
    item_widths,
    ada_weight,
    ada_bias,
    qkv_weight,
    query_gain,
    key_gain,
    proj_weight,
    gate_up_weight,
    down_weight,
    out_grad,
):
    _, n, width = block_in.shape
    items = item_lengths.shape[1]
    hd = query_gain.shape[0]
    heads = width // hd
    ff = down_weight.shape[0] * lax.axis_size("fsdp")
    score_scale = float(hd) ** (-0.5)
    c = score_scale * 1.4426950408889634
    shards = lax.axis_size("fsdp")
    fsdp_place = lax.axis_index("fsdp")
    odd = width + LANES if (width // LANES) % 2 else width

    g_qkv = Gather(to_parts(qkv_weight, heads, hd))
    g_proj = Gather(pad_columns(proj_weight, odd))
    g_gate = Gather(gate_up_weight[:, :ff])
    g_up = Gather(gate_up_weight[:, ff:])
    g_down = Gather(pad_columns(down_weight, odd))
    gathers = [g_qkv, g_proj, g_gate, g_up, g_down]

    cond_float = condition.astype(WIDE).reshape(items, width)
    cond_silu, silu_pull = jax.vjp(jax.nn.silu, cond_float)
    cond_act = cond_silu.astype(LOW)

    group_act = exchange(cond_act)
    g_qkv.z()
    member, segment, row_place, column_place = layout(item_lengths[0], item_widths[0], n)
    member_low = member.astype(LOW)
    keep_mask = (segment < items - 1).astype(WIDE).reshape(n, 1)
    rot = turn_tables(row_place, column_place, hd)
    spare = jnp.zeros((n, LANES - hd - items), LOW)
    ones_at = jnp.zeros((n, LANES - hd - items), LOW).at[:, :3].set(-1.0)
    blank = jnp.zeros((n, hd), LOW)
    query_tail = jnp.concatenate([blank, member_low, spare], 1)
    key_tail = jnp.concatenate([blank, (member_low - 1.0) * MASK, ones_at], 1)
    value_tail = jnp.zeros((1, LANES), LOW).at[:, hd : hd + 2].set(1.0)
    gain_q = pad_columns(query_gain.astype(WIDE)[None, :], LANES)
    gain_k = pad_columns(key_gain.astype(WIDE)[None, :], LANES)
    bias_row = lax.dynamic_update_slice(
        jnp.zeros((6 * width,), WIDE), ada_bias.astype(WIDE), (fsdp_place * ada_bias.shape[0],)
    )
    mod_part = (dot(group_act, ada_weight) + bias_row[None, :]).astype(LOW)
    tables = (rot, query_tail, key_tail)
    mod_part, tables, group_act = hold(gathers, (mod_part, tables, group_act))

    early = 2 * width
    mod_a = sum_back(mod_part[:, :early], items)
    g_qkv.y()
    g_qkv.x(early=True)
    g_qkv.core("own")
    g_proj.z()
    g_gate.z()
    mod_a, mod_part, tables, group_act = hold(gathers, (mod_a, mod_part, tables, group_act))

    mod_b = sum_back(mod_part[:, early:], items)
    g_qkv.x(late=True)
    g_qkv.core("far", "side")
    g_proj.y()
    g_up.z()
    every_act = across_replicas(group_act)
    mod_a, mod_b, tables = hold(gathers, (mod_a, mod_b, tables))

    g_qkv.core("side_far")
    modulation = jnp.concatenate([mod_a, mod_b], axis=1)
    mod_high = modulation.astype(LOW)
    mod_rest = (modulation - mod_high.astype(WIDE)).astype(LOW)
    mod_low = jnp.concatenate([mod_high, mod_rest], axis=0)
    hot = jnp.concatenate([member_low, member_low], axis=1)
    inputs_low = block_in[0]
    mod_low, tables, inputs_low = hold(gathers, (mod_low, tables, inputs_low))

    g_proj.x()
    g_gate.y()
    g_up.y()
    g_down.z()
    rot, query_tail, key_tail = tables
    qkv_full = g_qkv.whole()
    normed_a, q, k, v, raw_q, raw_k = prepare(
        inputs_low, hot, mod_low[:, :early], qkv_full, gain_q, gain_k, rot,
        query_tail, key_tail, value_tail, heads, hd,
    )
    gathers = gathers[1:]
    normed_a, q, k, v, raw_q, raw_k, qkv_full = hold(
        gathers, (normed_a, q, k, v, raw_q, raw_k, qkv_full)
    )

    g_proj.core("own", "far", "both")
    g_gate.x()
    g_down.y()
    mixed, q2 = attend(q, k, v, hd, c)
    mixed, q2 = hold(gathers, (mixed, q2))

    g_gate.core("own", "far", "both")
    g_up.x()
    proj_full = g_proj.whole()
    token_mod = dot(hot, mod_low)
    shift_a, scale_a, gate_a, shift_b, scale_b, gate_b = jnp.split(token_mod, 6, axis=1)
    inputs = inputs_low.astype(WIDE)
    attended = dot(mixed, proj_full[:, :width])
    middle = inputs + keep_mask * gate_a * attended
    normed_b = modulated(middle, shift_b, scale_b).astype(LOW)
    gathers = gathers[1:]
    middle, normed_b, attended, proj_full = hold(
        gathers, (middle, normed_b, attended, proj_full)
    )

    g_up.core("own", "far", "both")
    g_down.x()
    gate_full = g_gate.whole()
    gate = dot(normed_b, gate_full).astype(LOW)
    gathers = gathers[1:]
    gate, gate_full, normed_b = hold(gathers, (gate, gate_full, normed_b))

    g_down.core("own", "far", "both")
    up_full = g_up.whole()
    up = dot(normed_b, up_full)
    gate_wide = gate.astype(WIDE)
    inner = (jax.nn.silu(gate_wide) * up).astype(LOW)
    up = up.astype(LOW)
    gathers = gathers[1:]
    inner, up, gate, up_full, middle = hold(gathers, (inner, up, gate, up_full, middle))

    down_full = g_down.whole()
    returned = dot(inner, down_full[:, :width])
    block_out = (middle + keep_mask * gate_b * returned).astype(LOW)
    upstream = out_grad[0].astype(WIDE)
    grad_gate_b = upstream * keep_mask * returned
    grad_returned = (upstream * keep_mask * gate_b).astype(LOW)

    s_down = Scatter(inner, *column_halves(pad_columns(grad_returned, odd)))
    s_down.first()
    plans = [s_down]
    grad_returned, down_full, gate, up, gate_full, up_full, normed_b, middle, attended = hold(
        plans,
        (grad_returned, down_full, gate, up, gate_full, up_full, normed_b, middle, attended),
    )

    s_down.core()
    grad_inner = dot_right(grad_returned, down_full[:, :width])
    gate_wide = gate.astype(WIDE)
    sig = jax.nn.sigmoid(gate_wide)
    grad_gate = (grad_inner * up.astype(WIDE) * sig * (1.0 + gate_wide * (1.0 - sig))).astype(LOW)
    grad_up = (grad_inner * gate_wide * sig).astype(LOW)
    grad_gate, grad_up = hold(plans, (grad_gate, grad_up))

    s_down.second()
    chunk = ff // 2
    s_one = Scatter(normed_b, *mine_and_other(grad_gate[:, :chunk], grad_up[:, :chunk]))
    s_two = Scatter(normed_b, *mine_and_other(grad_gate[:, chunk:], grad_up[:, chunk:]))
    s_one.first()
    plans = [s_down, s_one, s_two]
    grad_gate, grad_up = hold(plans, (grad_gate, grad_up))

    s_down.x()
    s_one.core()
    s_two.first()
    grad_normed_b = dot_right(grad_gate, gate_full) + dot_right(grad_up, up_full)
    _, norm_pull_b = jax.vjp(modulated, middle, shift_b, scale_b)
    grad_middle_part, grad_shift_b, grad_scale_b = norm_pull_b(grad_normed_b)
    grad_middle = upstream + grad_middle_part
    grad_gate_a = grad_middle * keep_mask * attended
    grad_attended = (grad_middle * keep_mask * gate_a).astype(LOW)
    s_proj = Scatter(mixed, *column_halves(pad_columns(grad_attended, odd)))
    late = jnp.concatenate(
        [part.astype(LOW) for part in (grad_gate_a, grad_shift_b, grad_scale_b, grad_gate_b)],
        axis=1,
    )
    plans = [s_down, s_one, s_two, s_proj]
    grad_middle, grad_attended, late = hold(plans, (grad_middle, grad_attended, late))

    s_down.y()
    s_two.core()
    s_one.second()
    s_proj.first()
    late_sums = dot_left(member_low, late).astype(LOW)
    grad_mixed = spread(grad_attended, proj_full, mixed, heads, hd)
    late_sums, grad_mixed = hold(plans, (late_sums, grad_mixed))

    back = partial(
        attend_back, q2=q2, k=k, v=v, rq=raw_q, rk=raw_k, rot=rot, gq=gain_q, gk=gain_k,
        hd=hd, c=c, score_scale=score_scale,
    )
    s_down.z()
    s_one.x()
    s_proj.core()
    s_two.second()
    joint_0, gains_0 = back(0, do=grad_mixed)
    joint_0, gains_0, grad_mixed, late_sums = hold(
        plans, (joint_0, gains_0, grad_mixed, late_sums)
    )

    s_down.last_x()
    s_one.y()
    s_two.x()
    s_proj.second()
    late_group = gather_rows(late_sums)
    joint_1, gains_1 = back(1, do=grad_mixed)
    s_head = Scatter(normed_a, *mine_and_other(joint_0, joint_1))
    s_head.first()
    plans = plans + [s_head]
    joint_0, joint_1, gains_1, grad_mixed, late_group = hold(
        plans, (joint_0, joint_1, gains_1, grad_mixed, late_group)
    )

    s_down.last_core()
    s_one.z()
    s_two.y()
    s_proj.x()
    s_head.core()
    late_every = across_replicas(late_group)
    joint_2, gains_2 = back(2, do=grad_mixed)
    joint_2, gains_2, grad_mixed, late_every = hold(
        plans, (joint_2, gains_2, grad_mixed, late_every)
    )
    s_one.last_x()
    s_two.z()
    s_proj.y()
    s_head.second()
    joint_3, gains_3 = back(3, do=grad_mixed)
    s_tail = Scatter(normed_a, *mine_and_other(joint_2, joint_3))
    s_tail.first()
    plans = plans[1:] + [s_tail]
    joint_2, joint_3, gains_3 = hold(plans, (joint_2, joint_3, gains_3))

    s_one.last_core()
    s_two.last_x()
    s_proj.z()
    s_head.x()
    s_tail.core()
    joint = jnp.concatenate([joint_0, joint_1, joint_2, joint_3], axis=1)
    grad_normed_a = dot_right(joint, qkv_full)
    _, norm_pull_a = jax.vjp(modulated, inputs, shift_a, scale_a)
    grad_input_part, grad_shift_a, grad_scale_a = norm_pull_a(grad_normed_a)
    grad_input = grad_middle + grad_input_part
    soon = jnp.concatenate([grad_shift_a.astype(LOW), grad_scale_a.astype(LOW)], axis=1)
    plans = plans[1:]
    grad_input, soon = hold(plans, (grad_input, soon))

    s_two.last_core()
    s_proj.last_x()
    s_head.y()
    s_tail.second()
    early_sums = dot_left(member_low, soon)
    gain_row = jnp.sum(gains_0 + gains_1 + gains_2 + gains_3, axis=1)[:, :hd].reshape(1, 2 * hd)
    gain_high = gain_row.astype(LOW).astype(WIDE)
    gain_block = jnp.concatenate([gain_high, gain_row - gain_high], axis=0)
    gain_block = jnp.pad(gain_block, ((0, items - 2), (0, 2 * LANES - 2 * hd)))
    early_sums = jnp.concatenate([early_sums, gain_block], axis=1).astype(LOW)
    plans = plans[1:]
    early_sums, late_every = hold(plans, (early_sums, late_every))

    s_proj.last_core()
    s_head.z()
    s_tail.x()
    early_group = gather_rows(early_sums)
    shard_late = dot_left(every_act, late_every)
    early_group, shard_late = hold(plans, (early_group, shard_late))

    s_head.last_x()
    s_tail.y()
    early_every = across_replicas(early_group)
    cond_part = dot_right(early_group[:, :early], ada_weight[:, :early]) + dot_right(
        late_group, ada_weight[:, early:]
    )
    early_every, cond_part = hold(plans, (early_every, cond_part))

    s_head.last_core()
    s_tail.z()
    cond_back = lax.all_to_all(cond_part.astype(LOW).reshape(shards, items, -1), "fsdp", 0, 0)
    shard_early = dot_left(every_act, early_every[:, :early])
    cond_back, shard_early = hold(plans, (cond_back, shard_early))

    s_tail.last_x()
    grad_cond_act = cond_back.swapaxes(0, 1).reshape(items, width).astype(WIDE)
    grad_condition = silu_pull(grad_cond_act)[0]
    shard_ada = jnp.concatenate([shard_early, shard_late], axis=1)
    bias_sums = jnp.concatenate(
        [
            jnp.sum(early_every[:, :early].astype(WIDE), axis=0),
            jnp.sum(late_every.astype(WIDE), axis=0),
        ],
        axis=0,
    )
    shard_bias = lax.dynamic_slice(
        bias_sums, (fsdp_place * ada_bias.shape[0],), (ada_bias.shape[0],)
    )
    gain_sums = jnp.sum(early_every[:, early:].astype(WIDE), axis=0)[: 2 * hd]
    hold(plans, ())
    s_tail.last_core()
    shard_qkv = from_parts(
        jnp.concatenate(s_head.halves() + s_tail.halves(), axis=1), heads, hd
    )
    shard_proj = jnp.concatenate(s_proj.halves(), axis=1)[:, :width]
    gate_1, up_1 = s_one.halves()
    gate_2, up_2 = s_two.halves()
    shard_gate_up = jnp.concatenate([gate_1, gate_2, up_1, up_2], axis=1)
    shard_down = jnp.concatenate(s_down.halves(), axis=1)[:, :width]
    return (
        block_out[None],
        grad_input[None],
        grad_condition[None],
        shard_ada,
        shard_bias,
        shard_qkv,
        gain_sums[:hd],
        gain_sums[hd:],
        shard_proj,
        shard_gate_up,
        shard_down,
    )


def solution(mesh):
    return jax.shard_map(
        local,
        mesh=mesh,
        in_specs=(
            P(("rep", "fsdp"), None, None),
            P(("rep", "fsdp"), None, None),
            P(("rep", "fsdp"), None),
            P(("rep", "fsdp"), None),
            P("fsdp", None),
            P("fsdp"),
            P("fsdp", None),
            P(),
            P(),
            P("fsdp", None),
            P("fsdp", None),
            P("fsdp", None),
            P(("rep", "fsdp"), None, None),
        ),
        out_specs=(
            P(("rep", "fsdp"), None, None),
            P(("rep", "fsdp"), None, None),
            P(("rep", "fsdp"), None, None),
            P("fsdp", None),
            P("fsdp"),
            P("fsdp", None),
            P(),
            P(),
            P("fsdp", None),
            P("fsdp", None),
            P("fsdp", None),
        ),
        check_vma=False,
    )
```

time: 1900 us -> 994 us (0.52)
  waiting for transfers between devices: 1000 us -> 156 us
  matrix products: 437 us -> 225 us
  Pallas kernels: 0 us -> 195 us
  blocking collectives: 170 us -> 0 us
  starting transfers between devices: 13.8 us -> 145 us
  local copies, waits for them, and re-layouts: 64.2 us -> 100 us
  other arithmetic: 178 us -> 157 us
    reduce_scatter x6 -> x0, waiting for transfers between devices: 567 us -> none  [the longest x1 272 us: local(): lax.psum_scatter(grad_ada.astype(jnp.bfloat16), 'fsdp', scatter_dimension...]
    all_gather x7 -> x0, waiting for transfers between devices: 430 us -> none  [the longest x1 181 us: local(): lax.all_gather(ada_weight, 'fsdp', axis=0, tiled=True)]
    dot_general x29 -> x28, matrix products: 437 us -> 225 us  [the longest x16 81.3 us: dot_left(): lax.dot_general(left, right, (((0,), (0,)), ((), ())), preferred_element_...]
    pallas_call x0 -> x12, Pallas kernels: none -> 195 us  [the longest x4 96.6 us: attend_back(): pl.pallas_call(partial(back_kernel, hd, c, score_scale), grid=(n // BLOCK...]
    unnamed x5 -> x0, blocking collectives: 137 us -> none
    ppermute x0 -> x63, waiting for transfers between devices: none -> 83.5 us  [the longest x6 16.6 us: y(): self.live['far'] = lax.ppermute(self.row(1 - y), AXES, TO_Y)]
    all_to_all x0 -> x17, starting transfers between devices: none -> 81.3 us  [the longest x11 49.1 us: over_z(): return lax.all_to_all(operand, 'fsdp', 0, 0, axis_index_groups=Z_GROUPS)]
    all_to_all x0 -> x17, waiting for transfers between devices: none -> 72.9 us  [the longest x11 53.9 us: over_z(): return lax.all_to_all(operand, 'fsdp', 0, 0, axis_index_groups=Z_GROUPS)]
  transfers between devices with their start and end apart: 17 -> 80, of which waited for: 8 -> 22; matrix products, arithmetic and copies ran while one was open for 35% -> 35% of each run, Pallas kernels for 0% -> 19%
where the time goes in v2:
time: 994 us; the launch traced here: 983 us
  matrix products  225 us (23%)
  Pallas kernels  195 us (20%)
  other arithmetic  157 us (16%)
  waiting for transfers between devices  156 us (16%)
  starting transfers between devices  145 us (15%)
  local copies, waits for them, and re-layouts  100 us (10%)
    pallas_call x4, Pallas kernels, attend_back(): pl.pallas_call(partial(back_kernel, hd, c, score_scale), grid=(n // BLOCK...  96.6 us
    dot_general x16, matrix products, dot_left(): lax.dot_general(left, right, (((0,), (0,)), ((), ())), preferred_element_...  81.3 us
    dot_general x6, matrix products, dot(): return jnp.dot(left, right, preferred_element_type=WIDE)  75.2 us
    dot_general x6, matrix products, dot_right(): lax.dot_general(left, right, (((1,), (1,)), ((), ())), preferred_element_...  68.1 us
    all_to_all x11, waiting for transfers between devices, over_z(): return lax.all_to_all(operand, 'fsdp', 0, 0, axis_index_groups=Z_GROUPS)  53.9 us
    all_to_all x11, starting transfers between devices, over_z(): return lax.all_to_all(operand, 'fsdp', 0, 0, axis_index_groups=Z_GROUPS)  49.1 us
    pallas_call x1, Pallas kernels, prepare(): pl.pallas_call(partial(prepare_kernel, heads, hd), grid=(n // BLOCK,), in...  39 us
    pallas_call x1, Pallas kernels, attend(): pl.pallas_call(partial(attend_kernel, hd, c), grid=(n // BLOCK,), in_spec...  27.6 us
  transfers between devices with their start and end apart: 80, of which 22 were waited for; matrix products, arithmetic and copies ran while one was open for 35% of the time, Pallas kernels for 19%

profile of v2, /device:TPU:1, one launch (start us, length us, event | category | flops | bytes accessed | tf_op | source)
XLA Modules:
  0.0 982.9 jit_solution(1534919950458775027)
XLA Ops:
  2.1 6.4 all-to-all-start.1
  14.4 5.3 multiply_cosine_fusion
  29.9 4.5 all-to-all-start
  39.9 26.8 %all-to-all-done.a0 = bf16[4,2,48,1792]{3,2,1,0:T(8,128)(2,1)S(1)} async-done(((bf16[4,2,48,1792]{3,2,1,0:T(8,128)(2,1)}), bf16[4,2,48,1792]{3,2,1,0:T(8,128)(2,1)S(1)}, u32[]{:S(2)}, u32[]{:S(2)}) %all-to-all-start) | async-done | bytes 1376288 | tf_op jit(solution)/shard_map/all_to_all | solution.py:85
  71.0 7.2 all-to-all-done.4
  79.0 4.1 all-to-all-start.2
  85.1 8.9 all-to-all-done.2.a0
  95.1 4.2 all-to-all-start.3
  106.3 15.2 %collective-permute-done.1 = bf16[4,48,1792]{2,1,0:T(8,128)(2,1)S(1)} collective-permute-done((bf16[4,48,1792]{2,1,0:T(8,128)(2,1)S(1)}, bf16[4,48,1792]{2,1,0:T(8,128)(2,1)S(1)}, u32[]{:S(2)}, u32[]{:S(2)}) %collective-permute-start.1) | collective-permute-done | bytes 688160 | tf_op jit(solution)/shard_map/ppermute | solution.py:147
  121.5 8.3 collective-permute-done
  134.3 5.4 all-to-all-start.6
  141.7 9.5 all-to-all-done.6
  152.3 5.4 all-to-all-start.5
  169.8 7.8 collective-permute-done.6.a1
  180.7 5.0 all-to-all-done.5.a0
  209.5 6.3 place.5.w_ref
  215.8 39.0 %prepare.1 = (bf16[1024,1152]{1,0:T(8,128)(2,1)}, bf16[16,1024,128]{2,1,0:T(8,128)(2,1)}, bf16[16,1024,128]{2,1,0:T(8,128)(2,1)}, bf16[16,1024,128]{2,1,0:T(8,12...) custom-call(bf16[1024,1152]{1,0:T(8,128)(2,1)} %bitcast.342, ...), custom_call_target="tpu_custom_call" | custom-call | flops 8455716864 | bytes 41943040 | tf_op jit(solution)/shard_map/prepare/pallas_call | solution.py:378
  259.7 11.3 %fusion.106 = f32[1024,6912]{1,0:T(8,128)} fusion(bf16[16,6912]{1,0:T(8,128)(2,1)S(1)} %copy-done.81, bf16[1024,8]{1,0:T(8,128)(2,1)S(1)} %copy-done.45), kind=kOutput, calls=%fused_computation.353 | convolution fusion | flops 226557952 | bytes 28549120 | tf_op jit(solution)/shard_map/dot_general | solution.py:25
  273.1 27.6 %attend.1 = (bf16[1024,1152]{1,0:T(8,128)(2,1)}, bf16[16,1024,128]{2,1,0:T(8,128)(2,1)}) custom-call(bf16[16,1024,128]{2,1,0:T(8,128)(2,1)} %get-tuple-element.404.q_ref, bf16[16,1024,128]{2,1,0:T(8,128)(2,1)} %get-tuple-element.405.k_ref, bf16[16,1024,128]{2,1,0:T(8,128)(2,1)} %get-tuple-element.406.v_ref), custom_call_target="tpu_custom_call" | custom-call | flops 5368709120 | bytes 20971520 | tf_op jit(solution)/shard_map/attend/pallas_call | solution.py:454
  308.7 14.4 %fusion.111 = (f32[1024]{0:T(1024)S(1)}, f32[1024,1152]{1,0:T(8,128)}, bf16[1024,1152]{1,0:T(8,128)(2,1)S(1)}, f32[1024]{0:T(1024)}, f32[1024,1152]{1,0:T(8,128)}) fusion(f32[1024,6912]{1,0:T(8,128)} %fusion.106, f32[1024]{0:T(1024)S(1)} %compare_convert_fusion, bf16[1024,1152]{1,0:T(8,128)(2,1)} %bitcast.343, bf16[1,1024,1152]{2,1,0:T(8,128)(2,1)S(1)} %copy-done.36, ...), kind=kOutput, calls=%fused_computation.356 | convolution fusion | flops 2729703424 | bytes 30978048 | tf_op jit(solution)/shard_map/dot_general | solution.py:25
  328.1 5.4 fusion.41
  339.0 13.6 %convolution_convert_fusion.2 = bf16[1024,3072]{1,0:T(8,128)(2,1)} fusion(bf16[1024,1152]{1,0:T(8,128)(2,1)} %fusion.41, bf16[1152,3072]{1,0:T(8,128)(2,1)S(1)} %place.7), kind=kOutput, calls=%fused_computation.51 | convolution fusion | flops 7250903040 | bytes 15728640 | tf_op jit(solution)/shard_map/dot_general | solution.py:25
  354.7 11.3 %collective-permute-done.23.ax = bf16[4,2,128,640]{3,2,1,0:T(8,128)(2,1)S(1)} collective-permute-done((bf16[4,2,128,640]{3,2,1,0:T(8,128)(2,1)}, bf16[4,2,128,640]{3,2,1,0:T(8,128)(2,1)S(1)}, u32[]{:S(2)}, u32[]{:S(2)}) %collective-permute-start.23) | collective-permute-done | bytes 1310752 | tf_op jit(solution)/shard_map/ppermute | solution.py:151
  373.6 16.9 %fusion.112 = (bf16[1024,3072]{1,0:T(8,128)(2,1)}, bf16[1024,3072]{1,0:T(8,128)(2,1)}) fusion(bf16[1024,3072]{1,0:T(8,128)(2,1)} %convolution_convert_fusion.2, bf16[1024,1152]{1,0:T(8,128)(2,1)} %fusion.41, bf16[1152,3072]{1,0:T(8,128)(2,1)S(1)} %place.8), kind=kOutput, calls=%fused_computation.357 | convolution fusion | flops 7272923136 | bytes 28311552 | tf_op jit(solution)/shard_map/dot_general | solution.py:25
  390.6 9.5 convolution_convert_fusion.4
  400.0 5.4 place.9
  408.5 18.4 %fusion.11 = (bf16[1024,3072]{1,0:T(8,128)(2,1)}, bf16[1024,3072]{1,0:T(8,128)(2,1)}) fusion(bf16[1024,3072]{1,0:T(8,128)(2,1)} %convolution_convert_fusion.2, bf16[1024,3072]{1,0:T(8,128)(2,1)} %get-tuple-element.465, bf16[1024,1152]{1,0:T(8,128)(2,1)S(1)} %copy-done.35, bf16[3072,1280]{1,0:T(8,128)(2,1)} %place.9), kind=kOutput, calls=%fused_computation.16 | convolution fusion | flops 7294943232 | bytes 34603008 | tf_op jit(solution)/shard_map/dot_general | solution.py:33
  426.9 9.0 broadcast_select_fusion
  439.2 5.5 convolution_convert_fusion.1
  444.7 9.2 add_convert_fusion
  454.0 10.4 %fusion.118 = f32[1024,1152]{1,0:T(8,128)} fusion(bf16[1024,3072]{1,0:T(8,128)(2,1)S(1)} %copy-done.42, bf16[1152,3072]{1,0:T(8,128)(2,1)S(1)} %bitcast.312), kind=kOutput, calls=%fused_computation.361 | convolution fusion | flops 7247757312 | bytes 18087936 | tf_op jit(solution)/shard_map/dot_general | solution.py:33
  464.4 17.5 %multiply_reduce_fusion.1 = (f32[1024]{0:T(1024)S(1)}, f32[1024]{0:T(1024)S(1)}, bf16[1024,1152]{1,0:T(8,128)(2,1)}, f32[1024,1152]{1,0:T(8,128)}) fusion(f32[1024,1152]{1,0:T(8,128)S(1)} %bitcast.314, f32[1024]{0:T(1024)S(1)} %broadcast_multiply_fusion.1, f32[1024,6912]{1,0:T(8,128)} %fusion.106, f32[1024,1152]{1,0:T(8,128)} %fusion.118, ...), kind=kOutput, calls=%fused_computation.74 | convolution fusion | flops 7258372096 | bytes 34615296 | tf_op jit(solution)/shard_map/dot_general | solution.py:33
  481.9 6.1 fusion.110
  495.1 18.5 %multiply_convert_fusion.2 = (bf16[1024,1152]{1,0:T(8,128)(2,1)}, bf16[1,1024,1152]{2,1,0:T(8,128)(2,1)}, bf16[1024,1152]{1,0:T(8,128)(2,1)}) fusion(f32[1024,6912]{1,0:T(8,128)} %fusion.106, f32[1024,1152]{1,0:T(8,128)} %get-tuple-element.566, f32[1024]{0:T(1024)S(1)} %copy-done.109, f32[1024,1152]{1,0:T(8,128)S(1)} %bitcast.314, ...), kind=kOutput, calls=%fused_computation.72 | convolution fusion | flops 7260733440 | bytes 41684992 | tf_op jit(solution)/shard_map/dot_general | solution.py:25
  513.6 8.4 convolution_convert_fusion
  525.4 5.1 pad_maximum_fusion
  531.0 5.3 collective-permute-done.52
  548.1 11.7 %spread.1.do_ref = bf16[16,1024,128]{2,1,0:T(8,128)(2,1)} custom-call(bf16[1024,1152]{1,0:T(8,128)(2,1)} %get-tuple-element.498.ga_ref, bf16[1152,1280]{1,0:T(8,128)(2,1)} %copy-done, bf16[1024,1152]{1,0:T(8,128)(2,1)} %get-tuple-element.521.mix_ref), custom_call_target="tpu_custom_call" | custom-call | flops 2717908992 | bytes 12582912 | tf_op jit(solution)/shard_map/spread/pallas_call | solution.py:499
  559.8 6.5 fusion.14
  566.4 6.1 collective-permute-done.30
  576.8 4.8 all-to-all-start.8
  585.3 24.2 %attend_back.4 = (bf16[1024,896]{1,0:T(8,128)(2,1)}, f32[2,8,128]{2,1,0:T(8,128)}) custom-call(bf16[16,1024,128]{2,1,0:T(8,128)(2,1)} %get-tuple-element.510.q_ref, bf16[16,1024,128]{2,1,0:T(8,128)(2,1)} %get-tuple-element.405.k_ref, bf16[16,1024,128]{2,1,0:T(8,128)(2,1)} %get-tuple-element.406.v_ref, bf16[16,1024,128]{2,1,0:T(8,128)(2,1)} %spread.1.do_ref, ...), custom_call_target="tpu_custom_call" | custom-call | flops 3355443200 | bytes 10485760 | tf_op jit(solution)/shard_map/attend_back/pallas_call | solution.py:601
  609.5 6.4 fusion.15
  626.9 6.2 all-to-all-start.9
  633.1 5.6 fusion.45
  638.7 24.3 %attend_back.5 = (bf16[1024,896]{1,0:T(8,128)(2,1)}, f32[2,8,128]{2,1,0:T(8,128)}) custom-call(bf16[16,1024,128]{2,1,0:T(8,128)(2,1)} %get-tuple-element.510.q_ref, bf16[16,1024,128]{2,1,0:T(8,128)(2,1)} %get-tuple-element.405.k_ref, bf16[16,1024,128]{2,1,0:T(8,128)(2,1)} %get-tuple-element.406.v_ref, bf16[16,1024,128]{2,1,0:T(8,128)(2,1)} %spread.1.do_ref, ...), custom_call_target="tpu_custom_call" | custom-call | flops 3355443200 | bytes 10485760 | tf_op jit(solution)/shard_map/attend_back/pallas_call | solution.py:601
  663.0 5.8 convolution_convert_fusion.6
  680.9 5.0 all-to-all-start.10
  697.1 24.1 %attend_back.6 = (bf16[1024,896]{1,0:T(8,128)(2,1)}, f32[2,8,128]{2,1,0:T(8,128)}) custom-call(bf16[16,1024,128]{2,1,0:T(8,128)(2,1)} %get-tuple-element.510.q_ref, bf16[16,1024,128]{2,1,0:T(8,128)(2,1)} %get-tuple-element.405.k_ref, bf16[16,1024,128]{2,1,0:T(8,128)(2,1)} %get-tuple-element.406.v_ref, bf16[16,1024,128]{2,1,0:T(8,128)(2,1)} %spread.1.do_ref, ...), custom_call_target="tpu_custom_call" | custom-call | flops 3355443200 | bytes 10485760 | tf_op jit(solution)/shard_map/attend_back/pallas_call | solution.py:601
  733.7 4.6 all-to-all-start.11
  742.0 24.1 %attend_back.7 = (bf16[1024,896]{1,0:T(8,128)(2,1)}, f32[2,8,128]{2,1,0:T(8,128)}) custom-call(bf16[16,1024,128]{2,1,0:T(8,128)(2,1)} %get-tuple-element.510.q_ref, bf16[16,1024,128]{2,1,0:T(8,128)(2,1)} %get-tuple-element.405.k_ref, bf16[16,1024,128]{2,1,0:T(8,128)(2,1)} %get-tuple-element.406.v_ref, bf16[16,1024,128]{2,1,0:T(8,128)(2,1)} %spread.1.do_ref, ...), custom_call_target="tpu_custom_call" | custom-call | flops 3355443200 | bytes 10485760 | tf_op jit(solution)/shard_map/attend_back/pallas_call | solution.py:601
  773.3 5.6 fusion.43
  790.7 4.7 all-to-all-start.12
  802.8 17.5 %fusion.36 = (f32[1024]{0:T(1024)S(1)}, f32[1024]{0:T(1024)S(1)}, bf16[1024,1152]{1,0:T(8,128)(2,1)}, f32[1024,1152]{1,0:T(8,128)}) fusion(bf16[1024,1152]{1,0:T(8,128)(2,1)} %bitcast.344, f32[1024]{0:T(1024)S(1)} %broadcast_multiply_fusion, f32[1024,6912]{1,0:T(8,128)} %fusion.106, bf16[1152,3584]{1,0:T(8,128)(2,1)} %place.5.w_ref, ...), kind=kOutput, calls=%fused_computation.58 | convolution fusion | flops 8495691776 | bytes 29765632 | tf_op jit(solution)/shard_map/dot_general | solution.py:33
  820.3 5.8 fusion.109
  844.9 5.6 fusion.44
  851.3 7.7 collective-permute-done.49
  859.8 4.8 all-to-all-start.14
  872.4 4.6 all-to-all-start.13
  887.6 5.0 collective-permute-done.51
  912.5 6.2 collective-permute-done.57
  927.8 5.9 all-to-all-start.16
  947.9 11.5 %all-to-all-done.15 = bf16[4,2,48,896]{3,2,1,0:T(8,128)(2,1)S(1)} async-done(((bf16[4,2,48,896]{3,2,1,0:T(8,128)(2,1)}), bf16[4,2,48,896]{3,2,1,0:T(8,128)(2,1)S(1)}, u32[]{:S(2)}, u32[]{:S(2)}) %all-to-all-start.15) | async-done | bytes 688160 | tf_op jit(solution)/shard_map/all_to_all | solution.py:85
  971.8 4.1 reshape.645
  (657 shorter events, 332.2 us)
Async XLA Ops:
  2.1 26.6 %all-to-all-start.1 = ((bf16[8,8,144]{2,1,0:T(8,128)(2,1)}), bf16[8,8,144]{2,1,0:T(8,128)(2,1)S(1)}, u32[]{:S(2)}, u32[]{:S(2)}) async-start(bf16[8,8,144]{2,1,0:T(8,128)(2,1)} %copy.170), calls=%async_computation.1 | async-start | bytes 65536 | tf_op jit(solution)/shard_map/all_to_all | solution.py:308
  29.9 36.8 %all-to-all-start = ((bf16[4,2,48,1792]{3,2,1,0:T(8,128)(2,1)}), bf16[4,2,48,1792]{3,2,1,0:T(8,128)(2,1)S(1)}, u32[]{:S(2)}, u32[]{:S(2)}) async-start(bf16[4,2,48,1792]{3,2,1,0:T(8,128)(2,1)} %broadcast_in_dim.78), calls=%async_computation | async-start | bytes 2752512 | tf_op jit(solution)/shard_map/all_to_all | solution.py:85
  95.1 36.8 %all-to-all-start.3 = ((bf16[4,2,48,1536]{3,2,1,0:T(8,128)(2,1)}), bf16[4,2,48,1536]{3,2,1,0:T(8,128)(2,1)S(1)}, u32[]{:S(2)}, u32[]{:S(2)}) async-start(bf16[4,2,48,1536]{3,2,1,0:T(8,128)(2,1)} %broadcast_in_dim.83), calls=%async_computation.3 | async-start | bytes 2359296 | tf_op jit(solution)/shard_map/all_to_all | solution.py:85
  99.4 30.4 %collective-permute-start = (bf16[4,2,48,1792]{3,2,0,1:T(8,128)(2,1)S(1)}, bf16[4,2,48,1792]{3,2,0,1:T(8,128)(2,1)S(1)}, u32[]{:S(2)}, u32[]{:S(2)}) collective-permute-start(bf16[4,2,48,1792]{3,2,0,1:T(8,128)(2,1)S(1)} %copy.171), channel_id=1, source_target_pairs={{0,1},{1,0},{2,3},{3,2},{4,5},{5,4},{6,7},{7,6},{8,9},{9,8},{10,11... | collective-permute-start | bytes 4128776 | tf_op jit(solution)/shard_map/ppermute | solution.py:139
  101.8 29.0 %collective-permute-start.2 = (bf16[4,2,48,1792]{3,2,1,0:T(8,128)(2,1)S(1)}, bf16[4,2,48,1792]{3,2,1,0:T(8,128)(2,1)S(1)}, u32[]{:S(2)}, u32[]{:S(2)}) collective-permute-start(bf16[4,2,48,1792]{3,2,1,0:T(8,128)(2,1)S(1)} %all-to-all-done.a0), channel_id=1, source_target_pairs={{0,8},{1,9},{2,10},{3,11},{4,12},{5,13},{6,14},{7,15},{8,0},{9,1},... | collective-permute-start | bytes 4128776 | tf_op jit(solution)/shard_map/ppermute | solution.py:156
  104.4 17.1 %collective-permute-start.1 = (bf16[4,48,1792]{2,1,0:T(8,128)(2,1)S(1)}, bf16[4,48,1792]{2,1,0:T(8,128)(2,1)S(1)}, u32[]{:S(2)}, u32[]{:S(2)}) collective-permute-start(bf16[4,48,1792]{2,1,0:T(8,128)(2,1)S(1)} %slice_bitcast_fusion), channel_id=1, source_target_pairs={{0,16},{1,17},{2,18},{3,19},{4,20},{5,21},{6,22},{7,23},{8,24},{9,... | collective-permute-start | bytes 2064392 | tf_op jit(solution)/shard_map/ppermute | solution.py:147
  134.3 17.0 %all-to-all-start.6 = ((bf16[8,8,4608]{2,1,0:T(8,128)(2,1)}), bf16[8,8,4608]{2,1,0:T(8,128)(2,1)}, u32[]{:S(2)}, u32[]{:S(2)}) async-start(bf16[8,8,4608]{2,1,0:T(8,128)(2,1)} %slice_bitcast_fusion.2), calls=%async_computation.6 | async-start | bytes 1179648 | tf_op jit(solution)/shard_map/all_to_all | solution.py:314
  152.3 33.4 %all-to-all-start.5 = ((bf16[4,2,48,1536]{3,2,1,0:T(8,128)(2,1)}), bf16[4,2,48,1536]{3,2,1,0:T(8,128)(2,1)S(1)}, u32[]{:S(2)}, u32[]{:S(2)}) async-start(bf16[4,2,48,1536]{3,2,1,0:T(8,128)(2,1)} %broadcast_in_dim.84), calls=%async_computation.5 | async-start | bytes 2359296 | tf_op jit(solution)/shard_map/all_to_all | solution.py:85
  157.7 23.0 %collective-permute-start.4 = (bf16[4,2,48,1792]{3,2,0,1:T(8,128)(2,1)}, bf16[4,2,48,1792]{3,2,0,1:T(8,128)(2,1)}, u32[]{:S(2)}, u32[]{:S(2)}) collective-permute-start(bf16[4,2,48,1792]{3,2,0,1:T(8,128)(2,1)} %copy-done.49), channel_id=1, source_target_pairs={{0,8},{1,9},{2,10},{3,11},{4,12},{5,13},{6,14},{7,15},{8,0},{9,1},... | collective-permute-start | bytes 4128776 | tf_op jit(solution)/shard_map/ppermute | solution.py:156
  163.4 17.4 %collective-permute-start.3 = (bf16[4,48,1792]{2,1,0:T(8,128)(2,1)}, bf16[4,48,1792]{2,1,0:T(8,128)(2,1)}, u32[]{:S(2)}, u32[]{:S(2)}) collective-permute-start(bf16[4,48,1792]{2,1,0:T(8,128)(2,1)} %slice_bitcast_fusion.1), channel_id=1, source_target_pairs={{0,16},{1,17},{2,18},{3,19},{4,20},{5,21},{6,22},{7,23},{8,24},{9,... | collective-permute-start | bytes 2064392 | tf_op jit(solution)/shard_map/ppermute | solution.py:149
  193.9 61.7 %all-to-all-start.7 = ((bf16[4,2,128,640]{3,2,1,0:T(8,128)(2,1)}), bf16[4,2,128,640]{3,2,1,0:T(8,128)(2,1)S(1)}, u32[]{:S(2)}, u32[]{:S(2)}) async-start(bf16[4,2,128,640]{3,2,1,0:T(8,128)(2,1)} %broadcast_in_dim.85), calls=%async_computation.7 | async-start | bytes 2621440 | tf_op jit(solution)/shard_map/all_to_all | solution.py:85
  201.5 53.4 %collective-permute-start.8 = (bf16[4,2,48,640]{3,2,1,0:T(8,128)(2,1)S(1)}, bf16[4,2,48,640]{3,2,1,0:T(8,128)(2,1)S(1)}, u32[]{:S(2)}, u32[]{:S(2)}) collective-permute-start(bf16[4,2,48,640]{3,2,1,0:T(8,128)(2,1)S(1)} %pad_maximum_fusion.20), channel_id=1, source_target_pairs={{0,16},{1,17},{2,18},{3,19},{4,20},{5,21},{6,22},{7,23},{8,24},{9,... | collective-permute-start | bytes 1474568 | tf_op jit(solution)/shard_map/ppermute | solution.py:151
  202.7 52.1 %collective-permute-start.9 = (bf16[4,2,48,1536]{3,2,1,0:T(8,128)(2,1)S(1)}, bf16[4,2,48,1536]{3,2,1,0:T(8,128)(2,1)}, u32[]{:S(2)}, u32[]{:S(2)}) collective-permute-start(bf16[4,2,48,1536]{3,2,1,0:T(8,128)(2,1)S(1)} %copy-done.2), channel_id=1, source_target_pairs={{0,1},{1,0},{2,3},{3,2},{4,5},{5,4},{6,7},{7,6},{8,9},{9,8},{10,11... | collective-permute-start | bytes 3538952 | tf_op jit(solution)/shard_map/ppermute | solution.py:139
  204.4 51.3 %collective-permute-start.10 = (bf16[4,2,48,1536]{3,2,1,0:T(8,128)(2,1)S(1)}, bf16[4,2,48,1536]{3,2,1,0:T(8,128)(2,1)}, u32[]{:S(2)}, u32[]{:S(2)}) collective-permute-start(bf16[4,2,48,1536]{3,2,1,0:T(8,128)(2,1)S(1)} %copy-done.5), channel_id=1, source_target_pairs={{0,1},{1,0},{2,3},{3,2},{4,5},{5,4},{6,7},{7,6},{8,9},{9,8},{10,11... | collective-permute-start | bytes 3538952 | tf_op jit(solution)/shard_map/ppermute | solution.py:139
  258.0 43.6 %collective-permute-start.14 = (bf16[4,2,48,1536]{3,2,1,0:T(8,128)(2,1)}, bf16[4,2,48,1536]{3,2,1,0:T(8,128)(2,1)}, u32[]{:S(2)}, u32[]{:S(2)}) collective-permute-start(bf16[4,2,48,1536]{3,2,1,0:T(8,128)(2,1)} %pad_maximum_fusion.10), channel_id=1, source_target_pairs={{0,16},{1,17},{2,18},{3,19},{4,20},{5,21},{6,22},{7,23},{8,24},{9,... | collective-permute-start | bytes 3538952 | tf_op jit(solution)/shard_map/ppermute | solution.py:151
  258.3 43.4 %collective-permute-start.15 = (bf16[4,2,128,640]{3,2,1,0:T(8,128)(2,1)S(1)}, bf16[4,2,128,640]{3,2,1,0:T(8,128)(2,1)S(1)}, u32[]{:S(2)}, u32[]{:S(2)}) collective-permute-start(bf16[4,2,128,640]{3,2,1,0:T(8,128)(2,1)S(1)} %all-to-all-done.7.a0), channel_id=1, source_target_pairs={{0,1},{1,0},{2,3},{3,2},{4,5},{5,4},{6,7},{7,6},{8,9},{9,8},{10,11... | collective-permute-start | bytes 3932168 | tf_op jit(solution)/shard_map/ppermute | solution.py:139
  271.0 29.8 %collective-permute-start.11 = (bf16[4,2,48,640]{3,2,1,0:T(8,128)(2,1)S(1)}, bf16[4,2,48,640]{3,2,1,0:T(8,128)(2,1)S(1)}, u32[]{:S(2)}, u32[]{:S(2)}) collective-permute-start(bf16[4,2,48,640]{3,2,1,0:T(8,128)(2,1)S(1)} %copy-done.21), channel_id=1, source_target_pairs={{0,8},{1,9},{2,10},{3,11},{4,12},{5,13},{6,14},{7,15},{8,0},{9,1},... | collective-permute-start | bytes 1474568 | tf_op jit(solution)/shard_map/ppermute | solution.py:156
  272.6 28.2 %collective-permute-start.12 = (bf16[4,2,48,640]{3,2,1,0:T(8,128)(2,1)S(1)}, bf16[4,2,48,640]{3,2,1,0:T(8,128)(2,1)S(1)}, u32[]{:S(2)}, u32[]{:S(2)}) collective-permute-start(bf16[4,2,48,640]{3,2,1,0:T(8,128)(2,1)S(1)} %copy-done.18), channel_id=1, source_target_pairs={{0,8},{1,9},{2,10},{3,11},{4,12},{5,13},{6,14},{7,15},{8,0},{9,1},... | collective-permute-start | bytes 1474568 | tf_op jit(solution)/shard_map/ppermute | solution.py:156
  272.7 28.9 %collective-permute-start.13 = (bf16[4,2,48,640]{3,2,1,0:T(8,128)(2,1)S(1)}, bf16[4,2,48,640]{3,2,1,0:T(8,128)(2,1)}, u32[]{:S(2)}, u32[]{:S(2)}) collective-permute-start(bf16[4,2,48,640]{3,2,1,0:T(8,128)(2,1)S(1)} %all-to-all-done.2.a0), channel_id=1, source_target_pairs={{0,8},{1,9},{2,10},{3,11},{4,12},{5,13},{6,14},{7,15},{8,0},{9,1},... | collective-permute-start | bytes 1474568 | tf_op jit(solution)/shard_map/ppermute | solution.py:156
  301.7 31.9 %collective-permute-start.16 = (bf16[4,2,48,1536]{3,2,1,0:T(8,128)(2,1)}, bf16[4,2,48,1536]{3,2,1,0:T(8,128)(2,1)S(1)}, u32[]{:S(2)}, u32[]{:S(2)}) collective-permute-start(bf16[4,2,48,1536]{3,2,1,0:T(8,128)(2,1)} %collective-permute-done.14.ax), channel_id=1, source_target_pairs={{0,8},{1,9},{2,10},{3,11},{4,12},{5,13},{6,14},{7,15},{8,0},{9,1},... | collective-permute-start | bytes 3538952 | tf_op jit(solution)/shard_map/ppermute | solution.py:156
  301.8 31.7 %collective-permute-start.17 = (bf16[4,2,48,1536]{3,2,1,0:T(8,128)(2,1)}, bf16[4,2,48,1536]{3,2,1,0:T(8,128)(2,1)S(1)}, u32[]{:S(2)}, u32[]{:S(2)}) collective-permute-start(bf16[4,2,48,1536]{3,2,1,0:T(8,128)(2,1)} %collective-permute-done.9.a1), channel_id=1, source_target_pairs={{0,8},{1,9},{2,10},{3,11},{4,12},{5,13},{6,14},{7,15},{8,0},{9,1},... | collective-permute-start | bytes 3538952 | tf_op jit(solution)/shard_map/ppermute | solution.py:156
  302.3 31.3 %collective-permute-start.18 = (bf16[4,2,48,1536]{3,2,1,0:T(8,128)(2,1)S(1)}, bf16[4,2,48,1536]{3,2,1,0:T(8,128)(2,1)S(1)}, u32[]{:S(2)}, u32[]{:S(2)}) collective-permute-start(bf16[4,2,48,1536]{3,2,1,0:T(8,128)(2,1)S(1)} %copy-done.3), channel_id=1, source_target_pairs={{0,8},{1,9},{2,10},{3,11},{4,12},{5,13},{6,14},{7,15},{8,0},{9,1},... | collective-permute-start | bytes 3538952 | tf_op jit(solution)/shard_map/ppermute | solution.py:156
  303.9 29.7 %collective-permute-start.19 = (bf16[4,2,48,1536]{3,2,1,0:T(8,128)(2,1)S(1)}, bf16[4,2,48,1536]{3,2,1,0:T(8,128)(2,1)S(1)}, u32[]{:S(2)}, u32[]{:S(2)}) collective-permute-start(bf16[4,2,48,1536]{3,2,1,0:T(8,128)(2,1)S(1)} %pad_maximum_fusion.11), channel_id=1, source_target_pairs={{0,16},{1,17},{2,18},{3,19},{4,20},{5,21},{6,22},{7,23},{8,24},{9,... | collective-permute-start | bytes 3538952 | tf_op jit(solution)/shard_map/ppermute | solution.py:151
  333.6 19.1 %collective-permute-start.20 = (bf16[4,2,48,1536]{3,2,1,0:T(8,128)(2,1)S(1)}, bf16[4,2,48,1536]{3,2,1,0:T(8,128)(2,1)S(1)}, u32[]{:S(2)}, u32[]{:S(2)}) collective-permute-start(bf16[4,2,48,1536]{3,2,1,0:T(8,128)(2,1)S(1)} %collective-permute-done.19.ax), channel_id=1, source_target_pairs={{0,8},{1,9},{2,10},{3,11},{4,12},{5,13},{6,14},{7,15},{8,0},{9,1},... | collective-permute-start | bytes 3538952 | tf_op jit(solution)/shard_map/ppermute | solution.py:156
  334.1 19.6 %collective-permute-start.21 = (bf16[4,2,48,1536]{3,2,1,0:T(8,128)(2,1)}, bf16[4,2,48,1536]{3,2,1,0:T(8,128)(2,1)S(1)}, u32[]{:S(2)}, u32[]{:S(2)}) collective-permute-start(bf16[4,2,48,1536]{3,2,1,0:T(8,128)(2,1)} %collective-permute-done.10.a1), channel_id=1, source_target_pairs={{0,8},{1,9},{2,10},{3,11},{4,12},{5,13},{6,14},{7,15},{8,0},{9,1},... | collective-permute-start | bytes 3538952 | tf_op jit(solution)/shard_map/ppermute | solution.py:156
  334.2 20.5 %collective-permute-start.22 = (bf16[4,2,48,1536]{3,2,1,0:T(8,128)(2,1)S(1)}, bf16[4,2,48,1536]{3,2,1,0:T(8,128)(2,1)}, u32[]{:S(2)}, u32[]{:S(2)}) collective-permute-start(bf16[4,2,48,1536]{3,2,1,0:T(8,128)(2,1)S(1)} %copy-done.6), channel_id=1, source_target_pairs={{0,8},{1,9},{2,10},{3,11},{4,12},{5,13},{6,14},{7,15},{8,0},{9,1},... | collective-permute-start | bytes 3538952 | tf_op jit(solution)/shard_map/ppermute | solution.py:156
  335.9 30.2 %collective-permute-start.23 = (bf16[4,2,128,640]{3,2,1,0:T(8,128)(2,1)}, bf16[4,2,128,640]{3,2,1,0:T(8,128)(2,1)S(1)}, u32[]{:S(2)}, u32[]{:S(2)}) collective-permute-start(bf16[4,2,128,640]{3,2,1,0:T(8,128)(2,1)} %pad_maximum_fusion.7), channel_id=1, source_target_pairs={{0,16},{1,17},{2,18},{3,19},{4,20},{5,21},{6,22},{7,23},{8,24},{9,... | collective-permute-start | bytes 3932168 | tf_op jit(solution)/shard_map/ppermute | solution.py:151
  366.1 24.5 %collective-permute-start.24 = (bf16[4,2,128,640]{3,2,1,0:T(8,128)(2,1)S(1)}, bf16[4,2,128,640]{3,2,1,0:T(8,128)(2,1)S(1)}, u32[]{:S(2)}, u32[]{:S(2)}) collective-permute-start(bf16[4,2,128,640]{3,2,1,0:T(8,128)(2,1)S(1)} %collective-permute-done.23.ax), channel_id=1, source_target_pairs={{0,8},{1,9},{2,10},{3,11},{4,12},{5,13},{6,14},{7,15},{8,0},{9,1},... | collective-permute-start | bytes 3932168 | tf_op jit(solution)/shard_map/ppermute | solution.py:156
  367.3 23.2 %collective-permute-start.25 = (bf16[4,2,128,640]{3,2,1,0:T(8,128)(2,1)S(1)}, bf16[4,2,128,640]{3,2,1,0:T(8,128)(2,1)S(1)}, u32[]{:S(2)}, u32[]{:S(2)}) collective-permute-start(bf16[4,2,128,640]{3,2,1,0:T(8,128)(2,1)S(1)} %copy-done.10), channel_id=1, source_target_pairs={{0,8},{1,9},{2,10},{3,11},{4,12},{5,13},{6,14},{7,15},{8,0},{9,1},... | collective-permute-start | bytes 3932168 | tf_op jit(solution)/shard_map/ppermute | solution.py:156
  367.3 23.2 %collective-permute-start.26 = (bf16[4,2,128,640]{3,2,1,0:T(8,128)(2,1)S(1)}, bf16[4,2,128,640]{3,2,1,0:T(8,128)(2,1)S(1)}, u32[]{:S(2)}, u32[]{:S(2)}) collective-permute-start(bf16[4,2,128,640]{3,2,1,0:T(8,128)(2,1)S(1)} %all-to-all-done.7.a0), channel_id=1, source_target_pairs={{0,8},{1,9},{2,10},{3,11},{4,12},{5,13},{6,14},{7,15},{8,0},{9,1},... | collective-permute-start | bytes 3932168 | tf_op jit(solution)/shard_map/ppermute | solution.py:156
  408.2 18.7 %collective-permute-start.27 = (bf16[3072,640]{1,0:T(8,128)(2,1)}, bf16[3072,640]{1,0:T(8,128)(2,1)}, u32[]{:S(2)}, u32[]{:S(2)}) collective-permute-start(bf16[3072,640]{1,0:T(8,128)(2,1)} %convolution_convert_fusion.4), channel_id=1, source_target_pairs={{0,8},{1,9},{2,10},{3,11},{4,12},{5,13},{6,14},{7,15},{8,0},{9,1},... | collective-permute-start | bytes 11796488 | tf_op jit(solution)/shard_map/ppermute | solution.py:203
  490.6 39.9 %collective-permute-start.28 = (bf16[4,2,128,640]{3,2,1,0:T(8,128)(2,1)}, bf16[4,2,128,640]{3,2,1,0:T(8,128)(2,1)}, u32[]{:S(2)}, u32[]{:S(2)}) collective-permute-start(bf16[4,2,128,640]{3,2,1,0:T(8,128)(2,1)} %dynamic-slice_bitcast_fusion.6), channel_id=1, source_target_pairs={{0,16},{1,17},{2,18},{3,19},{4,20},{5,21},{6,22},{7,23},{8,24},{9,... | collective-permute-start | bytes 3932168 | tf_op jit(solution)/shard_map/ppermute | solution.py:218
  490.9 39.7 %collective-permute-start.29 = (bf16[1152,1536]{1,0:T(8,128)(2,1)}, bf16[1152,1536]{1,0:T(8,128)(2,1)}, u32[]{:S(2)}, u32[]{:S(2)}) collective-permute-start(bf16[1152,1536]{1,0:T(8,128)(2,1)} %convolution_convert_fusion.1), channel_id=1, source_target_pairs={{0,8},{1,9},{2,10},{3,11},{4,12},{5,13},{6,14},{7,15},{8,0},{9,1},... | collective-permute-start | bytes 10616840 | tf_op jit(solution)/shard_map/ppermute | solution.py:203
  530.5 42.0 %collective-permute-start.31 = (bf16[1152,1536]{1,0:T(8,128)(2,1)}, bf16[1152,1536]{1,0:T(8,128)(2,1)}, u32[]{:S(2)}, u32[]{:S(2)}) collective-permute-start(bf16[1152,1536]{1,0:T(8,128)(2,1)} %convolution_convert_fusion), channel_id=1, source_target_pairs={{0,8},{1,9},{2,10},{3,11},{4,12},{5,13},{6,14},{7,15},{8,0},{9,1},... | collective-permute-start | bytes 10616840 | tf_op jit(solution)/shard_map/ppermute | solution.py:203
  537.1 44.5 %collective-permute-start.53 = (bf16[2,64,144]{2,1,0:T(8,128)(2,1)}, bf16[2,64,144]{2,1,0:T(8,128)(2,1)}, u32[]{:S(2)}, u32[]{:S(2)}) collective-permute-start(bf16[2,64,144]{2,1,0:T(8,128)(2,1)} %pad_maximum_fusion.37), channel_id=1, source_target_pairs={{0,16},{1,17},{2,18},{3,19},{4,20},{5,21},{6,22},{7,23},{8,24},{9,... | collective-permute-start | bytes 110600 | tf_op jit(solution)/shard_map/ppermute | solution.py:292
  542.6 29.8 %collective-permute-start.30 = (bf16[4,2,128,640]{3,2,1,0:T(8,128)(2,1)S(1)}, bf16[4,2,128,640]{3,2,1,0:T(8,128)(2,1)}, u32[]{:S(2)}, u32[]{:S(2)}) collective-permute-start(bf16[4,2,128,640]{3,2,1,0:T(8,128)(2,1)S(1)} %pad_maximum_fusion.8), channel_id=1, source_target_pairs={{0,1},{1,0},{2,3},{3,2},{4,5},{5,4},{6,7},{7,6},{8,9},{9,8},{10,11... | collective-permute-start | bytes 3932168 | tf_op jit(solution)/shard_map/ppermute | solution.py:229
  576.8 39.2 %all-to-all-start.8 = ((bf16[4,2,128,640]{3,2,1,0:T(8,128)(2,1)}), bf16[4,2,128,640]{3,2,1,0:T(8,128)(2,1)}, u32[]{:S(2)}, u32[]{:S(2)}) async-start(bf16[4,2,128,640]{3,2,1,0:T(8,128)(2,1)} %add_convert_fusion.2), calls=%async_computation.8 | async-start | bytes 2621440 | tf_op jit(solution)/shard_map/all_to_all | solution.py:85
  583.1 32.8 %collective-permute-start.33 = (bf16[1152,640]{1,0:T(8,128)(2,1)}, bf16[1152,640]{1,0:T(8,128)(2,1)}, u32[]{:S(2)}, u32[]{:S(2)}) collective-permute-start(bf16[1152,640]{1,0:T(8,128)(2,1)} %convolution_convert_fusion.8), channel_id=1, source_target_pairs={{0,8},{1,9},{2,10},{3,11},{4,12},{5,13},{6,14},{7,15},{8,0},{9,1},... | collective-permute-start | bytes 4423688 | tf_op jit(solution)/shard_map/ppermute | solution.py:203
  585.0 30.9 %collective-permute-start.32 = (bf16[4,2,48,1536]{3,2,1,0:T(8,128)(2,1)S(1)}, bf16[4,2,48,1536]{3,2,1,0:T(8,128)(2,1)}, u32[]{:S(2)}, u32[]{:S(2)}) collective-permute-start(bf16[4,2,48,1536]{3,2,1,0:T(8,128)(2,1)S(1)} %dynamic-slice_bitcast_fusion.8), channel_id=1, source_target_pairs={{0,16},{1,17},{2,18},{3,19},{4,20},{5,21},{6,22},{7,23},{8,24},{9,... | collective-permute-start | bytes 3538952 | tf_op jit(solution)/shard_map/ppermute | solution.py:218
  619.3 50.9 %collective-permute-start.34 = (bf16[2,128,640]{2,1,0:T(8,128)(2,1)}, bf16[2,128,640]{2,1,0:T(8,128)(2,1)}, u32[]{:S(2)}, u32[]{:S(2)}) collective-permute-start(bf16[2,128,640]{2,1,0:T(8,128)(2,1)} %reduce_sum.270), channel_id=1, source_target_pairs={{0,16},{1,17},{2,18},{3,19},{4,20},{5,21},{6,22},{7,23},{8,24},{9,... | collective-permute-start | bytes 983048 | tf_op jit(solution)/shard_map/ppermute | solution.py:240
  624.5 45.7 %collective-permute-start.35 = (bf16[4,2,48,1536]{3,2,1,0:T(8,128)(2,1)}, bf16[4,2,48,1536]{3,2,1,0:T(8,128)(2,1)}, u32[]{:S(2)}, u32[]{:S(2)}) collective-permute-start(bf16[4,2,48,1536]{3,2,1,0:T(8,128)(2,1)} %pad_maximum_fusion.12), channel_id=1, source_target_pairs={{0,1},{1,0},{2,3},{3,2},{4,5},{5,4},{6,7},{7,6},{8,9},{9,8},{10,11... | collective-permute-start | bytes 3538952 | tf_op jit(solution)/shard_map/ppermute | solution.py:229
  625.6 44.6 %collective-permute-start.36 = (bf16[4,2,48,1536]{3,2,1,0:T(8,128)(2,1)}, bf16[4,2,48,1536]{3,2,1,0:T(8,128)(2,1)}, u32[]{:S(2)}, u32[]{:S(2)}) collective-permute-start(bf16[4,2,48,1536]{3,2,1,0:T(8,128)(2,1)} %dynamic-slice_bitcast_fusion.7), channel_id=1, source_target_pairs={{0,16},{1,17},{2,18},{3,19},{4,20},{5,21},{6,22},{7,23},{8,24},{9,... | collective-permute-start | bytes 3538952 | tf_op jit(solution)/shard_map/ppermute | solution.py:218
  626.9 43.3 %all-to-all-start.9 = ((bf16[8,8,4608]{2,1,0:T(8,128)(2,1)}), bf16[8,8,4608]{2,1,0:T(8,128)(2,1)}, u32[]{:S(2)}, u32[]{:S(2)}) async-start(bf16[8,8,4608]{2,1,0:T(8,128)(2,1)} %broadcast_in_dim.91), calls=%async_computation.9 | async-start | bytes 1179648 | tf_op jit(solution)/shard_map/all_to_all | solution.py:300
  673.1 50.7 %collective-permute-start.37 = (bf16[384,640]{1,0:T(8,128)(2,1)}, bf16[384,640]{1,0:T(8,128)(2,1)}, u32[]{:S(2)}, u32[]{:S(2)}) collective-permute-start(bf16[384,640]{1,0:T(8,128)(2,1)} %pad_maximum_fusion.21), channel_id=1, source_target_pairs={{0,8},{1,9},{2,10},{3,11},{4,12},{5,13},{6,14},{7,15},{8,0},{9,1},... | collective-permute-start | bytes 1474568 | tf_op jit(solution)/shard_map/ppermute | solution.py:250
  680.9 45.3 %all-to-all-start.10 = ((bf16[4,2,48,1536]{3,2,1,0:T(8,128)(2,1)}), bf16[4,2,48,1536]{3,2,1,0:T(8,128)(2,1)}, u32[]{:S(2)}, u32[]{:S(2)}) async-start(bf16[4,2,48,1536]{3,2,1,0:T(8,128)(2,1)} %add_convert_fusion.4), calls=%async_computation.10 | async-start | bytes 2359296 | tf_op jit(solution)/shard_map/all_to_all | solution.py:85
  688.6 34.8 %collective-permute-start.42 = (bf16[2,64,4608]{2,1,0:T(8,128)(2,1)}, bf16[2,64,4608]{2,1,0:T(8,128)(2,1)S(1)}, u32[]{:S(2)}, u32[]{:S(2)}) collective-permute-start(bf16[2,64,4608]{2,1,0:T(8,128)(2,1)} %pad_maximum_fusion.14), channel_id=1, source_target_pairs={{0,16},{1,17},{2,18},{3,19},{4,20},{5,21},{6,22},{7,23},{8,24},{9,... | collective-permute-start | bytes 3538952 | tf_op jit(solution)/shard_map/ppermute | solution.py:292
  691.9 34.3 %collective-permute-start.38 = (bf16[4,2,48,1536]{3,2,1,0:T(8,128)(2,1)}, bf16[4,2,48,1536]{3,2,1,0:T(8,128)(2,1)S(1)}, u32[]{:S(2)}, u32[]{:S(2)}) collective-permute-start(bf16[4,2,48,1536]{3,2,1,0:T(8,128)(2,1)} %pad_maximum_fusion.13), channel_id=1, source_target_pairs={{0,1},{1,0},{2,3},{3,2},{4,5},{5,4},{6,7},{7,6},{8,9},{9,8},{10,11... | collective-permute-start | bytes 3538952 | tf_op jit(solution)/shard_map/ppermute | solution.py:229
  695.0 31.2 %collective-permute-start.39 = (bf16[4,2,48,640]{3,2,1,0:T(8,128)(2,1)}, bf16[4,2,48,640]{3,2,1,0:T(8,128)(2,1)}, u32[]{:S(2)}, u32[]{:S(2)}) collective-permute-start(bf16[4,2,48,640]{3,2,1,0:T(8,128)(2,1)} %dynamic-slice_bitcast_fusion.17), channel_id=1, source_target_pairs={{0,16},{1,17},{2,18},{3,19},{4,20},{5,21},{6,22},{7,23},{8,24},{9,... | collective-permute-start | bytes 1474568 | tf_op jit(solution)/shard_map/ppermute | solution.py:218
  695.5 30.7 %collective-permute-start.40 = (bf16[1152,896]{1,0:T(8,128)(2,1)}, bf16[1152,896]{1,0:T(8,128)(2,1)}, u32[]{:S(2)}, u32[]{:S(2)}) collective-permute-start(bf16[1152,896]{1,0:T(8,128)(2,1)} %convolution_convert_fusion.6), channel_id=1, source_target_pairs={{0,8},{1,9},{2,10},{3,11},{4,12},{5,13},{6,14},{7,15},{8,0},{9,1},... | collective-permute-start | bytes 6193160 | tf_op jit(solution)/shard_map/ppermute | solution.py:203
  728.4 53.0 %collective-permute-start.43 = (bf16[2,48,1536]{2,1,0:T(8,128)(2,1)}, bf16[2,48,1536]{2,1,0:T(8,128)(2,1)}, u32[]{:S(2)}, u32[]{:S(2)}) collective-permute-start(bf16[2,48,1536]{2,1,0:T(8,128)(2,1)} %reduce_sum.271), channel_id=1, source_target_pairs={{0,16},{1,17},{2,18},{3,19},{4,20},{5,21},{6,22},{7,23},{8,24},{9,... | collective-permute-start | bytes 884744 | tf_op jit(solution)/shard_map/ppermute | solution.py:240
  733.7 47.7 %all-to-all-start.11 = ((bf16[4,2,48,1536]{3,2,1,0:T(8,128)(2,1)}), bf16[4,2,48,1536]{3,2,1,0:T(8,128)(2,1)S(1)}, u32[]{:S(2)}, u32[]{:S(2)}) async-start(bf16[4,2,48,1536]{3,2,1,0:T(8,128)(2,1)} %add_convert_fusion.3), calls=%async_computation.11 | async-start | bytes 2359296 | tf_op jit(solution)/shard_map/all_to_all | solution.py:85
  740.8 40.7 %collective-permute-start.44 = (bf16[4,2,48,640]{3,2,1,0:T(8,128)(2,1)S(1)}, bf16[4,2,48,640]{3,2,1,0:T(8,128)(2,1)}, u32[]{:S(2)}, u32[]{:S(2)}) collective-permute-start(bf16[4,2,48,640]{3,2,1,0:T(8,128)(2,1)S(1)} %pad_maximum_fusion.22), channel_id=1, source_target_pairs={{0,1},{1,0},{2,3},{3,2},{4,5},{5,4},{6,7},{7,6},{8,9},{9,8},{10,11... | collective-permute-start | bytes 1474568 | tf_op jit(solution)/shard_map/ppermute | solution.py:229
  785.8 49.2 %collective-permute-start.45 = (bf16[2,48,1536]{2,1,0:T(8,128)(2,1)}, bf16[2,48,1536]{2,1,0:T(8,128)(2,1)}, u32[]{:S(2)}, u32[]{:S(2)}) collective-permute-start(bf16[2,48,1536]{2,1,0:T(8,128)(2,1)} %reduce_sum.272), channel_id=1, source_target_pairs={{0,16},{1,17},{2,18},{3,19},{4,20},{5,21},{6,22},{7,23},{8,24},{9,... | collective-permute-start | bytes 884744 | tf_op jit(solution)/shard_map/ppermute | solution.py:240
  790.7 44.3 %all-to-all-start.12 = ((bf16[4,2,48,640]{3,2,1,0:T(8,128)(2,1)}), bf16[4,2,48,640]{3,2,1,0:T(8,128)(2,1)S(1)}, u32[]{:S(2)}, u32[]{:S(2)}) async-start(bf16[4,2,48,640]{3,2,1,0:T(8,128)(2,1)} %add_convert_fusion.7), calls=%async_computation.12 | async-start | bytes 983040 | tf_op jit(solution)/shard_map/all_to_all | solution.py:85
  797.5 37.6 %collective-permute-start.46 = (bf16[4,2,48,896]{3,2,1,0:T(8,128)(2,1)}, bf16[4,2,48,896]{3,2,1,0:T(8,128)(2,1)}, u32[]{:S(2)}, u32[]{:S(2)}) collective-permute-start(bf16[4,2,48,896]{3,2,1,0:T(8,128)(2,1)} %dynamic-slice_bitcast_fusion.16), channel_id=1, source_target_pairs={{0,16},{1,17},{2,18},{3,19},{4,20},{5,21},{6,22},{7,23},{8,24},{9,... | collective-permute-start | bytes 2064392 | tf_op jit(solution)/shard_map/ppermute | solution.py:218
  798.4 36.7 %collective-permute-start.47 = (bf16[1152,896]{1,0:T(8,128)(2,1)}, bf16[1152,896]{1,0:T(8,128)(2,1)}, u32[]{:S(2)}, u32[]{:S(2)}) collective-permute-start(bf16[1152,896]{1,0:T(8,128)(2,1)} %convolution_convert_fusion.5), channel_id=1, source_target_pairs={{0,8},{1,9},{2,10},{3,11},{4,12},{5,13},{6,14},{7,15},{8,0},{9,1},... | collective-permute-start | bytes 6193160 | tf_op jit(solution)/shard_map/ppermute | solution.py:203
  802.8 30.2 %collective-permute-start.61 = (bf16[144,1536]{1,0:T(8,128)(2,1)}, bf16[144,1536]{1,0:T(8,128)(2,1)}, u32[]{:S(2)}, u32[]{:S(2)}) collective-permute-start(bf16[144,1536]{1,0:T(8,128)(2,1)} %pad_maximum_fusion.23), channel_id=1, source_target_pairs={{0,8},{1,9},{2,10},{3,11},{4,12},{5,13},{6,14},{7,15},{8,0},{9,1},... | collective-permute-start | bytes 1327112 | tf_op jit(solution)/shard_map/ppermute | solution.py:250
  842.7 16.3 %collective-permute-start.49 = (bf16[4,2,48,896]{3,2,1,0:T(8,128)(2,1)S(1)}, bf16[4,2,48,896]{3,2,1,0:T(8,128)(2,1)}, u32[]{:S(2)}, u32[]{:S(2)}) collective-permute-start(bf16[4,2,48,896]{3,2,1,0:T(8,128)(2,1)S(1)} %pad_maximum_fusion.17), channel_id=1, source_target_pairs={{0,1},{1,0},{2,3},{3,2},{4,5},{5,4},{6,7},{7,6},{8,9},{9,8},{10,11... | collective-permute-start | bytes 2064392 | tf_op jit(solution)/shard_map/ppermute | solution.py:229
  843.8 20.8 %collective-permute-start.62 = (bf16[144,1536]{1,0:T(8,128)(2,1)}, bf16[144,1536]{1,0:T(8,128)(2,1)}, u32[]{:S(2)}, u32[]{:S(2)}) collective-permute-start(bf16[144,1536]{1,0:T(8,128)(2,1)} %pad_maximum_fusion.24), channel_id=1, source_target_pairs={{0,8},{1,9},{2,10},{3,11},{4,12},{5,13},{6,14},{7,15},{8,0},{9,1},... | collective-permute-start | bytes 1327112 | tf_op jit(solution)/shard_map/ppermute | solution.py:250
  872.4 21.9 %all-to-all-start.13 = ((bf16[4,2,48,896]{3,2,1,0:T(8,128)(2,1)}), bf16[4,2,48,896]{3,2,1,0:T(8,128)(2,1)S(1)}, u32[]{:S(2)}, u32[]{:S(2)}) async-start(bf16[4,2,48,896]{3,2,1,0:T(8,128)(2,1)} %add_convert_fusion.6), calls=%async_computation.13 | async-start | bytes 1376256 | tf_op jit(solution)/shard_map/all_to_all | solution.py:85
  902.3 16.4 %collective-permute-start.57 = (bf16[2,64,2560]{2,1,0:T(8,128)(2,1)}, bf16[2,64,2560]{2,1,0:T(8,128)(2,1)}, u32[]{:S(2)}, u32[]{:S(2)}) collective-permute-start(bf16[2,64,2560]{2,1,0:T(8,128)(2,1)} %pad_maximum_fusion.19), channel_id=1, source_target_pairs={{0,16},{1,17},{2,18},{3,19},{4,20},{5,21},{6,22},{7,23},{8,24},{9,... | collective-permute-start | bytes 1966088 | tf_op jit(solution)/shard_map/ppermute | solution.py:292
  905.6 16.7 %collective-permute-start.54 = (bf16[2,48,896]{2,1,0:T(8,128)(2,1)S(1)}, bf16[2,48,896]{2,1,0:T(8,128)(2,1)S(1)}, u32[]{:S(2)}, u32[]{:S(2)}) collective-permute-start(bf16[2,48,896]{2,1,0:T(8,128)(2,1)S(1)} %reduce_sum.279), channel_id=1, source_target_pairs={{0,16},{1,17},{2,18},{3,19},{4,20},{5,21},{6,22},{7,23},{8,24},{9,... | collective-permute-start | bytes 516104 | tf_op jit(solution)/shard_map/ppermute | solution.py:240
  908.8 16.2 %collective-permute-start.55 = (bf16[4,2,48,896]{3,2,1,0:T(8,128)(2,1)S(1)}, bf16[4,2,48,896]{3,2,1,0:T(8,128)(2,1)S(1)}, u32[]{:S(2)}, u32[]{:S(2)}) collective-permute-start(bf16[4,2,48,896]{3,2,1,0:T(8,128)(2,1)S(1)} %pad_maximum_fusion.18), channel_id=1, source_target_pairs={{0,1},{1,0},{2,3},{3,2},{4,5},{5,4},{6,7},{7,6},{8,9},{9,8},{10,11... | collective-permute-start | bytes 2064392 | tf_op jit(solution)/shard_map/ppermute | solution.py:229
  939.2 20.2 %all-to-all-start.15 = ((bf16[4,2,48,896]{3,2,1,0:T(8,128)(2,1)}), bf16[4,2,48,896]{3,2,1,0:T(8,128)(2,1)S(1)}, u32[]{:S(2)}, u32[]{:S(2)}) async-start(bf16[4,2,48,896]{3,2,1,0:T(8,128)(2,1)} %add_convert_fusion.5), calls=%async_computation.15 | async-start | bytes 1376256 | tf_op jit(solution)/shard_map/all_to_all | solution.py:85
  (154 other events, 1434.8 us)

commit v3 on v2

--- a/solution.py
+++ b/solution.py
@@ -207,6 +207,11 @@
         if self.fast:
             product = dot_left(live.pop("left"), live.pop("keep"))
             live["kept"] = (product + live.pop("got").astype(WIDE)).astype(LOW)
+
+    def join(self, other):
+        if self.fast:
+            kept = [self.live["kept"], other.live.pop("kept")]
+            self.live["kept"] = jnp.concatenate(kept, axis=1)
 
     def view(self):
         rows, half = self.live["kept"].shape
@@ -474,7 +479,7 @@
     width = heads * hd
     grad_scr[:, width:] = jnp.zeros((BLOCK, LANES), WIDE)
     mix_scr[:, width:] = jnp.zeros((BLOCK, LANES), WIDE)
-    grad_scr[:, :width] = dot_right(ga_ref[...], w_ref[:, :width]).astype(LOW).astype(WIDE)
+    grad_scr[:, :width] = dot_right(ga_ref[:, :width], w_ref[:, :width]).astype(LOW).astype(WIDE)
     mix_scr[:, :width] = mix_ref[...].astype(WIDE)
     lane = lax.broadcasted_iota(jnp.int32, (BLOCK, LANES), 1)
     ones = jnp.full((LANES, LANES), 1.0, LOW)
@@ -496,10 +501,11 @@
     n = ga.shape[0]
     width = heads * hd
     row = pl.BlockSpec((BLOCK, width), lambda i: (i, 0))
+    wide_row = pl.BlockSpec((BLOCK, ga.shape[1]), lambda i: (i, 0))
     return pl.pallas_call(
         partial(spread_kernel, heads, hd),
         grid=(n // BLOCK,),
-        in_specs=[row, whole_block(w), row],
+        in_specs=[wide_row, whole_block(w), row],
         out_specs=pl.BlockSpec((heads, BLOCK, LANES), lambda i: (0, i, 0)),
         out_shape=jax.ShapeDtypeStruct((heads, n, LANES), LOW),
         scratch_shapes=[
@@ -516,12 +522,14 @@
 
 def back_kernel(
     hd, c, score_scale, q_ref, k_ref, v_ref, do_ref, rq_ref, rk_ref, rot_ref, gq_ref, gk_ref,
-    joint_ref, gain_ref, dq_scr, dk_scr, dv_scr, gain_scr,
+    joint_0, joint_1, gain_ref, dq_scr, dk_scr, dv_scr, gain_scr,
 ):
     i = pl.program_id(0)
     n = pl.num_programs(0)
     heads = q_ref.shape[0]
-    tail = joint_ref.shape[1] - 3 * heads * hd
+    width = GROUP * hd
+    tail = joint_0.shape[1] - 3 * width
+    joints = (joint_0, joint_1)
 
     @pl.when(i == 0)
     def _():
@@ -569,13 +577,14 @@
 
     here = pl.ds(pl.multiple_of(i * BLOCK, BLOCK), BLOCK)
     rot = [rot_ref[t, here] for t in range(3)]
-    width = heads * hd
-    joint_ref[here, 3 * width :] = jnp.zeros((BLOCK, tail), LOW)
+    for joint_ref in joints:
+        joint_ref[here, 3 * width :] = jnp.zeros((BLOCK, tail), LOW)
     for h in range(heads):
+        joint_ref, at = joints[h // GROUP], hd * (h % GROUP)
         grad = finish(dk_scr[h], rk_ref[h], rot, gk_ref[...], 1)
-        joint_ref[here, width + hd * h : width + hd * (h + 1)] = grad[:, :hd]
+        joint_ref[here, width + at : width + at + hd] = grad[:, :hd]
         value = dv_scr[h].astype(LOW)
-        joint_ref[here, 2 * width + hd * h : 2 * width + hd * (h + 1)] = value[:, :hd]
+        joint_ref[here, 2 * width + at : 2 * width + at + hd] = value[:, :hd]
 
     @pl.when(i == n - 1)
     def _():
@@ -583,8 +592,9 @@
             at = pl.ds(pl.multiple_of(b * BLOCK, BLOCK), BLOCK)
             turn = [rot_ref[t, at] for t in range(3)]
             for h in range(heads):
+                start = hd * (h % GROUP)
                 grad = finish(dq_scr[h, at], rq_ref[h, at], turn, gq_ref[...], 0)
-                joint_ref[at, hd * h : hd * (h + 1)] = grad[:, :hd]
+                joints[h // GROUP][at, start : start + hd] = grad[:, :hd]
             return carry
 
         lax.fori_loop(0, n, rows, 0)
@@ -594,8 +604,8 @@
 def attend_back(part, q2, k, v, do, rq, rk, rot, gq, gk, hd, c, score_scale):
     _, n, _ = q2.shape
     one = pl.Buffered(1)
-    full = pl.BlockSpec((GROUP, n, LANES), lambda i: (part, 0, 0), pipeline_mode=one)
-    block = pl.BlockSpec((GROUP, BLOCK, LANES), lambda i: (part, i, 0))
+    full = pl.BlockSpec((2 * GROUP, n, LANES), lambda i: (part, 0, 0), pipeline_mode=one)
+    block = pl.BlockSpec((2 * GROUP, BLOCK, LANES), lambda i: (part, i, 0))
     small = pl.BlockSpec((1, LANES), lambda i: (0, 0))
     width = part_width(hd)
     return pl.pallas_call(
@@ -604,26 +614,161 @@
         in_specs=[full, block, block, full, full, block, whole_block(rot), small, small],
         out_specs=[
             pl.BlockSpec((n, width), lambda i: (0, 0), pipeline_mode=one),
+            pl.BlockSpec((n, width), lambda i: (0, 0), pipeline_mode=one),
             pl.BlockSpec((2, 8, LANES), lambda i: (0, 0, 0)),
         ],
         out_shape=[
             jax.ShapeDtypeStruct((n, width), LOW),
+            jax.ShapeDtypeStruct((n, width), LOW),
             jax.ShapeDtypeStruct((2, 8, LANES), WIDE),
         ],
         scratch_shapes=[
-            pltpu.VMEM((GROUP, n, LANES), WIDE),
-            pltpu.VMEM((GROUP, BLOCK, LANES), WIDE),
-            pltpu.VMEM((GROUP, BLOCK, LANES), WIDE),
+            pltpu.VMEM((2 * GROUP, n, LANES), WIDE),
+            pltpu.VMEM((2 * GROUP, BLOCK, LANES), WIDE),
+            pltpu.VMEM((2 * GROUP, BLOCK, LANES), WIDE),
             pltpu.VMEM((2, 8, LANES), WIDE),
         ],
         compiler_params=pltpu.CompilerParams(vmem_limit_bytes=56 * MIB),
         cost_estimate=pl.CostEstimate(
-            flops=10 * n * 640 * LANES * GROUP,
-            bytes_accessed=10 * MIB,
-            transcendentals=GROUP * n * 640,
+            flops=10 * n * 640 * LANES * 2 * GROUP,
+            bytes_accessed=20 * MIB,
+            transcendentals=2 * GROUP * n * 640,
         ),
         name="attend_back",
     )(q2, k, v, do, rq, rk, rot, gq, gk)
+
+
+def normed_rows(values):
+    centred = values - jnp.mean(values, axis=-1, keepdims=True)
+    scale = lax.rsqrt(jnp.mean(centred * centred, axis=-1, keepdims=True) + EPSILON)
+    return centred * scale, scale
+
+
+def norm_back(normed, scale, grad):
+    inner = jnp.mean(grad * normed, axis=-1, keepdims=True)
+    return scale * (grad - jnp.mean(grad, axis=-1, keepdims=True) - normed * inner)
+
+
+def add_sums(out_ref, at, hot, values):
+    width = values.shape[1]
+    term = dot_left(hot, values.astype(LOW))
+    here = (slice(None), slice(at * width, (at + 1) * width))
+
+    @pl.when(pl.program_id(0) == 0)
+    def _():
+        out_ref[here] = term
+
+    @pl.when(pl.program_id(0) > 0)
+    def _():
+        out_ref[here] += term
+
+
+def rows_of(array):
+    return pl.BlockSpec((BLOCK, array.shape[1]), lambda i: (i, 0))
+
+
+def call_rows(kernel, name, streamed, fixed, outs, sums=()):
+    n = streamed[0].shape[0]
+    width_of = lambda a: a.shape[1] * a.dtype.itemsize
+    work = sum(2 * n * a.shape[0] * a.shape[1] for a in fixed if a.shape[0] > 256)
+    moved = sum(n * width_of(a) for a in streamed) + sum(a.shape[0] * width_of(a) for a in fixed)
+    return pl.pallas_call(
+        kernel,
+        grid=(n // BLOCK,),
+        in_specs=[rows_of(a) for a in streamed] + [whole_block(a) for a in fixed],
+        out_specs=[pl.BlockSpec((BLOCK, w), lambda i: (i, 0)) for w, _ in outs]
+        + [pl.BlockSpec(shape, lambda i: (0, 0)) for shape in sums],
+        out_shape=[jax.ShapeDtypeStruct((n, w), t) for w, t in outs]
+        + [jax.ShapeDtypeStruct(shape, WIDE) for shape in sums],
+        compiler_params=pltpu.CompilerParams(vmem_limit_bytes=56 * MIB),
+        cost_estimate=pl.CostEstimate(flops=work, bytes_accessed=moved, transcendentals=0),
+        name=name,
+    )(*streamed, *fixed)
+
+
+def join_kernel(mix_ref, x_ref, hot_ref, keep_ref, w_ref, mod_ref, att_ref, mid_ref, norm_ref):
+    width = x_ref.shape[1]
+    hot = hot_ref[...]
+    attended = dot(mix_ref[...], w_ref[:, :width])
+    att_ref[...] = attended.astype(LOW)
+    gate = dot(hot, mod_ref[:, :width]) * keep_ref[...]
+    middle = x_ref[...].astype(WIDE) + gate * attended
+    mid_ref[...] = middle
+    normed, _ = normed_rows(middle)
+    scale = dot(hot, mod_ref[:, 2 * width : 3 * width])
+    shift = dot(hot, mod_ref[:, width : 2 * width])
+    norm_ref[...] = (normed * (1.0 + scale) + shift).astype(LOW)
+
+
+def gate_kernel(x_ref, w_ref, out_ref):
+    out_ref[...] = dot(x_ref[...], w_ref[...]).astype(LOW)
+
+
+def up_kernel(x_ref, gate_ref, w_ref, up_ref, inner_ref):
+    up = dot(x_ref[...], w_ref[...])
+    up_ref[...] = up.astype(LOW)
+    gate = gate_ref[...].astype(WIDE)
+    inner_ref[...] = (gate * jax.nn.sigmoid(gate) * up).astype(LOW)
+
+
+def down_kernel(
+    inner_ref, mid_ref, grad_ref, hot_ref, keep_ref, w_ref, mod_ref, out_ref, back_ref, sum_ref
+):
+    width = mid_ref.shape[1]
+    hot = hot_ref[...]
+    returned = dot(inner_ref[...], w_ref[:, :width])
+    gate = dot(hot, mod_ref[...]) * keep_ref[...]
+    out_ref[...] = (mid_ref[...] + gate * returned).astype(LOW)
+    upstream = grad_ref[...].astype(WIDE)
+    back_ref[:, :width] = (upstream * gate).astype(LOW)
+    if back_ref.shape[1] > width:
+        back_ref[:, width:] = jnp.zeros((BLOCK, back_ref.shape[1] - width), LOW)
+    add_sums(sum_ref, 0, hot, upstream * keep_ref[...] * returned)
+
+
+def inner_back_kernel(grad_ref, gate_ref, up_ref, w_ref, gg_ref, gu_ref):
+    grad = dot_right(grad_ref[...], w_ref[...])
+    gate = gate_ref[...].astype(WIDE)
+    sig = jax.nn.sigmoid(gate)
+    act = gate * sig
+    gg_ref[...] = (grad * up_ref[...].astype(WIDE) * (sig + act * (1.0 - sig))).astype(LOW)
+    gu_ref[...] = (grad * act).astype(LOW)
+
+
+def middle_back_kernel(
+    gg_ref, gu_ref, mid_ref, grad_ref, att_ref, hot_ref, keep_ref, wg_ref, wu_ref, mod_ref,
+    out_ref, back_ref, sum_ref,
+):
+    width = mid_ref.shape[1]
+    hot = hot_ref[...]
+    keep = keep_ref[...]
+    grad = dot_right(gg_ref[...], wg_ref[...]) + dot_right(gu_ref[...], wu_ref[...])
+    normed, scale = normed_rows(mid_ref[...])
+    turned = grad * (1.0 + dot(hot, mod_ref[:, 2 * width : 3 * width]))
+    total = grad_ref[...].astype(WIDE) + norm_back(normed, scale, turned)
+    out_ref[...] = total
+    gate = dot(hot, mod_ref[:, :width]) * keep
+    back_ref[:, :width] = (total * gate).astype(LOW)
+    if back_ref.shape[1] > width:
+        back_ref[:, width:] = jnp.zeros((BLOCK, back_ref.shape[1] - width), LOW)
+    add_sums(sum_ref, 0, hot, total * keep * att_ref[...].astype(WIDE))
+    add_sums(sum_ref, 1, hot, grad)
+    add_sums(sum_ref, 2, hot, grad * normed)
+
+
+def input_back_kernel(j0, j1, j2, j3, mid_ref, x_ref, hot_ref, w_ref, mod_ref, out_ref, sum_ref):
+    width = x_ref.shape[1]
+    hot = hot_ref[...]
+    step = j0.shape[1]
+    grad = None
+    for part, ref in enumerate((j0, j1, j2, j3)):
+        term = dot_right(ref[...], w_ref[:, part * step : (part + 1) * step])
+        grad = term if grad is None else grad + term
+    normed, scale = normed_rows(x_ref[...].astype(WIDE))
+    turned = grad * (1.0 + dot(hot, mod_ref[:, width : 2 * width]))
+    out_ref[...] = mid_ref[...] + norm_back(normed, scale, turned)
+    add_sums(sum_ref, 0, hot, grad)
+    add_sums(sum_ref, 1, hot, grad * normed)
 
 
 def turn_tables(row_place, column_place, hd):
@@ -643,6 +788,11 @@
         ],
         0,
     )
+
+
+def high_and_rest(values):
+    high = values.astype(LOW)
+    return jnp.concatenate([high, (values - high.astype(WIDE)).astype(LOW)], axis=0)
 
 
 def pad_columns(array, width):
@@ -701,11 +851,11 @@
     cond_silu, silu_pull = jax.vjp(jax.nn.silu, cond_float)
     cond_act = cond_silu.astype(LOW)
 
+    g_qkv.z()
     group_act = exchange(cond_act)
-    g_qkv.z()
     member, segment, row_place, column_place = layout(item_lengths[0], item_widths[0], n)
     member_low = member.astype(LOW)
-    keep_mask = (segment < items - 1).astype(WIDE).reshape(n, 1)
+    keep = (segment < items - 1).astype(WIDE).reshape(n, 1)
     rot = turn_tables(row_place, column_place, hd)
     spare = jnp.zeros((n, LANES - hd - items), LOW)
     ones_at = jnp.zeros((n, LANES - hd - items), LOW).at[:, :3].set(-1.0)
@@ -715,98 +865,92 @@
     value_tail = jnp.zeros((1, LANES), LOW).at[:, hd : hd + 2].set(1.0)
     gain_q = pad_columns(query_gain.astype(WIDE)[None, :], LANES)
     gain_k = pad_columns(key_gain.astype(WIDE)[None, :], LANES)
-    bias_row = lax.dynamic_update_slice(
-        jnp.zeros((6 * width,), WIDE), ada_bias.astype(WIDE), (fsdp_place * ada_bias.shape[0],)
-    )
-    mod_part = (dot(group_act, ada_weight) + bias_row[None, :]).astype(LOW)
-    tables = (rot, query_tail, key_tail)
-    mod_part, tables, group_act = hold(gathers, (mod_part, tables, group_act))
-
-    early = 2 * width
-    mod_a = sum_back(mod_part[:, :early], items)
+    hot = jnp.concatenate([member_low, member_low], axis=1)
+    tables = (rot, query_tail, key_tail, hot, keep)
+    tables, group_act = hold(gathers, (tables, group_act))
+
     g_qkv.y()
     g_qkv.x(early=True)
     g_qkv.core("own")
-    g_proj.z()
     g_gate.z()
-    mod_a, mod_part, tables, group_act = hold(gathers, (mod_a, mod_part, tables, group_act))
-
-    mod_b = sum_back(mod_part[:, early:], items)
+    bias_row = lax.dynamic_update_slice(
+        jnp.zeros((6 * width,), WIDE), ada_bias.astype(WIDE), (fsdp_place * ada_bias.shape[0],)
+    )
+    mod_part = (dot(group_act, ada_weight) + bias_row[None, :]).astype(LOW)
+    mod_part, group_act, tables = hold(gathers, (mod_part, group_act, tables))
+
+    early = 2 * width
+    modulation = high_and_rest(sum_back(mod_part, items))
     g_qkv.x(late=True)
     g_qkv.core("far", "side")
+    g_proj.z()
+    inputs_low = block_in[0]
+    modulation, tables, inputs_low = hold(gathers, (modulation, tables, inputs_low))
+    mod_a, mod_b = modulation[:, :early], modulation[:, early:]
+
+    g_qkv.core("side_far")
     g_proj.y()
+    g_gate.y()
     g_up.z()
-    every_act = across_replicas(group_act)
-    mod_a, mod_b, tables = hold(gathers, (mod_a, mod_b, tables))
-
-    g_qkv.core("side_far")
-    modulation = jnp.concatenate([mod_a, mod_b], axis=1)
-    mod_high = modulation.astype(LOW)
-    mod_rest = (modulation - mod_high.astype(WIDE)).astype(LOW)
-    mod_low = jnp.concatenate([mod_high, mod_rest], axis=0)
-    hot = jnp.concatenate([member_low, member_low], axis=1)
-    inputs_low = block_in[0]
-    mod_low, tables, inputs_low = hold(gathers, (mod_low, tables, inputs_low))
+    rot, query_tail, key_tail, hot, keep = tables
+    qkv_full = g_qkv.whole()
+    normed_a, q, k, v, raw_q, raw_k = prepare(
+        inputs_low, hot, mod_a, qkv_full, gain_q, gain_k, rot,
+        query_tail, key_tail, value_tail, heads, hd,
+    )
+    gathers = gathers[1:]
+    normed_a, q, k, v, raw_q, raw_k, qkv_full, mod_b = hold(
+        gathers, (normed_a, q, k, v, raw_q, raw_k, qkv_full, mod_b)
+    )
 
     g_proj.x()
-    g_gate.y()
+    g_proj.core("own", "far")
+    g_gate.x()
+    g_gate.core("own", "far")
     g_up.y()
     g_down.z()
-    rot, query_tail, key_tail = tables
-    qkv_full = g_qkv.whole()
-    normed_a, q, k, v, raw_q, raw_k = prepare(
-        inputs_low, hot, mod_low[:, :early], qkv_full, gain_q, gain_k, rot,
-        query_tail, key_tail, value_tail, heads, hd,
-    )
-    gathers = gathers[1:]
-    normed_a, q, k, v, raw_q, raw_k, qkv_full = hold(
-        gathers, (normed_a, q, k, v, raw_q, raw_k, qkv_full)
-    )
-
-    g_proj.core("own", "far", "both")
-    g_gate.x()
-    g_down.y()
     mixed, q2 = attend(q, k, v, hd, c)
     mixed, q2 = hold(gathers, (mixed, q2))
 
-    g_gate.core("own", "far", "both")
+    g_proj.core("both")
+    g_gate.core("both")
     g_up.x()
+    g_up.core("own", "far")
+    g_down.y()
     proj_full = g_proj.whole()
-    token_mod = dot(hot, mod_low)
-    shift_a, scale_a, gate_a, shift_b, scale_b, gate_b = jnp.split(token_mod, 6, axis=1)
-    inputs = inputs_low.astype(WIDE)
-    attended = dot(mixed, proj_full[:, :width])
-    middle = inputs + keep_mask * gate_a * attended
-    normed_b = modulated(middle, shift_b, scale_b).astype(LOW)
+    mod_mid = mod_b[:, : 3 * width]
+    attended, middle, normed_b = call_rows(
+        join_kernel, "join", (mixed, inputs_low, hot, keep), (proj_full, mod_mid),
+        ((width, LOW), (width, WIDE), (width, LOW)),
+    )
     gathers = gathers[1:]
     middle, normed_b, attended, proj_full = hold(
         gathers, (middle, normed_b, attended, proj_full)
     )
 
-    g_up.core("own", "far", "both")
+    g_up.core("both")
     g_down.x()
+    g_down.core("own", "far")
     gate_full = g_gate.whole()
-    gate = dot(normed_b, gate_full).astype(LOW)
+    (gate,) = call_rows(gate_kernel, "gate", (normed_b,), (gate_full,), ((ff, LOW),))
     gathers = gathers[1:]
     gate, gate_full, normed_b = hold(gathers, (gate, gate_full, normed_b))
 
-    g_down.core("own", "far", "both")
+    g_down.core("both")
     up_full = g_up.whole()
-    up = dot(normed_b, up_full)
-    gate_wide = gate.astype(WIDE)
-    inner = (jax.nn.silu(gate_wide) * up).astype(LOW)
-    up = up.astype(LOW)
+    up, inner = call_rows(
+        up_kernel, "up", (normed_b, gate), (up_full,), ((ff, LOW), (ff, LOW))
+    )
     gathers = gathers[1:]
     inner, up, gate, up_full, middle = hold(gathers, (inner, up, gate, up_full, middle))
 
     down_full = g_down.whole()
-    returned = dot(inner, down_full[:, :width])
-    block_out = (middle + keep_mask * gate_b * returned).astype(LOW)
-    upstream = out_grad[0].astype(WIDE)
-    grad_gate_b = upstream * keep_mask * returned
-    grad_returned = (upstream * keep_mask * gate_b).astype(LOW)
-
-    s_down = Scatter(inner, *column_halves(pad_columns(grad_returned, odd)))
+    block_out, grad_returned, sums_gate_b = call_rows(
+        down_kernel, "down", (inner, middle, out_grad[0], hot, keep),
+        (down_full, mod_b[:, 3 * width :]), ((width, LOW), (odd, LOW)), ((2 * items, width),),
+    )
+
+    s_down = Scatter(inner, *column_halves(grad_returned))
     s_down.first()
     plans = [s_down]
     grad_returned, down_full, gate, up, gate_full, up_full, normed_b, middle, attended = hold(
@@ -815,43 +959,33 @@
     )
 
     s_down.core()
-    grad_inner = dot_right(grad_returned, down_full[:, :width])
-    gate_wide = gate.astype(WIDE)
-    sig = jax.nn.sigmoid(gate_wide)
-    grad_gate = (grad_inner * up.astype(WIDE) * sig * (1.0 + gate_wide * (1.0 - sig))).astype(LOW)
-    grad_up = (grad_inner * gate_wide * sig).astype(LOW)
+    grad_gate, grad_up = call_rows(
+        inner_back_kernel, "inner_back", (grad_returned, gate, up), (down_full,),
+        ((ff, LOW), (ff, LOW)),
+    )
     grad_gate, grad_up = hold(plans, (grad_gate, grad_up))
 
     s_down.second()
-    chunk = ff // 2
-    s_one = Scatter(normed_b, *mine_and_other(grad_gate[:, :chunk], grad_up[:, :chunk]))
-    s_two = Scatter(normed_b, *mine_and_other(grad_gate[:, chunk:], grad_up[:, chunk:]))
-    s_one.first()
-    plans = [s_down, s_one, s_two]
+    s_wide = Scatter(normed_b, *mine_and_other(grad_gate, grad_up))
+    s_wide.first()
+    plans = [s_down, s_wide]
     grad_gate, grad_up = hold(plans, (grad_gate, grad_up))
 
     s_down.x()
-    s_one.core()
-    s_two.first()
-    grad_normed_b = dot_right(grad_gate, gate_full) + dot_right(grad_up, up_full)
-    _, norm_pull_b = jax.vjp(modulated, middle, shift_b, scale_b)
-    grad_middle_part, grad_shift_b, grad_scale_b = norm_pull_b(grad_normed_b)
-    grad_middle = upstream + grad_middle_part
-    grad_gate_a = grad_middle * keep_mask * attended
-    grad_attended = (grad_middle * keep_mask * gate_a).astype(LOW)
-    s_proj = Scatter(mixed, *column_halves(pad_columns(grad_attended, odd)))
-    late = jnp.concatenate(
-        [part.astype(LOW) for part in (grad_gate_a, grad_shift_b, grad_scale_b, grad_gate_b)],
-        axis=1,
-    )
-    plans = [s_down, s_one, s_two, s_proj]
-    grad_middle, grad_attended, late = hold(plans, (grad_middle, grad_attended, late))
+    s_wide.core()
+    grad_middle, grad_attended, sums_mid = call_rows(
+        middle_back_kernel, "middle_back",
+        (grad_gate, grad_up, middle, out_grad[0], attended, hot, keep),
+        (gate_full, up_full, mod_mid), ((width, WIDE), (odd, LOW)), ((2 * items, 3 * width),),
+    )
+    s_proj = Scatter(mixed, *column_halves(grad_attended))
+    plans = [s_down, s_wide, s_proj]
+    grad_middle, grad_attended, sums_mid = hold(plans, (grad_middle, grad_attended, sums_mid))
 
     s_down.y()
-    s_two.core()
-    s_one.second()
+    s_wide.second()
     s_proj.first()
-    late_sums = dot_left(member_low, late).astype(LOW)
+    late_sums = jnp.concatenate([sums_mid[:items], sums_gate_b[:items]], axis=1).astype(LOW)
     grad_mixed = spread(grad_attended, proj_full, mixed, heads, hd)
     late_sums, grad_mixed = hold(plans, (late_sums, grad_mixed))
 
@@ -860,98 +994,78 @@
         hd=hd, c=c, score_scale=score_scale,
     )
     s_down.z()
-    s_one.x()
+    s_wide.x()
     s_proj.core()
-    s_two.second()
-    joint_0, gains_0 = back(0, do=grad_mixed)
-    joint_0, gains_0, grad_mixed, late_sums = hold(
-        plans, (joint_0, gains_0, grad_mixed, late_sums)
-    )
-
-    s_down.last_x()
-    s_one.y()
-    s_two.x()
-    s_proj.second()
-    late_group = gather_rows(late_sums)
-    joint_1, gains_1 = back(1, do=grad_mixed)
+    joint_0, joint_1, gains_0 = back(0, do=grad_mixed)
     s_head = Scatter(normed_a, *mine_and_other(joint_0, joint_1))
     s_head.first()
     plans = plans + [s_head]
-    joint_0, joint_1, gains_1, grad_mixed, late_group = hold(
-        plans, (joint_0, joint_1, gains_1, grad_mixed, late_group)
+    joint_0, joint_1, gains_0, grad_mixed, late_sums = hold(
+        plans, (joint_0, joint_1, gains_0, grad_mixed, late_sums)
+    )
+
+    s_down.last_x()
+    s_wide.y()
+    s_head.core()
+    late_group = gather_rows(late_sums)
+    joint_2, joint_3, gains_1 = back(1, do=grad_mixed)
+    s_tail = Scatter(normed_a, *mine_and_other(joint_2, joint_3))
+    plans = plans + [s_tail]
+    joint_0, joint_1, joint_2, joint_3, gains_1, late_group = hold(
+        plans, (joint_0, joint_1, joint_2, joint_3, gains_1, late_group)
     )
 
     s_down.last_core()
-    s_one.z()
-    s_two.y()
-    s_proj.x()
-    s_head.core()
+    s_wide.z()
+    s_tail.first()
+    s_tail.core()
+    s_proj.second()
+    s_head.second()
+    s_head.join(s_proj)
+    s_head.x()
     late_every = across_replicas(late_group)
-    joint_2, gains_2 = back(2, do=grad_mixed)
-    joint_2, gains_2, grad_mixed, late_every = hold(
-        plans, (joint_2, gains_2, grad_mixed, late_every)
-    )
-    s_one.last_x()
-    s_two.z()
-    s_proj.y()
-    s_head.second()
-    joint_3, gains_3 = back(3, do=grad_mixed)
-    s_tail = Scatter(normed_a, *mine_and_other(joint_2, joint_3))
-    s_tail.first()
-    plans = plans[1:] + [s_tail]
-    joint_2, joint_3, gains_3 = hold(plans, (joint_2, joint_3, gains_3))
-
-    s_one.last_core()
-    s_two.last_x()
-    s_proj.z()
-    s_head.x()
-    s_tail.core()
-    joint = jnp.concatenate([joint_0, joint_1, joint_2, joint_3], axis=1)
-    grad_normed_a = dot_right(joint, qkv_full)
-    _, norm_pull_a = jax.vjp(modulated, inputs, shift_a, scale_a)
-    grad_input_part, grad_shift_a, grad_scale_a = norm_pull_a(grad_normed_a)
-    grad_input = grad_middle + grad_input_part
-    soon = jnp.concatenate([grad_shift_a.astype(LOW), grad_scale_a.astype(LOW)], axis=1)
-    plans = plans[1:]
-    grad_input, soon = hold(plans, (grad_input, soon))
-
-    s_two.last_core()
-    s_proj.last_x()
+    grad_input, sums_early = call_rows(
+        input_back_kernel, "input_back",
+        (joint_0, joint_1, joint_2, joint_3, grad_middle, inputs_low, hot),
+        (qkv_full, mod_a), ((width, WIDE),), ((2 * items, 2 * width),),
+    )
+    s_tail.second()
+    plans = [s_down, s_wide, s_head, s_tail]
+    grad_input, sums_early, late_every = hold(plans, (grad_input, sums_early, late_every))
+
+    s_wide.last_x()
     s_head.y()
-    s_tail.second()
-    early_sums = dot_left(member_low, soon)
-    gain_row = jnp.sum(gains_0 + gains_1 + gains_2 + gains_3, axis=1)[:, :hd].reshape(1, 2 * hd)
+    s_tail.x()
+    early_sums = sums_early[:items]
+    gain_row = jnp.sum(gains_0 + gains_1, axis=1)[:, :hd].reshape(1, 2 * hd)
     gain_high = gain_row.astype(LOW).astype(WIDE)
     gain_block = jnp.concatenate([gain_high, gain_row - gain_high], axis=0)
     gain_block = jnp.pad(gain_block, ((0, items - 2), (0, 2 * LANES - 2 * hd)))
     early_sums = jnp.concatenate([early_sums, gain_block], axis=1).astype(LOW)
-    plans = plans[1:]
-    early_sums, late_every = hold(plans, (early_sums, late_every))
-
-    s_proj.last_core()
+    early_group = gather_rows(early_sums)
+    every_act = across_replicas(group_act)
+    early_group, late_every, every_act = hold(plans, (early_group, late_every, every_act))
+
+    s_wide.last_core()
     s_head.z()
-    s_tail.x()
-    early_group = gather_rows(early_sums)
-    shard_late = dot_left(every_act, late_every)
-    early_group, shard_late = hold(plans, (early_group, shard_late))
-
-    s_head.last_x()
     s_tail.y()
     early_every = across_replicas(early_group)
+    shard_late = dot_left(every_act, late_every)
     cond_part = dot_right(early_group[:, :early], ada_weight[:, :early]) + dot_right(
         late_group, ada_weight[:, early:]
     )
-    early_every, cond_part = hold(plans, (early_every, cond_part))
+    early_every, cond_part, shard_late, every_act = hold(
+        plans, (early_every, cond_part, shard_late, every_act)
+    )
+
+    s_head.last_x()
+    s_tail.z()
+    shard_early = dot_left(every_act, early_every[:, :early])
+    shard_early, cond_part = hold(plans, (shard_early, cond_part))
 
     s_head.last_core()
-    s_tail.z()
+    s_tail.last_x()
     cond_back = lax.all_to_all(cond_part.astype(LOW).reshape(shards, items, -1), "fsdp", 0, 0)
-    shard_early = dot_left(every_act, early_every[:, :early])
-    cond_back, shard_early = hold(plans, (cond_back, shard_early))
-
-    s_tail.last_x()
-    grad_cond_act = cond_back.swapaxes(0, 1).reshape(items, width).astype(WIDE)
-    grad_condition = silu_pull(grad_cond_act)[0]
     shard_ada = jnp.concatenate([shard_early, shard_late], axis=1)
     bias_sums = jnp.concatenate(
         [
@@ -964,15 +1078,22 @@
         bias_sums, (fsdp_place * ada_bias.shape[0],), (ada_bias.shape[0],)
     )
     gain_sums = jnp.sum(early_every[:, early:].astype(WIDE), axis=0)[: 2 * hd]
-    hold(plans, ())
+    cond_back = hold(plans, cond_back)
     s_tail.last_core()
+    grad_cond_act = cond_back.swapaxes(0, 1).reshape(items, width).astype(WIDE)
+    grad_condition = silu_pull(grad_cond_act)[0]
+    cut = part_width(hd)
+    if s_head.fast:
+        head_0, head_1 = s_head.halves()
+        proj_halves = (head_0[:, cut:], head_1[:, cut:])
+    else:
+        head_0, head_1 = s_head.halves()
+        proj_halves = s_proj.halves()
     shard_qkv = from_parts(
-        jnp.concatenate(s_head.halves() + s_tail.halves(), axis=1), heads, hd
-    )
-    shard_proj = jnp.concatenate(s_proj.halves(), axis=1)[:, :width]
-    gate_1, up_1 = s_one.halves()
-    gate_2, up_2 = s_two.halves()
-    shard_gate_up = jnp.concatenate([gate_1, gate_2, up_1, up_2], axis=1)
+        jnp.concatenate((head_0[:, :cut], head_1[:, :cut]) + s_tail.halves(), axis=1), heads, hd
+    )
+    shard_proj = jnp.concatenate(proj_halves, axis=1)[:, :width]
+    shard_gate_up = jnp.concatenate(s_wide.halves(), axis=1)
     shard_down = jnp.concatenate(s_down.halves(), axis=1)[:, :width]
     return (
         block_out[None],

time: 994 us -> 891 us (0.90)
  matrix products: 225 us -> 79.9 us
  Pallas kernels: 195 us -> 322 us
  other arithmetic: 157 us -> 97.1 us
  starting transfers between devices: 145 us -> 123 us
  waiting for transfers between devices: 156 us -> 144 us
  local copies, waits for them, and re-layouts: 100 us -> 110 us
    pallas_call x0 -> x7, Pallas kernels: none -> 127 us  [call_rows(): pl.pallas_call(kernel, grid=(n // BLOCK,), in_specs=[rows_of(a) for a in...]
    dot_general x6 -> x1, matrix products: 75.2 us -> 2.89 us  [dot(): return jnp.dot(left, right, preferred_element_type=WIDE)]
    dot_general x6 -> x2, matrix products: 68.1 us -> 4.84 us  [dot_right(): lax.dot_general(left, right, (((1,), (1,)), ((), ())), preferred_element_...]
    ppermute x3, waiting for transfers between devices: 6.21 us -> 31.5 us  [across_replicas(): far = lax.ppermute(chip, AXES, TO_X)]
    reduce_sum x5 -> x1, other arithmetic: 18.5 us -> 0.02 us  [local(): gain_row = jnp.sum(gains_0 + gains_1, axis=1)[:, :hd].reshape(1, 2 * hd)]
    ppermute x6 -> x4, waiting for transfers between devices: 16.6 us -> 0.74 us  [y(): self.live['far'] = lax.ppermute(self.row(1 - y), AXES, TO_Y)]
    all_to_all x11 -> x9, waiting for transfers between devices: 53.9 us -> 38.2 us  [over_z(): return lax.all_to_all(operand, 'fsdp', 0, 0, axis_index_groups=Z_GROUPS)]
    all_to_all x2, waiting for transfers between devices: 1.01 us -> 11.4 us  [gather_rows(): lax.all_to_all(jnp.broadcast_to(rows, (shards, count, width)), 'fsdp', 0, 0)]
  transfers between devices with their start and end apart: 80 -> 68, of which waited for: 22 -> 21; matrix products, arithmetic and copies ran while one was open for 35% -> 20% of each run, Pallas kernels for 19% -> 34%
where the time goes in v3:
time: 891 us; the launch traced here: 880 us
  Pallas kernels  322 us (36%)
  waiting for transfers between devices  144 us (16%)
  starting transfers between devices  123 us (14%)
  local copies, waits for them, and re-layouts  110 us (12%)
  other arithmetic  97.1 us (11%)
  matrix products  79.9 us (9%)
    pallas_call x7, Pallas kernels, call_rows(): pl.pallas_call(kernel, grid=(n // BLOCK,), in_specs=[rows_of(a) for a in...  127 us
    pallas_call x2, Pallas kernels, attend_back(): pl.pallas_call(partial(back_kernel, hd, c, score_scale), grid=(n // BLOCK...  95.1 us
    dot_general x12, matrix products, dot_left(): lax.dot_general(left, right, (((0,), (0,)), ((), ())), preferred_element_...  72.2 us
    all_to_all x9, starting transfers between devices, over_z(): return lax.all_to_all(operand, 'fsdp', 0, 0, axis_index_groups=Z_GROUPS)  40.9 us
    pallas_call x1, Pallas kernels, prepare(): pl.pallas_call(partial(prepare_kernel, heads, hd), grid=(n // BLOCK,), in...  39.1 us
    all_to_all x9, waiting for transfers between devices, over_z(): return lax.all_to_all(operand, 'fsdp', 0, 0, axis_index_groups=Z_GROUPS)  38.2 us
    ppermute x3, waiting for transfers between devices, across_replicas(): far = lax.ppermute(chip, AXES, TO_X)  31.5 us
    pallas_call x1, Pallas kernels, attend(): pl.pallas_call(partial(attend_kernel, hd, c), grid=(n // BLOCK,), in_spec...  27.4 us
  transfers between devices with their start and end apart: 68, of which 21 were waited for; matrix products, arithmetic and copies ran while one was open for 20% of the time, Pallas kernels for 34%

profile of v3, /device:TPU:1, one launch (start us, length us, event | category | flops | bytes accessed | tf_op | source)
XLA Modules:
  0.0 880.3 jit_solution(5333393950772976059)
XLA Ops:
  2.1 6.4 all-to-all-start.1
  18.0 4.5 all-to-all-start
  22.5 5.4 multiply_cosine_fusion
  41.4 13.3 %all-to-all-done.a0 = bf16[4,2,48,1792]{3,2,1,0:T(8,128)(2,1)S(1)} async-done(((bf16[4,2,48,1792]{3,2,1,0:T(8,128)(2,1)}), bf16[4,2,48,1792]{3,2,1,0:T(8,128)(2,1)S(1)}, u32[]{:S(2)}, u32[]{:S(2)}) %all-to-all-start) | async-done | bytes 1376288 | tf_op jit(solution)/shard_map/all_to_all | solution.py:85
  56.0 3.5 all-to-all-start.2
  68.7 13.2 %collective-permute-done.1 = bf16[4,48,1792]{2,1,0:T(8,128)(2,1)S(1)} collective-permute-done((bf16[4,48,1792]{2,1,0:T(8,128)(2,1)}, bf16[4,48,1792]{2,1,0:T(8,128)(2,1)S(1)}, u32[]{:S(2)}, u32[]{:S(2)}) %collective-permute-start.1) | collective-permute-done | bytes 688160 | tf_op jit(solution)/shard_map/ppermute | solution.py:147
  81.9 9.3 %collective-permute-done = bf16[4,2,48,1792]{3,2,0,1:T(8,128)(2,1)} collective-permute-done((bf16[4,2,48,1792]{3,2,0,1:T(8,128)(2,1)}, bf16[4,2,48,1792]{3,2,0,1:T(8,128)(2,1)}, u32[]{:S(2)}, u32[]{:S(2)}) %collective-permute-start) | collective-permute-done | bytes 1376288 | tf_op jit(solution)/shard_map/ppermute | solution.py:139
  91.3 5.1 all-to-all-start.4
  105.3 11.7 %all-to-all-done.4 = bf16[8,8,6912]{2,1,0:T(8,128)(2,1)S(1)} async-done(((bf16[8,8,6912]{2,1,0:T(8,128)(2,1)}), bf16[8,8,6912]{2,1,0:T(8,128)(2,1)S(1)}, u32[]{:S(2)}, u32[]{:S(2)}) %all-to-all-start.4) | async-done | bytes 884768 | tf_op jit(solution)/shard_map/all_to_all | solution.py:319
  118.8 3.5 all-to-all-start.3
  123.7 9.2 %all-to-all-done.3.a0 = bf16[4,2,48,640]{3,2,1,0:T(8,128)(2,1)S(1)} async-done(((bf16[4,2,48,640]{3,2,1,0:T(8,128)(2,1)}), bf16[4,2,48,640]{3,2,1,0:T(8,128)(2,1)S(1)}, u32[]{:S(2)}, u32[]{:S(2)}) %all-to-all-start.3) | async-done | bytes 491552 | tf_op jit(solution)/shard_map/all_to_all | solution.py:85
  136.1 4.9 all-to-all-start.5
  141.0 3.9 collective-permute-start.8
  159.1 6.9 place.5.w_ref
  166.0 39.1 %prepare.1 = (bf16[1024,1152]{1,0:T(8,128)(2,1)}, bf16[16,1024,128]{2,1,0:T(8,128)(2,1)}, bf16[16,1024,128]{2,1,0:T(8,128)(2,1)}, bf16[16,1024,128]{2,1,0:T(8,12...) custom-call(bf16[1024,1152]{1,0:T(8,128)(2,1)} %bitcast.280, bf16[1024,16]{1,0:T(8,128)(2,1)} %copy.148.hot_ref, ...), custom_call_target="tpu_custom_call" | custom-call | flops 8455716864 | bytes 41943040 | tf_op jit(solution)/shard_map/prepare/pallas_call | solution.py:383
  206.4 4.8 all-to-all-start.6
  218.0 5.3 collective-permute-done.9.ax
  228.3 27.4 %attend.1 = (bf16[1024,1152]{1,0:T(8,128)(2,1)}, bf16[16,1024,128]{2,1,0:T(8,128)(2,1)}) custom-call(bf16[16,1024,128]{2,1,0:T(8,128)(2,1)} %get-tuple-element.361.q_ref, bf16[16,1024,128]{2,1,0:T(8,128)(2,1)} %get-tuple-element.362.k_ref, bf16[16,1024,128]{2,1,0:T(8,128)(2,1)} %get-tuple-element.363.v_ref), custom_call_target="tpu_custom_call" | custom-call | flops 5368709120 | bytes 20971520 | tf_op jit(solution)/shard_map/attend/pallas_call | solution.py:459
  277.1 10.1 %join.1 = (bf16[1024,1152]{1,0:T(8,128)(2,1)}, f32[1024,1152]{1,0:T(8,128)}, bf16[1024,1152]{1,0:T(8,128)(2,1)}) custom-call(bf16[1024,1152]{1,0:T(8,128)(2,1)} %get-tuple-element.510.mix_ref, bf16[1024,1152]{1,0:T(8,128)(2,1)} %bitcast.281, bf16[1024,16]{1,0:T(8,128)(2,1)} %copy.148.hot_ref, f32[1024,1]{1,0:T(8,128)} %copy.150.keep_ref, ...), custom_call_target="tpu_custom_call" | custom-call | flops 3019898880 | bytes 7815168 | tf_op jit(solution)/shard_map/join/pallas_call | solution.py:675
  287.2 4.0 collective-permute-done.17.ax
  297.3 3.3 place.7.w_ref.wg_ref
  303.4 13.2 %gate.1.gate_ref = bf16[1024,3072]{1,0:T(8,128)(2,1)} custom-call(bf16[1024,1152]{1,0:T(8,128)(2,1)} %get-tuple-element.460.x_ref, bf16[1152,3072]{1,0:T(8,128)(2,1)} %copy-done.1), custom_call_target="tpu_custom_call" | custom-call | flops 7247757312 | bytes 9437184 | tf_op jit(solution)/shard_map/gate/pallas_call | solution.py:675
  316.6 6.8 collective-permute-done.23.ax
  329.1 4.1 place.8.w_ref.wu_ref
  336.1 15.6 %up.1 = (bf16[1024,3072]{1,0:T(8,128)(2,1)}, bf16[1024,3072]{1,0:T(8,128)(2,1)}) custom-call(bf16[1024,1152]{1,0:T(8,128)(2,1)} %get-tuple-element.460.x_ref, bf16[1024,3072]{1,0:T(8,128)(2,1)} %gate.1.gate_ref, bf16[1152,3072]{1,0:T(8,128)(2,1)} %copy-done.2), custom_call_target="tpu_custom_call" | custom-call | flops 7247757312 | bytes 15728640 | tf_op jit(solution)/shard_map/up/pallas_call | solution.py:675
  351.7 6.0 place.9.w_ref
  357.7 16.1 %down.1 = (bf16[1024,1152]{1,0:T(8,128)(2,1)}, bf16[1024,1280]{1,0:T(8,128)(2,1)}, f32[16,1152]{1,0:T(8,128)}) custom-call(bf16[1024,3072]{1,0:T(8,128)(2,1)} %get-tuple-element.439.inner_ref, f32[1024,1152]{1,0:T(8,128)} %get-tuple-element.451.mid_ref, bf16[1024,1152]{1,0:T(8,128)(2,1)} %bitcast.278, bf16[1024,16]{1,0:T(8,128)(2,1)} %copy.148.hot_ref, ...), custom_call_target="tpu_custom_call" | custom-call | flops 8053063680 | bytes 21307392 | tf_op jit(solution)/shard_map/down/pallas_call | solution.py:675
  376.4 9.8 %convolution_convert_fusion.1 = bf16[3072,640]{1,0:T(8,128)(2,1)} fusion(bf16[1024,3072]{1,0:T(8,128)(2,1)} %get-tuple-element.439.inner_ref, bf16[1024,1280]{1,0:T(8,128)(2,1)S(1)} %copy-done.50, s32[]{:T(128)S(6)} %select_n.458), kind=kOutput, calls=%fused_computation.8 | convolution fusion | flops 4028497920 | bytes 11534340 | tf_op jit(solution)/shard_map/dot_general | solution.py:29
  386.3 17.3 %inner_back.1 = (bf16[1024,3072]{1,0:T(8,128)(2,1)}, bf16[1024,3072]{1,0:T(8,128)(2,1)}) custom-call(bf16[1024,1280]{1,0:T(8,128)(2,1)} %get-tuple-element.433.grad_ref, bf16[1024,3072]{1,0:T(8,128)(2,1)} %gate.1.gate_ref, bf16[1024,3072]{1,0:T(8,128)(2,1)} %get-tuple-element.435.up_ref, bf16[3072,1280]{1,0:T(8,128)(2,1)} %place.9.w_ref), custom_call_target="tpu_custom_call" | custom-call | flops 8053063680 | bytes 23068672 | tf_op jit(solution)/shard_map/inner_back/pallas_call | solution.py:675
  403.6 6.2 broadcast_select_fusion
  409.7 11.5 %convolution_convert_fusion = bf16[1152,3072]{1,0:T(8,128)(2,1)} fusion(bf16[1024,1152]{1,0:T(8,128)(2,1)} %get-tuple-element.460.x_ref, bf16[1024,3072]{1,0:T(8,128)(2,1)} %get-tuple-element.450.gu_ref, bf16[1024,3072]{1,0:T(8,128)(2,1)S(1)} %copy-done.23, pred[]{:T(512)S(6)} %eq.84), kind=kOutput, calls=%fused_computation.1 | convolution fusion | flops 7254441984 | bytes 22020096 | tf_op jit(solution)/shard_map/dot_general | solution.py:29
  421.2 9.1 %add_convert_fusion.1 = bf16[3072,640]{1,0:T(8,128)(2,1)} fusion(bf16[3072,640]{1,0:T(8,128)(2,1)} %collective-permute-done.27, bf16[1024,3072]{1,0:T(8,128)(2,1)} %get-tuple-element.439.inner_ref, bf16[1024,640]{1,0:T(8,128)(2,1)S(1)} %copy-done.43), kind=kOutput, calls=%fused_computation.4 | convolution fusion | flops 4032430080 | bytes 15466496 | tf_op jit(solution)/shard_map/dot_general | solution.py:29
  435.3 33.4 %middle_back.1 = (f32[1024,1152]{1,0:T(8,128)}, bf16[1024,1280]{1,0:T(8,128)(2,1)}, f32[16,3456]{1,0:T(8,128)}) custom-call(bf16[1024,3072]{1,0:T(8,128)(2,1)} %get-tuple-element.449.gg_ref, bf16[1024,3072]{1,0:T(8,128)(2,1)} %get-tuple-element.450.gu_ref, f32[1024,1152]{1,0:T(8,128)} %get-tuple-element.451.mid_ref, bf16[1024,1152]{1,0:T(8,128)(2,1)} %bitcast.279, ...), custom_call_target="tpu_custom_call" | custom-call | flops 14495514624 | bytes 36323328 | tf_op jit(solution)/shard_map/middle_back/pallas_call | solution.py:675
  475.8 3.2 convolution_convert_fusion.4
  479.1 11.5 %spread.1.do_ref = bf16[16,1024,128]{2,1,0:T(8,128)(2,1)} custom-call(bf16[1024,1280]{1,0:T(8,128)(2,1)} %get-tuple-element.468.ga_ref, bf16[1152,1280]{1,0:T(8,128)(2,1)} %copy-done, bf16[1024,1152]{1,0:T(8,128)(2,1)} %get-tuple-element.510.mix_ref), custom_call_target="tpu_custom_call" | custom-call | flops 2717908992 | bytes 12582912 | tf_op jit(solution)/shard_map/spread/pallas_call | solution.py:505
  490.5 13.2 %add_convert_fusion = bf16[1152,3072]{1,0:T(8,128)(2,1)} fusion(bf16[1152,3072]{1,0:T(8,128)(2,1)} %collective-permute-done.29, bf16[1024,1152]{1,0:T(8,128)(2,1)S(1)} %copy-done.67, bf16[1024,3072]{1,0:T(8,128)(2,1)} %broadcast_select_fusion), kind=kOutput, calls=%fused_computation | convolution fusion | flops 7258374144 | bytes 22806528 | tf_op jit(solution)/shard_map/dot_general | solution.py:29
  504.2 3.9 dynamic-slice_bitcast_fusion.2
  512.3 4.8 all-to-all-start.7
  518.7 47.8 %attend_back.2 = (bf16[1024,896]{1,0:T(8,128)(2,1)}, bf16[1024,896]{1,0:T(8,128)(2,1)}, f32[2,8,128]{2,1,0:T(8,128)}) custom-call(bf16[16,1024,128]{2,1,0:T(8,128)(2,1)} %get-tuple-element.477.q_ref, bf16[16,1024,128]{2,1,0:T(8,128)(2,1)} %get-tuple-element.362.k_ref, bf16[16,1024,128]{2,1,0:T(8,128)(2,1)} %get-tuple-element.363.v_ref, ...), custom_call_target="tpu_custom_call" | custom-call | flops 6710886400 | bytes 20971520 | tf_op jit(solution)/shard_map/attend_back/pallas_call | solution.py:611
  569.7 4.0 convolution_convert_fusion.3
  582.3 3.6 collective-permute-done.44
  589.3 4.8 all-to-all-start.8
  594.1 47.3 %attend_back.3 = (bf16[1024,896]{1,0:T(8,128)(2,1)}, bf16[1024,896]{1,0:T(8,128)(2,1)}, f32[2,8,128]{2,1,0:T(8,128)}) custom-call(bf16[16,1024,128]{2,1,0:T(8,128)(2,1)} %get-tuple-element.477.q_ref, bf16[16,1024,128]{2,1,0:T(8,128)(2,1)} %get-tuple-element.362.k_ref, bf16[16,1024,128]{2,1,0:T(8,128)(2,1)} %get-tuple-element.363.v_ref, ...), custom_call_target="tpu_custom_call" | custom-call | flops 6710886400 | bytes 20971520 | tf_op jit(solution)/shard_map/attend_back/pallas_call | solution.py:611
  641.5 4.2 broadcast_select_fusion.1
  652.1 4.0 add_convert_fusion.2
  656.1 5.1 all-to-all-start.9
  661.6 4.0 fusion.5
  665.6 4.3 fusion.3
  676.0 4.0 convolution_convert_fusion.2
  680.8 21.3 %input_back.1 = (f32[1024,1152]{1,0:T(8,128)}, f32[16,2304]{1,0:T(8,128)}) custom-call(bf16[1024,896]{1,0:T(8,128)(2,1)} %get-tuple-element.516.j0, bf16[1024,896]{1,0:T(8,128)(2,1)} %get-tuple-element.517.j1, bf16[1024,896]{1,0:T(8,128)(2,1)} %get-tuple-element.518.j2, bf16[1024,896]{1,0:T(8,128)(2,1)} %get-tuple-element.519.j3, ...), custom_call_target="tpu_custom_call" | custom-call | flops 8455716864 | bytes 22781952 | tf_op jit(solution)/shard_map/input_back/pallas_call | solution.py:675
  702.1 22.1 %collective-permute-done.40 = bf16[2,64,4608]{2,1,0:T(8,128)(2,1)} collective-permute-done((bf16[2,64,4608]{2,1,0:T(8,128)(2,1)}, bf16[2,64,4608]{2,1,0:T(8,128)(2,1)}, u32[]{:S(2)}, u32[]{:S(2)}) %collective-permute-start.40) | collective-permute-done | bytes 1179680 | tf_op jit(solution)/shard_map/ppermute | solution.py:297
  728.8 5.6 fusion.4
  745.8 5.7 all-to-all-start.10
  755.8 11.4 %all-to-all-done.10 = bf16[8,8,2560]{2,1,0:T(8,128)(2,1)} async-done(((bf16[8,8,2560]{2,1,0:T(8,128)(2,1)}), bf16[8,8,2560]{2,1,0:T(8,128)(2,1)}, u32[]{:S(2)}, u32[]{:S(2)}) %all-to-all-start.10) | async-done | bytes 327712 | tf_op jit(solution)/shard_map/all_to_all | solution.py:305
  778.8 5.6 all-to-all-start.11
  793.1 9.4 %collective-permute-done.49 = bf16[2,64,2560]{2,1,0:T(8,128)(2,1)S(1)} collective-permute-done((bf16[2,64,2560]{2,1,0:T(8,128)(2,1)S(1)}, bf16[2,64,2560]{2,1,0:T(8,128)(2,1)S(1)}, u32[]{:S(2)}, u32[]{:S(2)}) %collective-permute-start.49) | collective-permute-done | bytes 655392 | tf_op jit(solution)/shard_map/ppermute | solution.py:297
  805.0 7.4 all-to-all-done.11
  816.1 4.2 all-to-all-start.12
  829.6 8.2 all-to-all-done.12
  843.8 3.6 all-to-all-start.13
  847.4 3.5 pad_maximum_fusion
  869.2 4.1 reshape.467
  873.2 3.2 copy.172
  876.5 3.6 reshape.468
  (453 shorter events, 243.9 us)
Async XLA Ops:
  2.1 14.7 %all-to-all-start.1 = ((bf16[8,8,144]{2,1,0:T(8,128)(2,1)}), bf16[8,8,144]{2,1,0:T(8,128)(2,1)S(1)}, u32[]{:S(2)}, u32[]{:S(2)}) async-start(bf16[8,8,144]{2,1,0:T(8,128)(2,1)} %copy.141), calls=%async_computation.1 | async-start | bytes 65536 | tf_op jit(solution)/shard_map/all_to_all | solution.py:313
  18.0 36.8 %all-to-all-start = ((bf16[4,2,48,1792]{3,2,1,0:T(8,128)(2,1)}), bf16[4,2,48,1792]{3,2,1,0:T(8,128)(2,1)S(1)}, u32[]{:S(2)}, u32[]{:S(2)}) async-start(bf16[4,2,48,1792]{3,2,1,0:T(8,128)(2,1)} %broadcast_in_dim.60), calls=%async_computation | async-start | bytes 2752512 | tf_op jit(solution)/shard_map/all_to_all | solution.py:85
  56.0 35.3 %all-to-all-start.2 = ((bf16[4,2,48,1536]{3,2,1,0:T(8,128)(2,1)}), bf16[4,2,48,1536]{3,2,1,0:T(8,128)(2,1)S(1)}, u32[]{:S(2)}, u32[]{:S(2)}) async-start(bf16[4,2,48,1536]{3,2,1,0:T(8,128)(2,1)} %broadcast_in_dim.64), calls=%async_computation.2 | async-start | bytes 2359296 | tf_op jit(solution)/shard_map/all_to_all | solution.py:85
  60.7 30.5 %collective-permute-start = (bf16[4,2,48,1792]{3,2,0,1:T(8,128)(2,1)}, bf16[4,2,48,1792]{3,2,0,1:T(8,128)(2,1)}, u32[]{:S(2)}, u32[]{:S(2)}) collective-permute-start(bf16[4,2,48,1792]{3,2,0,1:T(8,128)(2,1)} %copy.142), channel_id=1, source_target_pairs={{0,1},{1,0},{2,3},{3,2},{4,5},{5,4},{6,7},{7,6},{8,9},{9,8},{10,11... | collective-permute-start | bytes 4128776 | tf_op jit(solution)/shard_map/ppermute | solution.py:139
  61.9 29.4 %collective-permute-start.2 = (bf16[4,2,48,1792]{3,2,1,0:T(8,128)(2,1)S(1)}, bf16[4,2,48,1792]{3,2,1,0:T(8,128)(2,1)}, u32[]{:S(2)}, u32[]{:S(2)}) collective-permute-start(bf16[4,2,48,1792]{3,2,1,0:T(8,128)(2,1)S(1)} %all-to-all-done.a0), channel_id=1, source_target_pairs={{0,8},{1,9},{2,10},{3,11},{4,12},{5,13},{6,14},{7,15},{8,0},{9,1},... | collective-permute-start | bytes 4128776 | tf_op jit(solution)/shard_map/ppermute | solution.py:156
  64.5 17.4 %collective-permute-start.1 = (bf16[4,48,1792]{2,1,0:T(8,128)(2,1)}, bf16[4,48,1792]{2,1,0:T(8,128)(2,1)S(1)}, u32[]{:S(2)}, u32[]{:S(2)}) collective-permute-start(bf16[4,48,1792]{2,1,0:T(8,128)(2,1)} %slice_bitcast_fusion), channel_id=1, source_target_pairs={{0,16},{1,17},{2,18},{3,19},{4,20},{5,21},{6,22},{7,23},{8,24},{9,... | collective-permute-start | bytes 2064392 | tf_op jit(solution)/shard_map/ppermute | solution.py:147
  91.3 25.7 %all-to-all-start.4 = ((bf16[8,8,6912]{2,1,0:T(8,128)(2,1)}), bf16[8,8,6912]{2,1,0:T(8,128)(2,1)S(1)}, u32[]{:S(2)}, u32[]{:S(2)}) async-start(bf16[8,8,6912]{2,1,0:T(8,128)(2,1)} %bitcast.20), calls=%async_computation.4 | async-start | bytes 1769472 | tf_op jit(solution)/shard_map/all_to_all | solution.py:319
  96.4 36.5 %collective-permute-start.4 = (bf16[4,2,48,1792]{3,2,0,1:T(8,128)(2,1)}, bf16[4,2,48,1792]{3,2,0,1:T(8,128)(2,1)}, u32[]{:S(2)}, u32[]{:S(2)}) collective-permute-start(bf16[4,2,48,1792]{3,2,0,1:T(8,128)(2,1)} %collective-permute-done), channel_id=1, source_target_pairs={{0,8},{1,9},{2,10},{3,11},{4,12},{5,13},{6,14},{7,15},{8,0},{9,1},... | collective-permute-start | bytes 4128776 | tf_op jit(solution)/shard_map/ppermute | solution.py:156
  101.3 22.3 %collective-permute-start.3 = (bf16[4,48,1792]{2,1,0:T(8,128)(2,1)}, bf16[4,48,1792]{2,1,0:T(8,128)(2,1)}, u32[]{:S(2)}, u32[]{:S(2)}) collective-permute-start(bf16[4,48,1792]{2,1,0:T(8,128)(2,1)} %slice_bitcast_fusion.1), channel_id=1, source_target_pairs={{0,16},{1,17},{2,18},{3,19},{4,20},{5,21},{6,22},{7,23},{8,24},{9,... | collective-permute-start | bytes 2064392 | tf_op jit(solution)/shard_map/ppermute | solution.py:149
  102.5 21.1 %collective-permute-start.5 = (bf16[4,48,1792]{2,1,0:T(8,128)(2,1)}, bf16[4,48,1792]{2,1,0:T(8,128)(2,1)}, u32[]{:S(2)}, u32[]{:S(2)}) collective-permute-start(bf16[4,48,1792]{2,1,0:T(8,128)(2,1)} %copy-done.47), channel_id=1, source_target_pairs={{0,8},{1,9},{2,10},{3,11},{4,12},{5,13},{6,14},{7,15},{8,0},{9,1},... | collective-permute-start | bytes 2064392 | tf_op jit(solution)/shard_map/ppermute | solution.py:156
  118.8 14.1 %all-to-all-start.3 = ((bf16[4,2,48,640]{3,2,1,0:T(8,128)(2,1)}), bf16[4,2,48,640]{3,2,1,0:T(8,128)(2,1)S(1)}, u32[]{:S(2)}, u32[]{:S(2)}) async-start(bf16[4,2,48,640]{3,2,1,0:T(8,128)(2,1)} %broadcast_in_dim.65), calls=%async_computation.3 | async-start | bytes 983040 | tf_op jit(solution)/shard_map/all_to_all | solution.py:85
  136.1 69.0 %all-to-all-start.5 = ((bf16[4,2,48,1536]{3,2,1,0:T(8,128)(2,1)}), bf16[4,2,48,1536]{3,2,1,0:T(8,128)(2,1)}, u32[]{:S(2)}, u32[]{:S(2)}) async-start(bf16[4,2,48,1536]{3,2,1,0:T(8,128)(2,1)} %broadcast_in_dim.66), calls=%async_computation.5 | async-start | bytes 2359296 | tf_op jit(solution)/shard_map/all_to_all | solution.py:85
  141.0 16.6 %collective-permute-start.8 = (bf16[4,48,1792]{2,1,0:T(8,128)(2,1)}, bf16[4,48,1792]{2,1,0:T(8,128)(2,1)}, u32[]{:S(2)}, u32[]{:S(2)}) collective-permute-start(bf16[4,48,1792]{2,1,0:T(8,128)(2,1)} %collective-permute-done.3), channel_id=1, source_target_pairs={{0,8},{1,9},{2,10},{3,11},{4,12},{5,13},{6,14},{7,15},{8,0},{9,1},... | collective-permute-start | bytes 2064392 | tf_op jit(solution)/shard_map/ppermute | solution.py:156
  148.8 56.3 %collective-permute-start.6 = (bf16[4,2,48,640]{3,2,1,0:T(8,128)(2,1)S(1)}, bf16[4,2,48,640]{3,2,1,0:T(8,128)(2,1)S(1)}, u32[]{:S(2)}, u32[]{:S(2)}) collective-permute-start(bf16[4,2,48,640]{3,2,1,0:T(8,128)(2,1)S(1)} %all-to-all-done.3.a0), channel_id=1, source_target_pairs={{0,1},{1,0},{2,3},{3,2},{4,5},{5,4},{6,7},{7,6},{8,9},{9,8},{10,11... | collective-permute-start | bytes 1474568 | tf_op jit(solution)/shard_map/ppermute | solution.py:139
  150.2 54.9 %collective-permute-start.7 = (bf16[4,2,48,1536]{3,2,1,0:T(8,128)(2,1)S(1)}, bf16[4,2,48,1536]{3,2,1,0:T(8,128)(2,1)}, u32[]{:S(2)}, u32[]{:S(2)}) collective-permute-start(bf16[4,2,48,1536]{3,2,1,0:T(8,128)(2,1)S(1)} %all-to-all-done.2.a0), channel_id=1, source_target_pairs={{0,1},{1,0},{2,3},{3,2},{4,5},{5,4},{6,7},{7,6},{8,9},{9,8},{10,11... | collective-permute-start | bytes 3538952 | tf_op jit(solution)/shard_map/ppermute | solution.py:139
  206.4 52.1 %all-to-all-start.6 = ((bf16[4,2,128,640]{3,2,1,0:T(8,128)(2,1)}), bf16[4,2,128,640]{3,2,1,0:T(8,128)(2,1)S(1)}, u32[]{:S(2)}, u32[]{:S(2)}) async-start(bf16[4,2,128,640]{3,2,1,0:T(8,128)(2,1)} %broadcast_in_dim.69), calls=%async_computation.6 | async-start | bytes 2621440 | tf_op jit(solution)/shard_map/all_to_all | solution.py:85
  211.3 12.0 %collective-permute-start.9 = (bf16[4,2,48,640]{3,2,1,0:T(8,128)(2,1)S(1)}, bf16[4,2,48,640]{3,2,1,0:T(8,128)(2,1)S(1)}, u32[]{:S(2)}, u32[]{:S(2)}) collective-permute-start(bf16[4,2,48,640]{3,2,1,0:T(8,128)(2,1)S(1)} %pad_maximum_fusion.20), channel_id=1, source_target_pairs={{0,16},{1,17},{2,18},{3,19},{4,20},{5,21},{6,22},{7,23},{8,24},{9,... | collective-permute-start | bytes 1474568 | tf_op jit(solution)/shard_map/ppermute | solution.py:151
  213.7 42.8 %collective-permute-start.13 = (bf16[4,2,48,1536]{3,2,1,0:T(8,128)(2,1)}, bf16[4,2,48,1536]{3,2,1,0:T(8,128)(2,1)S(1)}, u32[]{:S(2)}, u32[]{:S(2)}) collective-permute-start(bf16[4,2,48,1536]{3,2,1,0:T(8,128)(2,1)} %collective-permute-done.7.a1), channel_id=1, source_target_pairs={{0,8},{1,9},{2,10},{3,11},{4,12},{5,13},{6,14},{7,15},{8,0},{9,1},... | collective-permute-start | bytes 3538952 | tf_op jit(solution)/shard_map/ppermute | solution.py:156
  216.1 40.4 %collective-permute-start.12 = (bf16[4,2,48,1536]{3,2,1,0:T(8,128)(2,1)}, bf16[4,2,48,1536]{3,2,1,0:T(8,128)(2,1)}, u32[]{:S(2)}, u32[]{:S(2)}) collective-permute-start(bf16[4,2,48,1536]{3,2,1,0:T(8,128)(2,1)} %pad_maximum_fusion.11), channel_id=1, source_target_pairs={{0,16},{1,17},{2,18},{3,19},{4,20},{5,21},{6,22},{7,23},{8,24},{9,... | collective-permute-start | bytes 3538952 | tf_op jit(solution)/shard_map/ppermute | solution.py:151
  216.3 41.2 %collective-permute-start.14 = (bf16[4,2,48,1536]{3,2,1,0:T(8,128)(2,1)S(1)}, bf16[4,2,48,1536]{3,2,1,0:T(8,128)(2,1)S(1)}, u32[]{:S(2)}, u32[]{:S(2)}) collective-permute-start(bf16[4,2,48,1536]{3,2,1,0:T(8,128)(2,1)S(1)} %all-to-all-done.2.a0), channel_id=1, source_target_pairs={{0,8},{1,9},{2,10},{3,11},{4,12},{5,13},{6,14},{7,15},{8,0},{9,1},... | collective-permute-start | bytes 3538952 | tf_op jit(solution)/shard_map/ppermute | solution.py:156
  216.6 41.9 %collective-permute-start.15 = (bf16[4,2,48,1536]{3,2,1,0:T(8,128)(2,1)}, bf16[4,2,48,1536]{3,2,1,0:T(8,128)(2,1)}, u32[]{:S(2)}, u32[]{:S(2)}) collective-permute-start(bf16[4,2,48,1536]{3,2,1,0:T(8,128)(2,1)} %all-to-all-done.5.a0), channel_id=1, source_target_pairs={{0,1},{1,0},{2,3},{3,2},{4,5},{5,4},{6,7},{7,6},{8,9},{9,8},{10,11... | collective-permute-start | bytes 3538952 | tf_op jit(solution)/shard_map/ppermute | solution.py:139
  227.9 27.8 %collective-permute-start.11 = (bf16[4,2,48,640]{3,2,1,0:T(8,128)(2,1)S(1)}, bf16[4,2,48,640]{3,2,1,0:T(8,128)(2,1)S(1)}, u32[]{:S(2)}, u32[]{:S(2)}) collective-permute-start(bf16[4,2,48,640]{3,2,1,0:T(8,128)(2,1)S(1)} %all-to-all-done.3.a0), channel_id=1, source_target_pairs={{0,8},{1,9},{2,10},{3,11},{4,12},{5,13},{6,14},{7,15},{8,0},{9,1},... | collective-permute-start | bytes 1474568 | tf_op jit(solution)/shard_map/ppermute | solution.py:156
  259.8 31.4 %collective-permute-start.18 = (bf16[4,2,48,1536]{3,2,1,0:T(8,128)(2,1)}, bf16[4,2,48,1536]{3,2,1,0:T(8,128)(2,1)}, u32[]{:S(2)}, u32[]{:S(2)}) collective-permute-start(bf16[4,2,48,1536]{3,2,1,0:T(8,128)(2,1)} %collective-permute-done.15.a1), channel_id=1, source_target_pairs={{0,8},{1,9},{2,10},{3,11},{4,12},{5,13},{6,14},{7,15},{8,0},{9,1},... | collective-permute-start | bytes 3538952 | tf_op jit(solution)/shard_map/ppermute | solution.py:156
  260.2 26.9 %collective-permute-start.16 = (bf16[4,2,48,1536]{3,2,1,0:T(8,128)(2,1)}, bf16[4,2,48,1536]{3,2,1,0:T(8,128)(2,1)}, u32[]{:S(2)}, u32[]{:S(2)}) collective-permute-start(bf16[4,2,48,1536]{3,2,1,0:T(8,128)(2,1)} %collective-permute-done.12.ax), channel_id=1, source_target_pairs={{0,8},{1,9},{2,10},{3,11},{4,12},{5,13},{6,14},{7,15},{8,0},{9,1},... | collective-permute-start | bytes 3538952 | tf_op jit(solution)/shard_map/ppermute | solution.py:156
  261.5 30.2 %collective-permute-start.20 = (bf16[4,2,128,640]{3,2,1,0:T(8,128)(2,1)S(1)}, bf16[4,2,128,640]{3,2,1,0:T(8,128)(2,1)}, u32[]{:S(2)}, u32[]{:S(2)}) collective-permute-start(bf16[4,2,128,640]{3,2,1,0:T(8,128)(2,1)S(1)} %all-to-all-done.6.a0), channel_id=1, source_target_pairs={{0,1},{1,0},{2,3},{3,2},{4,5},{5,4},{6,7},{7,6},{8,9},{9,8},{10,11... | collective-permute-start | bytes 3932168 | tf_op jit(solution)/shard_map/ppermute | solution.py:139
  264.0 27.2 %collective-permute-start.17 = (bf16[4,2,48,1536]{3,2,1,0:T(8,128)(2,1)}, bf16[4,2,48,1536]{3,2,1,0:T(8,128)(2,1)}, u32[]{:S(2)}, u32[]{:S(2)}) collective-permute-start(bf16[4,2,48,1536]{3,2,1,0:T(8,128)(2,1)} %pad_maximum_fusion.12), channel_id=1, source_target_pairs={{0,16},{1,17},{2,18},{3,19},{4,20},{5,21},{6,22},{7,23},{8,24},{9,... | collective-permute-start | bytes 3538952 | tf_op jit(solution)/shard_map/ppermute | solution.py:151
  266.0 25.1 %collective-permute-start.19 = (bf16[4,2,48,1536]{3,2,1,0:T(8,128)(2,1)}, bf16[4,2,48,1536]{3,2,1,0:T(8,128)(2,1)}, u32[]{:S(2)}, u32[]{:S(2)}) collective-permute-start(bf16[4,2,48,1536]{3,2,1,0:T(8,128)(2,1)} %all-to-all-done.5.a0), channel_id=1, source_target_pairs={{0,8},{1,9},{2,10},{3,11},{4,12},{5,13},{6,14},{7,15},{8,0},{9,1},... | collective-permute-start | bytes 3538952 | tf_op jit(solution)/shard_map/ppermute | solution.py:156
  294.1 29.4 %collective-permute-start.23 = (bf16[4,2,128,640]{3,2,1,0:T(8,128)(2,1)}, bf16[4,2,128,640]{3,2,1,0:T(8,128)(2,1)}, u32[]{:S(2)}, u32[]{:S(2)}) collective-permute-start(bf16[4,2,128,640]{3,2,1,0:T(8,128)(2,1)} %pad_maximum_fusion.8), channel_id=1, source_target_pairs={{0,16},{1,17},{2,18},{3,19},{4,20},{5,21},{6,22},{7,23},{8,24},{9,... | collective-permute-start | bytes 3932168 | tf_op jit(solution)/shard_map/ppermute | solution.py:151
  295.3 28.2 %collective-permute-start.24 = (bf16[4,2,128,640]{3,2,1,0:T(8,128)(2,1)}, bf16[4,2,128,640]{3,2,1,0:T(8,128)(2,1)S(1)}, u32[]{:S(2)}, u32[]{:S(2)}) collective-permute-start(bf16[4,2,128,640]{3,2,1,0:T(8,128)(2,1)} %collective-permute-done.20.a1), channel_id=1, source_target_pairs={{0,8},{1,9},{2,10},{3,11},{4,12},{5,13},{6,14},{7,15},{8,0},{9,1},... | collective-permute-start | bytes 3932168 | tf_op jit(solution)/shard_map/ppermute | solution.py:156
  296.8 27.8 %collective-permute-start.25 = (bf16[4,2,128,640]{3,2,1,0:T(8,128)(2,1)S(1)}, bf16[4,2,128,640]{3,2,1,0:T(8,128)(2,1)S(1)}, u32[]{:S(2)}, u32[]{:S(2)}) collective-permute-start(bf16[4,2,128,640]{3,2,1,0:T(8,128)(2,1)S(1)} %all-to-all-done.6.a0), channel_id=1, source_target_pairs={{0,8},{1,9},{2,10},{3,11},{4,12},{5,13},{6,14},{7,15},{8,0},{9,1},... | collective-permute-start | bytes 3932168 | tf_op jit(solution)/shard_map/ppermute | solution.py:156
  296.8 19.9 %collective-permute-start.22 = (bf16[4,2,48,1536]{3,2,1,0:T(8,128)(2,1)}, bf16[4,2,48,1536]{3,2,1,0:T(8,128)(2,1)}, u32[]{:S(2)}, u32[]{:S(2)}) collective-permute-start(bf16[4,2,48,1536]{3,2,1,0:T(8,128)(2,1)} %collective-permute-done.17.ax), channel_id=1, source_target_pairs={{0,8},{1,9},{2,10},{3,11},{4,12},{5,13},{6,14},{7,15},{8,0},{9,1},... | collective-permute-start | bytes 3538952 | tf_op jit(solution)/shard_map/ppermute | solution.py:156
  325.6 26.1 %collective-permute-start.26 = (bf16[4,2,128,640]{3,2,1,0:T(8,128)(2,1)}, bf16[4,2,128,640]{3,2,1,0:T(8,128)(2,1)S(1)}, u32[]{:S(2)}, u32[]{:S(2)}) collective-permute-start(bf16[4,2,128,640]{3,2,1,0:T(8,128)(2,1)} %collective-permute-done.23.ax), channel_id=1, source_target_pairs={{0,8},{1,9},{2,10},{3,11},{4,12},{5,13},{6,14},{7,15},{8,0},{9,1},... | collective-permute-start | bytes 3932168 | tf_op jit(solution)/shard_map/ppermute | solution.py:156
  386.2 17.3 %collective-permute-start.27 = (bf16[3072,640]{1,0:T(8,128)(2,1)}, bf16[3072,640]{1,0:T(8,128)(2,1)}, u32[]{:S(2)}, u32[]{:S(2)}) collective-permute-start(bf16[3072,640]{1,0:T(8,128)(2,1)} %convolution_convert_fusion.1), channel_id=1, source_target_pairs={{0,8},{1,9},{2,10},{3,11},{4,12},{5,13},{6,14},{7,15},{8,0},{9,1},... | collective-permute-start | bytes 11796488 | tf_op jit(solution)/shard_map/ppermute | solution.py:203
  430.4 41.5 %collective-permute-start.29 = (bf16[1152,3072]{1,0:T(8,128)(2,1)}, bf16[1152,3072]{1,0:T(8,128)(2,1)}, u32[]{:S(2)}, u32[]{:S(2)}) collective-permute-start(bf16[1152,3072]{1,0:T(8,128)(2,1)} %convolution_convert_fusion), channel_id=1, source_target_pairs={{0,8},{1,9},{2,10},{3,11},{4,12},{5,13},{6,14},{7,15},{8,0},{9,1},... | collective-permute-start | bytes 21233672 | tf_op jit(solution)/shard_map/ppermute | solution.py:203
  434.0 37.9 %collective-permute-start.28 = (bf16[4,2,128,640]{3,2,1,0:T(8,128)(2,1)S(1)}, bf16[4,2,128,640]{3,2,1,0:T(8,128)(2,1)S(1)}, u32[]{:S(2)}, u32[]{:S(2)}) collective-permute-start(bf16[4,2,128,640]{3,2,1,0:T(8,128)(2,1)S(1)} %dynamic-slice_bitcast_fusion.7), channel_id=1, source_target_pairs={{0,16},{1,17},{2,18},{3,19},{4,20},{5,21},{6,22},{7,23},{8,24},{9,... | collective-permute-start | bytes 3932168 | tf_op jit(solution)/shard_map/ppermute | solution.py:223
  473.6 30.4 %collective-permute-start.30 = (bf16[4,2,128,640]{3,2,1,0:T(8,128)(2,1)}, bf16[4,2,128,640]{3,2,1,0:T(8,128)(2,1)}, u32[]{:S(2)}, u32[]{:S(2)}) collective-permute-start(bf16[4,2,128,640]{3,2,1,0:T(8,128)(2,1)} %pad_maximum_fusion.9), channel_id=1, source_target_pairs={{0,1},{1,0},{2,3},{3,2},{4,5},{5,4},{6,7},{7,6},{8,9},{9,8},{10,11... | collective-permute-start | bytes 3932168 | tf_op jit(solution)/shard_map/ppermute | solution.py:234
  508.1 65.5 %collective-permute-start.31 = (bf16[4,2,48,3072]{3,2,1,0:T(8,128)(2,1)}, bf16[4,2,48,3072]{3,2,1,0:T(8,128)(2,1)}, u32[]{:S(2)}, u32[]{:S(2)}) collective-permute-start(bf16[4,2,48,3072]{3,2,1,0:T(8,128)(2,1)} %dynamic-slice_bitcast_fusion.2), channel_id=1, source_target_pairs={{0,16},{1,17},{2,18},{3,19},{4,20},{5,21},{6,22},{7,23},{8,24},{9,... | collective-permute-start | bytes 7077896 | tf_op jit(solution)/shard_map/ppermute | solution.py:223
  512.3 61.4 %all-to-all-start.7 = ((bf16[4,2,128,640]{3,2,1,0:T(8,128)(2,1)}), bf16[4,2,128,640]{3,2,1,0:T(8,128)(2,1)S(1)}, u32[]{:S(2)}, u32[]{:S(2)}) async-start(bf16[4,2,128,640]{3,2,1,0:T(8,128)(2,1)} %add_convert_fusion.3), calls=%async_computation.7 | async-start | bytes 2621440 | tf_op jit(solution)/shard_map/all_to_all | solution.py:85
  517.0 56.6 %collective-permute-start.32 = (bf16[1152,640]{1,0:T(8,128)(2,1)}, bf16[1152,640]{1,0:T(8,128)(2,1)S(1)}, u32[]{:S(2)}, u32[]{:S(2)}) collective-permute-start(bf16[1152,640]{1,0:T(8,128)(2,1)} %convolution_convert_fusion.4), channel_id=1, source_target_pairs={{0,8},{1,9},{2,10},{3,11},{4,12},{5,13},{6,14},{7,15},{8,0},{9,1},... | collective-permute-start | bytes 4423688 | tf_op jit(solution)/shard_map/ppermute | solution.py:203
  580.3 65.4 %collective-permute-start.34 = (bf16[4,2,48,3072]{3,2,1,0:T(8,128)(2,1)}, bf16[4,2,48,3072]{3,2,1,0:T(8,128)(2,1)}, u32[]{:S(2)}, u32[]{:S(2)}) collective-permute-start(bf16[4,2,48,3072]{3,2,1,0:T(8,128)(2,1)} %pad_maximum_fusion.2), channel_id=1, source_target_pairs={{0,1},{1,0},{2,3},{3,2},{4,5},{5,4},{6,7},{7,6},{8,9},{9,8},{10,11... | collective-permute-start | bytes 7077896 | tf_op jit(solution)/shard_map/ppermute | solution.py:234
  581.8 64.0 %collective-permute-start.35 = (bf16[1152,896]{1,0:T(8,128)(2,1)}, bf16[1152,896]{1,0:T(8,128)(2,1)}, u32[]{:S(2)}, u32[]{:S(2)}) collective-permute-start(bf16[1152,896]{1,0:T(8,128)(2,1)} %convolution_convert_fusion.3), channel_id=1, source_target_pairs={{0,8},{1,9},{2,10},{3,11},{4,12},{5,13},{6,14},{7,15},{8,0},{9,1},... | collective-permute-start | bytes 6193160 | tf_op jit(solution)/shard_map/ppermute | solution.py:203
  586.6 164.9 %collective-permute-start.45 = (bf16[2,64,144]{2,1,0:T(8,128)(2,1)}, bf16[2,64,144]{2,1,0:T(8,128)(2,1)}, u32[]{:S(2)}, u32[]{:S(2)}) collective-permute-start(bf16[2,64,144]{2,1,0:T(8,128)(2,1)} %pad_maximum_fusion.32), channel_id=1, source_target_pairs={{0,16},{1,17},{2,18},{3,19},{4,20},{5,21},{6,22},{7,23},{8,24},{9,... | collective-permute-start | bytes 110600 | tf_op jit(solution)/shard_map/ppermute | solution.py:297
  588.1 57.6 %collective-permute-start.33 = (bf16[2,128,640]{2,1,0:T(8,128)(2,1)S(1)}, bf16[2,128,640]{2,1,0:T(8,128)(2,1)S(1)}, u32[]{:S(2)}, u32[]{:S(2)}) collective-permute-start(bf16[2,128,640]{2,1,0:T(8,128)(2,1)S(1)} %reduce_sum.124), channel_id=1, source_target_pairs={{0,16},{1,17},{2,18},{3,19},{4,20},{5,21},{6,22},{7,23},{8,24},{9,... | collective-permute-start | bytes 983048 | tf_op jit(solution)/shard_map/ppermute | solution.py:245
  589.3 56.4 %all-to-all-start.8 = ((bf16[8,8,4608]{2,1,0:T(8,128)(2,1)}), bf16[8,8,4608]{2,1,0:T(8,128)(2,1)}, u32[]{:S(2)}, u32[]{:S(2)}) async-start(bf16[8,8,4608]{2,1,0:T(8,128)(2,1)} %broadcast_in_dim.71), calls=%async_computation.8 | async-start | bytes 1179648 | tf_op jit(solution)/shard_map/all_to_all | solution.py:305
  646.7 87.7 %collective-permute-start.36 = (bf16[384,640]{1,0:T(8,128)(2,1)}, bf16[384,640]{1,0:T(8,128)(2,1)}, u32[]{:S(2)}, u32[]{:S(2)}) collective-permute-start(bf16[384,640]{1,0:T(8,128)(2,1)} %pad_maximum_fusion.21), channel_id=1, source_target_pairs={{0,8},{1,9},{2,10},{3,11},{4,12},{5,13},{6,14},{7,15},{8,0},{9,1},... | collective-permute-start | bytes 1474568 | tf_op jit(solution)/shard_map/ppermute | solution.py:255
  656.1 78.3 %all-to-all-start.9 = ((bf16[4,2,48,3072]{3,2,1,0:T(8,128)(2,1)}), bf16[4,2,48,3072]{3,2,1,0:T(8,128)(2,1)}, u32[]{:S(2)}, u32[]{:S(2)}) async-start(bf16[4,2,48,3072]{3,2,1,0:T(8,128)(2,1)} %add_convert_fusion.2), calls=%async_computation.9 | async-start | bytes 4718592 | tf_op jit(solution)/shard_map/all_to_all | solution.py:85
  661.2 11.3 %collective-permute-start.39 = (bf16[64,4608]{1,0:T(8,128)(2,1)}, bf16[64,4608]{1,0:T(8,128)(2,1)S(1)}, u32[]{:S(2)}, u32[]{:S(2)}) collective-permute-start(bf16[64,4608]{1,0:T(8,128)(2,1)} %bitcast.52), channel_id=1, source_target_pairs={{0,8},{1,9},{2,10},{3,11},{4,12},{5,13},{6,14},{7,15},{8,0},{9,1},... | collective-permute-start | bytes 1769480 | tf_op jit(solution)/shard_map/ppermute | solution.py:295
  671.3 63.1 %collective-permute-start.37 = (bf16[4,2,48,1536]{3,2,1,0:T(8,128)(2,1)}, bf16[4,2,48,1536]{3,2,1,0:T(8,128)(2,1)}, u32[]{:S(2)}, u32[]{:S(2)}) collective-permute-start(bf16[4,2,48,1536]{3,2,1,0:T(8,128)(2,1)} %dynamic-slice_bitcast_fusion.8), channel_id=1, source_target_pairs={{0,16},{1,17},{2,18},{3,19},{4,20},{5,21},{6,22},{7,23},{8,24},{9,... | collective-permute-start | bytes 3538952 | tf_op jit(solution)/shard_map/ppermute | solution.py:223
  675.6 48.6 %collective-permute-start.40 = (bf16[2,64,4608]{2,1,0:T(8,128)(2,1)}, bf16[2,64,4608]{2,1,0:T(8,128)(2,1)}, u32[]{:S(2)}, u32[]{:S(2)}) collective-permute-start(bf16[2,64,4608]{2,1,0:T(8,128)(2,1)} %pad_maximum_fusion.13), channel_id=1, source_target_pairs={{0,16},{1,17},{2,18},{3,19},{4,20},{5,21},{6,22},{7,23},{8,24},{9,... | collective-permute-start | bytes 3538952 | tf_op jit(solution)/shard_map/ppermute | solution.py:297
  680.0 47.3 %collective-permute-start.38 = (bf16[1152,896]{1,0:T(8,128)(2,1)}, bf16[1152,896]{1,0:T(8,128)(2,1)}, u32[]{:S(2)}, u32[]{:S(2)}) collective-permute-start(bf16[1152,896]{1,0:T(8,128)(2,1)} %convolution_convert_fusion.2), channel_id=1, source_target_pairs={{0,8},{1,9},{2,10},{3,11},{4,12},{5,13},{6,14},{7,15},{8,0},{9,1},... | collective-permute-start | bytes 6193160 | tf_op jit(solution)/shard_map/ppermute | solution.py:203
  736.9 31.9 %collective-permute-start.42 = (bf16[4,2,48,1536]{3,2,1,0:T(8,128)(2,1)}, bf16[4,2,48,1536]{3,2,1,0:T(8,128)(2,1)}, u32[]{:S(2)}, u32[]{:S(2)}) collective-permute-start(bf16[4,2,48,1536]{3,2,1,0:T(8,128)(2,1)} %pad_maximum_fusion.14), channel_id=1, source_target_pairs={{0,1},{1,0},{2,3},{3,2},{4,5},{5,4},{6,7},{7,6},{8,9},{9,8},{10,11... | collective-permute-start | bytes 3538952 | tf_op jit(solution)/shard_map/ppermute | solution.py:234
  740.7 26.5 %collective-permute-start.41 = (bf16[2,48,3072]{2,1,0:T(8,128)(2,1)}, bf16[2,48,3072]{2,1,0:T(8,128)(2,1)}, u32[]{:S(2)}, u32[]{:S(2)}) collective-permute-start(bf16[2,48,3072]{2,1,0:T(8,128)(2,1)} %reduce_sum.125), channel_id=1, source_target_pairs={{0,16},{1,17},{2,18},{3,19},{4,20},{5,21},{6,22},{7,23},{8,24},{9,... | collective-permute-start | bytes 1769480 | tf_op jit(solution)/shard_map/ppermute | solution.py:245
  743.9 24.9 %collective-permute-start.43 = (bf16[4,2,48,896]{3,2,1,0:T(8,128)(2,1)}, bf16[4,2,48,896]{3,2,1,0:T(8,128)(2,1)}, u32[]{:S(2)}, u32[]{:S(2)}) collective-permute-start(bf16[4,2,48,896]{3,2,1,0:T(8,128)(2,1)} %dynamic-slice_bitcast_fusion.11), channel_id=1, source_target_pairs={{0,16},{1,17},{2,18},{3,19},{4,20},{5,21},{6,22},{7,23},{8,24},{9,... | collective-permute-start | bytes 2064392 | tf_op jit(solution)/shard_map/ppermute | solution.py:223
  745.8 21.4 %all-to-all-start.10 = ((bf16[8,8,2560]{2,1,0:T(8,128)(2,1)}), bf16[8,8,2560]{2,1,0:T(8,128)(2,1)}, u32[]{:S(2)}, u32[]{:S(2)}) async-start(bf16[8,8,2560]{2,1,0:T(8,128)(2,1)} %broadcast_in_dim.73), calls=%async_computation.10 | async-start | bytes 655360 | tf_op jit(solution)/shard_map/all_to_all | solution.py:305
  772.0 33.0 %collective-permute-start.46 = (bf16[144,3072]{1,0:T(8,128)(2,1)}, bf16[144,3072]{1,0:T(8,128)(2,1)}, u32[]{:S(2)}, u32[]{:S(2)}) collective-permute-start(bf16[144,3072]{1,0:T(8,128)(2,1)} %pad_maximum_fusion.16), channel_id=1, source_target_pairs={{0,8},{1,9},{2,10},{3,11},{4,12},{5,13},{6,14},{7,15},{8,0},{9,1},... | collective-permute-start | bytes 2654216 | tf_op jit(solution)/shard_map/ppermute | solution.py:255
  776.1 9.5 %collective-permute-start.48 = (bf16[64,2560]{1,0:T(8,128)(2,1)}, bf16[64,2560]{1,0:T(8,128)(2,1)}, u32[]{:S(2)}, u32[]{:S(2)}) collective-permute-start(bf16[64,2560]{1,0:T(8,128)(2,1)} %bitcast.72), channel_id=1, source_target_pairs={{0,8},{1,9},{2,10},{3,11},{4,12},{5,13},{6,14},{7,15},{8,0},{9,1},... | collective-permute-start | bytes 983048 | tf_op jit(solution)/shard_map/ppermute | solution.py:295
  778.8 33.7 %all-to-all-start.11 = ((bf16[4,2,48,1536]{3,2,1,0:T(8,128)(2,1)}), bf16[4,2,48,1536]{3,2,1,0:T(8,128)(2,1)S(1)}, u32[]{:S(2)}, u32[]{:S(2)}) async-start(bf16[4,2,48,1536]{3,2,1,0:T(8,128)(2,1)} %add_convert_fusion.4), calls=%async_computation.11 | async-start | bytes 2359296 | tf_op jit(solution)/shard_map/all_to_all | solution.py:85
  786.9 15.6 %collective-permute-start.49 = (bf16[2,64,2560]{2,1,0:T(8,128)(2,1)S(1)}, bf16[2,64,2560]{2,1,0:T(8,128)(2,1)S(1)}, u32[]{:S(2)}, u32[]{:S(2)}) collective-permute-start(bf16[2,64,2560]{2,1,0:T(8,128)(2,1)S(1)} %pad_maximum_fusion.19), channel_id=1, source_target_pairs={{0,16},{1,17},{2,18},{3,19},{4,20},{5,21},{6,22},{7,23},{8,24},{9,... | collective-permute-start | bytes 1966088 | tf_op jit(solution)/shard_map/ppermute | solution.py:297
  788.2 15.9 %collective-permute-start.47 = (bf16[4,2,48,896]{3,2,1,0:T(8,128)(2,1)S(1)}, bf16[4,2,48,896]{3,2,1,0:T(8,128)(2,1)S(1)}, u32[]{:S(2)}, u32[]{:S(2)}) collective-permute-start(bf16[4,2,48,896]{3,2,1,0:T(8,128)(2,1)S(1)} %pad_maximum_fusion.17), channel_id=1, source_target_pairs={{0,1},{1,0},{2,3},{3,2},{4,5},{5,4},{6,7},{7,6},{8,9},{9,8},{10,11... | collective-permute-start | bytes 2064392 | tf_op jit(solution)/shard_map/ppermute | solution.py:234
  816.1 21.7 %all-to-all-start.12 = ((bf16[4,2,48,896]{3,2,1,0:T(8,128)(2,1)}), bf16[4,2,48,896]{3,2,1,0:T(8,128)(2,1)}, u32[]{:S(2)}, u32[]{:S(2)}) async-start(bf16[4,2,48,896]{3,2,1,0:T(8,128)(2,1)} %add_convert_fusion.5), calls=%async_computation.12 | async-start | bytes 1376256 | tf_op jit(solution)/shard_map/all_to_all | solution.py:85
  839.7 13.1 %collective-permute-start.51 = (bf16[144,1536]{1,0:T(8,128)(2,1)S(1)}, bf16[144,1536]{1,0:T(8,128)(2,1)}, u32[]{:S(2)}, u32[]{:S(2)}) collective-permute-start(bf16[144,1536]{1,0:T(8,128)(2,1)S(1)} %pad_maximum_fusion.22), channel_id=1, source_target_pairs={{0,8},{1,9},{2,10},{3,11},{4,12},{5,13},{6,14},{7,15},{8,0},{9,1},... | collective-permute-start | bytes 1327112 | tf_op jit(solution)/shard_map/ppermute | solution.py:255
  842.4 10.4 %collective-permute-start.52 = (bf16[2,48,896]{2,1,0:T(8,128)(2,1)S(1)}, bf16[2,48,896]{2,1,0:T(8,128)(2,1)S(1)}, u32[]{:S(2)}, u32[]{:S(2)}) collective-permute-start(bf16[2,48,896]{2,1,0:T(8,128)(2,1)S(1)} %reduce_sum.128), channel_id=1, source_target_pairs={{0,16},{1,17},{2,18},{3,19},{4,20},{5,21},{6,22},{7,23},{8,24},{9,... | collective-permute-start | bytes 516104 | tf_op jit(solution)/shard_map/ppermute | solution.py:245
  843.8 9.1 %all-to-all-start.13 = ((bf16[8,8,144]{2,1,0:T(8,128)(2,1)}), bf16[8,8,144]{2,1,0:T(8,128)(2,1)S(1)}, u32[]{:S(2)}, u32[]{:S(2)}) async-start(bf16[8,8,144]{2,1,0:T(8,128)(2,1)} %bitcast.203), calls=%async_computation.13 | async-start | bytes 65536 | tf_op jit(solution)/shard_map/all_to_all | solution.py:1068
  853.7 10.0 %collective-permute-start.53 = (bf16[144,896]{1,0:T(8,128)(2,1)S(1)}, bf16[144,896]{1,0:T(8,128)(2,1)S(1)}, u32[]{:S(2)}, u32[]{:S(2)}) collective-permute-start(bf16[144,896]{1,0:T(8,128)(2,1)S(1)} %pad_maximum_fusion.27), channel_id=1, source_target_pairs={{0,8},{1,9},{2,10},{3,11},{4,12},{5,13},{6,14},{7,15},{8,0},{9,1},... | collective-permute-start | bytes 774152 | tf_op jit(solution)/shard_map/ppermute | solution.py:255
  (76 other events, 579.3 us)

commit v4 on v3

--- a/solution.py
+++ b/solution.py
@@ -64,6 +64,10 @@
 TO_CORE = [(device_index(x, c, z, y), device_index(x, 1 - c, z, y)) for x, c, z, y in PLACES]
 TO_X = [(device_index(x, c, z, y), device_index(1 - x, c, z, y)) for x, c, z, y in PLACES]
 TO_Y = [(device_index(x, c, z, y), device_index(x, c, z, 1 - y)) for x, c, z, y in PLACES]
+TO_Z = [
+    [(device_index(x, c, z, y), device_index(x, c, (z + k) % 4, y)) for x, c, z, y in PLACES]
+    for k in range(4)
+]
 Z_GROUPS = [[0, 2, 4, 6], [1, 3, 5, 7]]
 
 
@@ -94,8 +98,8 @@
     return values
 
 
-def place_kernel(rows, half, where, a0, a1, ax, b0, b1, bx, out, sems):
-    x, core, y = where[0], where[1], where[2]
+def place_kernel(rows, half, apart, where, a0, a1, ax, b0, b1, bx, out, sems):
+    x, core, z, y = where[0], where[1], where[2], where[3]
     h = rows // PARTS
     copies = []
     for p0, p1, px, c in ((a0, a1, ax, core), (b0, b1, bx, 1 - core)):
@@ -108,7 +112,8 @@
                 (px.at[q, 0], y, 1 - x),
                 (px.at[q, 1], 1 - y, 1 - x),
             ):
-                row = pl.multiple_of((2 * q + yy) * rows + third * h, 16)
+                zz = (z + HIGH_Z - q) % HIGH_Z if apart else q
+                row = pl.multiple_of((2 * zz + yy) * rows + third * h, 16)
                 column = pl.multiple_of(c * half, LANES)
                 target = out.at[pl.ds(row, h), pl.ds(column, half)]
                 copy = pltpu.make_async_copy(source, target, sems.at[len(copies)])
@@ -124,31 +129,29 @@
         self.live = {"weight": weight}
         self.fast = is_fast() and self.rows % 48 == 0
 
-    def z(self):
+    def z(self, apart=False):
         if not self.fast:
             return
+        self.apart = apart
         x, core, _, _ = coordinates()
         h, half = self.rows // PARTS, self.width // 2
         weight = self.live.pop("weight")
         mine = lax.dynamic_slice_in_dim(weight, core * half, half, 1).reshape(PARTS, h, half)
         base = jnp.stack([pick(mine, x, 0), mine[2]], 0)
+        if apart:
+            lines = [base] + [lax.ppermute(base, AXES, TO_Z[k]) for k in (1, 2, 3)]
+            self.live["own"] = jnp.stack(lines, 0)
+            return
         self.live["own"] = over_z(jnp.broadcast_to(base, (HIGH_Z, 2, h, half)))
 
     def y(self):
         if self.fast:
             self.live["far"] = lax.ppermute(self.live["own"], AXES, TO_Y)
 
-    def x(self, early=False, late=False):
-        if not self.fast:
-            return
-        own = None if late else self.live["own"][:, 0]
-        far = None if early else self.live["far"][:, 0]
-        if early:
-            self.live["side"] = lax.ppermute(own, AXES, TO_X)
-        elif late:
-            self.live["side_far"] = lax.ppermute(far, AXES, TO_X)
-        else:
-            self.live["both"] = lax.ppermute(jnp.stack([own, far], 1), AXES, TO_X)
+    def x(self):
+        if self.fast:
+            ends = jnp.stack([self.live["own"][:, 0], self.live["far"][:, 0]], 1)
+            self.live["both"] = lax.ppermute(ends, AXES, TO_X)
 
     def core(self, *names):
         if self.fast:
@@ -158,16 +161,12 @@
     def whole(self):
         if not self.fast:
             return lax.all_gather(self.live["weight"], "fsdp", axis=0, tiled=True)
-        x, core, _, y = coordinates()
         live = self.live
-        if "both" not in live:
-            live["both"] = jnp.stack([live["side"], live["side_far"]], 1)
-            live["twin_both"] = jnp.stack([live["twin_side"], live["twin_side_far"]], 1)
-        where = jnp.stack([x, core, y]).astype(jnp.int32)
+        where = jnp.stack(coordinates()).astype(jnp.int32)
         any_space = pl.BlockSpec(memory_space=pl.ANY)
         shape = (8 * self.rows, self.width)
         return pl.pallas_call(
-            partial(place_kernel, self.rows, self.width // 2),
+            partial(place_kernel, self.rows, self.width // 2, self.apart),
             out_shape=jax.ShapeDtypeStruct(shape, LOW),
             in_specs=[pl.BlockSpec(memory_space=pltpu.SMEM)] + [any_space] * 6,
             out_specs=pl.BlockSpec(memory_space=pltpu.VMEM),
@@ -233,15 +232,26 @@
             _, _, _, y = coordinates()
             self.live["far"] = lax.ppermute(self.row(1 - y), AXES, TO_Y)
 
-    def z(self):
+    def z(self, apart=False):
         if self.fast:
             _, _, _, y = coordinates()
-            line = self.row(y).astype(WIDE) + self.live["far"].astype(WIDE)
-            self.live = {"line": over_z(line.astype(LOW))}
+            line = (self.row(y).astype(WIDE) + self.live["far"].astype(WIDE)).astype(LOW)
+            if apart:
+                _, _, z, _ = coordinates()
+                live = {"0": pick(line, z, 0)}
+                for k in (2, 1, 3):
+                    live[str(k)] = lax.ppermute(pick(line, (z + k) % 4, 0), AXES, TO_Z[k])
+                self.live = {"lines": live}
+            else:
+                self.live = {"line": over_z(line)}
 
     def last_x(self):
         if self.fast:
-            part = jnp.sum(self.live["line"].astype(WIDE), axis=0).astype(LOW)
+            if "lines" in self.live:
+                lines = [self.live["lines"][k].astype(WIDE) for k in ("0", "1", "2", "3")]
+                part = (lines[0] + lines[1] + lines[2] + lines[3]).astype(LOW)
+            else:
+                part = jnp.sum(self.live["line"].astype(WIDE), axis=0).astype(LOW)
             self.live = {"part": part, "other": lax.ppermute(part, AXES, TO_X)}
 
     def last_core(self):
@@ -274,11 +284,6 @@
         return sums[0], sums[1]
 
 
-def mine_and_other(first, second):
-    _, core, _, _ = coordinates()
-    return jnp.where(core == 0, second, first), jnp.where(core == 0, first, second)
-
-
 def column_halves(array):
     _, core, _, _ = coordinates()
     half = array.shape[1] // 2
@@ -287,16 +292,19 @@
     return send, keep
 
 
-def across_replicas(rows):
+def across_x(rows):
+    return lax.ppermute(rows, AXES, TO_X) if is_fast() else rows
+
+
+def across_replicas(rows, far):
     if not is_fast():
         return lax.all_gather(rows, "rep", axis=0, tiled=True)
     x, core, _, _ = coordinates()
     count, width = rows.shape
-    twin = lax.ppermute(rows, AXES, TO_CORE)
-    chip = jnp.stack([jnp.where(core == 0, rows, twin), jnp.where(core == 0, twin, rows)], 0)
-    far = lax.ppermute(chip, AXES, TO_X)
-    every = jnp.stack([jnp.where(x == 0, chip, far), jnp.where(x == 0, far, chip)], 0)
-    return every.reshape(4 * count, width)
+    line = jnp.stack([jnp.where(x == 0, rows, far), jnp.where(x == 0, far, rows)], 0)
+    twin = lax.ppermute(line, AXES, TO_CORE)
+    every = [jnp.where(core == 0, line, twin), jnp.where(core == 0, twin, line)]
+    return jnp.stack(every, 1).reshape(4 * count, width)
 
 
 def gather_rows(rows):
@@ -331,20 +339,21 @@
 
 
 def prepare_kernel(
-    heads, hd, x_ref, hot_ref, mod_ref, w_ref, gq_ref, gk_ref, rot_ref, qt_ref, kt_ref, vt_ref,
-    normed_ref, q_ref, k_ref, v_ref, rq_ref, rk_ref, wide_ref,
+    first, heads, hd, x_ref, hot_ref, mod_ref, w_ref, gq_ref, gk_ref, rot_ref, qt_ref, kt_ref,
+    vt_ref, *refs
 ):
-    width = heads * hd
+    normed_ref, q_ref, k_ref, v_ref, rq_ref, rk_ref, wide_ref = refs if first else (x_ref, *refs)
     step = part_width(hd)
-    x = x_ref[...].astype(WIDE)
-    hot = hot_ref[...]
-    shift = dot(hot, mod_ref[:, :width])
-    scale = dot(hot, mod_ref[:, width:])
-    mean = jnp.mean(x, axis=-1, keepdims=True)
-    centred = x - mean
-    var = jnp.mean(centred * centred, axis=-1, keepdims=True)
-    normed = (centred * lax.rsqrt(var + EPSILON) * (1.0 + scale) + shift).astype(LOW)
-    normed_ref[...] = normed
+    if first:
+        width = x_ref.shape[1]
+        hot = hot_ref[...]
+        shift = dot(hot, mod_ref[:, :width])
+        scale = dot(hot, mod_ref[:, width:])
+        normed, _ = normed_rows(x_ref[...].astype(WIDE))
+        normed = (normed * (1.0 + scale) + shift).astype(LOW)
+        normed_ref[...] = normed
+    else:
+        normed = x_ref[...]
     cosine, plus, minus = rot_ref[0], rot_ref[1], rot_ref[2]
     lane = lax.broadcasted_iota(jnp.int32, (BLOCK, LANES), 1)
     inside = lane < hd
@@ -374,14 +383,14 @@
                 o_ref[h] = raw.astype(LOW) + tail
 
 
-def prepare(x, hot, mod, w, gq, gk, rot, qt, kt, vt, heads, hd):
-    n = x.shape[0]
-    width = heads * hd
+def prepare(first, x, hot, mod, w, gq, gk, rot, qt, kt, vt, heads, hd):
+    n, width = x.shape
     rows = pl.BlockSpec((BLOCK, width), lambda i: (i, 0))
     head_spec = pl.BlockSpec((heads, BLOCK, LANES), lambda i: (0, i, 0))
     tail = pl.BlockSpec((BLOCK, LANES), lambda i: (i, 0))
+    normed_spec, normed_shape = [rows], [jax.ShapeDtypeStruct((n, width), LOW)]
     return pl.pallas_call(
-        partial(prepare_kernel, heads, hd),
+        partial(prepare_kernel, first, heads, hd),
         grid=(n // BLOCK,),
         in_specs=[
             rows,
@@ -395,13 +404,13 @@
             tail,
             pl.BlockSpec((1, LANES), lambda i: (0, 0)),
         ],
-        out_specs=[rows] + [head_spec] * 5,
-        out_shape=[jax.ShapeDtypeStruct((n, width), LOW)]
+        out_specs=(normed_spec if first else []) + [head_spec] * 5,
+        out_shape=(normed_shape if first else [])
         + [jax.ShapeDtypeStruct((heads, n, LANES), LOW)] * 5,
         scratch_shapes=[pltpu.VMEM((BLOCK, part_width(hd) + LANES), WIDE)],
         compiler_params=pltpu.CompilerParams(vmem_limit_bytes=56 * MIB),
         cost_estimate=pl.CostEstimate(
-            flops=2 * n * width * w.shape[1], bytes_accessed=40 * MIB, transcendentals=0
+            flops=2 * n * width * w.shape[1], bytes_accessed=20 * MIB, transcendentals=0
         ),
         name="prepare",
     )(x, hot, mod, w, gq, gk, rot, qt, kt, vt)
@@ -424,13 +433,16 @@
         run((-1, 0, 1))
 
 
-def attend_kernel(hd, c, q_ref, k_ref, v_ref, mix_ref, q2_ref):
+def attend_kernel(hd, c, *refs):
     i = pl.program_id(0)
-    heads = q_ref.shape[0]
+    mix_ref = refs[6]
     lane = lax.broadcasted_iota(jnp.int32, (BLOCK, LANES), 1)
+    heads = refs[0].shape[0]
 
     def run(blocks):
-        for h in range(heads):
+        for head in range(2 * heads):
+            half, h = head // heads, head % heads
+            q_ref, k_ref, v_ref = refs[3 * half : 3 * half + 3]
             q = q_ref[h]
             total = None
             for j in blocks:
@@ -440,46 +452,46 @@
                 total = term if total is None else total + term
             norm = total[:, hd : hd + 1]
             out = (total * (1.0 / norm)).astype(LOW)
-            mix_ref[:, hd * h : hd * (h + 1)] = out[:, :hd]
+            mix_ref[:, hd * head : hd * (head + 1)] = out[:, :hd]
             rest = jnp.log2(norm) * (1.0 / c)
             first = rest.astype(LOW).astype(WIDE)
             rest = rest - first
             second = rest.astype(LOW).astype(WIDE)
             third = rest - second
             logs = jnp.where(lane == hd + 8, first, jnp.where(lane == hd + 9, second, third))
-            q2_ref[h] = jnp.where((lane >= hd + 8) & (lane < hd + 11), logs.astype(LOW), q)
+            marked = jnp.where((lane >= hd + 8) & (lane < hd + 11), logs.astype(LOW), q)
+            refs[7 + half][h] = marked
 
     near_blocks(run)
 
 
-def attend(q, k, v, hd, c):
-    heads, n, _ = q.shape
+def attend(one, two, hd, c):
+    heads, n, _ = one[0].shape
     full = pl.BlockSpec((heads, n, LANES), lambda i: (0, 0, 0), pipeline_mode=pl.Buffered(1))
     block = pl.BlockSpec((heads, BLOCK, LANES), lambda i: (0, i, 0))
+    width = 2 * heads * hd
     return pl.pallas_call(
         partial(attend_kernel, hd, c),
         grid=(n // BLOCK,),
-        in_specs=[block, full, full],
-        out_specs=[pl.BlockSpec((BLOCK, heads * hd), lambda i: (i, 0)), block],
-        out_shape=[
-            jax.ShapeDtypeStruct((n, heads * hd), LOW),
-            jax.ShapeDtypeStruct((heads, n, LANES), LOW),
-        ],
+        in_specs=[block, full, full] * 2,
+        out_specs=[pl.BlockSpec((BLOCK, width), lambda i: (i, 0)), block, block],
+        out_shape=[jax.ShapeDtypeStruct((n, width), LOW)]
+        + [jax.ShapeDtypeStruct((heads, n, LANES), LOW)] * 2,
         compiler_params=pltpu.CompilerParams(vmem_limit_bytes=56 * MIB),
         cost_estimate=pl.CostEstimate(
-            flops=4 * n * 640 * LANES * heads,
+            flops=8 * n * 640 * LANES * heads,
             bytes_accessed=20 * MIB,
-            transcendentals=heads * n * 640,
+            transcendentals=2 * heads * n * 640,
         ),
         name="attend",
-    )(q, k, v)
-
-
-def spread_kernel(heads, hd, ga_ref, w_ref, mix_ref, out_ref, grad_scr, mix_scr):
+    )(*one, *two)
+
+
+def spread_kernel(heads, hd, proj_at, ga_ref, w_ref, mix_ref, out_ref, grad_scr, mix_scr):
     width = heads * hd
     grad_scr[:, width:] = jnp.zeros((BLOCK, LANES), WIDE)
     mix_scr[:, width:] = jnp.zeros((BLOCK, LANES), WIDE)
-    grad_scr[:, :width] = dot_right(ga_ref[:, :width], w_ref[:, :width]).astype(LOW).astype(WIDE)
+    grad_scr[:, :width] = dot_right(ga_ref[:, :width], w_ref[:, proj_at : proj_at + width]).astype(LOW).astype(WIDE)
     mix_scr[:, :width] = mix_ref[...].astype(WIDE)
     lane = lax.broadcasted_iota(jnp.int32, (BLOCK, LANES), 1)
     ones = jnp.full((LANES, LANES), 1.0, LOW)
@@ -497,13 +509,13 @@
         )
 
 
-def spread(ga, w, mix, heads, hd):
+def spread(ga, w, mix, heads, hd, proj_at):
     n = ga.shape[0]
     width = heads * hd
     row = pl.BlockSpec((BLOCK, width), lambda i: (i, 0))
     wide_row = pl.BlockSpec((BLOCK, ga.shape[1]), lambda i: (i, 0))
     return pl.pallas_call(
-        partial(spread_kernel, heads, hd),
+        partial(spread_kernel, heads, hd, proj_at),
         grid=(n // BLOCK,),
         in_specs=[wide_row, whole_block(w), row],
         out_specs=pl.BlockSpec((heads, BLOCK, LANES), lambda i: (0, i, 0)),
@@ -521,15 +533,16 @@
 
 
 def back_kernel(
-    hd, c, score_scale, q_ref, k_ref, v_ref, do_ref, rq_ref, rk_ref, rot_ref, gq_ref, gk_ref,
-    joint_0, joint_1, gain_ref, dq_scr, dk_scr, dv_scr, gain_scr,
+    hd, c, score_scale, core_ref, q_ref, k_ref, v_ref, do_ref, rq_ref, rk_ref, rot_ref, gq_ref, gk_ref,
+    joint_ref, gain_ref, dq_scr, dk_scr, dv_scr, gain_scr,
 ):
     i = pl.program_id(0)
     n = pl.num_programs(0)
     heads = q_ref.shape[0]
     width = GROUP * hd
-    tail = joint_0.shape[1] - 3 * width
-    joints = (joint_0, joint_1)
+    tail = joint_ref.shape[2] - 3 * width
+    core = core_ref[0]
+    slots = (1 - core, core)
 
     @pl.when(i == 0)
     def _():
@@ -577,14 +590,14 @@
 
     here = pl.ds(pl.multiple_of(i * BLOCK, BLOCK), BLOCK)
     rot = [rot_ref[t, here] for t in range(3)]
-    for joint_ref in joints:
-        joint_ref[here, 3 * width :] = jnp.zeros((BLOCK, tail), LOW)
+    for slot in range(2):
+        joint_ref[slot, here, 3 * width :] = jnp.zeros((BLOCK, tail), LOW)
     for h in range(heads):
-        joint_ref, at = joints[h // GROUP], hd * (h % GROUP)
+        slot, at = slots[h // GROUP], hd * (h % GROUP)
         grad = finish(dk_scr[h], rk_ref[h], rot, gk_ref[...], 1)
-        joint_ref[here, width + at : width + at + hd] = grad[:, :hd]
+        joint_ref[slot, here, width + at : width + at + hd] = grad[:, :hd]
         value = dv_scr[h].astype(LOW)
-        joint_ref[here, 2 * width + at : 2 * width + at + hd] = value[:, :hd]
+        joint_ref[slot, here, 2 * width + at : 2 * width + at + hd] = value[:, :hd]
 
     @pl.when(i == n - 1)
     def _():
@@ -594,32 +607,35 @@
             for h in range(heads):
                 start = hd * (h % GROUP)
                 grad = finish(dq_scr[h, at], rq_ref[h, at], turn, gq_ref[...], 0)
-                joints[h // GROUP][at, start : start + hd] = grad[:, :hd]
+                joint_ref[slots[h // GROUP], at, start : start + hd] = grad[:, :hd]
             return carry
 
         lax.fori_loop(0, n, rows, 0)
         gain_ref[...] = gain_scr[...]
 
 
-def attend_back(part, q2, k, v, do, rq, rk, rot, gq, gk, hd, c, score_scale):
+def attend_back(part, core, q2, k, v, do, rq, rk, rot, gq, gk, hd, c, score_scale):
     _, n, _ = q2.shape
     one = pl.Buffered(1)
-    full = pl.BlockSpec((2 * GROUP, n, LANES), lambda i: (part, 0, 0), pipeline_mode=one)
-    block = pl.BlockSpec((2 * GROUP, BLOCK, LANES), lambda i: (part, i, 0))
+    full = pl.BlockSpec((2 * GROUP, n, LANES), lambda i: (0, 0, 0), pipeline_mode=one)
+    block = pl.BlockSpec((2 * GROUP, BLOCK, LANES), lambda i: (0, i, 0))
     small = pl.BlockSpec((1, LANES), lambda i: (0, 0))
     width = part_width(hd)
     return pl.pallas_call(
         partial(back_kernel, hd, c, score_scale),
         grid=(n // BLOCK,),
-        in_specs=[full, block, block, full, full, block, whole_block(rot), small, small],
+        in_specs=[
+            pl.BlockSpec(memory_space=pltpu.SMEM),
+            *(full, block, block),
+            pl.BlockSpec((2 * GROUP, n, LANES), lambda i: (part, 0, 0), pipeline_mode=one),
+            *(full, block, whole_block(rot), small, small),
+        ],
         out_specs=[
-            pl.BlockSpec((n, width), lambda i: (0, 0), pipeline_mode=one),
-            pl.BlockSpec((n, width), lambda i: (0, 0), pipeline_mode=one),
+            pl.BlockSpec((2, n, width), lambda i: (0, 0, 0), pipeline_mode=one),
             pl.BlockSpec((2, 8, LANES), lambda i: (0, 0, 0)),
         ],
         out_shape=[
-            jax.ShapeDtypeStruct((n, width), LOW),
-            jax.ShapeDtypeStruct((n, width), LOW),
+            jax.ShapeDtypeStruct((2, n, width), LOW),
             jax.ShapeDtypeStruct((2, 8, LANES), WIDE),
         ],
         scratch_shapes=[
@@ -635,7 +651,7 @@
             transcendentals=2 * GROUP * n * 640,
         ),
         name="attend_back",
-    )(q2, k, v, do, rq, rk, rot, gq, gk)
+    )(core, q2, k, v, do, rq, rk, rot, gq, gk)
 
 
 def normed_rows(values):
@@ -664,32 +680,39 @@
 
 
 def rows_of(array):
+    if array.ndim == 3:
+        return pl.BlockSpec((2, BLOCK, array.shape[2]), lambda i: (0, i, 0))
     return pl.BlockSpec((BLOCK, array.shape[1]), lambda i: (i, 0))
 
 
-def call_rows(kernel, name, streamed, fixed, outs, sums=()):
-    n = streamed[0].shape[0]
-    width_of = lambda a: a.shape[1] * a.dtype.itemsize
-    work = sum(2 * n * a.shape[0] * a.shape[1] for a in fixed if a.shape[0] > 256)
-    moved = sum(n * width_of(a) for a in streamed) + sum(a.shape[0] * width_of(a) for a in fixed)
+def call_rows(kernel, name, streamed, fixed, outs, sums=(), core=None, scratch=()):
+    n = streamed[0].shape[-2]
+    work = sum(2 * n * a.size for a in fixed if a.shape[0] > 256)
+    moved = sum(a.size * a.dtype.itemsize for a in (*streamed, *fixed))
+    scalars = () if core is None else (core,)
     return pl.pallas_call(
         kernel,
         grid=(n // BLOCK,),
-        in_specs=[rows_of(a) for a in streamed] + [whole_block(a) for a in fixed],
+        in_specs=[pl.BlockSpec(memory_space=pltpu.SMEM) for _ in scalars]
+        + [rows_of(a) for a in streamed]
+        + [whole_block(a) for a in fixed],
         out_specs=[pl.BlockSpec((BLOCK, w), lambda i: (i, 0)) for w, _ in outs]
         + [pl.BlockSpec(shape, lambda i: (0, 0)) for shape in sums],
         out_shape=[jax.ShapeDtypeStruct((n, w), t) for w, t in outs]
         + [jax.ShapeDtypeStruct(shape, WIDE) for shape in sums],
+        scratch_shapes=[pltpu.VMEM(shape, WIDE) for shape in scratch],
         compiler_params=pltpu.CompilerParams(vmem_limit_bytes=56 * MIB),
         cost_estimate=pl.CostEstimate(flops=work, bytes_accessed=moved, transcendentals=0),
         name=name,
-    )(*streamed, *fixed)
-
-
-def join_kernel(mix_ref, x_ref, hot_ref, keep_ref, w_ref, mod_ref, att_ref, mid_ref, norm_ref):
+    )(*scalars, *streamed, *fixed)
+
+
+def join_kernel(
+    proj_at, mix_ref, x_ref, hot_ref, keep_ref, w_ref, mod_ref, att_ref, mid_ref, norm_ref
+):
     width = x_ref.shape[1]
     hot = hot_ref[...]
-    attended = dot(mix_ref[...], w_ref[:, :width])
+    attended = dot(mix_ref[...], w_ref[:, proj_at : proj_at + width])
     att_ref[...] = attended.astype(LOW)
     gate = dot(hot, mod_ref[:, :width]) * keep_ref[...]
     middle = x_ref[...].astype(WIDE) + gate * attended
@@ -726,23 +749,44 @@
     add_sums(sum_ref, 0, hot, upstream * keep_ref[...] * returned)
 
 
-def inner_back_kernel(grad_ref, gate_ref, up_ref, w_ref, gg_ref, gu_ref):
+def inner_back_kernel(core_ref, grad_ref, gate_ref, up_ref, w_ref, send_ref, keep_ref):
     grad = dot_right(grad_ref[...], w_ref[...])
     gate = gate_ref[...].astype(WIDE)
     sig = jax.nn.sigmoid(gate)
     act = gate * sig
-    gg_ref[...] = (grad * up_ref[...].astype(WIDE) * (sig + act * (1.0 - sig))).astype(LOW)
-    gu_ref[...] = (grad * act).astype(LOW)
+    for_gate = (grad * up_ref[...].astype(WIDE) * (sig + act * (1.0 - sig))).astype(LOW)
+    for_up = (grad * act).astype(LOW)
+
+    @pl.when(core_ref[0] == 0)
+    def _():
+        send_ref[...] = for_up
+        keep_ref[...] = for_gate
+
+    @pl.when(core_ref[0] != 0)
+    def _():
+        send_ref[...] = for_gate
+        keep_ref[...] = for_up
 
 
 def middle_back_kernel(
-    gg_ref, gu_ref, mid_ref, grad_ref, att_ref, hot_ref, keep_ref, wg_ref, wu_ref, mod_ref,
-    out_ref, back_ref, sum_ref,
+    core_ref, send_ref, mine_ref, mid_ref, grad_ref, att_ref, hot_ref, keep_ref, wg_ref, wu_ref,
+    mod_ref, out_ref, back_ref, sum_ref, total_ref,
 ):
     width = mid_ref.shape[1]
     hot = hot_ref[...]
     keep = keep_ref[...]
-    grad = dot_right(gg_ref[...], wg_ref[...]) + dot_right(gu_ref[...], wu_ref[...])
+
+    @pl.when(core_ref[0] == 0)
+    def _():
+        total_ref[...] = dot_right(mine_ref[...], wg_ref[...])
+        total_ref[...] += dot_right(send_ref[...], wu_ref[...])
+
+    @pl.when(core_ref[0] != 0)
+    def _():
+        total_ref[...] = dot_right(send_ref[...], wg_ref[...])
+        total_ref[...] += dot_right(mine_ref[...], wu_ref[...])
+
+    grad = total_ref[...]
     normed, scale = normed_rows(mid_ref[...])
     turned = grad * (1.0 + dot(hot, mod_ref[:, 2 * width : 3 * width]))
     total = grad_ref[...].astype(WIDE) + norm_back(normed, scale, turned)
@@ -756,19 +800,63 @@
     add_sums(sum_ref, 2, hot, grad * normed)
 
 
-def input_back_kernel(j0, j1, j2, j3, mid_ref, x_ref, hot_ref, w_ref, mod_ref, out_ref, sum_ref):
+def input_back_kernel(
+    core_ref, one_ref, two_ref, mid_ref, x_ref, hot_ref, wo_ref, wt_ref, mod_ref, out_ref, sum_ref
+):
     width = x_ref.shape[1]
     hot = hot_ref[...]
-    step = j0.shape[1]
+    step = one_ref.shape[2]
+    core = core_ref[0]
     grad = None
-    for part, ref in enumerate((j0, j1, j2, j3)):
-        term = dot_right(ref[...], w_ref[:, part * step : (part + 1) * step])
+    for ref, w_ref in ((one_ref, wo_ref), (two_ref, wt_ref)):
+        term = dot_right(ref[1 - core], w_ref[:, :step]) + dot_right(ref[core], w_ref[:, step : 2 * step])
         grad = term if grad is None else grad + term
     normed, scale = normed_rows(x_ref[...].astype(WIDE))
     turned = grad * (1.0 + dot(hot, mod_ref[:, width : 2 * width]))
     out_ref[...] = mid_ref[...] + norm_back(normed, scale, turned)
     add_sums(sum_ref, 0, hot, grad)
     add_sums(sum_ref, 1, hot, grad * normed)
+
+
+def finish_kernel(hd, core_ref, head_done, head_twin, tail_done, tail_twin, qkv_ref, proj_ref):
+    step = part_width(hd)
+    short = GROUP * hd
+    total = qkv_ref.shape[1] // 3
+
+    def write(sources):
+        for part, source in enumerate(sources):
+            values = source[:, :step].astype(WIDE)
+            for kind in range(3):
+                at = kind * total + part * short
+                qkv_ref[:, at : at + short] = values[:, kind * short : (kind + 1) * short]
+        half = sources[0].shape[1] - step
+        proj_ref[:, :half] = sources[0][:, step:].astype(WIDE)
+        rest = proj_ref.shape[1] - half
+        proj_ref[:, half:] = sources[1][:, step : step + rest].astype(WIDE)
+
+    @pl.when(core_ref[0] == 0)
+    def _():
+        write((head_done, head_twin, tail_done, tail_twin))
+
+    @pl.when(core_ref[0] != 0)
+    def _():
+        write((head_twin, head_done, tail_twin, tail_done))
+
+
+def finish(core, head, tail, hd, width):
+    rows = head["done"].shape[0]
+    return pl.pallas_call(
+        partial(finish_kernel, hd),
+        in_specs=[pl.BlockSpec(memory_space=pltpu.SMEM)]
+        + [pl.BlockSpec(memory_space=pltpu.VMEM)] * 4,
+        out_specs=[pl.BlockSpec(memory_space=pltpu.VMEM)] * 2,
+        out_shape=[
+            jax.ShapeDtypeStruct((rows, 3 * width), WIDE),
+            jax.ShapeDtypeStruct((rows, width), WIDE),
+        ],
+        compiler_params=pltpu.CompilerParams(vmem_limit_bytes=40 * MIB),
+        name="finish",
+    )(core, head["done"], head["twin"], tail["done"], tail["twin"])
 
 
 def turn_tables(row_place, column_place, hd):
@@ -840,18 +928,21 @@
     fsdp_place = lax.axis_index("fsdp")
     odd = width + LANES if (width // LANES) % 2 else width
 
-    g_qkv = Gather(to_parts(qkv_weight, heads, hd))
-    g_proj = Gather(pad_columns(proj_weight, odd))
+    qkv_parts = to_parts(qkv_weight, heads, hd)
+    cut = qkv_parts.shape[1] // 2
+    g_one = Gather(qkv_parts[:, :cut])
+    g_two = Gather(jnp.concatenate([qkv_parts[:, cut:], pad_columns(proj_weight, odd)], axis=1))
     g_gate = Gather(gate_up_weight[:, :ff])
     g_up = Gather(gate_up_weight[:, ff:])
     g_down = Gather(pad_columns(down_weight, odd))
-    gathers = [g_qkv, g_proj, g_gate, g_up, g_down]
+    gathers = [g_one, g_two, g_gate, g_up, g_down]
+    core_place = (lax.axis_index("rep") % 2).astype(jnp.int32).reshape(1)
 
     cond_float = condition.astype(WIDE).reshape(items, width)
     cond_silu, silu_pull = jax.vjp(jax.nn.silu, cond_float)
     cond_act = cond_silu.astype(LOW)
 
-    g_qkv.z()
+    g_one.z()
     group_act = exchange(cond_act)
     member, segment, row_place, column_place = layout(item_lengths[0], item_widths[0], n)
     member_low = member.astype(LOW)
@@ -867,12 +958,10 @@
     gain_k = pad_columns(key_gain.astype(WIDE)[None, :], LANES)
     hot = jnp.concatenate([member_low, member_low], axis=1)
     tables = (rot, query_tail, key_tail, hot, keep)
-    tables, group_act = hold(gathers, (tables, group_act))
-
-    g_qkv.y()
-    g_qkv.x(early=True)
-    g_qkv.core("own")
-    g_gate.z()
+    group_act = hold(gathers, group_act)
+
+    g_one.y()
+    g_two.z()
     bias_row = lax.dynamic_update_slice(
         jnp.zeros((6 * width,), WIDE), ada_bias.astype(WIDE), (fsdp_place * ada_bias.shape[0],)
     )
@@ -881,52 +970,57 @@
 
     early = 2 * width
     modulation = high_and_rest(sum_back(mod_part, items))
-    g_qkv.x(late=True)
-    g_qkv.core("far", "side")
-    g_proj.z()
+    g_one.x()
+    g_one.core("own", "far")
+    g_two.y()
     inputs_low = block_in[0]
     modulation, tables, inputs_low = hold(gathers, (modulation, tables, inputs_low))
     mod_a, mod_b = modulation[:, :early], modulation[:, early:]
 
-    g_qkv.core("side_far")
-    g_proj.y()
+    g_one.core("both")
+    g_two.x()
+    g_two.core("own", "far")
+    g_gate.z()
+    rot, query_tail, key_tail, hot, keep = tables
+    set_out = (gain_q, gain_k, rot, query_tail, key_tail, value_tail, heads // 2, hd)
+    one_full = g_one.whole()
+    normed_a, q_one, k_one, v_one, rq_one, rk_one = prepare(
+        True, inputs_low, hot, mod_a, one_full, *set_out
+    )
+    gathers = gathers[1:]
+    normed_a, q_one, k_one, v_one, rq_one, rk_one, one_full = hold(
+        gathers, (normed_a, q_one, k_one, v_one, rq_one, rk_one, one_full)
+    )
+
+    g_two.core("both")
     g_gate.y()
     g_up.z()
-    rot, query_tail, key_tail, hot, keep = tables
-    qkv_full = g_qkv.whole()
-    normed_a, q, k, v, raw_q, raw_k = prepare(
-        inputs_low, hot, mod_a, qkv_full, gain_q, gain_k, rot,
-        query_tail, key_tail, value_tail, heads, hd,
+    two_full = g_two.whole()
+    q_two, k_two, v_two, rq_two, rk_two = prepare(
+        False, normed_a, hot, mod_a, two_full, *set_out
     )
     gathers = gathers[1:]
-    normed_a, q, k, v, raw_q, raw_k, qkv_full, mod_b = hold(
-        gathers, (normed_a, q, k, v, raw_q, raw_k, qkv_full, mod_b)
-    )
-
-    g_proj.x()
-    g_proj.core("own", "far")
+    normed_a, q_two, k_two, v_two, rq_two, rk_two, two_full, q_one, k_one, v_one = hold(
+        gathers, (normed_a, q_two, k_two, v_two, rq_two, rk_two, two_full, q_one, k_one, v_one)
+    )
+
     g_gate.x()
     g_gate.core("own", "far")
     g_up.y()
     g_down.z()
-    mixed, q2 = attend(q, k, v, hd, c)
-    mixed, q2 = hold(gathers, (mixed, q2))
-
-    g_proj.core("both")
+    mixed, q2_one, q2_two = attend((q_one, k_one, v_one), (q_two, k_two, v_two), hd, c)
+    mixed, q2_one, q2_two = hold(gathers, (mixed, q2_one, q2_two))
+
     g_gate.core("both")
     g_up.x()
     g_up.core("own", "far")
     g_down.y()
-    proj_full = g_proj.whole()
     mod_mid = mod_b[:, : 3 * width]
     attended, middle, normed_b = call_rows(
-        join_kernel, "join", (mixed, inputs_low, hot, keep), (proj_full, mod_mid),
+        partial(join_kernel, cut), "join", (mixed, inputs_low, hot, keep), (two_full, mod_mid),
         ((width, LOW), (width, WIDE), (width, LOW)),
     )
-    gathers = gathers[1:]
-    middle, normed_b, attended, proj_full = hold(
-        gathers, (middle, normed_b, attended, proj_full)
-    )
+    middle, normed_b, attended = hold(gathers, (middle, normed_b, attended))
 
     g_up.core("both")
     g_down.x()
@@ -959,24 +1053,25 @@
     )
 
     s_down.core()
-    grad_gate, grad_up = call_rows(
+    grad_send, grad_keep = call_rows(
         inner_back_kernel, "inner_back", (grad_returned, gate, up), (down_full,),
-        ((ff, LOW), (ff, LOW)),
-    )
-    grad_gate, grad_up = hold(plans, (grad_gate, grad_up))
+        ((ff, LOW), (ff, LOW)), core=core_place,
+    )
+    grad_send, grad_keep = hold(plans, (grad_send, grad_keep))
 
     s_down.second()
-    s_wide = Scatter(normed_b, *mine_and_other(grad_gate, grad_up))
+    s_wide = Scatter(normed_b, grad_send, grad_keep)
     s_wide.first()
     plans = [s_down, s_wide]
-    grad_gate, grad_up = hold(plans, (grad_gate, grad_up))
+    grad_send, grad_keep = hold(plans, (grad_send, grad_keep))
 
     s_down.x()
     s_wide.core()
     grad_middle, grad_attended, sums_mid = call_rows(
         middle_back_kernel, "middle_back",
-        (grad_gate, grad_up, middle, out_grad[0], attended, hot, keep),
+        (grad_send, grad_keep, middle, out_grad[0], attended, hot, keep),
         (gate_full, up_full, mod_mid), ((width, WIDE), (odd, LOW)), ((2 * items, 3 * width),),
+        core=core_place, scratch=((BLOCK, width),),
     )
     s_proj = Scatter(mixed, *column_halves(grad_attended))
     plans = [s_down, s_wide, s_proj]
@@ -986,56 +1081,65 @@
     s_wide.second()
     s_proj.first()
     late_sums = jnp.concatenate([sums_mid[:items], sums_gate_b[:items]], axis=1).astype(LOW)
-    grad_mixed = spread(grad_attended, proj_full, mixed, heads, hd)
+    grad_mixed = spread(grad_attended, two_full, mixed, heads, hd, cut)
     late_sums, grad_mixed = hold(plans, (late_sums, grad_mixed))
 
     back = partial(
-        attend_back, q2=q2, k=k, v=v, rq=raw_q, rk=raw_k, rot=rot, gq=gain_q, gk=gain_k,
-        hd=hd, c=c, score_scale=score_scale,
+        attend_back, core=core_place, rot=rot, gq=gain_q, gk=gain_k, hd=hd, c=c,
+        score_scale=score_scale,
     )
     s_down.z()
     s_wide.x()
     s_proj.core()
-    joint_0, joint_1, gains_0 = back(0, do=grad_mixed)
-    s_head = Scatter(normed_a, *mine_and_other(joint_0, joint_1))
+    joint_one, gains_0 = back(
+        0, q2=q2_one, k=k_one, v=v_one, do=grad_mixed, rq=rq_one, rk=rk_one
+    )
+    s_head = Scatter(normed_a, joint_one[0], joint_one[1])
     s_head.first()
+    s_proj.second()
     plans = plans + [s_head]
-    joint_0, joint_1, gains_0, grad_mixed, late_sums = hold(
-        plans, (joint_0, joint_1, gains_0, grad_mixed, late_sums)
-    )
-
+    joint_one, gains_0, grad_mixed, late_sums = hold(
+        plans, (joint_one, gains_0, grad_mixed, late_sums)
+    )
+
+    s_head.core()
+    s_wide.y()
+    late_sums = hold([s_head], late_sums)
     s_down.last_x()
-    s_wide.y()
-    s_head.core()
+    s_head.second()
+    s_head.join(s_proj)
+    grad_mixed = hold([s_head], grad_mixed)
+    s_head.x()
     late_group = gather_rows(late_sums)
-    joint_2, joint_3, gains_1 = back(1, do=grad_mixed)
-    s_tail = Scatter(normed_a, *mine_and_other(joint_2, joint_3))
-    plans = plans + [s_tail]
-    joint_0, joint_1, joint_2, joint_3, gains_1, late_group = hold(
-        plans, (joint_0, joint_1, joint_2, joint_3, gains_1, late_group)
-    )
-
+    joint_two, gains_1 = back(
+        1, q2=q2_two, k=k_two, v=v_two, do=grad_mixed, rq=rq_two, rk=rk_two
+    )
+    s_tail = Scatter(normed_a, joint_two[0], joint_two[1])
+    s_tail.first()
+    plans = [s_down, s_wide, s_head, s_tail]
+    joint_one, joint_two, gains_1, late_group = hold(
+        plans, (joint_one, joint_two, gains_1, late_group)
+    )
+
+    s_tail.core()
     s_down.last_core()
     s_wide.z()
-    s_tail.first()
-    s_tail.core()
-    s_proj.second()
-    s_head.second()
-    s_head.join(s_proj)
-    s_head.x()
-    late_every = across_replicas(late_group)
+    s_head.y()
+    s_tail.second()
+    joint_two = hold([s_tail], joint_two)
+    s_tail.x()
     grad_input, sums_early = call_rows(
         input_back_kernel, "input_back",
-        (joint_0, joint_1, joint_2, joint_3, grad_middle, inputs_low, hot),
-        (qkv_full, mod_a), ((width, WIDE),), ((2 * items, 2 * width),),
-    )
-    s_tail.second()
+        (joint_one, joint_two, grad_middle, inputs_low, hot),
+        (one_full, two_full, mod_a), ((width, WIDE),), ((2 * items, 2 * width),),
+        core=core_place,
+    )
     plans = [s_down, s_wide, s_head, s_tail]
-    grad_input, sums_early, late_every = hold(plans, (grad_input, sums_early, late_every))
+    grad_input, sums_early, late_group = hold(plans, (grad_input, sums_early, late_group))
 
     s_wide.last_x()
-    s_head.y()
-    s_tail.x()
+    s_head.z(apart=True)
+    s_tail.y()
     early_sums = sums_early[:items]
     gain_row = jnp.sum(gains_0 + gains_1, axis=1)[:, :hd].reshape(1, 2 * hd)
     gain_high = gain_row.astype(LOW).astype(WIDE)
@@ -1043,29 +1147,35 @@
     gain_block = jnp.pad(gain_block, ((0, items - 2), (0, 2 * LANES - 2 * hd)))
     early_sums = jnp.concatenate([early_sums, gain_block], axis=1).astype(LOW)
     early_group = gather_rows(early_sums)
-    every_act = across_replicas(group_act)
-    early_group, late_every, every_act = hold(plans, (early_group, late_every, every_act))
+    act_far = across_x(group_act)
+    late_far = across_x(late_group)
+    shard_down = jnp.concatenate(s_down.halves(), axis=1)[:, :width]
+    plans = [s_wide, s_head, s_tail]
+    early_group, late_far, act_far, shard_down = hold(
+        plans, (early_group, late_far, act_far, shard_down)
+    )
 
     s_wide.last_core()
-    s_head.z()
-    s_tail.y()
-    early_every = across_replicas(early_group)
+    s_head.last_x()
+    s_tail.z(apart=True)
+    early_far = across_x(early_group)
+    every_act = across_replicas(group_act, act_far)
+    late_every = across_replicas(late_group, late_far)
     shard_late = dot_left(every_act, late_every)
     cond_part = dot_right(early_group[:, :early], ada_weight[:, :early]) + dot_right(
         late_group, ada_weight[:, early:]
     )
-    early_every, cond_part, shard_late, every_act = hold(
-        plans, (early_every, cond_part, shard_late, every_act)
-    )
-
-    s_head.last_x()
-    s_tail.z()
-    shard_early = dot_left(every_act, early_every[:, :early])
-    shard_early, cond_part = hold(plans, (shard_early, cond_part))
+    early_far, cond_part, shard_late, every_act, late_every = hold(
+        plans, (early_far, cond_part, shard_late, every_act, late_every)
+    )
 
     s_head.last_core()
     s_tail.last_x()
     cond_back = lax.all_to_all(cond_part.astype(LOW).reshape(shards, items, -1), "fsdp", 0, 0)
+    early_every = across_replicas(early_group, early_far)
+    shard_early = dot_left(every_act, early_every[:, :early])
+    shard_wide = jnp.concatenate(s_wide.halves(), axis=1)
+    shard_early, shard_wide = hold(plans, (shard_early, shard_wide))
     shard_ada = jnp.concatenate([shard_early, shard_late], axis=1)
     bias_sums = jnp.concatenate(
         [
@@ -1082,19 +1192,13 @@
     s_tail.last_core()
     grad_cond_act = cond_back.swapaxes(0, 1).reshape(items, width).astype(WIDE)
     grad_condition = silu_pull(grad_cond_act)[0]
-    cut = part_width(hd)
     if s_head.fast:
-        head_0, head_1 = s_head.halves()
-        proj_halves = (head_0[:, cut:], head_1[:, cut:])
+        shard_qkv, shard_proj = finish(core_place, s_head.live, s_tail.live, hd, width)
     else:
-        head_0, head_1 = s_head.halves()
-        proj_halves = s_proj.halves()
-    shard_qkv = from_parts(
-        jnp.concatenate((head_0[:, :cut], head_1[:, :cut]) + s_tail.halves(), axis=1), heads, hd
-    )
-    shard_proj = jnp.concatenate(proj_halves, axis=1)[:, :width]
-    shard_gate_up = jnp.concatenate(s_wide.halves(), axis=1)
-    shard_down = jnp.concatenate(s_down.halves(), axis=1)[:, :width]
+        shard_qkv = jnp.concatenate(s_head.halves() + s_tail.halves(), axis=1)
+        shard_qkv = from_parts(shard_qkv, heads, hd)
+        shard_proj = jnp.concatenate(s_proj.halves(), axis=1)[:, :width]
+    shard_gate_up = shard_wide
     return (
         block_out[None],
         grad_input[None],

time: 891 us -> 812 us (0.911)
  local copies, waits for them, and re-layouts: 110 us -> 86.6 us
  starting transfers between devices: 123 us -> 105 us
  waiting for transfers between devices: 144 us -> 126 us
  other arithmetic: 97.1 us -> 80.3 us
    ppermute x12 -> x17, waiting for transfers between devices: 64.5 us -> 50 us  [the longest x6 32.1 us: z(): live[str(k)] = lax.ppermute(pick(line, (z + k) % 4, 0), AXES, TO_Z[k])]
    select_n x3 -> x0, other arithmetic: 13.5 us -> none  [the longest x2 9.3 us: mine_and_other(): jnp.where(core == 0, first, second)]
    ppermute x5, waiting for transfers between devices: 9.81 us -> 22.3 us  [y(): self.live['far'] = lax.ppermute(self.live['own'], AXES, TO_Y)]
    all_to_all x2, waiting for transfers between devices: 11.4 us -> 0.01 us  [gather_rows(): lax.all_to_all(jnp.broadcast_to(rows, (shards, count, width)), 'fsdp', 0, 0)]
    reshape x3 -> x0, local copies, waits for them, and re-layouts: 9.78 us -> none  [the longest x1 4.06 us: from_parts(): shaped = shaped.reshape(rows, heads // GROUP, 3, GROUP * hd).swapaxes(1, 2)]
    all_to_all x9 -> x7, starting transfers between devices: 40.9 us -> 31.2 us  [over_z(): return lax.all_to_all(operand, 'fsdp', 0, 0, axis_index_groups=Z_GROUPS)]
    ppermute x16 -> x15, starting transfers between devices: 19.6 us -> 12 us  [core(): self.live['twin_' + name] = lax.ppermute(self.live[name], AXES, TO_CORE)]
    another operation x22 -> x21, other arithmetic: 19 us -> 11.7 us  [the longest x5 4.47 us: x(): ends = jnp.stack([self.live['own'][:, 0], self.live['far'][:, 0]], 1)]
  transfers between devices with their start and end apart: 68 -> 70, of which waited for: 21 -> 16; matrix products, arithmetic and copies ran while one was open for 20% -> 19% of each run, Pallas kernels for 34% -> 37%
where the time goes in v4:
time: 812 us; the launch traced here: 801 us
  Pallas kernels  324 us (40%)
  waiting for transfers between devices  126 us (16%)
  starting transfers between devices  105 us (13%)
  local copies, waits for them, and re-layouts  86.6 us (11%)
  other arithmetic  80.3 us (10%)
  matrix products  75.6 us (9%)
    pallas_call x7, Pallas kernels, call_rows(): pl.pallas_call(kernel, grid=(n // BLOCK,), in_specs=[pl.BlockSpec(memory_...  130 us
    pallas_call x2, Pallas kernels, attend_back(): pl.pallas_call(partial(back_kernel, hd, c, score_scale), grid=(n // BLOCK...  94.8 us
    dot_general x12, matrix products, dot_left(): lax.dot_general(left, right, (((0,), (0,)), ((), ())), preferred_element_...  70.9 us
    all_to_all x7, waiting for transfers between devices, over_z(): return lax.all_to_all(operand, 'fsdp', 0, 0, axis_index_groups=Z_GROUPS)  37.4 us
    pallas_call x2, Pallas kernels, prepare(): pl.pallas_call(partial(prepare_kernel, first, heads, hd), grid=(n // BLOC...  37.4 us
    ppermute x6, waiting for transfers between devices, z(): live[str(k)] = lax.ppermute(pick(line, (z + k) % 4, 0), AXES, TO_Z[k])  32.1 us
    all_to_all x7, starting transfers between devices, over_z(): return lax.all_to_all(operand, 'fsdp', 0, 0, axis_index_groups=Z_GROUPS)  31.2 us
    pallas_call x1, Pallas kernels, attend(): pl.pallas_call(partial(attend_kernel, hd, c), grid=(n // BLOCK,), in_spec...  27.8 us
  transfers between devices with their start and end apart: 70, of which 16 were waited for; matrix products, arithmetic and copies ran while one was open for 19% of the time, Pallas kernels for 37%

profile of v4, /device:TPU:1, one launch (start us, length us, event | category | flops | bytes accessed | tf_op | source)
XLA Modules:
  0.0 801.5 jit_solution(10289575167946241801)
XLA Ops:
  2.1 6.4 all-to-all-start.1
  17.1 4.7 all-to-all-start
  24.5 2.9 fusion.48
  27.4 11.9 %all-to-all-done.a0 = bf16[4,2,48,896]{3,2,1,0:T(8,128)(2,1)S(1)} async-done(((bf16[4,2,48,896]{3,2,1,0:T(8,128)(2,1)}), bf16[4,2,48,896]{3,2,1,0:T(8,128)(2,1)S(1)}, u32[]{:S(2)}, u32[]{:S(2)}) %all-to-all-start) | async-done | bytes 688160 | tf_op jit(solution)/shard_map/all_to_all | solution.py:89
  40.5 3.5 all-to-all-start.2
  44.1 5.4 multiply_cosine_fusion
  52.8 2.5 concatenate.73
  57.8 2.8 pad_maximum_fusion.4.rot_ref
  63.7 3.3 collective-permute-done.a1
  67.0 5.0 all-to-all-done.2.a0
  72.0 3.6 all-to-all-start.3
  81.2 15.1 %all-to-all-done.3 = bf16[8,8,6912]{2,1,0:T(8,128)(2,1)S(1)} async-done(((bf16[8,8,6912]{2,1,0:T(8,128)(2,1)}), bf16[8,8,6912]{2,1,0:T(8,128)(2,1)S(1)}, u32[]{:S(2)}, u32[]{:S(2)}) %all-to-all-start.3) | async-done | bytes 884768 | tf_op jit(solution)/shard_map/all_to_all | solution.py:327
  96.5 17.0 %collective-permute-done.4.a1 = bf16[4,2,48,1536]{3,2,1,0:T(8,128)(2,1)} collective-permute-done((bf16[4,2,48,1536]{3,2,1,0:T(8,128)(2,1)S(1)}, bf16[4,2,48,1536]{3,2,1,0:T(8,128)(2,1)}, u32[]{:S(2)}, u32[]{:S(2)}) %collective-permute-start.4) | collective-permute-done | bytes 1179680 | tf_op jit(solution)/shard_map/ppermute | solution.py:149
  114.8 4.6 all-to-all-start.4
  130.8 2.9 place.5.w_ref.wo_ref
  135.7 18.5 %prepare.2 = (bf16[1024,1152]{1,0:T(8,128)(2,1)}, bf16[8,1024,128]{2,1,0:T(8,128)(2,1)}, bf16[8,1024,128]{2,1,0:T(8,128)(2,1)}, bf16[8,1024,128]{2,1,0:T(8,128)(...) custom-call(bf16[1024,1152]{1,0:T(8,128)(2,1)} %bitcast.296, bf16[1024,16]{1,0:T(8,128)(2,1)} %copy.89.hot_ref, ...), custom_call_target="tpu_custom_call" | custom-call | flops 4227858432 | bytes 20971520 | tf_op jit(solution)/shard_map/prepare/pallas_call | solution.py:392
  157.8 4.8 all-to-all-start.5
  162.6 3.9 place.6.w_ref.wt_ref
  166.5 2.8 copy-done
  169.3 18.9 %prepare.3 = (bf16[8,1024,128]{2,1,0:T(8,128)(2,1)}, bf16[8,1024,128]{2,1,0:T(8,128)(2,1)}, bf16[8,1024,128]{2,1,0:T(8,128)(2,1)}, bf16[8,1024,128]{2,1,0:T(8,128)(2,1)}, bf16[8,1024,128]{2,1,0:T(8,128)(2,1)}) custom-call(bf16[1024,1152]{1,0:T(8,128)(2,1)} %get-tuple-element.522.x_ref, bf16[1024,16]{1,0:T(8,128)(2,1)} %copy.89.hot_ref, ...), custom_call_target="tpu_custom_call" | custom-call | flops 7247757312 | bytes 20971520 | tf_op jit(solution)/shard_map/prepare/pallas_call | solution.py:392
  192.3 3.5 all-to-all-start.6
  199.4 27.8 %attend.1 = (bf16[1024,1152]{1,0:T(8,128)(2,1)}, bf16[8,1024,128]{2,1,0:T(8,128)(2,1)}, bf16[8,1024,128]{2,1,0:T(8,128)(2,1)}) custom-call(bf16[8,1024,128]{2,1,0:T(8,128)(2,1)} %get-tuple-element.372.refs_0_, bf16[8,1024,128]{2,1,0:T(8,128)(2,1)} %get-tuple-element.373.refs_1_.k_ref, bf16[8,1024,128]{2,1,0:T(8,128)(2,1)} %get-tuple-element.374.refs_2_.v_ref, ...), custom_call_target="tpu_custom_call" | custom-call | flops 5368709120 | bytes 20971520 | tf_op jit(solution)/shard_map/attend/pallas_call | solution.py:473
  238.6 11.3 %join.1 = (bf16[1024,1152]{1,0:T(8,128)(2,1)}, f32[1024,1152]{1,0:T(8,128)}, bf16[1024,1152]{1,0:T(8,128)(2,1)}) custom-call(bf16[1024,1152]{1,0:T(8,128)(2,1)} %get-tuple-element.483.mix_ref, bf16[1024,1152]{1,0:T(8,128)(2,1)} %bitcast.297, bf16[1024,16]{1,0:T(8,128)(2,1)} %copy.89.hot_ref, f32[1024,1]{1,0:T(8,128)} %copy.92.keep_ref, ...), custom_call_target="tpu_custom_call" | custom-call | flops 7247757312 | bytes 11943936 | tf_op jit(solution)/shard_map/join/pallas_call | solution.py:693
  249.8 11.3 %collective-permute-done.16.ax = bf16[4,2,48,1536]{3,2,1,0:T(8,128)(2,1)} collective-permute-done((bf16[4,2,48,1536]{3,2,1,0:T(8,128)(2,1)}, bf16[4,2,48,1536]{3,2,1,0:T(8,128)(2,1)}, u32[]{:S(2)}, u32[]{:S(2)}) %collective-permute-start.16) | collective-permute-done | bytes 1179680 | tf_op jit(solution)/shard_map/ppermute | solution.py:154
  267.4 3.3 place.7.w_ref.wg_ref
  270.7 2.9 copy-done.1
  273.6 13.2 %gate.1.gate_ref = bf16[1024,3072]{1,0:T(8,128)(2,1)} custom-call(bf16[1024,1152]{1,0:T(8,128)(2,1)} %get-tuple-element.470.x_ref, bf16[1152,3072]{1,0:T(8,128)(2,1)} %copy-done.1), custom_call_target="tpu_custom_call" | custom-call | flops 7247757312 | bytes 9437184 | tf_op jit(solution)/shard_map/gate/pallas_call | solution.py:693
  286.8 6.5 collective-permute-done.21.ax
  298.4 4.1 place.8.w_ref.wu_ref
  302.5 2.9 copy-done.2
  305.4 15.5 %up.1 = (bf16[1024,3072]{1,0:T(8,128)(2,1)}, bf16[1024,3072]{1,0:T(8,128)(2,1)}) custom-call(bf16[1024,1152]{1,0:T(8,128)(2,1)} %get-tuple-element.470.x_ref, bf16[1024,3072]{1,0:T(8,128)(2,1)} %gate.1.gate_ref, bf16[1152,3072]{1,0:T(8,128)(2,1)} %copy-done.2), custom_call_target="tpu_custom_call" | custom-call | flops 7247757312 | bytes 15728640 | tf_op jit(solution)/shard_map/up/pallas_call | solution.py:693
  320.9 6.0 place.9.w_ref
  327.0 16.0 %down.1 = (bf16[1024,1152]{1,0:T(8,128)(2,1)}, bf16[1024,1280]{1,0:T(8,128)(2,1)}, f32[16,1152]{1,0:T(8,128)}) custom-call(bf16[1024,3072]{1,0:T(8,128)(2,1)} %get-tuple-element.449.inner_ref, f32[1024,1152]{1,0:T(8,128)} %get-tuple-element.461.mid_ref, bf16[1024,1152]{1,0:T(8,128)(2,1)} %bitcast.294, bf16[1024,16]{1,0:T(8,128)(2,1)} %copy.89.hot_ref, ...), custom_call_target="tpu_custom_call" | custom-call | flops 8053063680 | bytes 21307392 | tf_op jit(solution)/shard_map/down/pallas_call | solution.py:693
  345.1 9.4 %convolution_convert_fusion.1 = bf16[3072,640]{1,0:T(8,128)(2,1)} fusion(bf16[1024,3072]{1,0:T(8,128)(2,1)} %get-tuple-element.449.inner_ref, bf16[1024,1280]{1,0:T(8,128)(2,1)S(1)} %copy-done.41, s32[]{:T(128)S(6)} %select_n.439), kind=kOutput, calls=%fused_computation.6 | convolution fusion | flops 4028497920 | bytes 11534340 | tf_op jit(solution)/shard_map/dot_general | solution.py:29
  354.6 18.8 %inner_back.1 = (bf16[1024,3072]{1,0:T(8,128)(2,1)}, bf16[1024,3072]{1,0:T(8,128)(2,1)}) custom-call(s32[1]{0:T(128)} %bitcast.21.core_ref, bf16[1024,1280]{1,0:T(8,128)(2,1)} %get-tuple-element.443.grad_ref, bf16[1024,3072]{1,0:T(8,128)(2,1)} %gate.1.gate_ref, bf16[1024,3072]{1,0:T(8,128)(2,1)} %get-tuple-element.445.up_ref, bf16[3072,1280]{1,0:T(8,128)(2,1)} %place.9.w_ref), custom_call_target="tpu_custom_call" | custom-call | flops 8053063680 | bytes 23068672 | tf_op jit(solution)/shard_map/inner_back/pallas_call | solution.py:693
  373.3 12.3 %convolution_convert_fusion = bf16[1152,3072]{1,0:T(8,128)(2,1)} fusion(bf16[1024,1152]{1,0:T(8,128)(2,1)S(1)} %copy-done.66, bf16[1024,3072]{1,0:T(8,128)(2,1)} %get-tuple-element.459.send_ref), kind=kOutput, calls=%fused_computation.1 | convolution fusion | flops 7251296256 | bytes 15728640 | tf_op jit(solution)/shard_map/dot_general | solution.py:29
  385.6 9.8 %add_convert_fusion.1 = bf16[3072,640]{1,0:T(8,128)(2,1)} fusion(bf16[3072,640]{1,0:T(8,128)(2,1)S(1)} %collective-permute-done.25, bf16[1024,3072]{1,0:T(8,128)(2,1)} %get-tuple-element.449.inner_ref, bf16[1024,640]{1,0:T(8,128)(2,1)S(1)} %constant_dynamic-slice_fusion.2), kind=kOutput, calls=%fused_computation.4 | convolution fusion | flops 4032430080 | bytes 15466496 | tf_op jit(solution)/shard_map/dot_general | solution.py:29
  399.3 33.3 %middle_back.1 = (f32[1024,1152]{1,0:T(8,128)}, bf16[1024,1280]{1,0:T(8,128)(2,1)}, f32[16,3456]{1,0:T(8,128)}) custom-call(s32[1]{0:T(128)} %bitcast.21.core_ref, bf16[1024,3072]{1,0:T(8,128)(2,1)} %get-tuple-element.459.send_ref, bf16[1024,3072]{1,0:T(8,128)(2,1)} %get-tuple-element.471.mine_ref, f32[1024,1152]{1,0:T(8,128)} %get-tuple-element.461.mid_ref, ...), custom_call_target="tpu_custom_call" | custom-call | flops 14495514624 | bytes 36323328 | tf_op jit(solution)/shard_map/middle_back/pallas_call | solution.py:693
  432.6 3.7 constant_dynamic-slice_fusion
  440.3 12.7 %spread.1.do_ref = bf16[16,1024,128]{2,1,0:T(8,128)(2,1)} custom-call(bf16[1024,1280]{1,0:T(8,128)(2,1)} %get-tuple-element.478.ga_ref, bf16[1152,3072]{1,0:T(8,128)(2,1)} %copy-done, bf16[1024,1152]{1,0:T(8,128)(2,1)} %get-tuple-element.483.mix_ref), custom_call_target="tpu_custom_call" | custom-call | flops 2717908992 | bytes 12582912 | tf_op jit(solution)/shard_map/spread/pallas_call | solution.py:517
  453.7 4.6 convolution_convert_fusion.4
  458.3 11.6 %add_convert_fusion = bf16[1152,3072]{1,0:T(8,128)(2,1)S(1)} fusion(bf16[1152,3072]{1,0:T(8,128)(2,1)} %collective-permute-done.27, bf16[1024,1152]{1,0:T(8,128)(2,1)S(1)} %copy-done.67, bf16[1024,3072]{1,0:T(8,128)(2,1)} %get-tuple-element.471.mine_ref), kind=kOutput, calls=%fused_computation | convolution fusion | flops 7258374144 | bytes 22806528 | tf_op jit(solution)/shard_map/dot_general | solution.py:29
  474.2 2.7 add_convert_fusion.3
  476.9 5.0 all-to-all-start.7
  483.2 47.6 %attend_back.2 = (bf16[2,1024,896]{2,1,0:T(8,128)(2,1)}, f32[2,8,128]{2,1,0:T(8,128)}) custom-call(s32[1]{0:T(128)} %bitcast.21.core_ref, bf16[8,1024,128]{2,1,0:T(8,128)(2,1)} %get-tuple-element.486.q_ref, bf16[8,1024,128]{2,1,0:T(8,128)(2,1)} %get-tuple-element.373.refs_1_.k_ref, bf16[8,1024,128]{2,1,0:T(8,128)(2,1)} %get-tuple-element.374.refs_2_.v_ref, ...), custom_call_target="tpu_custom_call" | custom-call | flops 6710886400 | bytes 20971520 | tf_op jit(solution)/shard_map/attend_back/pallas_call | solution.py:624
  533.4 4.0 convolution_convert_fusion.3
  537.3 3.2 fusion.3
  550.1 4.2 fusion.1
  556.1 5.6 all-to-all-start.8
  564.1 47.2 %attend_back.3 = (bf16[2,1024,896]{2,1,0:T(8,128)(2,1)}, f32[2,8,128]{2,1,0:T(8,128)}) custom-call(s32[1]{0:T(128)} %bitcast.21.core_ref, bf16[8,1024,128]{2,1,0:T(8,128)(2,1)} %get-tuple-element.507.q_ref, bf16[8,1024,128]{2,1,0:T(8,128)(2,1)} %get-tuple-element.376.refs_4_.k_ref, bf16[8,1024,128]{2,1,0:T(8,128)(2,1)} %get-tuple-element.377.refs_5_.v_ref, ...), custom_call_target="tpu_custom_call" | custom-call | flops 6710886400 | bytes 20971520 | tf_op jit(solution)/shard_map/attend_back/pallas_call | solution.py:624
  611.4 5.6 convolution_convert_fusion.2
  624.7 4.0 add_convert_fusion.2
  628.8 5.0 all-to-all-start.9
  639.7 4.2 fusion.2
  645.8 21.5 %input_back.1 = (f32[1024,1152]{1,0:T(8,128)}, f32[16,2304]{1,0:T(8,128)}) custom-call(s32[1]{0:T(128)} %bitcast.21.core_ref, bf16[2,1024,896]{2,1,0:T(8,128)(2,1)} %get-tuple-element.527.one_ref, bf16[2,1024,896]{2,1,0:T(8,128)(2,1)} %get-tuple-element.528.two_ref, f32[1024,1152]{1,0:T(8,128)} %get-tuple-element.529.mid_ref, bf16[1024,1152]{1,0:T(8,128)(2,1)} %bitcast.298, ...), custom_call_target="tpu_custom_call" | custom-call | flops 11475615744 | bytes 25731072 | tf_op jit(solution)/shard_map/input_back/pallas_call | solution.py:693
  668.1 19.4 %all-to-all-done.9 = bf16[4,2,48,3072]{3,2,1,0:T(8,128)(2,1)} async-done(((bf16[4,2,48,3072]{3,2,1,0:T(8,128)(2,1)}), bf16[4,2,48,3072]{3,2,1,0:T(8,128)(2,1)}, u32[]{:S(2)}, u32[]{:S(2)}) %all-to-all-start.9) | async-done | bytes 2359328 | tf_op jit(solution)/shard_map/all_to_all | solution.py:89
  707.0 3.4 all-to-all-start.10
  716.5 21.8 %collective-permute-done.41 = bf16[2,48,1536]{2,1,0:T(8,128)(2,1)S(1)} collective-permute-done((bf16[2,48,1536]{2,1,0:T(8,128)(2,1)}, bf16[2,48,1536]{2,1,0:T(8,128)(2,1)S(1)}, u32[]{:S(2)}, u32[]{:S(2)}) %collective-permute-start.41) | collective-permute-done | bytes 294944 | tf_op jit(solution)/shard_map/ppermute | solution.py:243
  743.5 2.6 collective-permute-start.52
  754.3 5.9 collective-permute-done.50
  764.5 3.1 collective-permute-done.48
  768.8 6.0 all-to-all-start.11
  774.8 2.7 convert_reduce_fusion
  794.6 3.5 pad_maximum_fusion
  (442 shorter events, 188.3 us)
Async XLA Ops:
  2.1 14.1 %all-to-all-start.1 = ((bf16[8,8,144]{2,1,0:T(8,128)(2,1)}), bf16[8,8,144]{2,1,0:T(8,128)(2,1)}, u32[]{:S(2)}, u32[]{:S(2)}) async-start(bf16[8,8,144]{2,1,0:T(8,128)(2,1)} %fusion.35), calls=%async_computation.1 | async-start | bytes 65536 | tf_op jit(solution)/shard_map/all_to_all | solution.py:321
  17.1 22.2 %all-to-all-start = ((bf16[4,2,48,896]{3,2,1,0:T(8,128)(2,1)}), bf16[4,2,48,896]{3,2,1,0:T(8,128)(2,1)S(1)}, u32[]{:S(2)}, u32[]{:S(2)}) async-start(bf16[4,2,48,896]{3,2,1,0:T(8,128)(2,1)} %broadcast_in_dim.60), calls=%async_computation | async-start | bytes 1376256 | tf_op jit(solution)/shard_map/all_to_all | solution.py:89
  40.5 31.5 %all-to-all-start.2 = ((bf16[4,2,48,1536]{3,2,1,0:T(8,128)(2,1)}), bf16[4,2,48,1536]{3,2,1,0:T(8,128)(2,1)S(1)}, u32[]{:S(2)}, u32[]{:S(2)}) async-start(bf16[4,2,48,1536]{3,2,1,0:T(8,128)(2,1)} %broadcast_in_dim.61), calls=%async_computation.2 | async-start | bytes 2359296 | tf_op jit(solution)/shard_map/all_to_all | solution.py:89
  51.5 15.5 %collective-permute-start = (bf16[4,2,48,896]{3,2,1,0:T(8,128)(2,1)S(1)}, bf16[4,2,48,896]{3,2,1,0:T(8,128)(2,1)S(1)}, u32[]{:S(2)}, u32[]{:S(2)}) collective-permute-start(bf16[4,2,48,896]{3,2,1,0:T(8,128)(2,1)S(1)} %all-to-all-done.a0), channel_id=1, source_target_pairs={{0,1},{1,0},{2,3},{3,2},{4,5},{5,4},{6,7},{7,6},{8,9},{9,8},{10,11... | collective-permute-start | bytes 2064392 | tf_op jit(solution)/shard_map/ppermute | solution.py:149
  72.0 24.3 %all-to-all-start.3 = ((bf16[8,8,6912]{2,1,0:T(8,128)(2,1)}), bf16[8,8,6912]{2,1,0:T(8,128)(2,1)S(1)}, u32[]{:S(2)}, u32[]{:S(2)}) async-start(bf16[8,8,6912]{2,1,0:T(8,128)(2,1)} %bitcast.16), calls=%async_computation.3 | async-start | bytes 1769472 | tf_op jit(solution)/shard_map/all_to_all | solution.py:327
  75.6 20.9 %collective-permute-start.3 = (bf16[4,2,48,896]{3,2,1,0:T(8,128)(2,1)S(1)}, bf16[4,2,48,896]{3,2,1,0:T(8,128)(2,1)}, u32[]{:S(2)}, u32[]{:S(2)}) collective-permute-start(bf16[4,2,48,896]{3,2,1,0:T(8,128)(2,1)S(1)} %all-to-all-done.a0), channel_id=1, source_target_pairs={{0,8},{1,9},{2,10},{3,11},{4,12},{5,13},{6,14},{7,15},{8,0},{9,1},... | collective-permute-start | bytes 2064392 | tf_op jit(solution)/shard_map/ppermute | solution.py:159
  77.3 19.2 %collective-permute-start.2 = (bf16[4,2,48,896]{3,2,1,0:T(8,128)(2,1)S(1)}, bf16[4,2,48,896]{3,2,1,0:T(8,128)(2,1)}, u32[]{:S(2)}, u32[]{:S(2)}) collective-permute-start(bf16[4,2,48,896]{3,2,1,0:T(8,128)(2,1)S(1)} %collective-permute-done.a1), channel_id=1, source_target_pairs={{0,8},{1,9},{2,10},{3,11},{4,12},{5,13},{6,14},{7,15},{8,0},{9,1},... | collective-permute-start | bytes 2064392 | tf_op jit(solution)/shard_map/ppermute | solution.py:159
  78.3 18.2 %collective-permute-start.1 = (bf16[4,2,48,896]{3,2,1,0:T(8,128)(2,1)}, bf16[4,2,48,896]{3,2,1,0:T(8,128)(2,1)}, u32[]{:S(2)}, u32[]{:S(2)}) collective-permute-start(bf16[4,2,48,896]{3,2,1,0:T(8,128)(2,1)} %pad_maximum_fusion.15), channel_id=1, source_target_pairs={{0,16},{1,17},{2,18},{3,19},{4,20},{5,21},{6,22},{7,23},{8,24},{9,... | collective-permute-start | bytes 2064392 | tf_op jit(solution)/shard_map/ppermute | solution.py:154
  79.5 34.1 %collective-permute-start.4 = (bf16[4,2,48,1536]{3,2,1,0:T(8,128)(2,1)S(1)}, bf16[4,2,48,1536]{3,2,1,0:T(8,128)(2,1)}, u32[]{:S(2)}, u32[]{:S(2)}) collective-permute-start(bf16[4,2,48,1536]{3,2,1,0:T(8,128)(2,1)S(1)} %all-to-all-done.2.a0), channel_id=1, source_target_pairs={{0,1},{1,0},{2,3},{3,2},{4,5},{5,4},{6,7},{7,6},{8,9},{9,8},{10,11... | collective-permute-start | bytes 3538952 | tf_op jit(solution)/shard_map/ppermute | solution.py:149
  114.8 39.4 %all-to-all-start.4 = ((bf16[4,2,48,1536]{3,2,1,0:T(8,128)(2,1)}), bf16[4,2,48,1536]{3,2,1,0:T(8,128)(2,1)S(1)}, u32[]{:S(2)}, u32[]{:S(2)}) async-start(bf16[4,2,48,1536]{3,2,1,0:T(8,128)(2,1)} %broadcast_in_dim.65), calls=%async_computation.4 | async-start | bytes 2359296 | tf_op jit(solution)/shard_map/all_to_all | solution.py:89
  121.7 32.4 %collective-permute-start.5 = (bf16[4,2,48,1536]{3,2,1,0:T(8,128)(2,1)}, bf16[4,2,48,1536]{3,2,1,0:T(8,128)(2,1)}, u32[]{:S(2)}, u32[]{:S(2)}) collective-permute-start(bf16[4,2,48,1536]{3,2,1,0:T(8,128)(2,1)} %pad_maximum_fusion.8), channel_id=1, source_target_pairs={{0,16},{1,17},{2,18},{3,19},{4,20},{5,21},{6,22},{7,23},{8,24},{9,... | collective-permute-start | bytes 3538952 | tf_op jit(solution)/shard_map/ppermute | solution.py:154
  122.8 31.4 %collective-permute-start.7 = (bf16[4,2,48,1536]{3,2,1,0:T(8,128)(2,1)S(1)}, bf16[4,2,48,1536]{3,2,1,0:T(8,128)(2,1)}, u32[]{:S(2)}, u32[]{:S(2)}) collective-permute-start(bf16[4,2,48,1536]{3,2,1,0:T(8,128)(2,1)S(1)} %all-to-all-done.2.a0), channel_id=1, source_target_pairs={{0,8},{1,9},{2,10},{3,11},{4,12},{5,13},{6,14},{7,15},{8,0},{9,1},... | collective-permute-start | bytes 3538952 | tf_op jit(solution)/shard_map/ppermute | solution.py:159
  124.2 30.0 %collective-permute-start.6 = (bf16[4,2,48,1536]{3,2,1,0:T(8,128)(2,1)}, bf16[4,2,48,1536]{3,2,1,0:T(8,128)(2,1)}, u32[]{:S(2)}, u32[]{:S(2)}) collective-permute-start(bf16[4,2,48,1536]{3,2,1,0:T(8,128)(2,1)} %collective-permute-done.4.a1), channel_id=1, source_target_pairs={{0,8},{1,9},{2,10},{3,11},{4,12},{5,13},{6,14},{7,15},{8,0},{9,1},... | collective-permute-start | bytes 3538952 | tf_op jit(solution)/shard_map/ppermute | solution.py:159
  157.8 33.1 %all-to-all-start.5 = ((bf16[4,2,48,1536]{3,2,1,0:T(8,128)(2,1)}), bf16[4,2,48,1536]{3,2,1,0:T(8,128)(2,1)}, u32[]{:S(2)}, u32[]{:S(2)}) async-start(bf16[4,2,48,1536]{3,2,1,0:T(8,128)(2,1)} %broadcast_in_dim.68), calls=%async_computation.5 | async-start | bytes 2359296 | tf_op jit(solution)/shard_map/all_to_all | solution.py:89
  162.6 27.2 %collective-permute-start.9 = (bf16[4,2,48,1536]{3,2,1,0:T(8,128)(2,1)S(1)}, bf16[4,2,48,1536]{3,2,1,0:T(8,128)(2,1)}, u32[]{:S(2)}, u32[]{:S(2)}) collective-permute-start(bf16[4,2,48,1536]{3,2,1,0:T(8,128)(2,1)S(1)} %all-to-all-done.4.a0), channel_id=1, source_target_pairs={{0,1},{1,0},{2,3},{3,2},{4,5},{5,4},{6,7},{7,6},{8,9},{9,8},{10,11... | collective-permute-start | bytes 3538952 | tf_op jit(solution)/shard_map/ppermute | solution.py:149
  192.3 37.0 %all-to-all-start.6 = ((bf16[4,2,128,640]{3,2,1,0:T(8,128)(2,1)}), bf16[4,2,128,640]{3,2,1,0:T(8,128)(2,1)S(1)}, u32[]{:S(2)}, u32[]{:S(2)}) async-start(bf16[4,2,128,640]{3,2,1,0:T(8,128)(2,1)} %broadcast_in_dim.69), calls=%async_computation.6 | async-start | bytes 2621440 | tf_op jit(solution)/shard_map/all_to_all | solution.py:89
  197.1 30.1 %collective-permute-start.11 = (bf16[4,2,48,1536]{3,2,1,0:T(8,128)(2,1)S(1)}, bf16[4,2,48,1536]{3,2,1,0:T(8,128)(2,1)}, u32[]{:S(2)}, u32[]{:S(2)}) collective-permute-start(bf16[4,2,48,1536]{3,2,1,0:T(8,128)(2,1)S(1)} %pad_maximum_fusion.9), channel_id=1, source_target_pairs={{0,16},{1,17},{2,18},{3,19},{4,20},{5,21},{6,22},{7,23},{8,24},{9,... | collective-permute-start | bytes 3538952 | tf_op jit(solution)/shard_map/ppermute | solution.py:154
  197.4 29.8 %collective-permute-start.14 = (bf16[4,2,48,1536]{3,2,1,0:T(8,128)(2,1)}, bf16[4,2,48,1536]{3,2,1,0:T(8,128)(2,1)}, u32[]{:S(2)}, u32[]{:S(2)}) collective-permute-start(bf16[4,2,48,1536]{3,2,1,0:T(8,128)(2,1)} %all-to-all-done.5.a0), channel_id=1, source_target_pairs={{0,1},{1,0},{2,3},{3,2},{4,5},{5,4},{6,7},{7,6},{8,9},{9,8},{10,11... | collective-permute-start | bytes 3538952 | tf_op jit(solution)/shard_map/ppermute | solution.py:149
  197.4 29.8 %collective-permute-start.13 = (bf16[4,2,48,1536]{3,2,1,0:T(8,128)(2,1)S(1)}, bf16[4,2,48,1536]{3,2,1,0:T(8,128)(2,1)S(1)}, u32[]{:S(2)}, u32[]{:S(2)}) collective-permute-start(bf16[4,2,48,1536]{3,2,1,0:T(8,128)(2,1)S(1)} %all-to-all-done.4.a0), channel_id=1, source_target_pairs={{0,8},{1,9},{2,10},{3,11},{4,12},{5,13},{6,14},{7,15},{8,0},{9,1},... | collective-permute-start | bytes 3538952 | tf_op jit(solution)/shard_map/ppermute | solution.py:159
  199.4 28.8 %collective-permute-start.12 = (bf16[4,2,48,1536]{3,2,1,0:T(8,128)(2,1)}, bf16[4,2,48,1536]{3,2,1,0:T(8,128)(2,1)S(1)}, u32[]{:S(2)}, u32[]{:S(2)}) collective-permute-start(bf16[4,2,48,1536]{3,2,1,0:T(8,128)(2,1)} %collective-permute-done.9.a1), channel_id=1, source_target_pairs={{0,8},{1,9},{2,10},{3,11},{4,12},{5,13},{6,14},{7,15},{8,0},{9,1},... | collective-permute-start | bytes 3538952 | tf_op jit(solution)/shard_map/ppermute | solution.py:159
  231.5 30.0 %collective-permute-start.19 = (bf16[4,2,128,640]{3,2,1,0:T(8,128)(2,1)S(1)}, bf16[4,2,128,640]{3,2,1,0:T(8,128)(2,1)}, u32[]{:S(2)}, u32[]{:S(2)}) collective-permute-start(bf16[4,2,128,640]{3,2,1,0:T(8,128)(2,1)S(1)} %all-to-all-done.6.a0), channel_id=1, source_target_pairs={{0,1},{1,0},{2,3},{3,2},{4,5},{5,4},{6,7},{7,6},{8,9},{9,8},{10,11... | collective-permute-start | bytes 3932168 | tf_op jit(solution)/shard_map/ppermute | solution.py:149
  234.1 27.0 %collective-permute-start.16 = (bf16[4,2,48,1536]{3,2,1,0:T(8,128)(2,1)}, bf16[4,2,48,1536]{3,2,1,0:T(8,128)(2,1)}, u32[]{:S(2)}, u32[]{:S(2)}) collective-permute-start(bf16[4,2,48,1536]{3,2,1,0:T(8,128)(2,1)} %pad_maximum_fusion.10), channel_id=1, source_target_pairs={{0,16},{1,17},{2,18},{3,19},{4,20},{5,21},{6,22},{7,23},{8,24},{9,... | collective-permute-start | bytes 3538952 | tf_op jit(solution)/shard_map/ppermute | solution.py:154
  235.3 25.8 %collective-permute-start.15 = (bf16[4,2,48,1536]{3,2,1,0:T(8,128)(2,1)}, bf16[4,2,48,1536]{3,2,1,0:T(8,128)(2,1)}, u32[]{:S(2)}, u32[]{:S(2)}) collective-permute-start(bf16[4,2,48,1536]{3,2,1,0:T(8,128)(2,1)} %collective-permute-done.11.ax), channel_id=1, source_target_pairs={{0,8},{1,9},{2,10},{3,11},{4,12},{5,13},{6,14},{7,15},{8,0},{9,1},... | collective-permute-start | bytes 3538952 | tf_op jit(solution)/shard_map/ppermute | solution.py:159
  236.4 24.7 %collective-permute-start.18 = (bf16[4,2,48,1536]{3,2,1,0:T(8,128)(2,1)}, bf16[4,2,48,1536]{3,2,1,0:T(8,128)(2,1)}, u32[]{:S(2)}, u32[]{:S(2)}) collective-permute-start(bf16[4,2,48,1536]{3,2,1,0:T(8,128)(2,1)} %all-to-all-done.5.a0), channel_id=1, source_target_pairs={{0,8},{1,9},{2,10},{3,11},{4,12},{5,13},{6,14},{7,15},{8,0},{9,1},... | collective-permute-start | bytes 3538952 | tf_op jit(solution)/shard_map/ppermute | solution.py:159
  236.4 24.7 %collective-permute-start.17 = (bf16[4,2,48,1536]{3,2,1,0:T(8,128)(2,1)}, bf16[4,2,48,1536]{3,2,1,0:T(8,128)(2,1)}, u32[]{:S(2)}, u32[]{:S(2)}) collective-permute-start(bf16[4,2,48,1536]{3,2,1,0:T(8,128)(2,1)} %collective-permute-done.14.a1), channel_id=1, source_target_pairs={{0,8},{1,9},{2,10},{3,11},{4,12},{5,13},{6,14},{7,15},{8,0},{9,1},... | collective-permute-start | bytes 3538952 | tf_op jit(solution)/shard_map/ppermute | solution.py:159
  264.1 29.3 %collective-permute-start.21 = (bf16[4,2,128,640]{3,2,1,0:T(8,128)(2,1)}, bf16[4,2,128,640]{3,2,1,0:T(8,128)(2,1)}, u32[]{:S(2)}, u32[]{:S(2)}) collective-permute-start(bf16[4,2,128,640]{3,2,1,0:T(8,128)(2,1)} %pad_maximum_fusion.5), channel_id=1, source_target_pairs={{0,16},{1,17},{2,18},{3,19},{4,20},{5,21},{6,22},{7,23},{8,24},{9,... | collective-permute-start | bytes 3932168 | tf_op jit(solution)/shard_map/ppermute | solution.py:154
  265.3 28.1 %collective-permute-start.23 = (bf16[4,2,128,640]{3,2,1,0:T(8,128)(2,1)S(1)}, bf16[4,2,128,640]{3,2,1,0:T(8,128)(2,1)S(1)}, u32[]{:S(2)}, u32[]{:S(2)}) collective-permute-start(bf16[4,2,128,640]{3,2,1,0:T(8,128)(2,1)S(1)} %all-to-all-done.6.a0), channel_id=1, source_target_pairs={{0,8},{1,9},{2,10},{3,11},{4,12},{5,13},{6,14},{7,15},{8,0},{9,1},... | collective-permute-start | bytes 3932168 | tf_op jit(solution)/shard_map/ppermute | solution.py:159
  266.9 27.5 %collective-permute-start.22 = (bf16[4,2,128,640]{3,2,1,0:T(8,128)(2,1)}, bf16[4,2,128,640]{3,2,1,0:T(8,128)(2,1)S(1)}, u32[]{:S(2)}, u32[]{:S(2)}) collective-permute-start(bf16[4,2,128,640]{3,2,1,0:T(8,128)(2,1)} %collective-permute-done.19.a1), channel_id=1, source_target_pairs={{0,8},{1,9},{2,10},{3,11},{4,12},{5,13},{6,14},{7,15},{8,0},{9,1},... | collective-permute-start | bytes 3932168 | tf_op jit(solution)/shard_map/ppermute | solution.py:159
  266.9 19.9 %collective-permute-start.20 = (bf16[4,2,48,1536]{3,2,1,0:T(8,128)(2,1)}, bf16[4,2,48,1536]{3,2,1,0:T(8,128)(2,1)}, u32[]{:S(2)}, u32[]{:S(2)}) collective-permute-start(bf16[4,2,48,1536]{3,2,1,0:T(8,128)(2,1)} %collective-permute-done.16.ax), channel_id=1, source_target_pairs={{0,8},{1,9},{2,10},{3,11},{4,12},{5,13},{6,14},{7,15},{8,0},{9,1},... | collective-permute-start | bytes 3538952 | tf_op jit(solution)/shard_map/ppermute | solution.py:159
  295.5 25.4 %collective-permute-start.24 = (bf16[4,2,128,640]{3,2,1,0:T(8,128)(2,1)}, bf16[4,2,128,640]{3,2,1,0:T(8,128)(2,1)S(1)}, u32[]{:S(2)}, u32[]{:S(2)}) collective-permute-start(bf16[4,2,128,640]{3,2,1,0:T(8,128)(2,1)} %collective-permute-done.21.ax), channel_id=1, source_target_pairs={{0,8},{1,9},{2,10},{3,11},{4,12},{5,13},{6,14},{7,15},{8,0},{9,1},... | collective-permute-start | bytes 3932168 | tf_op jit(solution)/shard_map/ppermute | solution.py:159
  354.5 18.8 %collective-permute-start.25 = (bf16[3072,640]{1,0:T(8,128)(2,1)}, bf16[3072,640]{1,0:T(8,128)(2,1)S(1)}, u32[]{:S(2)}, u32[]{:S(2)}) collective-permute-start(bf16[3072,640]{1,0:T(8,128)(2,1)} %convolution_convert_fusion.1), channel_id=1, source_target_pairs={{0,8},{1,9},{2,10},{3,11},{4,12},{5,13},{6,14},{7,15},{8,0},{9,1},... | collective-permute-start | bytes 11796488 | tf_op jit(solution)/shard_map/ppermute | solution.py:202
  395.4 40.9 %collective-permute-start.27 = (bf16[1152,3072]{1,0:T(8,128)(2,1)}, bf16[1152,3072]{1,0:T(8,128)(2,1)}, u32[]{:S(2)}, u32[]{:S(2)}) collective-permute-start(bf16[1152,3072]{1,0:T(8,128)(2,1)} %convolution_convert_fusion), channel_id=1, source_target_pairs={{0,8},{1,9},{2,10},{3,11},{4,12},{5,13},{6,14},{7,15},{8,0},{9,1},... | collective-permute-start | bytes 21233672 | tf_op jit(solution)/shard_map/ppermute | solution.py:202
  398.0 38.3 %collective-permute-start.26 = (bf16[4,2,128,640]{3,2,1,0:T(8,128)(2,1)S(1)}, bf16[4,2,128,640]{3,2,1,0:T(8,128)(2,1)S(1)}, u32[]{:S(2)}, u32[]{:S(2)}) collective-permute-start(bf16[4,2,128,640]{3,2,1,0:T(8,128)(2,1)S(1)} %dynamic-slice_bitcast_fusion.7), channel_id=1, source_target_pairs={{0,16},{1,17},{2,18},{3,19},{4,20},{5,21},{6,22},{7,23},{8,24},{9,... | collective-permute-start | bytes 3932168 | tf_op jit(solution)/shard_map/ppermute | solution.py:222
  438.9 31.1 %collective-permute-start.28 = (bf16[4,2,128,640]{3,2,1,0:T(8,128)(2,1)}, bf16[4,2,128,640]{3,2,1,0:T(8,128)(2,1)}, u32[]{:S(2)}, u32[]{:S(2)}) collective-permute-start(bf16[4,2,128,640]{3,2,1,0:T(8,128)(2,1)} %pad_maximum_fusion.6), channel_id=1, source_target_pairs={{0,1},{1,0},{2,3},{3,2},{4,5},{5,4},{6,7},{7,6},{8,9},{9,8},{10,11... | collective-permute-start | bytes 3932168 | tf_op jit(solution)/shard_map/ppermute | solution.py:233
  473.7 66.8 %collective-permute-start.29 = (bf16[4,2,48,3072]{3,2,1,0:T(8,128)(2,1)}, bf16[4,2,48,3072]{3,2,1,0:T(8,128)(2,1)}, u32[]{:S(2)}, u32[]{:S(2)}) collective-permute-start(bf16[4,2,48,3072]{3,2,1,0:T(8,128)(2,1)} %dynamic-slice_bitcast_fusion.2), channel_id=1, source_target_pairs={{0,16},{1,17},{2,18},{3,19},{4,20},{5,21},{6,22},{7,23},{8,24},{9,... | collective-permute-start | bytes 7077896 | tf_op jit(solution)/shard_map/ppermute | solution.py:222
  476.9 63.6 %all-to-all-start.7 = ((bf16[4,2,128,640]{3,2,1,0:T(8,128)(2,1)}), bf16[4,2,128,640]{3,2,1,0:T(8,128)(2,1)S(1)}, u32[]{:S(2)}, u32[]{:S(2)}) async-start(bf16[4,2,128,640]{3,2,1,0:T(8,128)(2,1)} %add_convert_fusion.3), calls=%async_computation.7 | async-start | bytes 2621440 | tf_op jit(solution)/shard_map/all_to_all | solution.py:89
  481.9 55.4 %collective-permute-start.30 = (bf16[1152,640]{1,0:T(8,128)(2,1)}, bf16[1152,640]{1,0:T(8,128)(2,1)S(1)}, u32[]{:S(2)}, u32[]{:S(2)}) collective-permute-start(bf16[1152,640]{1,0:T(8,128)(2,1)} %convolution_convert_fusion.4), channel_id=1, source_target_pairs={{0,8},{1,9},{2,10},{3,11},{4,12},{5,13},{6,14},{7,15},{8,0},{9,1},... | collective-permute-start | bytes 4423688 | tf_op jit(solution)/shard_map/ppermute | solution.py:202
  540.5 8.9 %collective-permute-start.33 = (bf16[1152,896]{1,0:T(8,128)(2,1)}, bf16[1152,896]{1,0:T(8,128)(2,1)}, u32[]{:S(2)}, u32[]{:S(2)}) collective-permute-start(bf16[1152,896]{1,0:T(8,128)(2,1)} %convolution_convert_fusion.3), channel_id=1, source_target_pairs={{0,8},{1,9},{2,10},{3,11},{4,12},{5,13},{6,14},{7,15},{8,0},{9,1},... | collective-permute-start | bytes 6193160 | tf_op jit(solution)/shard_map/ppermute | solution.py:202
  540.6 171.0 %collective-permute-start.45 = (bf16[64,144]{1,0:T(8,128)(2,1)}, bf16[64,144]{1,0:T(8,128)(2,1)}, u32[]{:S(2)}, u32[]{:S(2)}) collective-permute-start(bf16[64,144]{1,0:T(8,128)(2,1)} %bitcast.4), channel_id=1, source_target_pairs={{0,16},{1,17},{2,18},{3,19},{4,20},{5,21},{6,22},{7,23},{8,24},{9,... | collective-permute-start | bytes 55304 | tf_op jit(solution)/shard_map/ppermute | solution.py:296
  542.9 75.4 %collective-permute-start.31 = (bf16[2,128,640]{2,1,0:T(8,128)(2,1)}, bf16[2,128,640]{2,1,0:T(8,128)(2,1)}, u32[]{:S(2)}, u32[]{:S(2)}) collective-permute-start(bf16[2,128,640]{2,1,0:T(8,128)(2,1)} %reduce_sum.100), channel_id=1, source_target_pairs={{0,16},{1,17},{2,18},{3,19},{4,20},{5,21},{6,22},{7,23},{8,24},{9,... | collective-permute-start | bytes 983048 | tf_op jit(solution)/shard_map/ppermute | solution.py:255
  549.2 69.1 %collective-permute-start.32 = (bf16[4,2,48,3072]{3,2,1,0:T(8,128)(2,1)}, bf16[4,2,48,3072]{3,2,1,0:T(8,128)(2,1)}, u32[]{:S(2)}, u32[]{:S(2)}) collective-permute-start(bf16[4,2,48,3072]{3,2,1,0:T(8,128)(2,1)} %pad_maximum_fusion.2), channel_id=1, source_target_pairs={{0,1},{1,0},{2,3},{3,2},{4,5},{5,4},{6,7},{7,6},{8,9},{9,8},{10,11... | collective-permute-start | bytes 7077896 | tf_op jit(solution)/shard_map/ppermute | solution.py:233
  556.1 62.3 %all-to-all-start.8 = ((bf16[8,8,4608]{2,1,0:T(8,128)(2,1)}), bf16[8,8,4608]{2,1,0:T(8,128)(2,1)}, u32[]{:S(2)}, u32[]{:S(2)}) async-start(bf16[8,8,4608]{2,1,0:T(8,128)(2,1)} %broadcast_in_dim.71), calls=%async_computation.8 | async-start | bytes 1179648 | tf_op jit(solution)/shard_map/all_to_all | solution.py:313
  562.9 55.5 %collective-permute-start.34 = (bf16[4,2,48,1536]{3,2,1,0:T(8,128)(2,1)}, bf16[4,2,48,1536]{3,2,1,0:T(8,128)(2,1)}, u32[]{:S(2)}, u32[]{:S(2)}) collective-permute-start(bf16[4,2,48,1536]{3,2,1,0:T(8,128)(2,1)} %dynamic-slice_bitcast_fusion.8), channel_id=1, source_target_pairs={{0,16},{1,17},{2,18},{3,19},{4,20},{5,21},{6,22},{7,23},{8,24},{9,... | collective-permute-start | bytes 3538952 | tf_op jit(solution)/shard_map/ppermute | solution.py:222
  622.9 16.9 %collective-permute-start.37 = (bf16[1152,896]{1,0:T(8,128)(2,1)}, bf16[1152,896]{1,0:T(8,128)(2,1)}, u32[]{:S(2)}, u32[]{:S(2)}) collective-permute-start(bf16[1152,896]{1,0:T(8,128)(2,1)} %convolution_convert_fusion.2), channel_id=1, source_target_pairs={{0,8},{1,9},{2,10},{3,11},{4,12},{5,13},{6,14},{7,15},{8,0},{9,1},... | collective-permute-start | bytes 6193160 | tf_op jit(solution)/shard_map/ppermute | solution.py:202
  628.8 58.7 %all-to-all-start.9 = ((bf16[4,2,48,3072]{3,2,1,0:T(8,128)(2,1)}), bf16[4,2,48,3072]{3,2,1,0:T(8,128)(2,1)}, u32[]{:S(2)}, u32[]{:S(2)}) async-start(bf16[4,2,48,3072]{3,2,1,0:T(8,128)(2,1)} %add_convert_fusion.2), calls=%async_computation.9 | async-start | bytes 4718592 | tf_op jit(solution)/shard_map/all_to_all | solution.py:89
  635.9 31.4 %collective-permute-start.35 = (bf16[384,640]{1,0:T(8,128)(2,1)S(1)}, bf16[384,640]{1,0:T(8,128)(2,1)S(1)}, u32[]{:S(2)}, u32[]{:S(2)}) collective-permute-start(bf16[384,640]{1,0:T(8,128)(2,1)S(1)} %pad_maximum_fusion.18), channel_id=1, source_target_pairs={{0,8},{1,9},{2,10},{3,11},{4,12},{5,13},{6,14},{7,15},{8,0},{9,1},... | collective-permute-start | bytes 1474568 | tf_op jit(solution)/shard_map/ppermute | solution.py:265
  638.1 29.2 %collective-permute-start.36 = (bf16[4,2,48,1536]{3,2,1,0:T(8,128)(2,1)S(1)}, bf16[4,2,48,1536]{3,2,1,0:T(8,128)(2,1)}, u32[]{:S(2)}, u32[]{:S(2)}) collective-permute-start(bf16[4,2,48,1536]{3,2,1,0:T(8,128)(2,1)S(1)} %pad_maximum_fusion.11), channel_id=1, source_target_pairs={{0,1},{1,0},{2,3},{3,2},{4,5},{5,4},{6,7},{7,6},{8,9},{9,8},{10,11... | collective-permute-start | bytes 3538952 | tf_op jit(solution)/shard_map/ppermute | solution.py:233
  645.4 22.7 %collective-permute-start.38 = (bf16[4,2,48,896]{3,2,1,0:T(8,128)(2,1)S(1)}, bf16[4,2,48,896]{3,2,1,0:T(8,128)(2,1)}, u32[]{:S(2)}, u32[]{:S(2)}) collective-permute-start(bf16[4,2,48,896]{3,2,1,0:T(8,128)(2,1)S(1)} %dynamic-slice_bitcast_fusion.11), channel_id=1, source_target_pairs={{0,16},{1,17},{2,18},{3,19},{4,20},{5,21},{6,22},{7,23},{8,24},{9,... | collective-permute-start | bytes 2064392 | tf_op jit(solution)/shard_map/ppermute | solution.py:222
  697.2 16.8 %collective-permute-start.42 = (bf16[2,48,1536]{2,1,0:T(8,128)(2,1)}, bf16[2,48,1536]{2,1,0:T(8,128)(2,1)}, u32[]{:S(2)}, u32[]{:S(2)}) collective-permute-start(bf16[2,48,1536]{2,1,0:T(8,128)(2,1)} %get-tuple-element.606), channel_id=1, source_target_pairs={{0,6},{1,7},{2,0},{3,1},{4,2},{5,3},{6,4},{7,5},{8,14},{9,15},{10,... | collective-permute-start | bytes 884744 | tf_op jit(solution)/shard_map/ppermute | solution.py:243
  700.6 37.8 %collective-permute-start.39 = (bf16[2,48,3072]{2,1,0:T(8,128)(2,1)S(1)}, bf16[2,48,3072]{2,1,0:T(8,128)(2,1)}, u32[]{:S(2)}, u32[]{:S(2)}) collective-permute-start(bf16[2,48,3072]{2,1,0:T(8,128)(2,1)S(1)} %reduce_sum.101), channel_id=1, source_target_pairs={{0,16},{1,17},{2,18},{3,19},{4,20},{5,21},{6,22},{7,23},{8,24},{9,... | collective-permute-start | bytes 1769480 | tf_op jit(solution)/shard_map/ppermute | solution.py:255
  701.0 37.3 %collective-permute-start.44 = (bf16[64,4608]{1,0:T(8,128)(2,1)}, bf16[64,4608]{1,0:T(8,128)(2,1)}, u32[]{:S(2)}, u32[]{:S(2)}) collective-permute-start(bf16[64,4608]{1,0:T(8,128)(2,1)} %bitcast.52), channel_id=1, source_target_pairs={{0,16},{1,17},{2,18},{3,19},{4,20},{5,21},{6,22},{7,23},{8,24},{9,... | collective-permute-start | bytes 1769480 | tf_op jit(solution)/shard_map/ppermute | solution.py:296
  703.0 35.4 %collective-permute-start.43 = (bf16[4,2,48,896]{3,2,1,0:T(8,128)(2,1)}, bf16[4,2,48,896]{3,2,1,0:T(8,128)(2,1)}, u32[]{:S(2)}, u32[]{:S(2)}) collective-permute-start(bf16[4,2,48,896]{3,2,1,0:T(8,128)(2,1)} %pad_maximum_fusion.16), channel_id=1, source_target_pairs={{0,1},{1,0},{2,3},{3,2},{4,5},{5,4},{6,7},{7,6},{8,9},{9,8},{10,11... | collective-permute-start | bytes 2064392 | tf_op jit(solution)/shard_map/ppermute | solution.py:233
  707.0 31.3 %all-to-all-start.10 = ((bf16[8,8,2560]{2,1,0:T(8,128)(2,1)}), bf16[8,8,2560]{2,1,0:T(8,128)(2,1)S(1)}, u32[]{:S(2)}, u32[]{:S(2)}) async-start(bf16[8,8,2560]{2,1,0:T(8,128)(2,1)} %broadcast_in_dim.73), calls=%async_computation.10 | async-start | bytes 655360 | tf_op jit(solution)/shard_map/all_to_all | solution.py:313
  711.6 26.7 %collective-permute-start.41 = (bf16[2,48,1536]{2,1,0:T(8,128)(2,1)}, bf16[2,48,1536]{2,1,0:T(8,128)(2,1)S(1)}, u32[]{:S(2)}, u32[]{:S(2)}) collective-permute-start(bf16[2,48,1536]{2,1,0:T(8,128)(2,1)} %get-tuple-element.607), channel_id=1, source_target_pairs={{0,4},{1,5},{2,6},{3,7},{4,0},{5,1},{6,2},{7,3},{8,12},{9,13},{10,... | collective-permute-start | bytes 884744 | tf_op jit(solution)/shard_map/ppermute | solution.py:243
  714.0 24.4 %collective-permute-start.40 = (bf16[2,48,1536]{2,1,0:T(8,128)(2,1)}, bf16[2,48,1536]{2,1,0:T(8,128)(2,1)}, u32[]{:S(2)}, u32[]{:S(2)}) collective-permute-start(bf16[2,48,1536]{2,1,0:T(8,128)(2,1)} %get-tuple-element.608), channel_id=1, source_target_pairs={{0,2},{1,3},{2,4},{3,5},{4,6},{5,7},{6,0},{7,1},{8,10},{9,11},{10,... | collective-permute-start | bytes 884744 | tf_op jit(solution)/shard_map/ppermute | solution.py:243
  741.3 26.3 %collective-permute-start.51 = (bf16[64,2560]{1,0:T(8,128)(2,1)S(1)}, bf16[64,2560]{1,0:T(8,128)(2,1)S(1)}, u32[]{:S(2)}, u32[]{:S(2)}) collective-permute-start(bf16[64,2560]{1,0:T(8,128)(2,1)S(1)} %bitcast.277), channel_id=1, source_target_pairs={{0,16},{1,17},{2,18},{3,19},{4,20},{5,21},{6,22},{7,23},{8,24},{9,... | collective-permute-start | bytes 983048 | tf_op jit(solution)/shard_map/ppermute | solution.py:296
  743.5 9.6 %collective-permute-start.52 = (bf16[2,64,144]{2,1,0:T(8,128)(2,1)S(1)}, bf16[2,64,144]{2,1,0:T(8,128)(2,1)S(1)}, u32[]{:S(2)}, u32[]{:S(2)}) collective-permute-start(bf16[2,64,144]{2,1,0:T(8,128)(2,1)S(1)} %pad_maximum_fusion.29), channel_id=1, source_target_pairs={{0,8},{1,9},{2,10},{3,11},{4,12},{5,13},{6,14},{7,15},{8,0},{9,1},... | collective-permute-start | bytes 110600 | tf_op jit(solution)/shard_map/ppermute | solution.py:305
  747.4 20.2 %collective-permute-start.47 = (bf16[2,48,1536]{2,1,0:T(8,128)(2,1)S(1)}, bf16[2,48,1536]{2,1,0:T(8,128)(2,1)S(1)}, u32[]{:S(2)}, u32[]{:S(2)}) collective-permute-start(bf16[2,48,1536]{2,1,0:T(8,128)(2,1)S(1)} %add_convert_fusion.6), channel_id=1, source_target_pairs={{0,16},{1,17},{2,18},{3,19},{4,20},{5,21},{6,22},{7,23},{8,24},{9,... | collective-permute-start | bytes 884744 | tf_op jit(solution)/shard_map/ppermute | solution.py:255
  753.0 7.1 collective-permute-start.50
  753.1 11.4 %collective-permute-start.49 = (bf16[2,48,896]{2,1,0:T(8,128)(2,1)S(1)}, bf16[2,48,896]{2,1,0:T(8,128)(2,1)S(1)}, u32[]{:S(2)}, u32[]{:S(2)}) collective-permute-start(bf16[2,48,896]{2,1,0:T(8,128)(2,1)S(1)} %get-tuple-element.615), channel_id=1, source_target_pairs={{0,4},{1,5},{2,6},{3,7},{4,0},{5,1},{6,2},{7,3},{8,12},{9,13},{10,... | collective-permute-start | bytes 516104 | tf_op jit(solution)/shard_map/ppermute | solution.py:243
  753.9 13.8 %collective-permute-start.46 = (bf16[144,3072]{1,0:T(8,128)(2,1)S(1)}, bf16[144,3072]{1,0:T(8,128)(2,1)S(1)}, u32[]{:S(2)}, u32[]{:S(2)}) collective-permute-start(bf16[144,3072]{1,0:T(8,128)(2,1)S(1)} %pad_maximum_fusion.14), channel_id=1, source_target_pairs={{0,8},{1,9},{2,10},{3,11},{4,12},{5,13},{6,14},{7,15},{8,0},{9,1},... | collective-permute-start | bytes 2654216 | tf_op jit(solution)/shard_map/ppermute | solution.py:265
  768.8 16.7 %all-to-all-start.11 = ((bf16[8,8,144]{2,1,0:T(8,128)(2,1)}), bf16[8,8,144]{2,1,0:T(8,128)(2,1)}, u32[]{:S(2)}, u32[]{:S(2)}) async-start(bf16[8,8,144]{2,1,0:T(8,128)(2,1)} %bitcast.223), calls=%async_computation.11 | async-start | bytes 65536 | tf_op jit(solution)/shard_map/all_to_all | solution.py:1174
  777.7 7.1 collective-permute-start.55
  778.3 7.2 collective-permute-start.54
  (79 other events, 481.1 us)

commit v5 on v4

--- a/solution.py
+++ b/solution.py
@@ -98,8 +98,10 @@
     return values
 
 
-def place_kernel(rows, half, apart, where, a0, a1, ax, b0, b1, bx, out, sems):
+def place_pieces(shape, apart, where, pieces, out, sems):
     x, core, z, y = where[0], where[1], where[2], where[3]
+    a0, a1, ax, b0, b1, bx = pieces
+    rows, half = shape[0] // 8, shape[1] // 2
     h = rows // PARTS
     copies = []
     for p0, p1, px, c in ((a0, a1, ax, core), (b0, b1, bx, 1 - core)):
@@ -123,6 +125,60 @@
         copy.wait()
 
 
+def placing(kernel, shape, apart, before, after):
+    def run(where, *refs):
+        pieces, refs = refs[:6], refs[6:]
+        inputs, rest = refs[: before + after], refs[before + after :]
+        *rest, laid, sems, out_sem = rest
+        outs, full, scratch = rest[0], rest[1], rest[2:]
+        step = pl.program_id(0)
+
+        @pl.when(step == 0)
+        def _():
+            place_pieces(shape, apart, where, pieces, laid, sems)
+            pltpu.make_async_copy(laid, full, out_sem).start()
+
+        kernel(*inputs[:before], laid, *inputs[before:], *outs, *scratch)
+
+        @pl.when(step == pl.num_programs(0) - 1)
+        def _():
+            pltpu.make_async_copy(laid, full, out_sem).wait()
+
+    return run
+
+
+def call_placed(kernel, gather, args, specs, before, out_shape, out_specs, scratch, **options):
+    if not gather.fast:
+        weight = gather.whole()
+        args = (*args[:before], weight, *args[before:])
+        specs = [*specs[:before], whole_block(weight), *specs[before:]]
+        got = pl.pallas_call(
+            kernel, in_specs=specs, out_shape=out_shape, out_specs=out_specs,
+            scratch_shapes=scratch, **options,
+        )(*args)
+        return (*got, weight)
+    shape = (8 * gather.rows, gather.width)
+    count = len(out_shape)
+    inner = placing(kernel, shape, gather.apart, before, len(args) - before)
+
+    def run(*refs):
+        at = 7 + len(args)
+        inner(*refs[:at], refs[at : at + count], *refs[at + count :])
+
+    any_space = pl.BlockSpec(memory_space=pl.ANY)
+    live = gather.live
+    pieces = [live[k] for k in ("own", "far", "both", "twin_own", "twin_far", "twin_both")]
+    return pl.pallas_call(
+        run,
+        in_specs=[pl.BlockSpec(memory_space=pltpu.SMEM)] + [any_space] * 6 + list(specs),
+        out_shape=list(out_shape) + [jax.ShapeDtypeStruct(shape, LOW)],
+        out_specs=list(out_specs) + [any_space],
+        scratch_shapes=list(scratch)
+        + [pltpu.VMEM(shape, LOW), pltpu.SemaphoreType.DMA((48,)), pltpu.SemaphoreType.DMA],
+        **options,
+    )(jnp.stack(coordinates()).astype(jnp.int32), *pieces, *args)
+
+
 class Gather:
     def __init__(self, weight):
         self.rows, self.width = weight.shape
@@ -159,43 +215,24 @@
                 self.live["twin_" + name] = lax.ppermute(self.live[name], AXES, TO_CORE)
 
     def whole(self):
-        if not self.fast:
-            return lax.all_gather(self.live["weight"], "fsdp", axis=0, tiled=True)
-        live = self.live
-        where = jnp.stack(coordinates()).astype(jnp.int32)
-        any_space = pl.BlockSpec(memory_space=pl.ANY)
-        shape = (8 * self.rows, self.width)
-        return pl.pallas_call(
-            partial(place_kernel, self.rows, self.width // 2, self.apart),
-            out_shape=jax.ShapeDtypeStruct(shape, LOW),
-            in_specs=[pl.BlockSpec(memory_space=pltpu.SMEM)] + [any_space] * 6,
-            out_specs=pl.BlockSpec(memory_space=pltpu.VMEM),
-            scratch_shapes=[pltpu.SemaphoreType.DMA((48,))],
-            compiler_params=pltpu.CompilerParams(vmem_limit_bytes=40 * MIB),
-            cost_estimate=pl.CostEstimate(
-                flops=0, bytes_accessed=4 * shape[0] * shape[1], transcendentals=0
-            ),
-            name="place",
-        )(
-            where,
-            live["own"],
-            live["far"],
-            live["both"],
-            live["twin_own"],
-            live["twin_far"],
-            live["twin_both"],
-        )
+        return lax.all_gather(self.live["weight"], "fsdp", axis=0, tiled=True)
 
 
 class Scatter:
-    def __init__(self, left, send, keep):
-        self.left, self.fast = None, is_fast() and left.shape[1] % 384 == 0
-        self.live = {"left": left, "send": send, "keep": keep}
+    def __init__(self, left, send=None, keep=None, pair=None):
+        self.left, self.fast = left, is_fast() and left.shape[1] % 384 == 0
+        self.live = {"send": send, "keep": keep} if pair is None else {"pair": pair}
+
+    def operand(self, name):
+        if "pair" in self.live:
+            return self.live["pair"][("send", "keep").index(name)]
+        return self.live[name]
 
     def first(self):
         live = self.live
         if self.fast:
-            live["out"] = dot_left(live["left"], live.pop("send")).astype(LOW)
+            live["out"] = dot_left(self.left, self.operand("send")).astype(LOW)
+            live.pop("send", None)
 
     def core(self):
         if self.fast:
@@ -204,8 +241,9 @@
     def second(self):
         live = self.live
         if self.fast:
-            product = dot_left(live.pop("left"), live.pop("keep"))
+            product = dot_left(self.left, self.operand("keep"))
             live["kept"] = (product + live.pop("got").astype(WIDE)).astype(LOW)
+            live.pop("keep", None)
 
     def join(self, other):
         if self.fast:
@@ -216,42 +254,103 @@
         rows, half = self.live["kept"].shape
         return self.live["kept"].reshape(HIGH_Z, 2, PARTS, rows // 24, half)
 
-    def x(self):
-        if self.fast:
-            x, _, _, _ = coordinates()
-            self.live["side"] = lax.ppermute(pick(self.view(), 1 - x, 2), AXES, TO_X)
-
-    def row(self, index):
+    def cut(self, start, sizes):
+        view = self.view()
+        return lax.dynamic_slice(view, (*start, 0, 0), (*sizes, *view.shape[3:])).reshape(
+            tuple(k for k in sizes if k > 1) + view.shape[3:]
+        )
+
+    def x(self, half=None):
+        if not self.fast:
+            return
         x, _, _, _ = coordinates()
-        view = pick(self.view(), index, 1)
-        own = pick(view, x, 1).astype(WIDE) + pick(self.live["side"], index, 1).astype(WIDE)
-        return jnp.stack([own.astype(LOW), view[:, 2]], 1)
-
-    def y(self):
+        if half is None:
+            self.live["side"] = lax.ppermute(
+                self.cut((0, 0, 1 - x), (HIGH_Z, 2, 1)), AXES, TO_X
+            )
+        else:
+            self.live["side_" + str(half)] = lax.ppermute(
+                self.cut((2 * half, 0, 1 - x), (2, 2, 1)), AXES, TO_X
+            )
+
+    def own(self, index):
+        x, _, _, _ = coordinates()
+        live = self.live
+        sides = [live["side"]] if "side" in live else [live["side_0"], live["side_1"]]
+        sides = [pick(side, index, 1) for side in sides]
+        side = jnp.concatenate(sides, 0) if len(sides) > 1 else sides[0]
+        mine = self.cut((0, index, x), (HIGH_Z, 1, 1))
+        return (mine.astype(WIDE) + side.astype(WIDE)).astype(LOW)
+
+    def common(self, index):
+        return self.cut((0, index, 2), (HIGH_Z, 1, 1))
+
+    def y_common(self):
         if self.fast:
             _, _, _, y = coordinates()
-            self.live["far"] = lax.ppermute(self.row(1 - y), AXES, TO_Y)
-
-    def z(self, apart=False):
+            self.live["far_common"] = lax.ppermute(self.common(1 - y), AXES, TO_Y)
+
+    def y_own(self):
         if self.fast:
             _, _, _, y = coordinates()
-            line = (self.row(y).astype(WIDE) + self.live["far"].astype(WIDE)).astype(LOW)
-            if apart:
-                _, _, z, _ = coordinates()
-                live = {"0": pick(line, z, 0)}
-                for k in (2, 1, 3):
-                    live[str(k)] = lax.ppermute(pick(line, (z + k) % 4, 0), AXES, TO_Z[k])
-                self.live = {"lines": live}
+            self.live["far_own"] = lax.ppermute(self.own(1 - y), AXES, TO_Y)
+
+    def y_both(self):
+        if self.fast:
+            _, _, _, y = coordinates()
+            both = jnp.stack([self.own(1 - y), self.common(1 - y)], 1)
+            self.live["far_both"] = lax.ppermute(both, AXES, TO_Y)
+
+    def line(self, name):
+        _, _, _, y = coordinates()
+        mine = self.common(y) if name == "common" else self.own(y)
+        if "far_both" in self.live:
+            far = self.live["far_both"][:, 1 if name == "common" else 0]
+        else:
+            far = self.live.pop("far_" + name)
+        return (mine.astype(WIDE) + far.astype(WIDE)).astype(LOW)
+
+    def z_common(self):
+        if self.fast:
+            self.live["sum_common"] = {"all": over_z(self.line("common"))}
+
+    def z_own(self, apart=False):
+        if not self.fast:
+            return
+        line = self.line("own")
+        self.forget()
+        if not apart:
+            self.live["sum_own"] = {"all": over_z(line)}
+            return
+        _, _, z, _ = coordinates()
+        lines = {"0": pick(line, z, 0)}
+        for k in (2, 1, 3):
+            lines[str(k)] = lax.ppermute(pick(line, (z + k) % 4, 0), AXES, TO_Z[k])
+        self.live["sum_own"] = lines
+
+    def z_both(self):
+        if self.fast:
+            lines = jnp.stack([self.line("own"), self.line("common")], 1)
+            self.forget()
+            self.live["sum_both"] = {"all": over_z(lines)}
+
+    def forget(self):
+        for name in ("kept", "side", "side_0", "side_1", "far_both"):
+            self.live.pop(name, None)
+
+    def total(self, name):
+        lines = self.live.pop(name)
+        if "all" in lines:
+            return jnp.sum(lines["all"].astype(WIDE), axis=0).astype(LOW)
+        wide = [lines[k].astype(WIDE) for k in ("0", "1", "2", "3")]
+        return (wide[0] + wide[1] + wide[2] + wide[3]).astype(LOW)
+
+    def last_x(self):
+        if self.fast:
+            if "sum_both" in self.live:
+                part = self.total("sum_both")
             else:
-                self.live = {"line": over_z(line)}
-
-    def last_x(self):
-        if self.fast:
-            if "lines" in self.live:
-                lines = [self.live["lines"][k].astype(WIDE) for k in ("0", "1", "2", "3")]
-                part = (lines[0] + lines[1] + lines[2] + lines[3]).astype(LOW)
-            else:
-                part = jnp.sum(self.live["line"].astype(WIDE), axis=0).astype(LOW)
+                part = jnp.stack([self.total("sum_own"), self.total("sum_common")], 0)
             self.live = {"part": part, "other": lax.ppermute(part, AXES, TO_X)}
 
     def last_core(self):
@@ -272,8 +371,8 @@
             second = jnp.where(core == 0, twin, done)
             return first.astype(WIDE), second.astype(WIDE)
         _, core, _, _ = coordinates()
-        left = self.live["left"]
-        keep, send = self.live["keep"], self.live["send"]
+        left = self.left
+        keep, send = self.operand("keep"), self.operand("send")
         first = jnp.where(core == 0, keep, send)
         second = jnp.where(core == 0, send, keep)
         sums = []
@@ -383,20 +482,20 @@
                 o_ref[h] = raw.astype(LOW) + tail
 
 
-def prepare(first, x, hot, mod, w, gq, gk, rot, qt, kt, vt, heads, hd):
+def prepare(first, x, hot, mod, gather, gq, gk, rot, qt, kt, vt, heads, hd):
     n, width = x.shape
     rows = pl.BlockSpec((BLOCK, width), lambda i: (i, 0))
     head_spec = pl.BlockSpec((heads, BLOCK, LANES), lambda i: (0, i, 0))
     tail = pl.BlockSpec((BLOCK, LANES), lambda i: (i, 0))
     normed_spec, normed_shape = [rows], [jax.ShapeDtypeStruct((n, width), LOW)]
-    return pl.pallas_call(
+    return call_placed(
         partial(prepare_kernel, first, heads, hd),
-        grid=(n // BLOCK,),
-        in_specs=[
+        gather,
+        (x, hot, mod, gq, gk, rot, qt, kt, vt),
+        [
             rows,
             pl.BlockSpec((BLOCK, hot.shape[1]), lambda i: (i, 0)),
             whole_block(mod),
-            whole_block(w),
             whole_block(gq),
             whole_block(gk),
             pl.BlockSpec((3, BLOCK, LANES), lambda i: (0, i, 0)),
@@ -404,16 +503,17 @@
             tail,
             pl.BlockSpec((1, LANES), lambda i: (0, 0)),
         ],
-        out_specs=(normed_spec if first else []) + [head_spec] * 5,
-        out_shape=(normed_shape if first else [])
-        + [jax.ShapeDtypeStruct((heads, n, LANES), LOW)] * 5,
-        scratch_shapes=[pltpu.VMEM((BLOCK, part_width(hd) + LANES), WIDE)],
+        3,
+        (normed_shape if first else []) + [jax.ShapeDtypeStruct((heads, n, LANES), LOW)] * 5,
+        (normed_spec if first else []) + [head_spec] * 5,
+        [pltpu.VMEM((BLOCK, part_width(hd) + LANES), WIDE)],
+        grid=(n // BLOCK,),
         compiler_params=pltpu.CompilerParams(vmem_limit_bytes=56 * MIB),
         cost_estimate=pl.CostEstimate(
-            flops=2 * n * width * w.shape[1], bytes_accessed=20 * MIB, transcendentals=0
+            flops=12 * n * width * width // 2, bytes_accessed=20 * MIB, transcendentals=0
         ),
         name="prepare",
-    )(x, hot, mod, w, gq, gk, rot, qt, kt, vt)
+    )
 
 
 def near_blocks(run):
@@ -422,34 +522,29 @@
 
     @pl.when(i == 0)
     def _():
-        run((0, 1))
+        run(pl.ds(0, 2 * BLOCK))
 
     @pl.when(i == n - 1)
     def _():
-        run((-1, 0))
+        run(pl.ds(pl.multiple_of((i - 1) * BLOCK, BLOCK), 2 * BLOCK))
 
     @pl.when((i > 0) & (i < n - 1))
     def _():
-        run((-1, 0, 1))
+        run(pl.ds(pl.multiple_of((i - 1) * BLOCK, BLOCK), 3 * BLOCK))
 
 
 def attend_kernel(hd, c, *refs):
-    i = pl.program_id(0)
     mix_ref = refs[6]
     lane = lax.broadcasted_iota(jnp.int32, (BLOCK, LANES), 1)
     heads = refs[0].shape[0]
 
-    def run(blocks):
+    def run(at):
         for head in range(2 * heads):
             half, h = head // heads, head % heads
             q_ref, k_ref, v_ref = refs[3 * half : 3 * half + 3]
             q = q_ref[h]
-            total = None
-            for j in blocks:
-                at = pl.ds(pl.multiple_of((i + j) * BLOCK, BLOCK), BLOCK)
-                p = jnp.exp2(dot_right(q, k_ref[h, at]) * c).astype(LOW)
-                term = dot(p, v_ref[h, at])
-                total = term if total is None else total + term
+            p = jnp.exp2(dot_right(q, k_ref[h, at]) * c).astype(LOW)
+            total = dot(p, v_ref[h, at])
             norm = total[:, hd : hd + 1]
             out = (total * (1.0 / norm)).astype(LOW)
             mix_ref[:, hd * head : hd * (head + 1)] = out[:, :hd]
@@ -533,16 +628,16 @@
 
 
 def back_kernel(
-    hd, c, score_scale, core_ref, q_ref, k_ref, v_ref, do_ref, rq_ref, rk_ref, rot_ref, gq_ref, gk_ref,
-    joint_ref, gain_ref, dq_scr, dk_scr, dv_scr, gain_scr,
+    hd, c, score_scale, part, core_ref, q_ref, k_ref, v_ref, do_ref, rq_ref, rk_ref, rot_ref, gq_ref, gk_ref,
+    *refs,
 ):
+    out_ref, gain_ref, joint_ref, dq_scr, dk_scr, dv_scr, gain_scr, out_sem = refs[part:]
     i = pl.program_id(0)
     n = pl.num_programs(0)
     heads = q_ref.shape[0]
     width = GROUP * hd
-    tail = joint_ref.shape[2] - 3 * width
-    core = core_ref[0]
-    slots = (1 - core, core)
+    tail = joint_ref.shape[1] - 3 * width
+    slot = core_ref[0] if part else 1 - core_ref[0]
 
     @pl.when(i == 0)
     def _():
@@ -551,27 +646,20 @@
 
     ones = jnp.full((LANES, LANES), 1.0, LOW)
 
-    def run(blocks):
+    def run(at):
         def body(h, carry):
             kk = k_ref[h]
             vv = v_ref[h]
-            dk = dv = None
-            for j in blocks:
-                at = pl.ds(pl.multiple_of((i + j) * BLOCK, BLOCK), BLOCK)
-                q = q_ref[h, at]
-                do = do_ref[h, at]
-                p = jnp.exp2(dot_right(kk, q) * c)
-                term = dot(p.astype(LOW), do)
-                dv = term if dv is None else dv + term
-                ds = (p * dot_right(vv, do)).astype(LOW)
-                term = dot(ds, q)
-                dk = term if dk is None else dk + term
-                dq_scr[h, at] += dot_left(ds, kk)
-            dk_scr[h] = dk
-            dv_scr[h] = dv
+            q = q_ref[h, at]
+            do = do_ref[h, at]
+            p = jnp.exp2(dot_right(kk, q) * c)
+            dv_scr[h] = dot(p.astype(LOW), do)
+            ds = (p * dot_right(vv, do)).astype(LOW)
+            dk_scr[h] = dot(ds, q)
+            dq_scr[h, at] += dot_left(ds, kk)
             return carry
 
-        lax.fori_loop(0, heads, body, 0, unroll=2)
+        lax.fori_loop(0, heads, body, 0, unroll=GROUP)
 
     near_blocks(run)
 
@@ -590,14 +678,13 @@
 
     here = pl.ds(pl.multiple_of(i * BLOCK, BLOCK), BLOCK)
     rot = [rot_ref[t, here] for t in range(3)]
-    for slot in range(2):
-        joint_ref[slot, here, 3 * width :] = jnp.zeros((BLOCK, tail), LOW)
+    joint_ref[here, 3 * width :] = jnp.zeros((BLOCK, tail), LOW)
     for h in range(heads):
-        slot, at = slots[h // GROUP], hd * (h % GROUP)
+        at = hd * h
         grad = finish(dk_scr[h], rk_ref[h], rot, gk_ref[...], 1)
-        joint_ref[slot, here, width + at : width + at + hd] = grad[:, :hd]
+        joint_ref[here, width + at : width + at + hd] = grad[:, :hd]
         value = dv_scr[h].astype(LOW)
-        joint_ref[slot, here, 2 * width + at : 2 * width + at + hd] = value[:, :hd]
+        joint_ref[here, 2 * width + at : 2 * width + at + hd] = value[:, :hd]
 
     @pl.when(i == n - 1)
     def _():
@@ -605,53 +692,59 @@
             at = pl.ds(pl.multiple_of(b * BLOCK, BLOCK), BLOCK)
             turn = [rot_ref[t, at] for t in range(3)]
             for h in range(heads):
-                start = hd * (h % GROUP)
+                start = hd * h
                 grad = finish(dq_scr[h, at], rq_ref[h, at], turn, gq_ref[...], 0)
-                joint_ref[slots[h // GROUP], at, start : start + hd] = grad[:, :hd]
+                joint_ref[at, start : start + hd] = grad[:, :hd]
             return carry
 
         lax.fori_loop(0, n, rows, 0)
         gain_ref[...] = gain_scr[...]
-
-
-def attend_back(part, core, q2, k, v, do, rq, rk, rot, gq, gk, hd, c, score_scale):
+        copy = pltpu.make_async_copy(joint_ref, out_ref.at[slot], out_sem)
+        copy.start()
+        copy.wait()
+
+
+def attend_back(half, part, before, core, q2, k, v, do, rq, rk, rot, gq, gk, hd, c, score_scale):
     _, n, _ = q2.shape
     one = pl.Buffered(1)
-    full = pl.BlockSpec((2 * GROUP, n, LANES), lambda i: (0, 0, 0), pipeline_mode=one)
-    block = pl.BlockSpec((2 * GROUP, BLOCK, LANES), lambda i: (0, i, 0))
+    full = pl.BlockSpec((GROUP, n, LANES), lambda i: (part, 0, 0), pipeline_mode=one)
+    block = pl.BlockSpec((GROUP, BLOCK, LANES), lambda i: (part, i, 0))
     small = pl.BlockSpec((1, LANES), lambda i: (0, 0))
+    any_space = pl.BlockSpec(memory_space=pl.ANY)
     width = part_width(hd)
+    at = 2 * half + part
     return pl.pallas_call(
-        partial(back_kernel, hd, c, score_scale),
+        partial(back_kernel, hd, c, score_scale, part),
         grid=(n // BLOCK,),
         in_specs=[
             pl.BlockSpec(memory_space=pltpu.SMEM),
             *(full, block, block),
-            pl.BlockSpec((2 * GROUP, n, LANES), lambda i: (part, 0, 0), pipeline_mode=one),
+            pl.BlockSpec((GROUP, n, LANES), lambda i: (at, 0, 0), pipeline_mode=one),
             *(full, block, whole_block(rot), small, small),
+            *([any_space] if part else []),
         ],
-        out_specs=[
-            pl.BlockSpec((2, n, width), lambda i: (0, 0, 0), pipeline_mode=one),
-            pl.BlockSpec((2, 8, LANES), lambda i: (0, 0, 0)),
-        ],
+        out_specs=[any_space, pl.BlockSpec((2, 8, LANES), lambda i: (0, 0, 0))],
         out_shape=[
             jax.ShapeDtypeStruct((2, n, width), LOW),
             jax.ShapeDtypeStruct((2, 8, LANES), WIDE),
         ],
         scratch_shapes=[
-            pltpu.VMEM((2 * GROUP, n, LANES), WIDE),
-            pltpu.VMEM((2 * GROUP, BLOCK, LANES), WIDE),
-            pltpu.VMEM((2 * GROUP, BLOCK, LANES), WIDE),
+            pltpu.VMEM((n, width), LOW),
+            pltpu.VMEM((GROUP, n, LANES), WIDE),
+            pltpu.VMEM((GROUP, BLOCK, LANES), WIDE),
+            pltpu.VMEM((GROUP, BLOCK, LANES), WIDE),
             pltpu.VMEM((2, 8, LANES), WIDE),
+            pltpu.SemaphoreType.DMA,
         ],
+        input_output_aliases={10: 0} if part else {},
         compiler_params=pltpu.CompilerParams(vmem_limit_bytes=56 * MIB),
         cost_estimate=pl.CostEstimate(
-            flops=10 * n * 640 * LANES * 2 * GROUP,
-            bytes_accessed=20 * MIB,
-            transcendentals=2 * GROUP * n * 640,
+            flops=10 * n * 640 * LANES * GROUP,
+            bytes_accessed=10 * MIB,
+            transcendentals=GROUP * n * 640,
         ),
         name="attend_back",
-    )(core, q2, k, v, do, rq, rk, rot, gq, gk)
+    )(core, q2, k, v, do, rq, rk, rot, gq, gk, *([before] if part else []))
 
 
 def normed_rows(values):
@@ -685,26 +778,38 @@
     return pl.BlockSpec((BLOCK, array.shape[1]), lambda i: (i, 0))
 
 
-def call_rows(kernel, name, streamed, fixed, outs, sums=(), core=None, scratch=()):
+def call_rows(
+    kernel, name, streamed, fixed, outs, sums=(), core=None, scratch=(), gather=None
+):
     n = streamed[0].shape[-2]
     work = sum(2 * n * a.size for a in fixed if a.shape[0] > 256)
     moved = sum(a.size * a.dtype.itemsize for a in (*streamed, *fixed))
     scalars = () if core is None else (core,)
-    return pl.pallas_call(
-        kernel,
+    args = (*scalars, *streamed, *fixed)
+    specs = [pl.BlockSpec(memory_space=pltpu.SMEM) for _ in scalars]
+    specs += [rows_of(a) for a in streamed] + [whole_block(a) for a in fixed]
+    out_specs = [pl.BlockSpec((BLOCK, w), lambda i: (i, 0)) for w, _ in outs]
+    out_specs += [pl.BlockSpec(shape, lambda i: (0, 0)) for shape in sums]
+    out_shape = [jax.ShapeDtypeStruct((n, w), t) for w, t in outs]
+    out_shape += [jax.ShapeDtypeStruct(shape, WIDE) for shape in sums]
+    scratch = [pltpu.VMEM(shape, WIDE) for shape in scratch]
+    if gather is not None:
+        work += 2 * n * gather.rows * lax.axis_size("fsdp") * gather.width
+    options = dict(
         grid=(n // BLOCK,),
-        in_specs=[pl.BlockSpec(memory_space=pltpu.SMEM) for _ in scalars]
-        + [rows_of(a) for a in streamed]
-        + [whole_block(a) for a in fixed],
-        out_specs=[pl.BlockSpec((BLOCK, w), lambda i: (i, 0)) for w, _ in outs]
-        + [pl.BlockSpec(shape, lambda i: (0, 0)) for shape in sums],
-        out_shape=[jax.ShapeDtypeStruct((n, w), t) for w, t in outs]
-        + [jax.ShapeDtypeStruct(shape, WIDE) for shape in sums],
-        scratch_shapes=[pltpu.VMEM(shape, WIDE) for shape in scratch],
         compiler_params=pltpu.CompilerParams(vmem_limit_bytes=56 * MIB),
         cost_estimate=pl.CostEstimate(flops=work, bytes_accessed=moved, transcendentals=0),
         name=name,
-    )(*scalars, *streamed, *fixed)
+    )
+    if gather is not None:
+        before = len(scalars) + len(streamed)
+        return call_placed(
+            kernel, gather, args, specs, before, out_shape, out_specs, scratch, **options
+        )
+    return pl.pallas_call(
+        kernel, in_specs=specs, out_specs=out_specs, out_shape=out_shape, scratch_shapes=scratch,
+        **options,
+    )(*args)
 
 
 def join_kernel(
@@ -724,7 +829,7 @@
 
 
 def gate_kernel(x_ref, w_ref, out_ref):
-    out_ref[...] = dot(x_ref[...], w_ref[...]).astype(LOW)
+    out_ref[...] = dot(x_ref[...], w_ref[:, : out_ref.shape[1]]).astype(LOW)
 
 
 def up_kernel(x_ref, gate_ref, w_ref, up_ref, inner_ref):
@@ -778,12 +883,12 @@
 
     @pl.when(core_ref[0] == 0)
     def _():
-        total_ref[...] = dot_right(mine_ref[...], wg_ref[...])
+        total_ref[...] = dot_right(mine_ref[...], wg_ref[:, : mine_ref.shape[1]])
         total_ref[...] += dot_right(send_ref[...], wu_ref[...])
 
     @pl.when(core_ref[0] != 0)
     def _():
-        total_ref[...] = dot_right(send_ref[...], wg_ref[...])
+        total_ref[...] = dot_right(send_ref[...], wg_ref[:, : send_ref.shape[1]])
         total_ref[...] += dot_right(mine_ref[...], wu_ref[...])
 
     grad = total_ref[...]
@@ -983,9 +1088,8 @@
     g_gate.z()
     rot, query_tail, key_tail, hot, keep = tables
     set_out = (gain_q, gain_k, rot, query_tail, key_tail, value_tail, heads // 2, hd)
-    one_full = g_one.whole()
-    normed_a, q_one, k_one, v_one, rq_one, rk_one = prepare(
-        True, inputs_low, hot, mod_a, one_full, *set_out
+    normed_a, q_one, k_one, v_one, rq_one, rk_one, one_full = prepare(
+        True, inputs_low, hot, mod_a, g_one, *set_out
     )
     gathers = gathers[1:]
     normed_a, q_one, k_one, v_one, rq_one, rk_one, one_full = hold(
@@ -995,9 +1099,8 @@
     g_two.core("both")
     g_gate.y()
     g_up.z()
-    two_full = g_two.whole()
-    q_two, k_two, v_two, rq_two, rk_two = prepare(
-        False, normed_a, hot, mod_a, two_full, *set_out
+    q_two, k_two, v_two, rq_two, rk_two, two_full = prepare(
+        False, normed_a, hot, mod_a, g_two, *set_out
     )
     gathers = gathers[1:]
     normed_a, q_two, k_two, v_two, rq_two, rk_two, two_full, q_one, k_one, v_one = hold(
@@ -1020,28 +1123,30 @@
         partial(join_kernel, cut), "join", (mixed, inputs_low, hot, keep), (two_full, mod_mid),
         ((width, LOW), (width, WIDE), (width, LOW)),
     )
-    middle, normed_b, attended = hold(gathers, (middle, normed_b, attended))
+    middle, normed_b, attended = hold([g_gate], (middle, normed_b, attended))
+
+    gate, gate_full = call_rows(
+        gate_kernel, "gate", (normed_b,), (), ((ff, LOW),), gather=g_gate
+    )
+    gathers = [g_up, g_down]
+    gate, gate_full, normed_b, middle, attended = hold(
+        gathers, (gate, gate_full, normed_b, middle, attended)
+    )
 
     g_up.core("both")
     g_down.x()
     g_down.core("own", "far")
-    gate_full = g_gate.whole()
-    (gate,) = call_rows(gate_kernel, "gate", (normed_b,), (gate_full,), ((ff, LOW),))
-    gathers = gathers[1:]
-    gate, gate_full, normed_b = hold(gathers, (gate, gate_full, normed_b))
+    normed_b = hold([g_up], normed_b)
+    up, inner, up_full = call_rows(
+        up_kernel, "up", (normed_b, gate), (), ((ff, LOW), (ff, LOW)), gather=g_up
+    )
+    gathers = [g_down]
+    inner, up, gate, up_full, middle = hold(gathers, (inner, up, gate, up_full, middle))
 
     g_down.core("both")
-    up_full = g_up.whole()
-    up, inner = call_rows(
-        up_kernel, "up", (normed_b, gate), (up_full,), ((ff, LOW), (ff, LOW))
-    )
-    gathers = gathers[1:]
-    inner, up, gate, up_full, middle = hold(gathers, (inner, up, gate, up_full, middle))
-
-    down_full = g_down.whole()
-    block_out, grad_returned, sums_gate_b = call_rows(
-        down_kernel, "down", (inner, middle, out_grad[0], hot, keep),
-        (down_full, mod_b[:, 3 * width :]), ((width, LOW), (odd, LOW)), ((2 * items, width),),
+    block_out, grad_returned, sums_gate_b, down_full = call_rows(
+        down_kernel, "down", (inner, middle, out_grad[0], hot, keep), (mod_b[:, 3 * width :],),
+        ((width, LOW), (odd, LOW)), ((2 * items, width),), gather=g_down,
     )
 
     s_down = Scatter(inner, *column_halves(grad_returned))
@@ -1077,71 +1182,80 @@
     plans = [s_down, s_wide, s_proj]
     grad_middle, grad_attended, sums_mid = hold(plans, (grad_middle, grad_attended, sums_mid))
 
-    s_down.y()
     s_wide.second()
+    grad_attended = hold([s_wide], grad_attended)
+    s_wide.x(0)
+    s_down.y_both()
     s_proj.first()
     late_sums = jnp.concatenate([sums_mid[:items], sums_gate_b[:items]], axis=1).astype(LOW)
     grad_mixed = spread(grad_attended, two_full, mixed, heads, hd, cut)
-    late_sums, grad_mixed = hold(plans, (late_sums, grad_mixed))
+    late_sums, grad_mixed = hold([s_down, s_wide, s_proj], (late_sums, grad_mixed))
 
     back = partial(
         attend_back, core=core_place, rot=rot, gq=gain_q, gk=gain_k, hd=hd, c=c,
         score_scale=score_scale,
     )
-    s_down.z()
-    s_wide.x()
+    one = dict(q2=q2_one, k=k_one, v=v_one, rq=rq_one, rk=rk_one)
+    two = dict(q2=q2_two, k=k_two, v=v_two, rq=rq_two, rk=rk_two)
+    s_down.z_both()
+    s_wide.x(1)
+    s_wide.y_common()
     s_proj.core()
-    joint_one, gains_0 = back(
-        0, q2=q2_one, k=k_one, v=v_one, do=grad_mixed, rq=rq_one, rk=rk_one
-    )
-    s_head = Scatter(normed_a, joint_one[0], joint_one[1])
+    joint_one, gains_0 = back(0, 0, None, do=grad_mixed, **one)
+    joint_one, gains_0, grad_mixed = hold([s_down, s_wide, s_proj], (joint_one, gains_0, grad_mixed))
+
+    s_down.last_x()
+    s_wide.y_own()
+    s_wide.z_common()
+    s_proj.second()
+    joint_one, gains_1 = back(0, 1, joint_one, do=grad_mixed, **one)
+    s_head = Scatter(normed_a, pair=joint_one)
     s_head.first()
-    s_proj.second()
-    plans = plans + [s_head]
-    joint_one, gains_0, grad_mixed, late_sums = hold(
-        plans, (joint_one, gains_0, grad_mixed, late_sums)
-    )
+    gains_1, grad_mixed = hold([s_down, s_wide, s_proj, s_head], (gains_1, grad_mixed))
 
     s_head.core()
-    s_wide.y()
-    late_sums = hold([s_head], late_sums)
-    s_down.last_x()
+    s_down.last_core()
+    s_wide.z_own()
+    joint_two, gains_2 = back(1, 0, None, do=grad_mixed, **two)
     s_head.second()
     s_head.join(s_proj)
-    grad_mixed = hold([s_head], grad_mixed)
+    joint_two, gains_2, grad_mixed, late_sums = hold(
+        [s_down, s_wide, s_head], (joint_two, gains_2, grad_mixed, late_sums)
+    )
+
     s_head.x()
+    s_head.y_common()
+    s_wide.last_x()
     late_group = gather_rows(late_sums)
-    joint_two, gains_1 = back(
-        1, q2=q2_two, k=k_two, v=v_two, do=grad_mixed, rq=rq_two, rk=rk_two
-    )
-    s_tail = Scatter(normed_a, joint_two[0], joint_two[1])
+    joint_two, gains_3 = back(1, 1, joint_two, do=grad_mixed, **two)
+    s_tail = Scatter(normed_a, pair=joint_two)
     s_tail.first()
-    plans = [s_down, s_wide, s_head, s_tail]
-    joint_one, joint_two, gains_1, late_group = hold(
-        plans, (joint_one, joint_two, gains_1, late_group)
-    )
+    gains_3, late_group = hold([s_wide, s_head, s_tail], (gains_3, late_group))
 
     s_tail.core()
-    s_down.last_core()
-    s_wide.z()
-    s_head.y()
+    s_head.y_own()
+    s_head.z_common()
     s_tail.second()
-    joint_two = hold([s_tail], joint_two)
+    grad_middle = hold([s_tail], grad_middle)
     s_tail.x()
+    s_wide.last_core()
     grad_input, sums_early = call_rows(
         input_back_kernel, "input_back",
-        (joint_one, joint_two, grad_middle, inputs_low, hot),
+        (s_head.live["pair"], s_tail.live["pair"], grad_middle, inputs_low, hot),
         (one_full, two_full, mod_a), ((width, WIDE),), ((2 * items, 2 * width),),
         core=core_place,
     )
+    if s_head.fast:
+        s_head.live.pop("pair")
+        s_tail.live.pop("pair")
     plans = [s_down, s_wide, s_head, s_tail]
     grad_input, sums_early, late_group = hold(plans, (grad_input, sums_early, late_group))
 
-    s_wide.last_x()
-    s_head.z(apart=True)
-    s_tail.y()
+    s_head.z_own(apart=True)
+    s_tail.y_both()
     early_sums = sums_early[:items]
-    gain_row = jnp.sum(gains_0 + gains_1, axis=1)[:, :hd].reshape(1, 2 * hd)
+    gains = gains_0 + gains_1 + gains_2 + gains_3
+    gain_row = jnp.sum(gains, axis=1)[:, :hd].reshape(1, 2 * hd)
     gain_high = gain_row.astype(LOW).astype(WIDE)
     gain_block = jnp.concatenate([gain_high, gain_row - gain_high], axis=0)
     gain_block = jnp.pad(gain_block, ((0, items - 2), (0, 2 * LANES - 2 * hd)))
@@ -1150,14 +1264,14 @@
     act_far = across_x(group_act)
     late_far = across_x(late_group)
     shard_down = jnp.concatenate(s_down.halves(), axis=1)[:, :width]
-    plans = [s_wide, s_head, s_tail]
-    early_group, late_far, act_far, shard_down = hold(
-        plans, (early_group, late_far, act_far, shard_down)
-    )
-
-    s_wide.last_core()
+    shard_wide = jnp.concatenate(s_wide.halves(), axis=1)
+    plans = [s_head, s_tail]
+    early_group, late_far, act_far, shard_down, shard_wide = hold(
+        plans, (early_group, late_far, act_far, shard_down, shard_wide)
+    )
+
     s_head.last_x()
-    s_tail.z(apart=True)
+    s_tail.z_both()
     early_far = across_x(early_group)
     every_act = across_replicas(group_act, act_far)
     late_every = across_replicas(late_group, late_far)
@@ -1174,8 +1288,7 @@
     cond_back = lax.all_to_all(cond_part.astype(LOW).reshape(shards, items, -1), "fsdp", 0, 0)
     early_every = across_replicas(early_group, early_far)
     shard_early = dot_left(every_act, early_every[:, :early])
-    shard_wide = jnp.concatenate(s_wide.halves(), axis=1)
-    shard_early, shard_wide = hold(plans, (shard_early, shard_wide))
+    shard_early = hold(plans, shard_early)
     shard_ada = jnp.concatenate([shard_early, shard_late], axis=1)
     bias_sums = jnp.concatenate(
         [

time: 812 us -> 788 us (0.970)
  Pallas kernels: 324 us -> 293 us
  local copies, waits for them, and re-layouts: 86.6 us -> 70.2 us
  starting transfers between devices: 105 us -> 118 us
  other arithmetic: 80.3 us -> 92.1 us
    pallas_call x16 -> x13, Pallas kernels: 282 us -> 256 us  [the longest x5 90.2 us: call_placed(): pl.pallas_call(run, in_specs=[pl.BlockSpec(memory_space=pltpu.SMEM)] + [a...]
    all_to_all x7 -> x10, starting transfers between devices: 31.2 us -> 45.5 us  [over_z(): return lax.all_to_all(operand, 'fsdp', 0, 0, axis_index_groups=Z_GROUPS)]
    ppermute x14, waiting for transfers between devices: 32.2 us -> 19 us  [the longest x2 8.61 us: x(): lax.ppermute(self.cut((2 * half, 0, 1 - x), (2, 2, 1)), AXES, TO_X)]
    unnamed x146 -> x122, local copies, waits for them, and re-layouts: 25.8 us -> 13.7 us
    ppermute x4, waiting for transfers between devices: 0.01 us -> 10.1 us  [last_x(): self.live = {'part': part, 'other': lax.ppermute(part, AXES, TO_X)}]
    squeeze x14 -> x5, local copies, waits for them, and re-layouts: 13.4 us -> 3.87 us  [pick(): return lax.dynamic_index_in_dim(operand, index, axis, keepdims=False)]
    reshape x1 -> x8, local copies, waits for them, and re-layouts: 0.08 us -> 8.9 us  [the longest x7 8.14 us: cut(): lax.dynamic_slice(view, (*start, 0, 0), (*sizes, *view.shape[3:]))]
    ppermute x5, waiting for transfers between devices: 22.3 us -> 30.6 us  [y(): self.live['far'] = lax.ppermute(self.live['own'], AXES, TO_Y)]
  transfers between devices with their start and end apart: 70 -> 73, of which waited for: 16 -> 26; matrix products, arithmetic and copies ran while one was open for 19% -> 20% of each run, Pallas kernels for 37% -> 35%
where the time goes in v5:
time: 788 us; the launch traced here: 778 us
  Pallas kernels  293 us (37%)
  waiting for transfers between devices  123 us (16%)
  starting transfers between devices  118 us (15%)
  other arithmetic  92.1 us (12%)
  matrix products  77.6 us (10%)
  local copies, waits for them, and re-layouts  70.2 us (9%)
    pallas_call x5, Pallas kernels, call_placed(): pl.pallas_call(run, in_specs=[pl.BlockSpec(memory_space=pltpu.SMEM)] + [a...  90.2 us
    pallas_call x4, Pallas kernels, call_rows(): pl.pallas_call(kernel, in_specs=specs, out_specs=out_specs, out_shape=out...  84.6 us
    pallas_call x4, Pallas kernels, attend_back(): pl.pallas_call(partial(back_kernel, hd, c, score_scale, part), grid=(n //...  81 us
    dot_general x12, matrix products, dot_left(): lax.dot_general(left, right, (((0,), (0,)), ((), ())), preferred_element_...  71.4 us
    all_to_all x10, starting transfers between devices, over_z(): return lax.all_to_all(operand, 'fsdp', 0, 0, axis_index_groups=Z_GROUPS)  45.5 us
    all_to_all x10, waiting for transfers between devices, over_z(): return lax.all_to_all(operand, 'fsdp', 0, 0, axis_index_groups=Z_GROUPS)  31.4 us
    ppermute x5, waiting for transfers between devices, y(): self.live['far'] = lax.ppermute(self.live['own'], AXES, TO_Y)  30.6 us
    pallas_call x1, Pallas kernels, attend(): pl.pallas_call(partial(attend_kernel, hd, c), grid=(n // BLOCK,), in_spec...  22.6 us
  transfers between devices with their start and end apart: 73, of which 26 were waited for; matrix products, arithmetic and copies ran while one was open for 20% of the time, Pallas kernels for 35%

profile of v5, /device:TPU:1, one launch (start us, length us, event | category | flops | bytes accessed | tf_op | source)
XLA Modules:
  0.0 777.9 jit_solution(8032478891343298030)
XLA Ops:
  2.1 6.4 all-to-all-start.1
  17.1 4.5 all-to-all-start
  24.6 2.7 fusion.57
  27.2 12.0 %all-to-all-done.refs_1_ = bf16[4,2,48,896]{3,2,1,0:T(8,128)(2,1)} async-done(((bf16[4,2,48,896]{3,2,1,0:T(8,128)(2,1)}), bf16[4,2,48,896]{3,2,1,0:T(8,128)(2,1)}, u32[]{:S(2)}, u32[]{:S(2)}) %all-to-all-start) | async-done | bytes 688160 | tf_op jit(solution)/shard_map/all_to_all | solution.py:89
  40.5 4.3 all-to-all-start.2
  44.8 5.4 multiply_cosine_fusion
  58.9 2.8 pad_maximum_fusion.3.refs_12_.rot_ref
  64.8 3.8 collective-permute-done.refs_2_
  68.7 4.2 all-to-all-done.2.refs_1_
  72.8 3.6 all-to-all-start.3
  84.0 13.1 %all-to-all-done.3 = bf16[8,8,6912]{2,1,0:T(8,128)(2,1)S(1)} async-done(((bf16[8,8,6912]{2,1,0:T(8,128)(2,1)}), bf16[8,8,6912]{2,1,0:T(8,128)(2,1)S(1)}, u32[]{:S(2)}, u32[]{:S(2)}) %all-to-all-start.3) | async-done | bytes 884768 | tf_op jit(solution)/shard_map/all_to_all | solution.py:426
  97.9 16.7 %collective-permute-done.4.refs_2_ = bf16[4,2,48,1536]{3,2,1,0:T(8,128)(2,1)} collective-permute-done((bf16[4,2,48,1536]{3,2,1,0:T(8,128)(2,1)}, bf16[4,2,48,1536]{3,2,1,0:T(8,128)(2,1)}, u32[]{:S(2)}, u32[]{:S(2)}) %collective-permute-start.4) | collective-permute-done | bytes 1179680 | tf_op jit(solution)/shard_map/ppermute | solution.py:205
  115.8 5.3 all-to-all-start.4
  131.4 20.6 %prepare.2 = (bf16[1024,1152]{1,0:T(8,128)(2,1)}, bf16[8,1024,128]{2,1,0:T(8,128)(2,1)}, bf16[8,1024,128]{2,1,0:T(8,128)(2,1)}, bf16[8,1024,128]{2,1,0:T(8,128)(...) custom-call(s32[4]{0:T(128)} %pad_add_fusion.refs_0_, ...), custom_call_target="tpu_custom_call" | custom-call | flops 8153726976 | bytes 20971520 | tf_op jit(solution)/shard_map/prepare/pallas_call | solution.py:171
  155.5 4.8 all-to-all-start.5
  160.4 21.0 %prepare.3 = (bf16[8,1024,128]{2,1,0:T(8,128)(2,1)}, bf16[8,1024,128]{2,1,0:T(8,128)(2,1)}, bf16[8,1024,128]{2,1,0:T(8,128)(2,1)}, bf16[8,1024,128]{2,1,0:T(8,12...) custom-call(s32[4]{0:T(128)} %pad_add_fusion.refs_0_, ...), custom_call_target="tpu_custom_call" | custom-call | flops 8153726976 | bytes 20971520 | tf_op jit(solution)/shard_map/prepare/pallas_call | solution.py:171
  181.4 6.3 collective-permute-done.9.refs_2_
  190.1 3.5 all-to-all-start.6
  197.7 22.6 %attend.1 = (bf16[1024,1152]{1,0:T(8,128)(2,1)}, bf16[8,1024,128]{2,1,0:T(8,128)(2,1)}, bf16[8,1024,128]{2,1,0:T(8,128)(2,1)}) custom-call(bf16[8,1024,128]{2,1,0:T(8,128)(2,1)} %get-tuple-element.386.refs_0_, bf16[8,1024,128]{2,1,0:T(8,128)(2,1)} %get-tuple-element.387.refs_1_.k_ref, bf16[8,1024,128]{2,1,0:T(8,128)(2,1)} %get-tuple-element.388.refs_2_.v_ref, ...), custom_call_target="tpu_custom_call" | custom-call | flops 5368709120 | bytes 20971520 | tf_op jit(solution)/shard_map/attend/pallas_call | solution.py:568
  230.9 11.3 %join.1 = (bf16[1024,1152]{1,0:T(8,128)(2,1)}, f32[1024,1152]{1,0:T(8,128)}, bf16[1024,1152]{1,0:T(8,128)(2,1)}) custom-call(bf16[1024,1152]{1,0:T(8,128)(2,1)} %get-tuple-element.403.mix_ref, bf16[1024,1152]{1,0:T(8,128)(2,1)} %bitcast.314, bf16[1024,16]{1,0:T(8,128)(2,1)} %copy.95.refs_8_.hot_ref.refs_10_, f32[1024,1]{1,0:T(8,128)} %copy.98.keep_ref.refs_11_, ...), custom_call_target="tpu_custom_call" | custom-call | flops 7247757312 | bytes 11943936 | tf_op jit(solution)/shard_map/join/pallas_call | solution.py:809
  242.2 14.6 %gate.1 = (bf16[1024,3072]{1,0:T(8,128)(2,1)}, bf16[1152,3072]{1,0:T(8,128)(2,1)}) custom-call(s32[4]{0:T(128)} %pad_add_fusion.refs_0_, bf16[4,2,48,1536]{3,2,1,0:T(8,128)(2,1)} %copy-done.8, bf16[4,2,48,1536]{3,2,1,0:T(8,128)(2,1)} %collective-permute-done.9.refs_2_, bf16[4,2,48,1536]{3,2,1,0:T(8,128)(2,1)} %copy-done.49, ...), custom_call_target="tpu_custom_call" | custom-call | flops 7247757312 | bytes 2359296 | tf_op jit(solution)/shard_map/gate/pallas_call | solution.py:171
  257.8 3.1 collective-permute-done.18.refs_2_
  265.8 16.6 %up.1 = (bf16[1024,3072]{1,0:T(8,128)(2,1)}, bf16[1024,3072]{1,0:T(8,128)(2,1)}, bf16[1152,3072]{1,0:T(8,128)(2,1)}) custom-call(s32[4]{0:T(128)} %pad_add_fusion.refs_0_, bf16[4,2,48,1536]{3,2,1,0:T(8,128)(2,1)} %all-to-all-done.5.refs_1_, bf16[4,2,48,1536]{3,2,1,0:T(8,128)(2,1)} %copy-done.35, bf16[4,2,48,1536]{3,2,1,0:T(8,128)(2,1)} %collective-permute-done.15.refs_3_, ...), custom_call_target="tpu_custom_call" | custom-call | flops 7247757312 | bytes 8650752 | tf_op jit(solution)/shard_map/up/pallas_call | solution.py:171
  282.4 10.5 %collective-permute-done.20.refs_3_ = bf16[4,2,128,640]{3,2,1,0:T(8,128)(2,1)} collective-permute-done((bf16[4,2,128,640]{3,2,1,0:T(8,128)(2,1)S(1)}, bf16[4,2,128,640]{3,2,1,0:T(8,128)(2,1)}, u32[]{:S(2)}, u32[]{:S(2)}) %collective-permute-start.20) | collective-permute-done | bytes 1310752 | tf_op jit(solution)/shard_map/ppermute | solution.py:210
  298.7 17.4 %down.1 = (bf16[1024,1152]{1,0:T(8,128)(2,1)}, bf16[1024,1280]{1,0:T(8,128)(2,1)}, f32[16,1152]{1,0:T(8,128)}, bf16[3072,1280]{1,0:T(8,128)(2,1)}) custom-call(s32[4]{0:T(128)} %pad_add_fusion.refs_0_, bf16[4,2,128,640]{3,2,1,0:T(8,128)(2,1)} %copy-done.5, bf16[4,2,128,640]{3,2,1,0:T(8,128)(2,1)} %copy-done.34, ...), custom_call_target="tpu_custom_call" | custom-call | flops 8053063680 | bytes 13443072 | tf_op jit(solution)/shard_map/down/pallas_call | solution.py:171
  318.2 9.4 %convolution_convert_fusion.1 = bf16[3072,640]{1,0:T(8,128)(2,1)} fusion(bf16[1024,3072]{1,0:T(8,128)(2,1)} %get-tuple-element.445.refs_7_, bf16[1024,1280]{1,0:T(8,128)(2,1)S(1)} %copy-done.32, s32[]{:T(128)S(6)} %select_n.433), kind=kOutput, calls=%fused_computation.6 | convolution fusion | flops 4028497920 | bytes 11534340 | tf_op jit(solution)/shard_map/dot_general | solution.py:29
  328.0 18.6 %inner_back.1 = (bf16[1024,3072]{1,0:T(8,128)(2,1)}, bf16[1024,3072]{1,0:T(8,128)(2,1)}) custom-call(s32[1]{0:T(128)} %bitcast.1.core_ref, bf16[1024,1280]{1,0:T(8,128)(2,1)} %get-tuple-element.457.grad_ref, bf16[1024,3072]{1,0:T(8,128)(2,1)} %get-tuple-element.458.refs_8_.gate_ref, bf16[1024,3072]{1,0:T(8,128)(2,1)} %get-tuple-element.459.up_ref, ...), custom_call_target="tpu_custom_call" | custom-call | flops 8053063680 | bytes 23068672 | tf_op jit(solution)/shard_map/inner_back/pallas_call | solution.py:809
  346.6 10.0 %add_convert_fusion.1 = bf16[3072,640]{1,0:T(8,128)(2,1)} fusion(bf16[3072,640]{1,0:T(8,128)(2,1)S(1)} %collective-permute-done.25, bf16[1024,3072]{1,0:T(8,128)(2,1)} %get-tuple-element.445.refs_7_, bf16[1024,640]{1,0:T(8,128)(2,1)S(1)} %constant_dynamic-slice_fusion.3), kind=kOutput, calls=%fused_computation.4 | convolution fusion | flops 4032430080 | bytes 15466496 | tf_op jit(solution)/shard_map/dot_general | solution.py:29
  356.5 9.5 %convolution_convert_fusion = bf16[1152,3072]{1,0:T(8,128)(2,1)} fusion(bf16[1024,1152]{1,0:T(8,128)(2,1)S(1)} %copy-done.54, bf16[1024,3072]{1,0:T(8,128)(2,1)S(1)} %copy-done.56), kind=kOutput, calls=%fused_computation.1 | convolution fusion | flops 7251296256 | bytes 15728640 | tf_op jit(solution)/shard_map/dot_general | solution.py:29
  369.2 33.3 %middle_back.1 = (f32[1024,1152]{1,0:T(8,128)}, bf16[1024,1280]{1,0:T(8,128)(2,1)}, f32[16,3456]{1,0:T(8,128)}) custom-call(s32[1]{0:T(128)} %bitcast.1.core_ref, bf16[1024,3072]{1,0:T(8,128)(2,1)} %get-tuple-element.471.send_ref, bf16[1024,3072]{1,0:T(8,128)(2,1)} %get-tuple-element.482.mine_ref, f32[1024,1152]{1,0:T(8,128)} %get-tuple-element.473.refs_8_.mid_ref, ...), custom_call_target="tpu_custom_call" | custom-call | flops 14495514624 | bytes 36323328 | tf_op jit(solution)/shard_map/middle_back/pallas_call | solution.py:809
  402.5 3.6 constant_dynamic-slice_fusion.1
  406.2 11.8 %add_convert_fusion = bf16[1152,3072]{1,0:T(8,128)(2,1)S(1)} fusion(bf16[1152,3072]{1,0:T(8,128)(2,1)} %collective-permute-done.27, bf16[1024,1152]{1,0:T(8,128)(2,1)S(1)} %copy-done.55, bf16[1024,3072]{1,0:T(8,128)(2,1)} %get-tuple-element.482.mine_ref), kind=kOutput, calls=%fused_computation | convolution fusion | flops 7258374144 | bytes 22806528 | tf_op jit(solution)/shard_map/dot_general | solution.py:29
  424.1 12.7 %spread.1.do_ref = bf16[16,1024,128]{2,1,0:T(8,128)(2,1)} custom-call(bf16[1024,1280]{1,0:T(8,128)(2,1)} %get-tuple-element.490.ga_ref, bf16[1152,3072]{1,0:T(8,128)(2,1)} %get-tuple-element.405.w_ref.wt_ref, bf16[1024,1152]{1,0:T(8,128)(2,1)} %get-tuple-element.403.mix_ref), custom_call_target="tpu_custom_call" | custom-call | flops 2717908992 | bytes 12582912 | tf_op jit(solution)/shard_map/spread/pallas_call | solution.py:612
  436.8 4.5 convolution_convert_fusion.4
  441.9 8.6 %collective-permute-done.29 = bf16[2,2,48,3072]{3,2,1,0:T(8,128)(2,1)} collective-permute-done((bf16[2,2,48,3072]{3,2,1,0:T(8,128)(2,1)}, bf16[2,2,48,3072]{3,2,1,0:T(8,128)(2,1)}, u32[]{:S(2)}, u32[]{:S(2)}) %collective-permute-start.29) | collective-permute-done | bytes 1179680 | tf_op jit(solution)/shard_map/ppermute | solution.py:272
  453.4 4.5 all-to-all-start.7
  463.3 20.0 %attend_back.4 = (bf16[2,1024,896]{2,1,0:T(8,128)(2,1)}, f32[2,8,128]{2,1,0:T(8,128)}) custom-call(s32[1]{0:T(128)} %bitcast.1.core_ref, bf16[8,1024,128]{2,1,0:T(8,128)(2,1)} %get-tuple-element.498.q_ref, bf16[8,1024,128]{2,1,0:T(8,128)(2,1)} %get-tuple-element.387.refs_1_.k_ref, bf16[8,1024,128]{2,1,0:T(8,128)(2,1)} %get-tuple-element.388.refs_2_.v_ref, ...), custom_call_target="tpu_custom_call" | custom-call | flops 3355443200 | bytes 10485760 | tf_op jit(solution)/shard_map/attend_back/pallas_call | solution.py:716
  483.3 6.7 collective-permute-done.30
  493.0 3.9 fusion.5
  496.9 5.2 all-to-all-start.8
  504.3 20.2 %attend_back.5 = (bf16[2,1024,896]{2,1,0:T(8,128)(2,1)}, f32[2,8,128]{2,1,0:T(8,128)}) custom-call(s32[1]{0:T(128)} %bitcast.1.core_ref, bf16[8,1024,128]{2,1,0:T(8,128)(2,1)} %get-tuple-element.498.q_ref, bf16[8,1024,128]{2,1,0:T(8,128)(2,1)} %get-tuple-element.387.refs_1_.k_ref, ...), custom_call_target="tpu_custom_call", output_to_operand_aliasing={{0}: (10, {})} | custom-call | flops 3355443200 | bytes 10485760 | tf_op jit(solution)/shard_map/attend_back/pallas_call | solution.py:716
  524.5 5.6 convolution_convert_fusion.3
  530.2 4.5 fusion.3
  539.1 2.9 add_convert_fusion.2
  542.0 5.0 all-to-all-start.9
  547.9 20.5 %attend_back.6 = (bf16[2,1024,896]{2,1,0:T(8,128)(2,1)}, f32[2,8,128]{2,1,0:T(8,128)}) custom-call(s32[1]{0:T(128)} %bitcast.1.core_ref, bf16[8,1024,128]{2,1,0:T(8,128)(2,1)} %get-tuple-element.526.q_ref, bf16[8,1024,128]{2,1,0:T(8,128)(2,1)} %get-tuple-element.390.refs_4_.k_ref, bf16[8,1024,128]{2,1,0:T(8,128)(2,1)} %get-tuple-element.391.refs_5_.v_ref, ...), custom_call_target="tpu_custom_call" | custom-call | flops 3355443200 | bytes 10485760 | tf_op jit(solution)/shard_map/attend_back/pallas_call | solution.py:716
  568.5 4.3 fusion.1
  583.4 4.4 all-to-all-start.10
  591.9 20.2 %attend_back.7 = (bf16[2,1024,896]{2,1,0:T(8,128)(2,1)}, f32[2,8,128]{2,1,0:T(8,128)}) custom-call(s32[1]{0:T(128)} %bitcast.1.core_ref, bf16[8,1024,128]{2,1,0:T(8,128)(2,1)} %get-tuple-element.526.q_ref, bf16[8,1024,128]{2,1,0:T(8,128)(2,1)} %get-tuple-element.390.refs_4_.k_ref, ...), custom_call_target="tpu_custom_call", output_to_operand_aliasing={{0}: (10, {})} | custom-call | flops 3355443200 | bytes 10485760 | tf_op jit(solution)/shard_map/attend_back/pallas_call | solution.py:716
  612.2 5.5 convolution_convert_fusion.2
  617.7 10.1 %collective-permute-done.37 = bf16[2,48,3072]{2,1,0:T(8,128)(2,1)} collective-permute-done((bf16[2,48,3072]{2,1,0:T(8,128)(2,1)S(1)}, bf16[2,48,3072]{2,1,0:T(8,128)(2,1)}, u32[]{:S(2)}, u32[]{:S(2)}) %collective-permute-start.37) | collective-permute-done | bytes 589856 | tf_op jit(solution)/shard_map/ppermute | solution.py:354
  629.8 2.5 fusion.23
  632.4 4.7 all-to-all-start.11
  637.4 3.4 collective-permute-start.42
  644.8 4.4 fusion.2
  652.1 21.5 %input_back.1 = (f32[1024,1152]{1,0:T(8,128)}, f32[16,2304]{1,0:T(8,128)}) custom-call(s32[1]{0:T(128)} %bitcast.1.core_ref, bf16[2,1024,896]{2,1,0:T(8,128)(2,1)} %get-tuple-element.553.one_ref, bf16[2,1024,896]{2,1,0:T(8,128)(2,1)} %get-tuple-element.554.two_ref, f32[1024,1152]{1,0:T(8,128)} %get-tuple-element.555.mid_ref, bf16[1024,1152]{1,0:T(8,128)(2,1)} %bitcast.315, ...), custom_call_target="tpu_custom_call" | custom-call | flops 11475615744 | bytes 25731072 | tf_op jit(solution)/shard_map/input_back/pallas_call | solution.py:809
  675.3 5.7 all-to-all-start.12
  684.7 3.3 collective-permute-start.46
  706.7 2.6 collective-permute-start.52
  720.4 3.6 all-to-all-start.13
  730.1 11.4 %all-to-all-done.13 = bf16[4,2,48,896]{3,2,1,0:T(8,128)(2,1)S(1)} async-done(((bf16[4,2,48,896]{3,2,1,0:T(8,128)(2,1)}), bf16[4,2,48,896]{3,2,1,0:T(8,128)(2,1)S(1)}, u32[]{:S(2)}, u32[]{:S(2)}) %all-to-all-start.13) | async-done | bytes 688160 | tf_op jit(solution)/shard_map/all_to_all | solution.py:89
  749.3 4.1 all-to-all-start.14
  755.6 2.7 convert_reduce_fusion
  771.1 3.5 pad_maximum_fusion
  (410 shorter events, 198.0 us)
Async XLA Ops:
  2.1 14.1 %all-to-all-start.1 = ((bf16[8,8,144]{2,1,0:T(8,128)(2,1)}), bf16[8,8,144]{2,1,0:T(8,128)(2,1)}, u32[]{:S(2)}, u32[]{:S(2)}) async-start(bf16[8,8,144]{2,1,0:T(8,128)(2,1)} %fusion.44), calls=%async_computation.1 | async-start | bytes 65536 | tf_op jit(solution)/shard_map/all_to_all | solution.py:420
  17.1 22.1 %all-to-all-start = ((bf16[4,2,48,896]{3,2,1,0:T(8,128)(2,1)}), bf16[4,2,48,896]{3,2,1,0:T(8,128)(2,1)}, u32[]{:S(2)}, u32[]{:S(2)}) async-start(bf16[4,2,48,896]{3,2,1,0:T(8,128)(2,1)} %broadcast_in_dim.60), calls=%async_computation | async-start | bytes 1376256 | tf_op jit(solution)/shard_map/all_to_all | solution.py:89
  40.5 32.4 %all-to-all-start.2 = ((bf16[4,2,48,1536]{3,2,1,0:T(8,128)(2,1)}), bf16[4,2,48,1536]{3,2,1,0:T(8,128)(2,1)}, u32[]{:S(2)}, u32[]{:S(2)}) async-start(bf16[4,2,48,1536]{3,2,1,0:T(8,128)(2,1)} %broadcast_in_dim.61), calls=%async_computation.2 | async-start | bytes 2359296 | tf_op jit(solution)/shard_map/all_to_all | solution.py:89
  52.9 15.8 %collective-permute-start = (bf16[4,2,48,896]{3,2,1,0:T(8,128)(2,1)}, bf16[4,2,48,896]{3,2,1,0:T(8,128)(2,1)}, u32[]{:S(2)}, u32[]{:S(2)}) collective-permute-start(bf16[4,2,48,896]{3,2,1,0:T(8,128)(2,1)} %all-to-all-done.refs_1_), channel_id=1, source_target_pairs={{0,1},{1,0},{2,3},{3,2},{4,5},{5,4},{6,7},{7,6},{8,9},{9,8},{10,11... | collective-permute-start | bytes 2064392 | tf_op jit(solution)/shard_map/ppermute | solution.py:205
  72.8 24.3 %all-to-all-start.3 = ((bf16[8,8,6912]{2,1,0:T(8,128)(2,1)}), bf16[8,8,6912]{2,1,0:T(8,128)(2,1)S(1)}, u32[]{:S(2)}, u32[]{:S(2)}) async-start(bf16[8,8,6912]{2,1,0:T(8,128)(2,1)} %bitcast.20), calls=%async_computation.3 | async-start | bytes 1769472 | tf_op jit(solution)/shard_map/all_to_all | solution.py:426
  77.4 20.4 %collective-permute-start.3 = (bf16[4,2,48,896]{3,2,1,0:T(8,128)(2,1)}, bf16[4,2,48,896]{3,2,1,0:T(8,128)(2,1)}, u32[]{:S(2)}, u32[]{:S(2)}) collective-permute-start(bf16[4,2,48,896]{3,2,1,0:T(8,128)(2,1)} %all-to-all-done.refs_1_), channel_id=1, source_target_pairs={{0,8},{1,9},{2,10},{3,11},{4,12},{5,13},{6,14},{7,15},{8,0},{9,1},... | collective-permute-start | bytes 2064392 | tf_op jit(solution)/shard_map/ppermute | solution.py:215
  80.0 17.8 %collective-permute-start.2 = (bf16[4,2,48,896]{3,2,1,0:T(8,128)(2,1)}, bf16[4,2,48,896]{3,2,1,0:T(8,128)(2,1)}, u32[]{:S(2)}, u32[]{:S(2)}) collective-permute-start(bf16[4,2,48,896]{3,2,1,0:T(8,128)(2,1)} %collective-permute-done.refs_2_), channel_id=1, source_target_pairs={{0,8},{1,9},{2,10},{3,11},{4,12},{5,13},{6,14},{7,15},{8,0},{9,1},... | collective-permute-start | bytes 2064392 | tf_op jit(solution)/shard_map/ppermute | solution.py:215
  81.0 16.8 %collective-permute-start.1 = (bf16[4,2,48,896]{3,2,1,0:T(8,128)(2,1)}, bf16[4,2,48,896]{3,2,1,0:T(8,128)(2,1)}, u32[]{:S(2)}, u32[]{:S(2)}) collective-permute-start(bf16[4,2,48,896]{3,2,1,0:T(8,128)(2,1)} %pad_maximum_fusion.14), channel_id=1, source_target_pairs={{0,16},{1,17},{2,18},{3,19},{4,20},{5,21},{6,22},{7,23},{8,24},{9,... | collective-permute-start | bytes 2064392 | tf_op jit(solution)/shard_map/ppermute | solution.py:210
  82.2 32.3 %collective-permute-start.4 = (bf16[4,2,48,1536]{3,2,1,0:T(8,128)(2,1)}, bf16[4,2,48,1536]{3,2,1,0:T(8,128)(2,1)}, u32[]{:S(2)}, u32[]{:S(2)}) collective-permute-start(bf16[4,2,48,1536]{3,2,1,0:T(8,128)(2,1)} %all-to-all-done.2.refs_1_), channel_id=1, source_target_pairs={{0,1},{1,0},{2,3},{3,2},{4,5},{5,4},{6,7},{7,6},{8,9},{9,8},{10,11... | collective-permute-start | bytes 3538952 | tf_op jit(solution)/shard_map/ppermute | solution.py:205
  115.8 37.6 %all-to-all-start.4 = ((bf16[4,2,48,1536]{3,2,1,0:T(8,128)(2,1)}), bf16[4,2,48,1536]{3,2,1,0:T(8,128)(2,1)S(1)}, u32[]{:S(2)}, u32[]{:S(2)}) async-start(bf16[4,2,48,1536]{3,2,1,0:T(8,128)(2,1)} %broadcast_in_dim.65), calls=%async_computation.4 | async-start | bytes 2359296 | tf_op jit(solution)/shard_map/all_to_all | solution.py:89
  125.5 27.9 %collective-permute-start.5 = (bf16[4,2,48,1536]{3,2,1,0:T(8,128)(2,1)}, bf16[4,2,48,1536]{3,2,1,0:T(8,128)(2,1)}, u32[]{:S(2)}, u32[]{:S(2)}) collective-permute-start(bf16[4,2,48,1536]{3,2,1,0:T(8,128)(2,1)} %pad_maximum_fusion.8), channel_id=1, source_target_pairs={{0,16},{1,17},{2,18},{3,19},{4,20},{5,21},{6,22},{7,23},{8,24},{9,... | collective-permute-start | bytes 3538952 | tf_op jit(solution)/shard_map/ppermute | solution.py:210
  126.2 27.2 %collective-permute-start.7 = (bf16[4,2,48,1536]{3,2,1,0:T(8,128)(2,1)}, bf16[4,2,48,1536]{3,2,1,0:T(8,128)(2,1)}, u32[]{:S(2)}, u32[]{:S(2)}) collective-permute-start(bf16[4,2,48,1536]{3,2,1,0:T(8,128)(2,1)} %all-to-all-done.2.refs_1_), channel_id=1, source_target_pairs={{0,8},{1,9},{2,10},{3,11},{4,12},{5,13},{6,14},{7,15},{8,0},{9,1},... | collective-permute-start | bytes 3538952 | tf_op jit(solution)/shard_map/ppermute | solution.py:215
  126.5 26.9 %collective-permute-start.6 = (bf16[4,2,48,1536]{3,2,1,0:T(8,128)(2,1)}, bf16[4,2,48,1536]{3,2,1,0:T(8,128)(2,1)}, u32[]{:S(2)}, u32[]{:S(2)}) collective-permute-start(bf16[4,2,48,1536]{3,2,1,0:T(8,128)(2,1)} %collective-permute-done.4.refs_2_), channel_id=1, source_target_pairs={{0,8},{1,9},{2,10},{3,11},{4,12},{5,13},{6,14},{7,15},{8,0},{9,1},... | collective-permute-start | bytes 3538952 | tf_op jit(solution)/shard_map/ppermute | solution.py:215
  155.5 33.2 %all-to-all-start.5 = ((bf16[4,2,48,1536]{3,2,1,0:T(8,128)(2,1)}), bf16[4,2,48,1536]{3,2,1,0:T(8,128)(2,1)}, u32[]{:S(2)}, u32[]{:S(2)}) async-start(bf16[4,2,48,1536]{3,2,1,0:T(8,128)(2,1)} %broadcast_in_dim.68), calls=%async_computation.5 | async-start | bytes 2359296 | tf_op jit(solution)/shard_map/all_to_all | solution.py:89
  160.4 27.3 %collective-permute-start.9 = (bf16[4,2,48,1536]{3,2,1,0:T(8,128)(2,1)S(1)}, bf16[4,2,48,1536]{3,2,1,0:T(8,128)(2,1)}, u32[]{:S(2)}, u32[]{:S(2)}) collective-permute-start(bf16[4,2,48,1536]{3,2,1,0:T(8,128)(2,1)S(1)} %all-to-all-done.4.refs_1_), channel_id=1, source_target_pairs={{0,1},{1,0},{2,3},{3,2},{4,5},{5,4},{6,7},{7,6},{8,9},{9,8},{10,11... | collective-permute-start | bytes 3538952 | tf_op jit(solution)/shard_map/ppermute | solution.py:205
  190.1 34.3 %all-to-all-start.6 = ((bf16[4,2,128,640]{3,2,1,0:T(8,128)(2,1)}), bf16[4,2,128,640]{3,2,1,0:T(8,128)(2,1)S(1)}, u32[]{:S(2)}, u32[]{:S(2)}) async-start(bf16[4,2,128,640]{3,2,1,0:T(8,128)(2,1)} %broadcast_in_dim.69), calls=%async_computation.6 | async-start | bytes 2621440 | tf_op jit(solution)/shard_map/all_to_all | solution.py:89
  195.0 26.2 %collective-permute-start.11 = (bf16[4,2,48,1536]{3,2,1,0:T(8,128)(2,1)S(1)}, bf16[4,2,48,1536]{3,2,1,0:T(8,128)(2,1)S(1)}, u32[]{:S(2)}, u32[]{:S(2)}) collective-permute-start(bf16[4,2,48,1536]{3,2,1,0:T(8,128)(2,1)S(1)} %pad_maximum_fusion.9), channel_id=1, source_target_pairs={{0,16},{1,17},{2,18},{3,19},{4,20},{5,21},{6,22},{7,23},{8,24},{9,... | collective-permute-start | bytes 3538952 | tf_op jit(solution)/shard_map/ppermute | solution.py:210
  195.8 26.1 %collective-permute-start.14 = (bf16[4,2,48,1536]{3,2,1,0:T(8,128)(2,1)}, bf16[4,2,48,1536]{3,2,1,0:T(8,128)(2,1)S(1)}, u32[]{:S(2)}, u32[]{:S(2)}) collective-permute-start(bf16[4,2,48,1536]{3,2,1,0:T(8,128)(2,1)} %all-to-all-done.5.refs_1_), channel_id=1, source_target_pairs={{0,1},{1,0},{2,3},{3,2},{4,5},{5,4},{6,7},{7,6},{8,9},{9,8},{10,11... | collective-permute-start | bytes 3538952 | tf_op jit(solution)/shard_map/ppermute | solution.py:205
  195.8 26.1 %collective-permute-start.13 = (bf16[4,2,48,1536]{3,2,1,0:T(8,128)(2,1)S(1)}, bf16[4,2,48,1536]{3,2,1,0:T(8,128)(2,1)S(1)}, u32[]{:S(2)}, u32[]{:S(2)}) collective-permute-start(bf16[4,2,48,1536]{3,2,1,0:T(8,128)(2,1)S(1)} %copy-done.9), channel_id=1, source_target_pairs={{0,8},{1,9},{2,10},{3,11},{4,12},{5,13},{6,14},{7,15},{8,0},{9,1},... | collective-permute-start | bytes 3538952 | tf_op jit(solution)/shard_map/ppermute | solution.py:215
  197.7 26.2 %collective-permute-start.12 = (bf16[4,2,48,1536]{3,2,1,0:T(8,128)(2,1)}, bf16[4,2,48,1536]{3,2,1,0:T(8,128)(2,1)}, u32[]{:S(2)}, u32[]{:S(2)}) collective-permute-start(bf16[4,2,48,1536]{3,2,1,0:T(8,128)(2,1)} %collective-permute-done.9.refs_2_), channel_id=1, source_target_pairs={{0,8},{1,9},{2,10},{3,11},{4,12},{5,13},{6,14},{7,15},{8,0},{9,1},... | collective-permute-start | bytes 3538952 | tf_op jit(solution)/shard_map/ppermute | solution.py:215
  224.5 17.7 %collective-permute-start.19 = (bf16[4,2,48,1536]{3,2,1,0:T(8,128)(2,1)}, bf16[4,2,48,1536]{3,2,1,0:T(8,128)(2,1)}, u32[]{:S(2)}, u32[]{:S(2)}) collective-permute-start(bf16[4,2,48,1536]{3,2,1,0:T(8,128)(2,1)} %copy-done.49), channel_id=1, source_target_pairs={{0,8},{1,9},{2,10},{3,11},{4,12},{5,13},{6,14},{7,15},{8,0},{9,1},... | collective-permute-start | bytes 3538952 | tf_op jit(solution)/shard_map/ppermute | solution.py:215
  229.3 28.6 %collective-permute-start.17 = (bf16[4,2,48,1536]{3,2,1,0:T(8,128)(2,1)}, bf16[4,2,48,1536]{3,2,1,0:T(8,128)(2,1)S(1)}, u32[]{:S(2)}, u32[]{:S(2)}) collective-permute-start(bf16[4,2,48,1536]{3,2,1,0:T(8,128)(2,1)} %all-to-all-done.5.refs_1_), channel_id=1, source_target_pairs={{0,8},{1,9},{2,10},{3,11},{4,12},{5,13},{6,14},{7,15},{8,0},{9,1},... | collective-permute-start | bytes 3538952 | tf_op jit(solution)/shard_map/ppermute | solution.py:215
  229.4 28.4 %collective-permute-start.16 = (bf16[4,2,48,1536]{3,2,1,0:T(8,128)(2,1)S(1)}, bf16[4,2,48,1536]{3,2,1,0:T(8,128)(2,1)}, u32[]{:S(2)}, u32[]{:S(2)}) collective-permute-start(bf16[4,2,48,1536]{3,2,1,0:T(8,128)(2,1)S(1)} %copy-done.36), channel_id=1, source_target_pairs={{0,8},{1,9},{2,10},{3,11},{4,12},{5,13},{6,14},{7,15},{8,0},{9,1},... | collective-permute-start | bytes 3538952 | tf_op jit(solution)/shard_map/ppermute | solution.py:215
  230.1 27.7 %collective-permute-start.15 = (bf16[4,2,48,1536]{3,2,1,0:T(8,128)(2,1)S(1)}, bf16[4,2,48,1536]{3,2,1,0:T(8,128)(2,1)}, u32[]{:S(2)}, u32[]{:S(2)}) collective-permute-start(bf16[4,2,48,1536]{3,2,1,0:T(8,128)(2,1)S(1)} %pad_maximum_fusion.10), channel_id=1, source_target_pairs={{0,16},{1,17},{2,18},{3,19},{4,20},{5,21},{6,22},{7,23},{8,24},{9,... | collective-permute-start | bytes 3538952 | tf_op jit(solution)/shard_map/ppermute | solution.py:210
  230.9 30.1 %collective-permute-start.18 = (bf16[4,2,128,640]{3,2,1,0:T(8,128)(2,1)S(1)}, bf16[4,2,128,640]{3,2,1,0:T(8,128)(2,1)S(1)}, u32[]{:S(2)}, u32[]{:S(2)}) collective-permute-start(bf16[4,2,128,640]{3,2,1,0:T(8,128)(2,1)S(1)} %all-to-all-done.6.refs_1_), channel_id=1, source_target_pairs={{0,1},{1,0},{2,3},{3,2},{4,5},{5,4},{6,7},{7,6},{8,9},{9,8},{10,11... | collective-permute-start | bytes 3932168 | tf_op jit(solution)/shard_map/ppermute | solution.py:205
  262.3 30.6 %collective-permute-start.20 = (bf16[4,2,128,640]{3,2,1,0:T(8,128)(2,1)S(1)}, bf16[4,2,128,640]{3,2,1,0:T(8,128)(2,1)}, u32[]{:S(2)}, u32[]{:S(2)}) collective-permute-start(bf16[4,2,128,640]{3,2,1,0:T(8,128)(2,1)S(1)} %pad_maximum_fusion.4), channel_id=1, source_target_pairs={{0,16},{1,17},{2,18},{3,19},{4,20},{5,21},{6,22},{7,23},{8,24},{9,... | collective-permute-start | bytes 3932168 | tf_op jit(solution)/shard_map/ppermute | solution.py:210
  263.1 29.8 %collective-permute-start.22 = (bf16[4,2,128,640]{3,2,1,0:T(8,128)(2,1)S(1)}, bf16[4,2,128,640]{3,2,1,0:T(8,128)(2,1)S(1)}, u32[]{:S(2)}, u32[]{:S(2)}) collective-permute-start(bf16[4,2,128,640]{3,2,1,0:T(8,128)(2,1)S(1)} %all-to-all-done.6.refs_1_), channel_id=1, source_target_pairs={{0,8},{1,9},{2,10},{3,11},{4,12},{5,13},{6,14},{7,15},{8,0},{9,1},... | collective-permute-start | bytes 3932168 | tf_op jit(solution)/shard_map/ppermute | solution.py:215
  263.4 29.5 %collective-permute-start.21 = (bf16[4,2,128,640]{3,2,1,0:T(8,128)(2,1)S(1)}, bf16[4,2,128,640]{3,2,1,0:T(8,128)(2,1)}, u32[]{:S(2)}, u32[]{:S(2)}) collective-permute-start(bf16[4,2,128,640]{3,2,1,0:T(8,128)(2,1)S(1)} %collective-permute-done.18.refs_2_), channel_id=1, source_target_pairs={{0,8},{1,9},{2,10},{3,11},{4,12},{5,13},{6,14},{7,15},{8,0},{9,1},... | collective-permute-start | bytes 3932168 | tf_op jit(solution)/shard_map/ppermute | solution.py:215
  327.6 19.0 %collective-permute-start.25 = (bf16[3072,640]{1,0:T(8,128)(2,1)}, bf16[3072,640]{1,0:T(8,128)(2,1)S(1)}, u32[]{:S(2)}, u32[]{:S(2)}) collective-permute-start(bf16[3072,640]{1,0:T(8,128)(2,1)} %convolution_convert_fusion.1), channel_id=1, source_target_pairs={{0,8},{1,9},{2,10},{3,11},{4,12},{5,13},{6,14},{7,15},{8,0},{9,1},... | collective-permute-start | bytes 11796488 | tf_op jit(solution)/shard_map/ppermute | solution.py:239
  366.1 40.1 %collective-permute-start.27 = (bf16[1152,3072]{1,0:T(8,128)(2,1)}, bf16[1152,3072]{1,0:T(8,128)(2,1)}, u32[]{:S(2)}, u32[]{:S(2)}) collective-permute-start(bf16[1152,3072]{1,0:T(8,128)(2,1)} %convolution_convert_fusion), channel_id=1, source_target_pairs={{0,8},{1,9},{2,10},{3,11},{4,12},{5,13},{6,14},{7,15},{8,0},{9,1},... | collective-permute-start | bytes 21233672 | tf_op jit(solution)/shard_map/ppermute | solution.py:239
  368.4 37.7 %collective-permute-start.26 = (bf16[4,2,128,640]{3,2,1,0:T(8,128)(2,1)S(1)}, bf16[4,2,128,640]{3,2,1,0:T(8,128)(2,1)S(1)}, u32[]{:S(2)}, u32[]{:S(2)}) collective-permute-start(bf16[4,2,128,640]{3,2,1,0:T(8,128)(2,1)S(1)} %dynamic-slice_bitcast_fusion), channel_id=1, source_target_pairs={{0,16},{1,17},{2,18},{3,19},{4,20},{5,21},{6,22},{7,23},{8,24},{9,... | collective-permute-start | bytes 3932168 | tf_op jit(solution)/shard_map/ppermute | solution.py:268
  419.7 30.8 %collective-permute-start.28 = (bf16[4,2,128,640]{3,2,1,0:T(8,128)(2,1)}, bf16[4,2,128,640]{3,2,1,0:T(8,128)(2,1)}, u32[]{:S(2)}, u32[]{:S(2)}) collective-permute-start(bf16[4,2,128,640]{3,2,1,0:T(8,128)(2,1)} %pad_maximum_fusion.5), channel_id=1, source_target_pairs={{0,1},{1,0},{2,3},{3,2},{4,5},{5,4},{6,7},{7,6},{8,9},{9,8},{10,11... | collective-permute-start | bytes 3932168 | tf_op jit(solution)/shard_map/ppermute | solution.py:302
  423.3 27.2 %collective-permute-start.29 = (bf16[2,2,48,3072]{3,2,1,0:T(8,128)(2,1)}, bf16[2,2,48,3072]{3,2,1,0:T(8,128)(2,1)}, u32[]{:S(2)}, u32[]{:S(2)}) collective-permute-start(bf16[2,2,48,3072]{3,2,1,0:T(8,128)(2,1)} %dynamic-slice_bitcast_fusion.3), channel_id=1, source_target_pairs={{0,16},{1,17},{2,18},{3,19},{4,20},{5,21},{6,22},{7,23},{8,24},{9,... | collective-permute-start | bytes 3538952 | tf_op jit(solution)/shard_map/ppermute | solution.py:272
  453.4 37.7 %all-to-all-start.7 = ((bf16[4,2,128,640]{3,2,1,0:T(8,128)(2,1)}), bf16[4,2,128,640]{3,2,1,0:T(8,128)(2,1)S(1)}, u32[]{:S(2)}, u32[]{:S(2)}) async-start(bf16[4,2,128,640]{3,2,1,0:T(8,128)(2,1)} %pad_maximum_fusion.6), calls=%async_computation.7 | async-start | bytes 2621440 | tf_op jit(solution)/shard_map/all_to_all | solution.py:89
  457.9 33.2 %collective-permute-start.32 = (bf16[1152,640]{1,0:T(8,128)(2,1)}, bf16[1152,640]{1,0:T(8,128)(2,1)}, u32[]{:S(2)}, u32[]{:S(2)}) collective-permute-start(bf16[1152,640]{1,0:T(8,128)(2,1)} %convolution_convert_fusion.4), channel_id=1, source_target_pairs={{0,8},{1,9},{2,10},{3,11},{4,12},{5,13},{6,14},{7,15},{8,0},{9,1},... | collective-permute-start | bytes 4423688 | tf_op jit(solution)/shard_map/ppermute | solution.py:239
  462.4 27.7 %collective-permute-start.30 = (bf16[4,48,3072]{2,1,0:T(8,128)(2,1)S(1)}, bf16[4,48,3072]{2,1,0:T(8,128)(2,1)S(1)}, u32[]{:S(2)}, u32[]{:S(2)}) collective-permute-start(bf16[4,48,3072]{2,1,0:T(8,128)(2,1)S(1)} %dynamic-slice_bitcast_fusion.2), channel_id=1, source_target_pairs={{0,1},{1,0},{2,3},{3,2},{4,5},{5,4},{6,7},{7,6},{8,9},{9,8},{10,11... | collective-permute-start | bytes 3538952 | tf_op jit(solution)/shard_map/ppermute | solution.py:291
  462.5 27.6 %collective-permute-start.31 = (bf16[2,2,48,3072]{3,2,1,0:T(8,128)(2,1)S(1)}, bf16[2,2,48,3072]{3,2,1,0:T(8,128)(2,1)S(1)}, u32[]{:S(2)}, u32[]{:S(2)}) collective-permute-start(bf16[2,2,48,3072]{3,2,1,0:T(8,128)(2,1)S(1)} %dynamic-slice_bitcast_fusion.1), channel_id=1, source_target_pairs={{0,16},{1,17},{2,18},{3,19},{4,20},{5,21},{6,22},{7,23},{8,24},{9,... | collective-permute-start | bytes 3538952 | tf_op jit(solution)/shard_map/ppermute | solution.py:272
  496.9 37.8 %all-to-all-start.8 = ((bf16[4,48,3072]{2,1,0:T(8,128)(2,1)}), bf16[4,48,3072]{2,1,0:T(8,128)(2,1)S(1)}, u32[]{:S(2)}, u32[]{:S(2)}) async-start(bf16[4,48,3072]{2,1,0:T(8,128)(2,1)} %get-tuple-element.616), calls=%async_computation.8 | async-start | bytes 2359296 | tf_op jit(solution)/shard_map/all_to_all | solution.py:89
  502.2 194.8 %collective-permute-start.49 = (bf16[64,144]{1,0:T(8,128)(2,1)}, bf16[64,144]{1,0:T(8,128)(2,1)}, u32[]{:S(2)}, u32[]{:S(2)}) collective-permute-start(bf16[64,144]{1,0:T(8,128)(2,1)} %bitcast.8), channel_id=1, source_target_pairs={{0,16},{1,17},{2,18},{3,19},{4,20},{5,21},{6,22},{7,23},{8,24},{9,... | collective-permute-start | bytes 55304 | tf_op jit(solution)/shard_map/ppermute | solution.py:395
  503.4 31.3 %collective-permute-start.33 = (bf16[2,128,640]{2,1,0:T(8,128)(2,1)S(1)}, bf16[2,128,640]{2,1,0:T(8,128)(2,1)S(1)}, u32[]{:S(2)}, u32[]{:S(2)}) collective-permute-start(bf16[2,128,640]{2,1,0:T(8,128)(2,1)S(1)} %reduce_sum.136), channel_id=1, source_target_pairs={{0,16},{1,17},{2,18},{3,19},{4,20},{5,21},{6,22},{7,23},{8,24},{9,... | collective-permute-start | bytes 983048 | tf_op jit(solution)/shard_map/ppermute | solution.py:354
  504.2 30.5 %collective-permute-start.34 = (bf16[4,48,3072]{2,1,0:T(8,128)(2,1)}, bf16[4,48,3072]{2,1,0:T(8,128)(2,1)S(1)}, u32[]{:S(2)}, u32[]{:S(2)}) collective-permute-start(bf16[4,48,3072]{2,1,0:T(8,128)(2,1)} %get-tuple-element.617), channel_id=1, source_target_pairs={{0,1},{1,0},{2,3},{3,2},{4,5},{5,4},{6,7},{7,6},{8,9},{9,8},{10,11... | collective-permute-start | bytes 3538952 | tf_op jit(solution)/shard_map/ppermute | solution.py:296
  534.7 33.7 %collective-permute-start.36 = (bf16[1152,896]{1,0:T(8,128)(2,1)}, bf16[1152,896]{1,0:T(8,128)(2,1)}, u32[]{:S(2)}, u32[]{:S(2)}) collective-permute-start(bf16[1152,896]{1,0:T(8,128)(2,1)} %convolution_convert_fusion.3), channel_id=1, source_target_pairs={{0,8},{1,9},{2,10},{3,11},{4,12},{5,13},{6,14},{7,15},{8,0},{9,1},... | collective-permute-start | bytes 6193160 | tf_op jit(solution)/shard_map/ppermute | solution.py:239
  542.0 33.2 %all-to-all-start.9 = ((bf16[4,48,3072]{2,1,0:T(8,128)(2,1)}), bf16[4,48,3072]{2,1,0:T(8,128)(2,1)}, u32[]{:S(2)}, u32[]{:S(2)}) async-start(bf16[4,48,3072]{2,1,0:T(8,128)(2,1)} %add_convert_fusion.2), calls=%async_computation.9 | async-start | bytes 2359296 | tf_op jit(solution)/shard_map/all_to_all | solution.py:89
  547.2 26.0 %collective-permute-start.35 = (bf16[384,640]{1,0:T(8,128)(2,1)S(1)}, bf16[384,640]{1,0:T(8,128)(2,1)}, u32[]{:S(2)}, u32[]{:S(2)}) collective-permute-start(bf16[384,640]{1,0:T(8,128)(2,1)S(1)} %pad_maximum_fusion.19), channel_id=1, source_target_pairs={{0,8},{1,9},{2,10},{3,11},{4,12},{5,13},{6,14},{7,15},{8,0},{9,1},... | collective-permute-start | bytes 1474568 | tf_op jit(solution)/shard_map/ppermute | solution.py:364
  583.4 44.4 %all-to-all-start.10 = ((bf16[8,8,4608]{2,1,0:T(8,128)(2,1)}), bf16[8,8,4608]{2,1,0:T(8,128)(2,1)}, u32[]{:S(2)}, u32[]{:S(2)}) async-start(bf16[8,8,4608]{2,1,0:T(8,128)(2,1)} %broadcast_in_dim.71), calls=%async_computation.10 | async-start | bytes 1179648 | tf_op jit(solution)/shard_map/all_to_all | solution.py:412
  587.8 29.8 %collective-permute-start.38 = (bf16[4,48,1536]{2,1,0:T(8,128)(2,1)}, bf16[4,48,1536]{2,1,0:T(8,128)(2,1)}, u32[]{:S(2)}, u32[]{:S(2)}) collective-permute-start(bf16[4,48,1536]{2,1,0:T(8,128)(2,1)} %dynamic-slice_bitcast_fusion.6), channel_id=1, source_target_pairs={{0,1},{1,0},{2,3},{3,2},{4,5},{5,4},{6,7},{7,6},{8,9},{9,8},{10,11... | collective-permute-start | bytes 1769480 | tf_op jit(solution)/shard_map/ppermute | solution.py:291
  589.3 38.5 %collective-permute-start.39 = (bf16[4,2,48,1536]{3,2,0,1:T(8,128)(2,1)}, bf16[4,2,48,1536]{3,2,0,1:T(8,128)(2,1)}, u32[]{:S(2)}, u32[]{:S(2)}) collective-permute-start(bf16[4,2,48,1536]{3,2,0,1:T(8,128)(2,1)} %copy_bitcast_fusion.1), channel_id=1, source_target_pairs={{0,16},{1,17},{2,18},{3,19},{4,20},{5,21},{6,22},{7,23},{8,24},{9,... | collective-permute-start | bytes 3538952 | tf_op jit(solution)/shard_map/ppermute | solution.py:268
  591.1 36.6 %collective-permute-start.37 = (bf16[2,48,3072]{2,1,0:T(8,128)(2,1)S(1)}, bf16[2,48,3072]{2,1,0:T(8,128)(2,1)}, u32[]{:S(2)}, u32[]{:S(2)}) collective-permute-start(bf16[2,48,3072]{2,1,0:T(8,128)(2,1)S(1)} %pad_maximum_fusion.18), channel_id=1, source_target_pairs={{0,16},{1,17},{2,18},{3,19},{4,20},{5,21},{6,22},{7,23},{8,24},{9,... | collective-permute-start | bytes 1769480 | tf_op jit(solution)/shard_map/ppermute | solution.py:354
  632.4 41.2 %all-to-all-start.11 = ((bf16[4,48,1536]{2,1,0:T(8,128)(2,1)}), bf16[4,48,1536]{2,1,0:T(8,128)(2,1)}, u32[]{:S(2)}, u32[]{:S(2)}) async-start(bf16[4,48,1536]{2,1,0:T(8,128)(2,1)} %get-tuple-element.620), calls=%async_computation.11 | async-start | bytes 1179648 | tf_op jit(solution)/shard_map/all_to_all | solution.py:89
  637.1 36.5 %collective-permute-start.41 = (bf16[4,48,1536]{2,1,0:T(8,128)(2,1)}, bf16[4,48,1536]{2,1,0:T(8,128)(2,1)}, u32[]{:S(2)}, u32[]{:S(2)}) collective-permute-start(bf16[4,48,1536]{2,1,0:T(8,128)(2,1)} %get-tuple-element.621), channel_id=1, source_target_pairs={{0,1},{1,0},{2,3},{3,2},{4,5},{5,4},{6,7},{7,6},{8,9},{9,8},{10,11... | collective-permute-start | bytes 1769480 | tf_op jit(solution)/shard_map/ppermute | solution.py:296
  644.1 29.6 %collective-permute-start.40 = (bf16[144,3072]{1,0:T(8,128)(2,1)}, bf16[144,3072]{1,0:T(8,128)(2,1)}, u32[]{:S(2)}, u32[]{:S(2)}) collective-permute-start(bf16[144,3072]{1,0:T(8,128)(2,1)} %pad_maximum_fusion.13), channel_id=1, source_target_pairs={{0,8},{1,9},{2,10},{3,11},{4,12},{5,13},{6,14},{7,15},{8,0},{9,1},... | collective-permute-start | bytes 2654216 | tf_op jit(solution)/shard_map/ppermute | solution.py:364
  651.4 22.2 %collective-permute-start.43 = (bf16[4,2,48,896]{3,2,1,0:T(8,128)(2,1)}, bf16[4,2,48,896]{3,2,1,0:T(8,128)(2,1)}, u32[]{:S(2)}, u32[]{:S(2)}) collective-permute-start(bf16[4,2,48,896]{3,2,1,0:T(8,128)(2,1)} %dynamic-slice_bitcast_fusion.4), channel_id=1, source_target_pairs={{0,16},{1,17},{2,18},{3,19},{4,20},{5,21},{6,22},{7,23},{8,24},{9,... | collective-permute-start | bytes 2064392 | tf_op jit(solution)/shard_map/ppermute | solution.py:268
  675.3 27.7 %all-to-all-start.12 = ((bf16[8,8,2560]{2,1,0:T(8,128)(2,1)}), bf16[8,8,2560]{2,1,0:T(8,128)(2,1)}, u32[]{:S(2)}, u32[]{:S(2)}) async-start(bf16[8,8,2560]{2,1,0:T(8,128)(2,1)} %broadcast_in_dim.73), calls=%async_computation.12 | async-start | bytes 655360 | tf_op jit(solution)/shard_map/all_to_all | solution.py:412
  684.7 15.5 %collective-permute-start.46 = (bf16[48,1536]{1,0:T(8,128)(2,1)S(1)}, bf16[48,1536]{1,0:T(8,128)(2,1)S(1)}, u32[]{:S(2)}, u32[]{:S(2)}) collective-permute-start(bf16[48,1536]{1,0:T(8,128)(2,1)S(1)} %get-tuple-element.648), channel_id=1, source_target_pairs={{0,6},{1,7},{2,0},{3,1},{4,2},{5,3},{6,4},{7,5},{8,14},{9,15},{10,... | collective-permute-start | bytes 442376 | tf_op jit(solution)/shard_map/ppermute | solution.py:328
  688.0 12.1 %collective-permute-start.45 = (bf16[48,1536]{1,0:T(8,128)(2,1)S(1)}, bf16[48,1536]{1,0:T(8,128)(2,1)S(1)}, u32[]{:S(2)}, u32[]{:S(2)}) collective-permute-start(bf16[48,1536]{1,0:T(8,128)(2,1)S(1)} %get-tuple-element.649), channel_id=1, source_target_pairs={{0,4},{1,5},{2,6},{3,7},{4,0},{5,1},{6,2},{7,3},{8,12},{9,13},{10,... | collective-permute-start | bytes 442376 | tf_op jit(solution)/shard_map/ppermute | solution.py:328
  688.0 14.9 %collective-permute-start.48 = (bf16[64,4608]{1,0:T(8,128)(2,1)}, bf16[64,4608]{1,0:T(8,128)(2,1)}, u32[]{:S(2)}, u32[]{:S(2)}) collective-permute-start(bf16[64,4608]{1,0:T(8,128)(2,1)} %bitcast.66), channel_id=1, source_target_pairs={{0,16},{1,17},{2,18},{3,19},{4,20},{5,21},{6,22},{7,23},{8,24},{9,... | collective-permute-start | bytes 1769480 | tf_op jit(solution)/shard_map/ppermute | solution.py:395
  689.7 15.5 %collective-permute-start.47 = (bf16[4,2,48,896]{3,2,1,0:T(8,128)(2,1)}, bf16[4,2,48,896]{3,2,1,0:T(8,128)(2,1)S(1)}, u32[]{:S(2)}, u32[]{:S(2)}) collective-permute-start(bf16[4,2,48,896]{3,2,1,0:T(8,128)(2,1)} %pad_maximum_fusion.15), channel_id=1, source_target_pairs={{0,1},{1,0},{2,3},{3,2},{4,5},{5,4},{6,7},{7,6},{8,9},{9,8},{10,11... | collective-permute-start | bytes 2064392 | tf_op jit(solution)/shard_map/ppermute | solution.py:302
  706.7 17.4 %collective-permute-start.52 = (bf16[2,64,144]{2,1,0:T(8,128)(2,1)}, bf16[2,64,144]{2,1,0:T(8,128)(2,1)}, u32[]{:S(2)}, u32[]{:S(2)}) collective-permute-start(bf16[2,64,144]{2,1,0:T(8,128)(2,1)} %pad_maximum_fusion.31), channel_id=1, source_target_pairs={{0,8},{1,9},{2,10},{3,11},{4,12},{5,13},{6,14},{7,15},{8,0},{9,1},... | collective-permute-start | bytes 110600 | tf_op jit(solution)/shard_map/ppermute | solution.py:404
  712.9 12.7 %collective-permute-start.53 = (bf16[2,64,4608]{2,1,0:T(8,128)(2,1)}, bf16[2,64,4608]{2,1,0:T(8,128)(2,1)}, u32[]{:S(2)}, u32[]{:S(2)}) collective-permute-start(bf16[2,64,4608]{2,1,0:T(8,128)(2,1)} %pad_maximum_fusion.11), channel_id=1, source_target_pairs={{0,8},{1,9},{2,10},{3,11},{4,12},{5,13},{6,14},{7,15},{8,0},{9,1},... | collective-permute-start | bytes 3538952 | tf_op jit(solution)/shard_map/ppermute | solution.py:404
  714.7 14.5 %collective-permute-start.50 = (bf16[2,48,1536]{2,1,0:T(8,128)(2,1)}, bf16[2,48,1536]{2,1,0:T(8,128)(2,1)}, u32[]{:S(2)}, u32[]{:S(2)}) collective-permute-start(bf16[2,48,1536]{2,1,0:T(8,128)(2,1)} %pad_maximum_fusion.25), channel_id=1, source_target_pairs={{0,16},{1,17},{2,18},{3,19},{4,20},{5,21},{6,22},{7,23},{8,24},{9,... | collective-permute-start | bytes 884744 | tf_op jit(solution)/shard_map/ppermute | solution.py:354
  715.4 14.7 %collective-permute-start.51 = (bf16[64,2560]{1,0:T(8,128)(2,1)}, bf16[64,2560]{1,0:T(8,128)(2,1)}, u32[]{:S(2)}, u32[]{:S(2)}) collective-permute-start(bf16[64,2560]{1,0:T(8,128)(2,1)} %bitcast.88), channel_id=1, source_target_pairs={{0,16},{1,17},{2,18},{3,19},{4,20},{5,21},{6,22},{7,23},{8,24},{9,... | collective-permute-start | bytes 983048 | tf_op jit(solution)/shard_map/ppermute | solution.py:395
  720.4 21.1 %all-to-all-start.13 = ((bf16[4,2,48,896]{3,2,1,0:T(8,128)(2,1)}), bf16[4,2,48,896]{3,2,1,0:T(8,128)(2,1)S(1)}, u32[]{:S(2)}, u32[]{:S(2)}) async-start(bf16[4,2,48,896]{3,2,1,0:T(8,128)(2,1)} %pad_maximum_fusion.16), calls=%async_computation.13 | async-start | bytes 1376256 | tf_op jit(solution)/shard_map/all_to_all | solution.py:89
  744.3 13.9 %collective-permute-start.56 = (bf16[2,64,2560]{2,1,0:T(8,128)(2,1)}, bf16[2,64,2560]{2,1,0:T(8,128)(2,1)}, u32[]{:S(2)}, u32[]{:S(2)}) collective-permute-start(bf16[2,64,2560]{2,1,0:T(8,128)(2,1)} %pad_maximum_fusion.17), channel_id=1, source_target_pairs={{0,8},{1,9},{2,10},{3,11},{4,12},{5,13},{6,14},{7,15},{8,0},{9,1},... | collective-permute-start | bytes 1966088 | tf_op jit(solution)/shard_map/ppermute | solution.py:404
  749.3 12.9 %all-to-all-start.14 = ((bf16[8,8,144]{2,1,0:T(8,128)(2,1)}), bf16[8,8,144]{2,1,0:T(8,128)(2,1)}, u32[]{:S(2)}, u32[]{:S(2)}) async-start(bf16[8,8,144]{2,1,0:T(8,128)(2,1)} %bitcast.245), calls=%async_computation.14 | async-start | bytes 65536 | tf_op jit(solution)/shard_map/all_to_all | solution.py:1288
  (69 other events, 527.3 us)

commit v6 on v5

--- a/solution.py
+++ b/solution.py
@@ -447,7 +447,7 @@
         width = x_ref.shape[1]
         hot = hot_ref[...]
         shift = dot(hot, mod_ref[:, :width])
-        scale = dot(hot, mod_ref[:, width:])
+        scale = dot(hot, mod_ref[:, width : 2 * width])
         normed, _ = normed_rows(x_ref[...].astype(WIDE))
         normed = (normed * (1.0 + scale) + shift).astype(LOW)
         normed_ref[...] = normed
@@ -819,12 +819,12 @@
     hot = hot_ref[...]
     attended = dot(mix_ref[...], w_ref[:, proj_at : proj_at + width])
     att_ref[...] = attended.astype(LOW)
-    gate = dot(hot, mod_ref[:, :width]) * keep_ref[...]
+    gate = dot(hot, mod_ref[:, 2 * width : 3 * width]) * keep_ref[...]
     middle = x_ref[...].astype(WIDE) + gate * attended
     mid_ref[...] = middle
     normed, _ = normed_rows(middle)
-    scale = dot(hot, mod_ref[:, 2 * width : 3 * width])
-    shift = dot(hot, mod_ref[:, width : 2 * width])
+    scale = dot(hot, mod_ref[:, 4 * width : 5 * width])
+    shift = dot(hot, mod_ref[:, 3 * width : 4 * width])
     norm_ref[...] = (normed * (1.0 + scale) + shift).astype(LOW)
 
 
@@ -845,7 +845,7 @@
     width = mid_ref.shape[1]
     hot = hot_ref[...]
     returned = dot(inner_ref[...], w_ref[:, :width])
-    gate = dot(hot, mod_ref[...]) * keep_ref[...]
+    gate = dot(hot, mod_ref[:, 5 * width : 6 * width]) * keep_ref[...]
     out_ref[...] = (mid_ref[...] + gate * returned).astype(LOW)
     upstream = grad_ref[...].astype(WIDE)
     back_ref[:, :width] = (upstream * gate).astype(LOW)
@@ -893,10 +893,10 @@
 
     grad = total_ref[...]
     normed, scale = normed_rows(mid_ref[...])
-    turned = grad * (1.0 + dot(hot, mod_ref[:, 2 * width : 3 * width]))
+    turned = grad * (1.0 + dot(hot, mod_ref[:, 4 * width : 5 * width]))
     total = grad_ref[...].astype(WIDE) + norm_back(normed, scale, turned)
     out_ref[...] = total
-    gate = dot(hot, mod_ref[:, :width]) * keep
+    gate = dot(hot, mod_ref[:, 2 * width : 3 * width]) * keep
     back_ref[:, :width] = (total * gate).astype(LOW)
     if back_ref.shape[1] > width:
         back_ref[:, width:] = jnp.zeros((BLOCK, back_ref.shape[1] - width), LOW)
@@ -1071,7 +1071,8 @@
         jnp.zeros((6 * width,), WIDE), ada_bias.astype(WIDE), (fsdp_place * ada_bias.shape[0],)
     )
     mod_part = (dot(group_act, ada_weight) + bias_row[None, :]).astype(LOW)
-    mod_part, group_act, tables = hold(gathers, (mod_part, group_act, tables))
+    act_far = across_x(group_act)
+    mod_part, group_act, act_far, tables = hold(gathers, (mod_part, group_act, act_far, tables))
 
     early = 2 * width
     modulation = high_and_rest(sum_back(mod_part, items))
@@ -1079,8 +1080,10 @@
     g_one.core("own", "far")
     g_two.y()
     inputs_low = block_in[0]
-    modulation, tables, inputs_low = hold(gathers, (modulation, tables, inputs_low))
-    mod_a, mod_b = modulation[:, :early], modulation[:, early:]
+    every_act = across_replicas(group_act, act_far)
+    modulation, tables, inputs_low, every_act = hold(
+        gathers, (modulation, tables, inputs_low, every_act)
+    )
 
     g_one.core("both")
     g_two.x()
@@ -1089,7 +1092,7 @@
     rot, query_tail, key_tail, hot, keep = tables
     set_out = (gain_q, gain_k, rot, query_tail, key_tail, value_tail, heads // 2, hd)
     normed_a, q_one, k_one, v_one, rq_one, rk_one, one_full = prepare(
-        True, inputs_low, hot, mod_a, g_one, *set_out
+        True, inputs_low, hot, modulation, g_one, *set_out
     )
     gathers = gathers[1:]
     normed_a, q_one, k_one, v_one, rq_one, rk_one, one_full = hold(
@@ -1100,7 +1103,7 @@
     g_gate.y()
     g_up.z()
     q_two, k_two, v_two, rq_two, rk_two, two_full = prepare(
-        False, normed_a, hot, mod_a, g_two, *set_out
+        False, normed_a, hot, modulation, g_two, *set_out
     )
     gathers = gathers[1:]
     normed_a, q_two, k_two, v_two, rq_two, rk_two, two_full, q_one, k_one, v_one = hold(
@@ -1118,9 +1121,8 @@
     g_up.x()
     g_up.core("own", "far")
     g_down.y()
-    mod_mid = mod_b[:, : 3 * width]
     attended, middle, normed_b = call_rows(
-        partial(join_kernel, cut), "join", (mixed, inputs_low, hot, keep), (two_full, mod_mid),
+        partial(join_kernel, cut), "join", (mixed, inputs_low, hot, keep), (two_full, modulation),
         ((width, LOW), (width, WIDE), (width, LOW)),
     )
     middle, normed_b, attended = hold([g_gate], (middle, normed_b, attended))
@@ -1145,7 +1147,7 @@
 
     g_down.core("both")
     block_out, grad_returned, sums_gate_b, down_full = call_rows(
-        down_kernel, "down", (inner, middle, out_grad[0], hot, keep), (mod_b[:, 3 * width :],),
+        down_kernel, "down", (inner, middle, out_grad[0], hot, keep), (modulation,),
         ((width, LOW), (odd, LOW)), ((2 * items, width),), gather=g_down,
     )
 
@@ -1175,7 +1177,7 @@
     grad_middle, grad_attended, sums_mid = call_rows(
         middle_back_kernel, "middle_back",
         (grad_send, grad_keep, middle, out_grad[0], attended, hot, keep),
-        (gate_full, up_full, mod_mid), ((width, WIDE), (odd, LOW)), ((2 * items, 3 * width),),
+        (gate_full, up_full, modulation), ((width, WIDE), (odd, LOW)), ((2 * items, 3 * width),),
         core=core_place, scratch=((BLOCK, width),),
     )
     s_proj = Scatter(mixed, *column_halves(grad_attended))
@@ -1230,7 +1232,10 @@
     joint_two, gains_3 = back(1, 1, joint_two, do=grad_mixed, **two)
     s_tail = Scatter(normed_a, pair=joint_two)
     s_tail.first()
-    gains_3, late_group = hold([s_wide, s_head, s_tail], (gains_3, late_group))
+    shard_down = jnp.concatenate(s_down.halves(), axis=1)[:, :width]
+    gains_3, late_group, shard_down = hold(
+        [s_wide, s_head, s_tail], (gains_3, late_group, shard_down)
+    )
 
     s_tail.core()
     s_head.y_own()
@@ -1242,13 +1247,13 @@
     grad_input, sums_early = call_rows(
         input_back_kernel, "input_back",
         (s_head.live["pair"], s_tail.live["pair"], grad_middle, inputs_low, hot),
-        (one_full, two_full, mod_a), ((width, WIDE),), ((2 * items, 2 * width),),
+        (one_full, two_full, modulation), ((width, WIDE),), ((2 * items, 2 * width),),
         core=core_place,
     )
     if s_head.fast:
         s_head.live.pop("pair")
         s_tail.live.pop("pair")
-    plans = [s_down, s_wide, s_head, s_tail]
+    plans = [s_wide, s_head, s_tail]
     grad_input, sums_early, late_group = hold(plans, (grad_input, sums_early, late_group))
 
     s_head.z_own(apart=True)
@@ -1261,26 +1266,22 @@
     gain_block = jnp.pad(gain_block, ((0, items - 2), (0, 2 * LANES - 2 * hd)))
     early_sums = jnp.concatenate([early_sums, gain_block], axis=1).astype(LOW)
     early_group = gather_rows(early_sums)
-    act_far = across_x(group_act)
     late_far = across_x(late_group)
-    shard_down = jnp.concatenate(s_down.halves(), axis=1)[:, :width]
-    shard_wide = jnp.concatenate(s_wide.halves(), axis=1)
-    plans = [s_head, s_tail]
-    early_group, late_far, act_far, shard_down, shard_wide = hold(
-        plans, (early_group, late_far, act_far, shard_down, shard_wide)
-    )
+    plans = [s_wide, s_head, s_tail]
+    early_group, late_far = hold(plans, (early_group, late_far))
 
     s_head.last_x()
     s_tail.z_both()
     early_far = across_x(early_group)
-    every_act = across_replicas(group_act, act_far)
     late_every = across_replicas(late_group, late_far)
-    shard_late = dot_left(every_act, late_every)
+    shard_late = dot_left(every_act, jnp.pad(late_every, ((0, 0), (early, 0))))
+    shard_wide = jnp.concatenate(s_wide.halves(), axis=1)
+    plans = [s_head, s_tail]
     cond_part = dot_right(early_group[:, :early], ada_weight[:, :early]) + dot_right(
         late_group, ada_weight[:, early:]
     )
-    early_far, cond_part, shard_late, every_act, late_every = hold(
-        plans, (early_far, cond_part, shard_late, every_act, late_every)
+    early_far, cond_part, shard_late, late_every, shard_wide = hold(
+        plans, (early_far, cond_part, shard_late, late_every, shard_wide)
     )
 
     s_head.last_core()
@@ -1289,7 +1290,7 @@
     early_every = across_replicas(early_group, early_far)
     shard_early = dot_left(every_act, early_every[:, :early])
     shard_early = hold(plans, shard_early)
-    shard_ada = jnp.concatenate([shard_early, shard_late], axis=1)
+    shard_ada = lax.dynamic_update_slice(shard_late, shard_early, (0, 0))
     bias_sums = jnp.concatenate(
         [
             jnp.sum(early_every[:, :early].astype(WIDE), axis=0),

time: 788 us -> 770 us (0.977)
  other arithmetic: 92.1 us -> 73.7 us
    ppermute x3, waiting for transfers between devices: 0.01 us -> 9.91 us  [x(): lax.ppermute(self.cut((0, 0, 1 - x), (HIGH_Z, 2, 1)), AXES, TO_X)]
    ppermute x3, waiting for transfers between devices: 1.49 us -> 10.5 us  [z_own(): lines[str(k)] = lax.ppermute(pick(line, (z + k) % 4, 0), AXES, TO_Z[k])]
    all_to_all x10, waiting for transfers between devices: 31.4 us -> 22.6 us  [over_z(): return lax.all_to_all(operand, 'fsdp', 0, 0, axis_index_groups=Z_GROUPS)]
    ppermute x4, waiting for transfers between devices: 10.1 us -> 1.69 us  [last_x(): self.live = {'part': part, 'other': lax.ppermute(part, AXES, TO_X)}]
  transfers between devices with their start and end apart: 73 -> 73, of which waited for: 26 -> 27; matrix products, arithmetic and copies ran while one was open for 20% -> 17% of each run, Pallas kernels for 35% -> 36%
where the time goes in v6:
time: 770 us; the launch traced here: 760 us
  Pallas kernels  293 us (38%)
  waiting for transfers between devices  123 us (16%)
  starting transfers between devices  120 us (16%)
  matrix products  75.9 us (10%)
  other arithmetic  73.7 us (10%)
  local copies, waits for them, and re-layouts  70.3 us (9%)
    pallas_call x5, Pallas kernels, call_placed(): pl.pallas_call(run, in_specs=[pl.BlockSpec(memory_space=pltpu.SMEM)] + [a...  90.6 us
    pallas_call x4, Pallas kernels, call_rows(): pl.pallas_call(kernel, in_specs=specs, out_specs=out_specs, out_shape=out...  84.7 us
    pallas_call x4, Pallas kernels, attend_back(): pl.pallas_call(partial(back_kernel, hd, c, score_scale, part), grid=(n //...  81 us
    dot_general x12, matrix products, dot_left(): lax.dot_general(left, right, (((0,), (0,)), ((), ())), preferred_element_...  70.8 us
    all_to_all x10, starting transfers between devices, over_z(): return lax.all_to_all(operand, 'fsdp', 0, 0, axis_index_groups=Z_GROUPS)  44.6 us
    ppermute x5, waiting for transfers between devices, y(): self.live['far'] = lax.ppermute(self.live['own'], AXES, TO_Y)  30 us
    all_to_all x10, waiting for transfers between devices, over_z(): return lax.all_to_all(operand, 'fsdp', 0, 0, axis_index_groups=Z_GROUPS)  22.6 us
    pallas_call x1, Pallas kernels, attend(): pl.pallas_call(partial(attend_kernel, hd, c), grid=(n // BLOCK,), in_spec...  22.6 us
  transfers between devices with their start and end apart: 73, of which 27 were waited for; matrix products, arithmetic and copies ran while one was open for 17% of the time, Pallas kernels for 36%

profile of v6, /device:TPU:1, one launch (start us, length us, event | category | flops | bytes accessed | tf_op | source)
XLA Modules:
  0.0 759.6 jit_solution(12816678759743381152)
XLA Ops:
  2.1 6.4 all-to-all-start.1
  17.1 4.5 all-to-all-start
  25.1 2.7 fusion.60
  27.7 11.5 %all-to-all-done.refs_1_ = bf16[4,2,48,896]{3,2,1,0:T(8,128)(2,1)} async-done(((bf16[4,2,48,896]{3,2,1,0:T(8,128)(2,1)}), bf16[4,2,48,896]{3,2,1,0:T(8,128)(2,1)}, u32[]{:S(2)}, u32[]{:S(2)}) %all-to-all-start) | async-done | bytes 688160 | tf_op jit(solution)/shard_map/all_to_all | solution.py:89
  40.5 4.3 all-to-all-start.2
  44.8 5.4 multiply_cosine_fusion
  59.5 2.8 pad_maximum_fusion.2.refs_12_.rot_ref
  67.1 4.6 collective-permute-done.refs_2_
  72.8 4.1 all-to-all-start.3
  77.9 3.0 collective-permute-start.4
  87.5 10.0 %all-to-all-done.3 = bf16[8,8,6912]{2,1,0:T(8,128)(2,1)S(1)} async-done(((bf16[8,8,6912]{2,1,0:T(8,128)(2,1)}), bf16[8,8,6912]{2,1,0:T(8,128)(2,1)S(1)}, u32[]{:S(2)}, u32[]{:S(2)}) %all-to-all-start.3) | async-done | bytes 884768 | tf_op jit(solution)/shard_map/all_to_all | solution.py:426
  98.3 2.6 collective-permute-done.2.refs_3_
  100.9 15.8 %collective-permute-done.5.refs_2_ = bf16[4,2,48,1536]{3,2,1,0:T(8,128)(2,1)} collective-permute-done((bf16[4,2,48,1536]{3,2,1,0:T(8,128)(2,1)}, bf16[4,2,48,1536]{3,2,1,0:T(8,128)(2,1)}, u32[]{:S(2)}, u32[]{:S(2)}) %collective-permute-start.5) | collective-permute-done | bytes 1179680 | tf_op jit(solution)/shard_map/ppermute | solution.py:205
  117.9 4.2 all-to-all-start.4
  131.7 20.7 %prepare.2 = (bf16[1024,1152]{1,0:T(8,128)(2,1)}, bf16[8,1024,128]{2,1,0:T(8,128)(2,1)}, bf16[8,1024,128]{2,1,0:T(8,128)(2,1)}, bf16[8,1024,128]{2,1,0:T(8,128)(...) custom-call(s32[4]{0:T(128)} %pad_add_fusion.refs_0_, ...), custom_call_target="tpu_custom_call" | custom-call | flops 8153726976 | bytes 20971520 | tf_op jit(solution)/shard_map/prepare/pallas_call | solution.py:171
  156.6 4.8 all-to-all-start.5
  161.7 21.1 %prepare.3 = (bf16[8,1024,128]{2,1,0:T(8,128)(2,1)}, bf16[8,1024,128]{2,1,0:T(8,128)(2,1)}, bf16[8,1024,128]{2,1,0:T(8,128)(2,1)}, bf16[8,1024,128]{2,1,0:T(8,12...) custom-call(s32[4]{0:T(128)} %pad_add_fusion.refs_0_, ...), custom_call_target="tpu_custom_call" | custom-call | flops 8153726976 | bytes 20971520 | tf_op jit(solution)/shard_map/prepare/pallas_call | solution.py:171
  182.7 6.0 collective-permute-done.11.refs_2_
  191.2 3.5 all-to-all-start.6
  198.7 22.6 %attend.1 = (bf16[1024,1152]{1,0:T(8,128)(2,1)}, bf16[8,1024,128]{2,1,0:T(8,128)(2,1)}, bf16[8,1024,128]{2,1,0:T(8,128)(2,1)}) custom-call(bf16[8,1024,128]{2,1,0:T(8,128)(2,1)} %get-tuple-element.388.refs_0_, bf16[8,1024,128]{2,1,0:T(8,128)(2,1)} %get-tuple-element.389.refs_1_.k_ref, bf16[8,1024,128]{2,1,0:T(8,128)(2,1)} %get-tuple-element.390.refs_2_.v_ref, ...), custom_call_target="tpu_custom_call" | custom-call | flops 5368709120 | bytes 20971520 | tf_op jit(solution)/shard_map/attend/pallas_call | solution.py:568
  231.7 11.3 %join.1 = (bf16[1024,1152]{1,0:T(8,128)(2,1)}, f32[1024,1152]{1,0:T(8,128)}, bf16[1024,1152]{1,0:T(8,128)(2,1)}) custom-call(bf16[1024,1152]{1,0:T(8,128)(2,1)} %get-tuple-element.405.mix_ref, bf16[1024,1152]{1,0:T(8,128)(2,1)} %bitcast.313, bf16[1024,16]{1,0:T(8,128)(2,1)} %copy.88.refs_8_.hot_ref.refs_10_, f32[1024,1]{1,0:T(8,128)} %copy.91.keep_ref.refs_11_, ...), custom_call_target="tpu_custom_call" | custom-call | flops 7247757312 | bytes 12054528 | tf_op jit(solution)/shard_map/join/pallas_call | solution.py:809
  243.1 14.6 %gate.1 = (bf16[1024,3072]{1,0:T(8,128)(2,1)}, bf16[1152,3072]{1,0:T(8,128)(2,1)}) custom-call(s32[4]{0:T(128)} %pad_add_fusion.refs_0_, bf16[4,2,48,1536]{3,2,1,0:T(8,128)(2,1)} %copy-done.9, bf16[4,2,48,1536]{3,2,1,0:T(8,128)(2,1)} %collective-permute-done.11.refs_2_, bf16[4,2,48,1536]{3,2,1,0:T(8,128)(2,1)} %copy-done.47, ...), custom_call_target="tpu_custom_call" | custom-call | flops 7247757312 | bytes 2359296 | tf_op jit(solution)/shard_map/gate/pallas_call | solution.py:171
  258.6 3.0 collective-permute-done.20.refs_2_
  265.8 16.6 %up.1 = (bf16[1024,3072]{1,0:T(8,128)(2,1)}, bf16[1024,3072]{1,0:T(8,128)(2,1)}, bf16[1152,3072]{1,0:T(8,128)(2,1)}) custom-call(s32[4]{0:T(128)} %pad_add_fusion.refs_0_, bf16[4,2,48,1536]{3,2,1,0:T(8,128)(2,1)} %all-to-all-done.5.refs_1_, bf16[4,2,48,1536]{3,2,1,0:T(8,128)(2,1)} %collective-permute-done.16.refs_2_, ...), custom_call_target="tpu_custom_call" | custom-call | flops 7247757312 | bytes 8650752 | tf_op jit(solution)/shard_map/up/pallas_call | solution.py:171
  282.4 11.4 %collective-permute-done.22.refs_3_ = bf16[4,2,128,640]{3,2,1,0:T(8,128)(2,1)} collective-permute-done((bf16[4,2,128,640]{3,2,1,0:T(8,128)(2,1)S(1)}, bf16[4,2,128,640]{3,2,1,0:T(8,128)(2,1)}, u32[]{:S(2)}, u32[]{:S(2)}) %collective-permute-start.22) | collective-permute-done | bytes 1310752 | tf_op jit(solution)/shard_map/ppermute | solution.py:210
  296.8 2.9 collective-permute-done.26.refs_6_
  300.7 17.5 %down.1 = (bf16[1024,1152]{1,0:T(8,128)(2,1)}, bf16[1024,1280]{1,0:T(8,128)(2,1)}, f32[16,1152]{1,0:T(8,128)}, bf16[3072,1280]{1,0:T(8,128)(2,1)}) custom-call(s32[4]{0:T(128)} %pad_add_fusion.refs_0_, bf16[4,2,128,640]{3,2,1,0:T(8,128)(2,1)} %copy-done.6, bf16[4,2,128,640]{3,2,1,0:T(8,128)(2,1)} %copy-done.32, ...), custom_call_target="tpu_custom_call" | custom-call | flops 8053063680 | bytes 13627392 | tf_op jit(solution)/shard_map/down/pallas_call | solution.py:171
  320.4 9.4 %convolution_convert_fusion.1 = bf16[3072,640]{1,0:T(8,128)(2,1)} fusion(bf16[1024,3072]{1,0:T(8,128)(2,1)} %get-tuple-element.447.refs_7_, bf16[1024,1280]{1,0:T(8,128)(2,1)S(1)} %copy-done.31, s32[]{:T(128)S(6)} %select_n.440), kind=kOutput, calls=%fused_computation.5 | convolution fusion | flops 4028497920 | bytes 11534340 | tf_op jit(solution)/shard_map/dot_general | solution.py:29
  330.2 18.6 %inner_back.1 = (bf16[1024,3072]{1,0:T(8,128)(2,1)}, bf16[1024,3072]{1,0:T(8,128)(2,1)}) custom-call(s32[1]{0:T(128)} %bitcast.1.core_ref, bf16[1024,1280]{1,0:T(8,128)(2,1)} %get-tuple-element.459.grad_ref, bf16[1024,3072]{1,0:T(8,128)(2,1)} %get-tuple-element.460.refs_8_.gate_ref, bf16[1024,3072]{1,0:T(8,128)(2,1)} %get-tuple-element.461.up_ref, ...), custom_call_target="tpu_custom_call" | custom-call | flops 8053063680 | bytes 23068672 | tf_op jit(solution)/shard_map/inner_back/pallas_call | solution.py:809
  348.8 10.0 %add_convert_fusion.1 = bf16[3072,640]{1,0:T(8,128)(2,1)} fusion(bf16[3072,640]{1,0:T(8,128)(2,1)S(1)} %collective-permute-done.27, bf16[1024,3072]{1,0:T(8,128)(2,1)} %get-tuple-element.447.refs_7_, bf16[1024,640]{1,0:T(8,128)(2,1)S(1)} %constant_dynamic-slice_fusion.3), kind=kOutput, calls=%fused_computation.4 | convolution fusion | flops 4032430080 | bytes 15466496 | tf_op jit(solution)/shard_map/dot_general | solution.py:29
  358.7 9.5 %convolution_convert_fusion = bf16[1152,3072]{1,0:T(8,128)(2,1)} fusion(bf16[1024,1152]{1,0:T(8,128)(2,1)S(1)} %copy-done.51, bf16[1024,3072]{1,0:T(8,128)(2,1)S(1)} %copy-done.53), kind=kOutput, calls=%fused_computation.1 | convolution fusion | flops 7251296256 | bytes 15728640 | tf_op jit(solution)/shard_map/dot_general | solution.py:29
  371.5 33.3 %middle_back.1 = (f32[1024,1152]{1,0:T(8,128)}, bf16[1024,1280]{1,0:T(8,128)(2,1)}, f32[16,3456]{1,0:T(8,128)}) custom-call(s32[1]{0:T(128)} %bitcast.1.core_ref, bf16[1024,3072]{1,0:T(8,128)(2,1)} %get-tuple-element.473.send_ref, bf16[1024,3072]{1,0:T(8,128)(2,1)} %get-tuple-element.484.mine_ref, f32[1024,1152]{1,0:T(8,128)} %get-tuple-element.475.refs_8_.mid_ref, ...), custom_call_target="tpu_custom_call" | custom-call | flops 14495514624 | bytes 36433920 | tf_op jit(solution)/shard_map/middle_back/pallas_call | solution.py:809
  404.8 3.6 constant_dynamic-slice_fusion.1
  408.5 11.8 %add_convert_fusion = bf16[1152,3072]{1,0:T(8,128)(2,1)S(1)} fusion(bf16[1152,3072]{1,0:T(8,128)(2,1)} %collective-permute-done.29, bf16[1024,1152]{1,0:T(8,128)(2,1)S(1)} %copy-done.52, bf16[1024,3072]{1,0:T(8,128)(2,1)} %get-tuple-element.484.mine_ref), kind=kOutput, calls=%fused_computation | convolution fusion | flops 7258374144 | bytes 22806528 | tf_op jit(solution)/shard_map/dot_general | solution.py:29
  426.3 12.7 %spread.1.do_ref = bf16[16,1024,128]{2,1,0:T(8,128)(2,1)} custom-call(bf16[1024,1280]{1,0:T(8,128)(2,1)} %get-tuple-element.492.ga_ref, bf16[1152,3072]{1,0:T(8,128)(2,1)} %get-tuple-element.407.w_ref.wt_ref, bf16[1024,1152]{1,0:T(8,128)(2,1)} %get-tuple-element.405.mix_ref), custom_call_target="tpu_custom_call" | custom-call | flops 2717908992 | bytes 12582912 | tf_op jit(solution)/shard_map/spread/pallas_call | solution.py:612
  439.0 4.5 convolution_convert_fusion.4
  444.1 8.7 %collective-permute-done.31 = bf16[2,2,48,3072]{3,2,1,0:T(8,128)(2,1)} collective-permute-done((bf16[2,2,48,3072]{3,2,1,0:T(8,128)(2,1)}, bf16[2,2,48,3072]{3,2,1,0:T(8,128)(2,1)}, u32[]{:S(2)}, u32[]{:S(2)}) %collective-permute-start.31) | collective-permute-done | bytes 1179680 | tf_op jit(solution)/shard_map/ppermute | solution.py:272
  455.7 4.1 all-to-all-start.7
  465.3 20.0 %attend_back.4 = (bf16[2,1024,896]{2,1,0:T(8,128)(2,1)}, f32[2,8,128]{2,1,0:T(8,128)}) custom-call(s32[1]{0:T(128)} %bitcast.1.core_ref, bf16[8,1024,128]{2,1,0:T(8,128)(2,1)} %get-tuple-element.500.q_ref, bf16[8,1024,128]{2,1,0:T(8,128)(2,1)} %get-tuple-element.389.refs_1_.k_ref, bf16[8,1024,128]{2,1,0:T(8,128)(2,1)} %get-tuple-element.390.refs_2_.v_ref, ...), custom_call_target="tpu_custom_call" | custom-call | flops 3355443200 | bytes 10485760 | tf_op jit(solution)/shard_map/attend_back/pallas_call | solution.py:716
  485.4 6.5 collective-permute-done.32
  494.8 3.9 fusion.7
  498.8 5.2 all-to-all-start.8
  505.5 20.2 %attend_back.5 = (bf16[2,1024,896]{2,1,0:T(8,128)(2,1)}, f32[2,8,128]{2,1,0:T(8,128)}) custom-call(s32[1]{0:T(128)} %bitcast.1.core_ref, bf16[8,1024,128]{2,1,0:T(8,128)(2,1)} %get-tuple-element.500.q_ref, bf16[8,1024,128]{2,1,0:T(8,128)(2,1)} %get-tuple-element.389.refs_1_.k_ref, ...), custom_call_target="tpu_custom_call", output_to_operand_aliasing={{0}: (10, {})} | custom-call | flops 3355443200 | bytes 10485760 | tf_op jit(solution)/shard_map/attend_back/pallas_call | solution.py:716
  525.7 5.6 convolution_convert_fusion.3
  531.3 4.5 fusion.5
  539.9 2.9 add_convert_fusion.2
  542.8 5.0 all-to-all-start.9
  548.7 20.5 %attend_back.6 = (bf16[2,1024,896]{2,1,0:T(8,128)(2,1)}, f32[2,8,128]{2,1,0:T(8,128)}) custom-call(s32[1]{0:T(128)} %bitcast.1.core_ref, bf16[8,1024,128]{2,1,0:T(8,128)(2,1)} %get-tuple-element.528.q_ref, bf16[8,1024,128]{2,1,0:T(8,128)(2,1)} %get-tuple-element.392.refs_4_.k_ref, bf16[8,1024,128]{2,1,0:T(8,128)(2,1)} %get-tuple-element.393.refs_5_.v_ref, ...), custom_call_target="tpu_custom_call" | custom-call | flops 3355443200 | bytes 10485760 | tf_op jit(solution)/shard_map/attend_back/pallas_call | solution.py:716
  569.3 4.3 fusion.1
  584.1 4.4 all-to-all-start.10
  592.7 20.2 %attend_back.7 = (bf16[2,1024,896]{2,1,0:T(8,128)(2,1)}, f32[2,8,128]{2,1,0:T(8,128)}) custom-call(s32[1]{0:T(128)} %bitcast.1.core_ref, bf16[8,1024,128]{2,1,0:T(8,128)(2,1)} %get-tuple-element.528.q_ref, bf16[8,1024,128]{2,1,0:T(8,128)(2,1)} %get-tuple-element.392.refs_4_.k_ref, ...), custom_call_target="tpu_custom_call", output_to_operand_aliasing={{0}: (10, {})} | custom-call | flops 3355443200 | bytes 10485760 | tf_op jit(solution)/shard_map/attend_back/pallas_call | solution.py:716
  615.6 4.0 convolution_convert_fusion.2
  619.6 9.9 %collective-permute-done.41 = bf16[4,2,48,1536]{3,2,0,1:T(8,128)(2,1)} collective-permute-done((bf16[4,2,48,1536]{3,2,0,1:T(8,128)(2,1)}, bf16[4,2,48,1536]{3,2,0,1:T(8,128)(2,1)}, u32[]{:S(2)}, u32[]{:S(2)}) %collective-permute-start.41) | collective-permute-done | bytes 1179680 | tf_op jit(solution)/shard_map/ppermute | solution.py:268
  634.1 4.7 all-to-all-start.11
  639.1 3.4 collective-permute-start.44
  646.5 4.4 fusion.2
  653.9 21.5 %input_back.1 = (f32[1024,1152]{1,0:T(8,128)}, f32[16,2304]{1,0:T(8,128)}) custom-call(s32[1]{0:T(128)} %bitcast.1.core_ref, bf16[2,1024,896]{2,1,0:T(8,128)(2,1)} %get-tuple-element.555.one_ref, bf16[2,1024,896]{2,1,0:T(8,128)(2,1)} %get-tuple-element.556.two_ref, f32[1024,1152]{1,0:T(8,128)} %get-tuple-element.557.mid_ref, bf16[1024,1152]{1,0:T(8,128)(2,1)} %bitcast.314, ...), custom_call_target="tpu_custom_call" | custom-call | flops 11475615744 | bytes 25878528 | tf_op jit(solution)/shard_map/input_back/pallas_call | solution.py:809
  677.1 5.7 all-to-all-start.12
  689.9 3.0 collective-permute-start.48
  695.4 10.2 %collective-permute-done.47 = bf16[48,1536]{1,0:T(8,128)(2,1)S(1)} collective-permute-done((bf16[48,1536]{1,0:T(8,128)(2,1)S(1)}, bf16[48,1536]{1,0:T(8,128)(2,1)S(1)}, u32[]{:S(2)}, u32[]{:S(2)}) %collective-permute-start.47) | collective-permute-done | bytes 147488 | tf_op jit(solution)/shard_map/ppermute | solution.py:328
  712.3 4.2 all-to-all-start.13
  725.8 2.6 fusion.3
  728.4 5.7 all-to-all-done.13
  741.4 3.5 all-to-all-start.14
  (404 shorter events, 185.7 us)
Async XLA Ops:
  2.1 14.1 %all-to-all-start.1 = ((bf16[8,8,144]{2,1,0:T(8,128)(2,1)}), bf16[8,8,144]{2,1,0:T(8,128)(2,1)S(1)}, u32[]{:S(2)}, u32[]{:S(2)}) async-start(bf16[8,8,144]{2,1,0:T(8,128)(2,1)} %copy.84), calls=%async_computation.1 | async-start | bytes 65536 | tf_op jit(solution)/shard_map/all_to_all | solution.py:420
  17.1 22.1 %all-to-all-start = ((bf16[4,2,48,896]{3,2,1,0:T(8,128)(2,1)}), bf16[4,2,48,896]{3,2,1,0:T(8,128)(2,1)}, u32[]{:S(2)}, u32[]{:S(2)}) async-start(bf16[4,2,48,896]{3,2,1,0:T(8,128)(2,1)} %broadcast_in_dim.60), calls=%async_computation | async-start | bytes 1376256 | tf_op jit(solution)/shard_map/all_to_all | solution.py:89
  40.5 32.4 %all-to-all-start.2 = ((bf16[4,2,48,1536]{3,2,1,0:T(8,128)(2,1)}), bf16[4,2,48,1536]{3,2,1,0:T(8,128)(2,1)}, u32[]{:S(2)}, u32[]{:S(2)}) async-start(bf16[4,2,48,1536]{3,2,1,0:T(8,128)(2,1)} %broadcast_in_dim.61), calls=%async_computation.2 | async-start | bytes 2359296 | tf_op jit(solution)/shard_map/all_to_all | solution.py:89
  55.9 15.8 %collective-permute-start = (bf16[4,2,48,896]{3,2,1,0:T(8,128)(2,1)}, bf16[4,2,48,896]{3,2,1,0:T(8,128)(2,1)}, u32[]{:S(2)}, u32[]{:S(2)}) collective-permute-start(bf16[4,2,48,896]{3,2,1,0:T(8,128)(2,1)} %all-to-all-done.refs_1_), channel_id=1, source_target_pairs={{0,1},{1,0},{2,3},{3,2},{4,5},{5,4},{6,7},{7,6},{8,9},{9,8},{10,11... | collective-permute-start | bytes 2064392 | tf_op jit(solution)/shard_map/ppermute | solution.py:205
  72.8 24.6 %all-to-all-start.3 = ((bf16[8,8,6912]{2,1,0:T(8,128)(2,1)}), bf16[8,8,6912]{2,1,0:T(8,128)(2,1)S(1)}, u32[]{:S(2)}, u32[]{:S(2)}) async-start(bf16[8,8,6912]{2,1,0:T(8,128)(2,1)} %bitcast.20), calls=%async_computation.3 | async-start | bytes 1769472 | tf_op jit(solution)/shard_map/all_to_all | solution.py:426
  77.9 23.0 %collective-permute-start.4 = (bf16[4,2,48,896]{3,2,1,0:T(8,128)(2,1)}, bf16[4,2,48,896]{3,2,1,0:T(8,128)(2,1)}, u32[]{:S(2)}, u32[]{:S(2)}) collective-permute-start(bf16[4,2,48,896]{3,2,1,0:T(8,128)(2,1)} %all-to-all-done.refs_1_), channel_id=1, source_target_pairs={{0,8},{1,9},{2,10},{3,11},{4,12},{5,13},{6,14},{7,15},{8,0},{9,1},... | collective-permute-start | bytes 2064392 | tf_op jit(solution)/shard_map/ppermute | solution.py:215
  81.9 19.0 %collective-permute-start.3 = (bf16[4,2,48,896]{3,2,1,0:T(8,128)(2,1)}, bf16[4,2,48,896]{3,2,1,0:T(8,128)(2,1)}, u32[]{:S(2)}, u32[]{:S(2)}) collective-permute-start(bf16[4,2,48,896]{3,2,1,0:T(8,128)(2,1)} %collective-permute-done.refs_2_), channel_id=1, source_target_pairs={{0,8},{1,9},{2,10},{3,11},{4,12},{5,13},{6,14},{7,15},{8,0},{9,1},... | collective-permute-start | bytes 2064392 | tf_op jit(solution)/shard_map/ppermute | solution.py:215
  83.5 17.4 %collective-permute-start.2 = (bf16[4,2,48,896]{3,2,1,0:T(8,128)(2,1)}, bf16[4,2,48,896]{3,2,1,0:T(8,128)(2,1)}, u32[]{:S(2)}, u32[]{:S(2)}) collective-permute-start(bf16[4,2,48,896]{3,2,1,0:T(8,128)(2,1)} %pad_maximum_fusion.13), channel_id=1, source_target_pairs={{0,16},{1,17},{2,18},{3,19},{4,20},{5,21},{6,22},{7,23},{8,24},{9,... | collective-permute-start | bytes 2064392 | tf_op jit(solution)/shard_map/ppermute | solution.py:210
  84.7 31.9 %collective-permute-start.5 = (bf16[4,2,48,1536]{3,2,1,0:T(8,128)(2,1)}, bf16[4,2,48,1536]{3,2,1,0:T(8,128)(2,1)}, u32[]{:S(2)}, u32[]{:S(2)}) collective-permute-start(bf16[4,2,48,1536]{3,2,1,0:T(8,128)(2,1)} %all-to-all-done.2.refs_1_), channel_id=1, source_target_pairs={{0,1},{1,0},{2,3},{3,2},{4,5},{5,4},{6,7},{7,6},{8,9},{9,8},{10,11... | collective-permute-start | bytes 3538952 | tf_op jit(solution)/shard_map/ppermute | solution.py:205
  117.9 36.6 %all-to-all-start.4 = ((bf16[4,2,48,1536]{3,2,1,0:T(8,128)(2,1)}), bf16[4,2,48,1536]{3,2,1,0:T(8,128)(2,1)S(1)}, u32[]{:S(2)}, u32[]{:S(2)}) async-start(bf16[4,2,48,1536]{3,2,1,0:T(8,128)(2,1)} %broadcast_in_dim.65), calls=%async_computation.4 | async-start | bytes 2359296 | tf_op jit(solution)/shard_map/all_to_all | solution.py:89
  122.1 9.6 %collective-permute-start.10 = (bf16[4,2,48,896]{3,2,1,0:T(8,128)(2,1)}, bf16[4,2,48,896]{3,2,1,0:T(8,128)(2,1)}, u32[]{:S(2)}, u32[]{:S(2)}) collective-permute-start(bf16[4,2,48,896]{3,2,1,0:T(8,128)(2,1)} %collective-permute-done.2.refs_3_), channel_id=1, source_target_pairs={{0,8},{1,9},{2,10},{3,11},{4,12},{5,13},{6,14},{7,15},{8,0},{9,1},... | collective-permute-start | bytes 2064392 | tf_op jit(solution)/shard_map/ppermute | solution.py:215
  126.6 27.9 %collective-permute-start.7 = (bf16[4,2,48,1536]{3,2,1,0:T(8,128)(2,1)}, bf16[4,2,48,1536]{3,2,1,0:T(8,128)(2,1)}, u32[]{:S(2)}, u32[]{:S(2)}) collective-permute-start(bf16[4,2,48,1536]{3,2,1,0:T(8,128)(2,1)} %pad_maximum_fusion.7), channel_id=1, source_target_pairs={{0,16},{1,17},{2,18},{3,19},{4,20},{5,21},{6,22},{7,23},{8,24},{9,... | collective-permute-start | bytes 3538952 | tf_op jit(solution)/shard_map/ppermute | solution.py:210
  127.3 27.2 %collective-permute-start.9 = (bf16[4,2,48,1536]{3,2,1,0:T(8,128)(2,1)}, bf16[4,2,48,1536]{3,2,1,0:T(8,128)(2,1)}, u32[]{:S(2)}, u32[]{:S(2)}) collective-permute-start(bf16[4,2,48,1536]{3,2,1,0:T(8,128)(2,1)} %all-to-all-done.2.refs_1_), channel_id=1, source_target_pairs={{0,8},{1,9},{2,10},{3,11},{4,12},{5,13},{6,14},{7,15},{8,0},{9,1},... | collective-permute-start | bytes 3538952 | tf_op jit(solution)/shard_map/ppermute | solution.py:215
  127.6 26.9 %collective-permute-start.8 = (bf16[4,2,48,1536]{3,2,1,0:T(8,128)(2,1)}, bf16[4,2,48,1536]{3,2,1,0:T(8,128)(2,1)}, u32[]{:S(2)}, u32[]{:S(2)}) collective-permute-start(bf16[4,2,48,1536]{3,2,1,0:T(8,128)(2,1)} %collective-permute-done.5.refs_2_), channel_id=1, source_target_pairs={{0,8},{1,9},{2,10},{3,11},{4,12},{5,13},{6,14},{7,15},{8,0},{9,1},... | collective-permute-start | bytes 3538952 | tf_op jit(solution)/shard_map/ppermute | solution.py:215
  156.6 33.2 %all-to-all-start.5 = ((bf16[4,2,48,1536]{3,2,1,0:T(8,128)(2,1)}), bf16[4,2,48,1536]{3,2,1,0:T(8,128)(2,1)}, u32[]{:S(2)}, u32[]{:S(2)}) async-start(bf16[4,2,48,1536]{3,2,1,0:T(8,128)(2,1)} %broadcast_in_dim.68), calls=%async_computation.5 | async-start | bytes 2359296 | tf_op jit(solution)/shard_map/all_to_all | solution.py:89
  161.4 27.3 %collective-permute-start.11 = (bf16[4,2,48,1536]{3,2,1,0:T(8,128)(2,1)S(1)}, bf16[4,2,48,1536]{3,2,1,0:T(8,128)(2,1)}, u32[]{:S(2)}, u32[]{:S(2)}) collective-permute-start(bf16[4,2,48,1536]{3,2,1,0:T(8,128)(2,1)S(1)} %all-to-all-done.4.refs_1_), channel_id=1, source_target_pairs={{0,1},{1,0},{2,3},{3,2},{4,5},{5,4},{6,7},{7,6},{8,9},{9,8},{10,11... | collective-permute-start | bytes 3538952 | tf_op jit(solution)/shard_map/ppermute | solution.py:205
  191.2 34.3 %all-to-all-start.6 = ((bf16[4,2,128,640]{3,2,1,0:T(8,128)(2,1)}), bf16[4,2,128,640]{3,2,1,0:T(8,128)(2,1)S(1)}, u32[]{:S(2)}, u32[]{:S(2)}) async-start(bf16[4,2,128,640]{3,2,1,0:T(8,128)(2,1)} %broadcast_in_dim.69), calls=%async_computation.6 | async-start | bytes 2621440 | tf_op jit(solution)/shard_map/all_to_all | solution.py:89
  196.0 26.3 %collective-permute-start.13 = (bf16[4,2,48,1536]{3,2,1,0:T(8,128)(2,1)S(1)}, bf16[4,2,48,1536]{3,2,1,0:T(8,128)(2,1)S(1)}, u32[]{:S(2)}, u32[]{:S(2)}) collective-permute-start(bf16[4,2,48,1536]{3,2,1,0:T(8,128)(2,1)S(1)} %pad_maximum_fusion.8), channel_id=1, source_target_pairs={{0,16},{1,17},{2,18},{3,19},{4,20},{5,21},{6,22},{7,23},{8,24},{9,... | collective-permute-start | bytes 3538952 | tf_op jit(solution)/shard_map/ppermute | solution.py:210
  196.8 26.2 %collective-permute-start.16 = (bf16[4,2,48,1536]{3,2,1,0:T(8,128)(2,1)}, bf16[4,2,48,1536]{3,2,1,0:T(8,128)(2,1)}, u32[]{:S(2)}, u32[]{:S(2)}) collective-permute-start(bf16[4,2,48,1536]{3,2,1,0:T(8,128)(2,1)} %all-to-all-done.5.refs_1_), channel_id=1, source_target_pairs={{0,1},{1,0},{2,3},{3,2},{4,5},{5,4},{6,7},{7,6},{8,9},{9,8},{10,11... | collective-permute-start | bytes 3538952 | tf_op jit(solution)/shard_map/ppermute | solution.py:205
  196.8 26.2 %collective-permute-start.15 = (bf16[4,2,48,1536]{3,2,1,0:T(8,128)(2,1)S(1)}, bf16[4,2,48,1536]{3,2,1,0:T(8,128)(2,1)S(1)}, u32[]{:S(2)}, u32[]{:S(2)}) collective-permute-start(bf16[4,2,48,1536]{3,2,1,0:T(8,128)(2,1)S(1)} %copy-done.10), channel_id=1, source_target_pairs={{0,8},{1,9},{2,10},{3,11},{4,12},{5,13},{6,14},{7,15},{8,0},{9,1},... | collective-permute-start | bytes 3538952 | tf_op jit(solution)/shard_map/ppermute | solution.py:215
  198.7 25.7 %collective-permute-start.14 = (bf16[4,2,48,1536]{3,2,1,0:T(8,128)(2,1)}, bf16[4,2,48,1536]{3,2,1,0:T(8,128)(2,1)}, u32[]{:S(2)}, u32[]{:S(2)}) collective-permute-start(bf16[4,2,48,1536]{3,2,1,0:T(8,128)(2,1)} %collective-permute-done.11.refs_2_), channel_id=1, source_target_pairs={{0,8},{1,9},{2,10},{3,11},{4,12},{5,13},{6,14},{7,15},{8,0},{9,1},... | collective-permute-start | bytes 3538952 | tf_op jit(solution)/shard_map/ppermute | solution.py:215
  225.5 17.5 %collective-permute-start.21 = (bf16[4,2,48,1536]{3,2,1,0:T(8,128)(2,1)}, bf16[4,2,48,1536]{3,2,1,0:T(8,128)(2,1)}, u32[]{:S(2)}, u32[]{:S(2)}) collective-permute-start(bf16[4,2,48,1536]{3,2,1,0:T(8,128)(2,1)} %copy-done.47), channel_id=1, source_target_pairs={{0,8},{1,9},{2,10},{3,11},{4,12},{5,13},{6,14},{7,15},{8,0},{9,1},... | collective-permute-start | bytes 3538952 | tf_op jit(solution)/shard_map/ppermute | solution.py:215
  229.1 29.4 %collective-permute-start.19 = (bf16[4,2,48,1536]{3,2,1,0:T(8,128)(2,1)}, bf16[4,2,48,1536]{3,2,1,0:T(8,128)(2,1)S(1)}, u32[]{:S(2)}, u32[]{:S(2)}) collective-permute-start(bf16[4,2,48,1536]{3,2,1,0:T(8,128)(2,1)} %all-to-all-done.5.refs_1_), channel_id=1, source_target_pairs={{0,8},{1,9},{2,10},{3,11},{4,12},{5,13},{6,14},{7,15},{8,0},{9,1},... | collective-permute-start | bytes 3538952 | tf_op jit(solution)/shard_map/ppermute | solution.py:215
  230.5 28.1 %collective-permute-start.18 = (bf16[4,2,48,1536]{3,2,1,0:T(8,128)(2,1)}, bf16[4,2,48,1536]{3,2,1,0:T(8,128)(2,1)S(1)}, u32[]{:S(2)}, u32[]{:S(2)}) collective-permute-start(bf16[4,2,48,1536]{3,2,1,0:T(8,128)(2,1)} %collective-permute-done.16.refs_2_), channel_id=1, source_target_pairs={{0,8},{1,9},{2,10},{3,11},{4,12},{5,13},{6,14},{7,15},{8,0},{9,1},... | collective-permute-start | bytes 3538952 | tf_op jit(solution)/shard_map/ppermute | solution.py:215
  231.0 27.6 %collective-permute-start.17 = (bf16[4,2,48,1536]{3,2,1,0:T(8,128)(2,1)S(1)}, bf16[4,2,48,1536]{3,2,1,0:T(8,128)(2,1)}, u32[]{:S(2)}, u32[]{:S(2)}) collective-permute-start(bf16[4,2,48,1536]{3,2,1,0:T(8,128)(2,1)S(1)} %pad_maximum_fusion.9), channel_id=1, source_target_pairs={{0,16},{1,17},{2,18},{3,19},{4,20},{5,21},{6,22},{7,23},{8,24},{9,... | collective-permute-start | bytes 3538952 | tf_op jit(solution)/shard_map/ppermute | solution.py:210
  231.7 29.9 %collective-permute-start.20 = (bf16[4,2,128,640]{3,2,1,0:T(8,128)(2,1)S(1)}, bf16[4,2,128,640]{3,2,1,0:T(8,128)(2,1)S(1)}, u32[]{:S(2)}, u32[]{:S(2)}) collective-permute-start(bf16[4,2,128,640]{3,2,1,0:T(8,128)(2,1)S(1)} %all-to-all-done.6.refs_1_), channel_id=1, source_target_pairs={{0,1},{1,0},{2,3},{3,2},{4,5},{5,4},{6,7},{7,6},{8,9},{9,8},{10,11... | collective-permute-start | bytes 3932168 | tf_op jit(solution)/shard_map/ppermute | solution.py:205
  263.2 30.6 %collective-permute-start.22 = (bf16[4,2,128,640]{3,2,1,0:T(8,128)(2,1)S(1)}, bf16[4,2,128,640]{3,2,1,0:T(8,128)(2,1)}, u32[]{:S(2)}, u32[]{:S(2)}) collective-permute-start(bf16[4,2,128,640]{3,2,1,0:T(8,128)(2,1)S(1)} %pad_maximum_fusion.3), channel_id=1, source_target_pairs={{0,16},{1,17},{2,18},{3,19},{4,20},{5,21},{6,22},{7,23},{8,24},{9,... | collective-permute-start | bytes 3932168 | tf_op jit(solution)/shard_map/ppermute | solution.py:210
  264.1 29.7 %collective-permute-start.24 = (bf16[4,2,128,640]{3,2,1,0:T(8,128)(2,1)S(1)}, bf16[4,2,128,640]{3,2,1,0:T(8,128)(2,1)S(1)}, u32[]{:S(2)}, u32[]{:S(2)}) collective-permute-start(bf16[4,2,128,640]{3,2,1,0:T(8,128)(2,1)S(1)} %all-to-all-done.6.refs_1_), channel_id=1, source_target_pairs={{0,8},{1,9},{2,10},{3,11},{4,12},{5,13},{6,14},{7,15},{8,0},{9,1},... | collective-permute-start | bytes 3932168 | tf_op jit(solution)/shard_map/ppermute | solution.py:215
  264.4 29.4 %collective-permute-start.23 = (bf16[4,2,128,640]{3,2,1,0:T(8,128)(2,1)S(1)}, bf16[4,2,128,640]{3,2,1,0:T(8,128)(2,1)S(1)}, u32[]{:S(2)}, u32[]{:S(2)}) collective-permute-start(bf16[4,2,128,640]{3,2,1,0:T(8,128)(2,1)S(1)} %collective-permute-done.20.refs_2_), channel_id=1, source_target_pairs={{0,8},{1,9},{2,10},{3,11},{4,12},{5,13},{6,14},{7,15},{8,0},{9,1},... | collective-permute-start | bytes 3932168 | tf_op jit(solution)/shard_map/ppermute | solution.py:215
  329.8 19.0 %collective-permute-start.27 = (bf16[3072,640]{1,0:T(8,128)(2,1)}, bf16[3072,640]{1,0:T(8,128)(2,1)S(1)}, u32[]{:S(2)}, u32[]{:S(2)}) collective-permute-start(bf16[3072,640]{1,0:T(8,128)(2,1)} %convolution_convert_fusion.1), channel_id=1, source_target_pairs={{0,8},{1,9},{2,10},{3,11},{4,12},{5,13},{6,14},{7,15},{8,0},{9,1},... | collective-permute-start | bytes 11796488 | tf_op jit(solution)/shard_map/ppermute | solution.py:239
  368.3 40.2 %collective-permute-start.29 = (bf16[1152,3072]{1,0:T(8,128)(2,1)}, bf16[1152,3072]{1,0:T(8,128)(2,1)}, u32[]{:S(2)}, u32[]{:S(2)}) collective-permute-start(bf16[1152,3072]{1,0:T(8,128)(2,1)} %convolution_convert_fusion), channel_id=1, source_target_pairs={{0,8},{1,9},{2,10},{3,11},{4,12},{5,13},{6,14},{7,15},{8,0},{9,1},... | collective-permute-start | bytes 21233672 | tf_op jit(solution)/shard_map/ppermute | solution.py:239
  370.6 37.8 %collective-permute-start.28 = (bf16[4,2,128,640]{3,2,1,0:T(8,128)(2,1)S(1)}, bf16[4,2,128,640]{3,2,1,0:T(8,128)(2,1)S(1)}, u32[]{:S(2)}, u32[]{:S(2)}) collective-permute-start(bf16[4,2,128,640]{3,2,1,0:T(8,128)(2,1)S(1)} %dynamic-slice_bitcast_fusion), channel_id=1, source_target_pairs={{0,16},{1,17},{2,18},{3,19},{4,20},{5,21},{6,22},{7,23},{8,24},{9,... | collective-permute-start | bytes 3932168 | tf_op jit(solution)/shard_map/ppermute | solution.py:268
  422.0 30.8 %collective-permute-start.30 = (bf16[4,2,128,640]{3,2,1,0:T(8,128)(2,1)}, bf16[4,2,128,640]{3,2,1,0:T(8,128)(2,1)}, u32[]{:S(2)}, u32[]{:S(2)}) collective-permute-start(bf16[4,2,128,640]{3,2,1,0:T(8,128)(2,1)} %pad_maximum_fusion.4), channel_id=1, source_target_pairs={{0,1},{1,0},{2,3},{3,2},{4,5},{5,4},{6,7},{7,6},{8,9},{9,8},{10,11... | collective-permute-start | bytes 3932168 | tf_op jit(solution)/shard_map/ppermute | solution.py:302
  425.5 27.2 %collective-permute-start.31 = (bf16[2,2,48,3072]{3,2,1,0:T(8,128)(2,1)}, bf16[2,2,48,3072]{3,2,1,0:T(8,128)(2,1)}, u32[]{:S(2)}, u32[]{:S(2)}) collective-permute-start(bf16[2,2,48,3072]{3,2,1,0:T(8,128)(2,1)} %dynamic-slice_bitcast_fusion.3), channel_id=1, source_target_pairs={{0,16},{1,17},{2,18},{3,19},{4,20},{5,21},{6,22},{7,23},{8,24},{9,... | collective-permute-start | bytes 3538952 | tf_op jit(solution)/shard_map/ppermute | solution.py:272
  455.7 37.3 %all-to-all-start.7 = ((bf16[4,2,128,640]{3,2,1,0:T(8,128)(2,1)}), bf16[4,2,128,640]{3,2,1,0:T(8,128)(2,1)S(1)}, u32[]{:S(2)}, u32[]{:S(2)}) async-start(bf16[4,2,128,640]{3,2,1,0:T(8,128)(2,1)} %pad_maximum_fusion.5), calls=%async_computation.7 | async-start | bytes 2621440 | tf_op jit(solution)/shard_map/all_to_all | solution.py:89
  459.8 33.2 %collective-permute-start.34 = (bf16[1152,640]{1,0:T(8,128)(2,1)}, bf16[1152,640]{1,0:T(8,128)(2,1)}, u32[]{:S(2)}, u32[]{:S(2)}) collective-permute-start(bf16[1152,640]{1,0:T(8,128)(2,1)} %convolution_convert_fusion.4), channel_id=1, source_target_pairs={{0,8},{1,9},{2,10},{3,11},{4,12},{5,13},{6,14},{7,15},{8,0},{9,1},... | collective-permute-start | bytes 4423688 | tf_op jit(solution)/shard_map/ppermute | solution.py:239
  464.3 27.7 %collective-permute-start.32 = (bf16[4,48,3072]{2,1,0:T(8,128)(2,1)S(1)}, bf16[4,48,3072]{2,1,0:T(8,128)(2,1)S(1)}, u32[]{:S(2)}, u32[]{:S(2)}) collective-permute-start(bf16[4,48,3072]{2,1,0:T(8,128)(2,1)S(1)} %dynamic-slice_bitcast_fusion.2), channel_id=1, source_target_pairs={{0,1},{1,0},{2,3},{3,2},{4,5},{5,4},{6,7},{7,6},{8,9},{9,8},{10,11... | collective-permute-start | bytes 3538952 | tf_op jit(solution)/shard_map/ppermute | solution.py:291
  464.6 27.4 %collective-permute-start.33 = (bf16[2,2,48,3072]{3,2,1,0:T(8,128)(2,1)S(1)}, bf16[2,2,48,3072]{3,2,1,0:T(8,128)(2,1)S(1)}, u32[]{:S(2)}, u32[]{:S(2)}) collective-permute-start(bf16[2,2,48,3072]{3,2,1,0:T(8,128)(2,1)S(1)} %dynamic-slice_bitcast_fusion.1), channel_id=1, source_target_pairs={{0,16},{1,17},{2,18},{3,19},{4,20},{5,21},{6,22},{7,23},{8,24},{9,... | collective-permute-start | bytes 3538952 | tf_op jit(solution)/shard_map/ppermute | solution.py:272
  498.8 37.1 %all-to-all-start.8 = ((bf16[4,48,3072]{2,1,0:T(8,128)(2,1)}), bf16[4,48,3072]{2,1,0:T(8,128)(2,1)S(1)}, u32[]{:S(2)}, u32[]{:S(2)}) async-start(bf16[4,48,3072]{2,1,0:T(8,128)(2,1)} %get-tuple-element.616), calls=%async_computation.8 | async-start | bytes 2359296 | tf_op jit(solution)/shard_map/all_to_all | solution.py:89
  504.4 31.5 %collective-permute-start.35 = (bf16[2,128,640]{2,1,0:T(8,128)(2,1)S(1)}, bf16[2,128,640]{2,1,0:T(8,128)(2,1)S(1)}, u32[]{:S(2)}, u32[]{:S(2)}) collective-permute-start(bf16[2,128,640]{2,1,0:T(8,128)(2,1)S(1)} %reduce_sum.136), channel_id=1, source_target_pairs={{0,16},{1,17},{2,18},{3,19},{4,20},{5,21},{6,22},{7,23},{8,24},{9,... | collective-permute-start | bytes 983048 | tf_op jit(solution)/shard_map/ppermute | solution.py:354
  505.2 30.6 %collective-permute-start.36 = (bf16[4,48,3072]{2,1,0:T(8,128)(2,1)}, bf16[4,48,3072]{2,1,0:T(8,128)(2,1)S(1)}, u32[]{:S(2)}, u32[]{:S(2)}) collective-permute-start(bf16[4,48,3072]{2,1,0:T(8,128)(2,1)} %get-tuple-element.617), channel_id=1, source_target_pairs={{0,1},{1,0},{2,3},{3,2},{4,5},{5,4},{6,7},{7,6},{8,9},{9,8},{10,11... | collective-permute-start | bytes 3538952 | tf_op jit(solution)/shard_map/ppermute | solution.py:296
  535.9 33.4 %collective-permute-start.38 = (bf16[1152,896]{1,0:T(8,128)(2,1)}, bf16[1152,896]{1,0:T(8,128)(2,1)}, u32[]{:S(2)}, u32[]{:S(2)}) collective-permute-start(bf16[1152,896]{1,0:T(8,128)(2,1)} %convolution_convert_fusion.3), channel_id=1, source_target_pairs={{0,8},{1,9},{2,10},{3,11},{4,12},{5,13},{6,14},{7,15},{8,0},{9,1},... | collective-permute-start | bytes 6193160 | tf_op jit(solution)/shard_map/ppermute | solution.py:239
  542.8 33.2 %all-to-all-start.9 = ((bf16[4,48,3072]{2,1,0:T(8,128)(2,1)}), bf16[4,48,3072]{2,1,0:T(8,128)(2,1)}, u32[]{:S(2)}, u32[]{:S(2)}) async-start(bf16[4,48,3072]{2,1,0:T(8,128)(2,1)} %add_convert_fusion.2), calls=%async_computation.9 | async-start | bytes 2359296 | tf_op jit(solution)/shard_map/all_to_all | solution.py:89
  548.0 26.0 %collective-permute-start.37 = (bf16[384,640]{1,0:T(8,128)(2,1)S(1)}, bf16[384,640]{1,0:T(8,128)(2,1)}, u32[]{:S(2)}, u32[]{:S(2)}) collective-permute-start(bf16[384,640]{1,0:T(8,128)(2,1)S(1)} %pad_maximum_fusion.18), channel_id=1, source_target_pairs={{0,8},{1,9},{2,10},{3,11},{4,12},{5,13},{6,14},{7,15},{8,0},{9,1},... | collective-permute-start | bytes 1474568 | tf_op jit(solution)/shard_map/ppermute | solution.py:364
  584.1 35.4 %all-to-all-start.10 = ((bf16[8,8,4608]{2,1,0:T(8,128)(2,1)}), bf16[8,8,4608]{2,1,0:T(8,128)(2,1)}, u32[]{:S(2)}, u32[]{:S(2)}) async-start(bf16[8,8,4608]{2,1,0:T(8,128)(2,1)} %broadcast_in_dim.71), calls=%async_computation.10 | async-start | bytes 1179648 | tf_op jit(solution)/shard_map/all_to_all | solution.py:412
  588.6 31.0 %collective-permute-start.40 = (bf16[4,48,1536]{2,1,0:T(8,128)(2,1)}, bf16[4,48,1536]{2,1,0:T(8,128)(2,1)}, u32[]{:S(2)}, u32[]{:S(2)}) collective-permute-start(bf16[4,48,1536]{2,1,0:T(8,128)(2,1)} %dynamic-slice_bitcast_fusion.6), channel_id=1, source_target_pairs={{0,1},{1,0},{2,3},{3,2},{4,5},{5,4},{6,7},{7,6},{8,9},{9,8},{10,11... | collective-permute-start | bytes 1769480 | tf_op jit(solution)/shard_map/ppermute | solution.py:291
  591.1 28.4 %collective-permute-start.39 = (bf16[2,48,3072]{2,1,0:T(8,128)(2,1)S(1)}, bf16[2,48,3072]{2,1,0:T(8,128)(2,1)}, u32[]{:S(2)}, u32[]{:S(2)}) collective-permute-start(bf16[2,48,3072]{2,1,0:T(8,128)(2,1)S(1)} %pad_maximum_fusion.17), channel_id=1, source_target_pairs={{0,16},{1,17},{2,18},{3,19},{4,20},{5,21},{6,22},{7,23},{8,24},{9,... | collective-permute-start | bytes 1769480 | tf_op jit(solution)/shard_map/ppermute | solution.py:354
  591.9 37.6 %collective-permute-start.41 = (bf16[4,2,48,1536]{3,2,0,1:T(8,128)(2,1)}, bf16[4,2,48,1536]{3,2,0,1:T(8,128)(2,1)}, u32[]{:S(2)}, u32[]{:S(2)}) collective-permute-start(bf16[4,2,48,1536]{3,2,0,1:T(8,128)(2,1)} %copy_bitcast_fusion.1), channel_id=1, source_target_pairs={{0,16},{1,17},{2,18},{3,19},{4,20},{5,21},{6,22},{7,23},{8,24},{9,... | collective-permute-start | bytes 3538952 | tf_op jit(solution)/shard_map/ppermute | solution.py:268
  634.1 41.3 %all-to-all-start.11 = ((bf16[4,48,1536]{2,1,0:T(8,128)(2,1)}), bf16[4,48,1536]{2,1,0:T(8,128)(2,1)}, u32[]{:S(2)}, u32[]{:S(2)}) async-start(bf16[4,48,1536]{2,1,0:T(8,128)(2,1)} %get-tuple-element.620), calls=%async_computation.11 | async-start | bytes 1179648 | tf_op jit(solution)/shard_map/all_to_all | solution.py:89
  638.8 36.6 %collective-permute-start.43 = (bf16[4,48,1536]{2,1,0:T(8,128)(2,1)}, bf16[4,48,1536]{2,1,0:T(8,128)(2,1)}, u32[]{:S(2)}, u32[]{:S(2)}) collective-permute-start(bf16[4,48,1536]{2,1,0:T(8,128)(2,1)} %get-tuple-element.621), channel_id=1, source_target_pairs={{0,1},{1,0},{2,3},{3,2},{4,5},{5,4},{6,7},{7,6},{8,9},{9,8},{10,11... | collective-permute-start | bytes 1769480 | tf_op jit(solution)/shard_map/ppermute | solution.py:296
  639.1 7.4 collective-permute-start.44
  645.8 29.7 %collective-permute-start.42 = (bf16[144,3072]{1,0:T(8,128)(2,1)}, bf16[144,3072]{1,0:T(8,128)(2,1)}, u32[]{:S(2)}, u32[]{:S(2)}) collective-permute-start(bf16[144,3072]{1,0:T(8,128)(2,1)} %pad_maximum_fusion.12), channel_id=1, source_target_pairs={{0,8},{1,9},{2,10},{3,11},{4,12},{5,13},{6,14},{7,15},{8,0},{9,1},... | collective-permute-start | bytes 2654216 | tf_op jit(solution)/shard_map/ppermute | solution.py:364
  653.2 22.2 %collective-permute-start.45 = (bf16[4,2,48,896]{3,2,1,0:T(8,128)(2,1)}, bf16[4,2,48,896]{3,2,1,0:T(8,128)(2,1)}, u32[]{:S(2)}, u32[]{:S(2)}) collective-permute-start(bf16[4,2,48,896]{3,2,1,0:T(8,128)(2,1)} %dynamic-slice_bitcast_fusion.4), channel_id=1, source_target_pairs={{0,16},{1,17},{2,18},{3,19},{4,20},{5,21},{6,22},{7,23},{8,24},{9,... | collective-permute-start | bytes 2064392 | tf_op jit(solution)/shard_map/ppermute | solution.py:268
  677.1 28.5 %all-to-all-start.12 = ((bf16[8,8,2560]{2,1,0:T(8,128)(2,1)}), bf16[8,8,2560]{2,1,0:T(8,128)(2,1)}, u32[]{:S(2)}, u32[]{:S(2)}) async-start(bf16[8,8,2560]{2,1,0:T(8,128)(2,1)} %broadcast_in_dim.73), calls=%async_computation.12 | async-start | bytes 655360 | tf_op jit(solution)/shard_map/all_to_all | solution.py:412
  685.0 20.6 %collective-permute-start.50 = (bf16[64,4608]{1,0:T(8,128)(2,1)}, bf16[64,4608]{1,0:T(8,128)(2,1)}, u32[]{:S(2)}, u32[]{:S(2)}) collective-permute-start(bf16[64,4608]{1,0:T(8,128)(2,1)} %bitcast.70), channel_id=1, source_target_pairs={{0,16},{1,17},{2,18},{3,19},{4,20},{5,21},{6,22},{7,23},{8,24},{9,... | collective-permute-start | bytes 1769480 | tf_op jit(solution)/shard_map/ppermute | solution.py:395
  686.7 18.9 %collective-permute-start.49 = (bf16[4,2,48,896]{3,2,1,0:T(8,128)(2,1)}, bf16[4,2,48,896]{3,2,1,0:T(8,128)(2,1)}, u32[]{:S(2)}, u32[]{:S(2)}) collective-permute-start(bf16[4,2,48,896]{3,2,1,0:T(8,128)(2,1)} %pad_maximum_fusion.14), channel_id=1, source_target_pairs={{0,1},{1,0},{2,3},{3,2},{4,5},{5,4},{6,7},{7,6},{8,9},{9,8},{10,11... | collective-permute-start | bytes 2064392 | tf_op jit(solution)/shard_map/ppermute | solution.py:302
  692.9 12.7 %collective-permute-start.47 = (bf16[48,1536]{1,0:T(8,128)(2,1)S(1)}, bf16[48,1536]{1,0:T(8,128)(2,1)S(1)}, u32[]{:S(2)}, u32[]{:S(2)}) collective-permute-start(bf16[48,1536]{1,0:T(8,128)(2,1)S(1)} %get-tuple-element.649), channel_id=1, source_target_pairs={{0,4},{1,5},{2,6},{3,7},{4,0},{5,1},{6,2},{7,3},{8,12},{9,13},{10,... | collective-permute-start | bytes 442376 | tf_op jit(solution)/shard_map/ppermute | solution.py:328
  692.9 12.7 %collective-permute-start.46 = (bf16[48,1536]{1,0:T(8,128)(2,1)S(1)}, bf16[48,1536]{1,0:T(8,128)(2,1)S(1)}, u32[]{:S(2)}, u32[]{:S(2)}) collective-permute-start(bf16[48,1536]{1,0:T(8,128)(2,1)S(1)} %get-tuple-element.650), channel_id=1, source_target_pairs={{0,2},{1,3},{2,4},{3,5},{4,6},{5,7},{6,0},{7,1},{8,10},{9,11},{10,... | collective-permute-start | bytes 442376 | tf_op jit(solution)/shard_map/ppermute | solution.py:328
  706.9 21.5 %collective-permute-start.51 = (bf16[2,48,1536]{2,1,0:T(8,128)(2,1)S(1)}, bf16[2,48,1536]{2,1,0:T(8,128)(2,1)}, u32[]{:S(2)}, u32[]{:S(2)}) collective-permute-start(bf16[2,48,1536]{2,1,0:T(8,128)(2,1)S(1)} %pad_maximum_fusion.24), channel_id=1, source_target_pairs={{0,16},{1,17},{2,18},{3,19},{4,20},{5,21},{6,22},{7,23},{8,24},{9,... | collective-permute-start | bytes 884744 | tf_op jit(solution)/shard_map/ppermute | solution.py:354
  707.7 20.7 %collective-permute-start.52 = (bf16[64,2560]{1,0:T(8,128)(2,1)}, bf16[64,2560]{1,0:T(8,128)(2,1)}, u32[]{:S(2)}, u32[]{:S(2)}) collective-permute-start(bf16[64,2560]{1,0:T(8,128)(2,1)} %bitcast.92), channel_id=1, source_target_pairs={{0,16},{1,17},{2,18},{3,19},{4,20},{5,21},{6,22},{7,23},{8,24},{9,... | collective-permute-start | bytes 983048 | tf_op jit(solution)/shard_map/ppermute | solution.py:395
  712.3 21.7 %all-to-all-start.13 = ((bf16[4,2,48,896]{3,2,1,0:T(8,128)(2,1)}), bf16[4,2,48,896]{3,2,1,0:T(8,128)(2,1)}, u32[]{:S(2)}, u32[]{:S(2)}) async-start(bf16[4,2,48,896]{3,2,1,0:T(8,128)(2,1)} %pad_maximum_fusion.15), calls=%async_computation.13 | async-start | bytes 1376256 | tf_op jit(solution)/shard_map/all_to_all | solution.py:89
  716.6 8.1 %collective-permute-start.53 = (bf16[2,64,4608]{2,1,0:T(8,128)(2,1)S(1)}, bf16[2,64,4608]{2,1,0:T(8,128)(2,1)S(1)}, u32[]{:S(2)}, u32[]{:S(2)}) collective-permute-start(bf16[2,64,4608]{2,1,0:T(8,128)(2,1)S(1)} %pad_maximum_fusion.10), channel_id=1, source_target_pairs={{0,8},{1,9},{2,10},{3,11},{4,12},{5,13},{6,14},{7,15},{8,0},{9,1},... | collective-permute-start | bytes 3538952 | tf_op jit(solution)/shard_map/ppermute | solution.py:404
  736.8 9.6 %collective-permute-start.56 = (bf16[2,64,2560]{2,1,0:T(8,128)(2,1)}, bf16[2,64,2560]{2,1,0:T(8,128)(2,1)}, u32[]{:S(2)}, u32[]{:S(2)}) collective-permute-start(bf16[2,64,2560]{2,1,0:T(8,128)(2,1)} %pad_maximum_fusion.16), channel_id=1, source_target_pairs={{0,8},{1,9},{2,10},{3,11},{4,12},{5,13},{6,14},{7,15},{8,0},{9,1},... | collective-permute-start | bytes 1966088 | tf_op jit(solution)/shard_map/ppermute | solution.py:404
  741.4 10.3 %all-to-all-start.14 = ((bf16[8,8,144]{2,1,0:T(8,128)(2,1)}), bf16[8,8,144]{2,1,0:T(8,128)(2,1)S(1)}, u32[]{:S(2)}, u32[]{:S(2)}) async-start(bf16[8,8,144]{2,1,0:T(8,128)(2,1)} %bitcast.240), calls=%async_computation.14 | async-start | bytes 65536 | tf_op jit(solution)/shard_map/all_to_all | solution.py:1289
  (66 other events, 479.9 us)

commit v7 on v6

--- a/solution.py
+++ b/solution.py
@@ -206,7 +206,7 @@
 
     def x(self):
         if self.fast:
-            ends = jnp.stack([self.live["own"][:, 0], self.live["far"][:, 0]], 1)
+            ends = jnp.concatenate([self.live["own"][:, :1], self.live["far"][:, :1]], 1)
             self.live["both"] = lax.ppermute(ends, AXES, TO_X)
 
     def core(self, *names):
@@ -1227,7 +1227,6 @@
 
     s_head.x()
     s_head.y_common()
-    s_wide.last_x()
     late_group = gather_rows(late_sums)
     joint_two, gains_3 = back(1, 1, joint_two, do=grad_mixed, **two)
     s_tail = Scatter(normed_a, pair=joint_two)
@@ -1238,12 +1237,12 @@
     )
 
     s_tail.core()
+    s_wide.last_x()
     s_head.y_own()
     s_head.z_common()
     s_tail.second()
     grad_middle = hold([s_tail], grad_middle)
     s_tail.x()
-    s_wide.last_core()
     grad_input, sums_early = call_rows(
         input_back_kernel, "input_back",
         (s_head.live["pair"], s_tail.live["pair"], grad_middle, inputs_low, hot),
@@ -1256,6 +1255,7 @@
     plans = [s_wide, s_head, s_tail]
     grad_input, sums_early, late_group = hold(plans, (grad_input, sums_early, late_group))
 
+    s_wide.last_core()
     s_head.z_own(apart=True)
     s_tail.y_both()
     early_sums = sums_early[:items]

time: 770 us -> 763 us (level)
  waiting for transfers between devices: 123 us -> 114 us
    ppermute x3, waiting for transfers between devices: 9.91 us -> 0.01 us  [x(): lax.ppermute(self.cut((0, 0, 1 - x), (HIGH_Z, 2, 1)), AXES, TO_X)]
  transfers between devices with their start and end apart: 73 -> 73, of which waited for: 27 -> 25; matrix products, arithmetic and copies ran while one was open for 17% -> 18% of each run, Pallas kernels for 36% -> 36%
where the time goes in v7:
time: 763 us; the launch traced here: 753 us
  Pallas kernels  293 us (38%)
  starting transfers between devices  120 us (16%)
  waiting for transfers between devices  114 us (15%)
  matrix products  77.3 us (10%)
  other arithmetic  76 us (10%)
  local copies, waits for them, and re-layouts  69.3 us (9%)
    pallas_call x5, Pallas kernels, call_placed(): pl.pallas_call(run, in_specs=[pl.BlockSpec(memory_space=pltpu.SMEM)] + [a...  90.5 us
    pallas_call x4, Pallas kernels, call_rows(): pl.pallas_call(kernel, in_specs=specs, out_specs=out_specs, out_shape=out...  84.7 us
    pallas_call x4, Pallas kernels, attend_back(): pl.pallas_call(partial(back_kernel, hd, c, score_scale, part), grid=(n //...  81 us
    dot_general x12, matrix products, dot_left(): lax.dot_general(left, right, (((0,), (0,)), ((), ())), preferred_element_...  72.2 us
    all_to_all x10, starting transfers between devices, over_z(): return lax.all_to_all(operand, 'fsdp', 0, 0, axis_index_groups=Z_GROUPS)  44.5 us
    ppermute x5, waiting for transfers between devices, y(): self.live['far'] = lax.ppermute(self.live['own'], AXES, TO_Y)  30.1 us
    all_to_all x10, waiting for transfers between devices, over_z(): return lax.all_to_all(operand, 'fsdp', 0, 0, axis_index_groups=Z_GROUPS)  23.4 us
    pallas_call x1, Pallas kernels, attend(): pl.pallas_call(partial(attend_kernel, hd, c), grid=(n // BLOCK,), in_spec...  22.7 us
  transfers between devices with their start and end apart: 73, of which 25 were waited for; matrix products, arithmetic and copies ran while one was open for 18% of the time, Pallas kernels for 36%

profile of v7, /device:TPU:1, one launch (start us, length us, event | category | flops | bytes accessed | tf_op | source)
XLA Modules:
  0.0 752.8 jit_solution(16246316325374994670)
XLA Ops:
  2.1 6.4 all-to-all-start.1
  17.1 4.5 all-to-all-start
  25.1 2.7 fusion.60
  27.7 11.5 %all-to-all-done.refs_1_ = bf16[4,2,48,896]{3,2,1,0:T(8,128)(2,1)} async-done(((bf16[4,2,48,896]{3,2,1,0:T(8,128)(2,1)}), bf16[4,2,48,896]{3,2,1,0:T(8,128)(2,1)}, u32[]{:S(2)}, u32[]{:S(2)}) %all-to-all-start) | async-done | bytes 688160 | tf_op jit(solution)/shard_map/all_to_all | solution.py:89
  40.5 4.3 all-to-all-start.2
  44.7 5.4 multiply_cosine_fusion
  59.5 2.8 pad_maximum_fusion.2.refs_12_.rot_ref
  67.1 4.6 collective-permute-done.refs_2_
  72.8 4.1 all-to-all-start.3
  77.9 3.0 collective-permute-start.4
  87.5 10.0 %all-to-all-done.3 = bf16[8,8,6912]{2,1,0:T(8,128)(2,1)S(1)} async-done(((bf16[8,8,6912]{2,1,0:T(8,128)(2,1)}), bf16[8,8,6912]{2,1,0:T(8,128)(2,1)S(1)}, u32[]{:S(2)}, u32[]{:S(2)}) %all-to-all-start.3) | async-done | bytes 884768 | tf_op jit(solution)/shard_map/all_to_all | solution.py:426
  98.3 2.6 collective-permute-done.2.refs_3_
  100.9 15.8 %collective-permute-done.5.refs_2_ = bf16[4,2,48,1536]{3,2,1,0:T(8,128)(2,1)} collective-permute-done((bf16[4,2,48,1536]{3,2,1,0:T(8,128)(2,1)}, bf16[4,2,48,1536]{3,2,1,0:T(8,128)(2,1)}, u32[]{:S(2)}, u32[]{:S(2)}) %collective-permute-start.5) | collective-permute-done | bytes 1179680 | tf_op jit(solution)/shard_map/ppermute | solution.py:205
  117.9 4.2 all-to-all-start.4
  131.6 20.7 %prepare.2 = (bf16[1024,1152]{1,0:T(8,128)(2,1)}, bf16[8,1024,128]{2,1,0:T(8,128)(2,1)}, bf16[8,1024,128]{2,1,0:T(8,128)(2,1)}, bf16[8,1024,128]{2,1,0:T(8,128)(...) custom-call(s32[4]{0:T(128)} %pad_add_fusion.refs_0_, ...), custom_call_target="tpu_custom_call" | custom-call | flops 8153726976 | bytes 20971520 | tf_op jit(solution)/shard_map/prepare/pallas_call | solution.py:171
  156.6 4.8 all-to-all-start.5
  161.7 21.0 %prepare.3 = (bf16[8,1024,128]{2,1,0:T(8,128)(2,1)}, bf16[8,1024,128]{2,1,0:T(8,128)(2,1)}, bf16[8,1024,128]{2,1,0:T(8,128)(2,1)}, bf16[8,1024,128]{2,1,0:T(8,12...) custom-call(s32[4]{0:T(128)} %pad_add_fusion.refs_0_, ...), custom_call_target="tpu_custom_call" | custom-call | flops 8153726976 | bytes 20971520 | tf_op jit(solution)/shard_map/prepare/pallas_call | solution.py:171
  182.7 6.1 collective-permute-done.11.refs_2_
  191.2 3.5 all-to-all-start.6
  198.7 22.7 %attend.1 = (bf16[1024,1152]{1,0:T(8,128)(2,1)}, bf16[8,1024,128]{2,1,0:T(8,128)(2,1)}, bf16[8,1024,128]{2,1,0:T(8,128)(2,1)}) custom-call(bf16[8,1024,128]{2,1,0:T(8,128)(2,1)} %get-tuple-element.388.refs_0_, bf16[8,1024,128]{2,1,0:T(8,128)(2,1)} %get-tuple-element.389.refs_1_.k_ref, bf16[8,1024,128]{2,1,0:T(8,128)(2,1)} %get-tuple-element.390.refs_2_.v_ref, ...), custom_call_target="tpu_custom_call" | custom-call | flops 5368709120 | bytes 20971520 | tf_op jit(solution)/shard_map/attend/pallas_call | solution.py:568
  231.7 11.3 %join.1 = (bf16[1024,1152]{1,0:T(8,128)(2,1)}, f32[1024,1152]{1,0:T(8,128)}, bf16[1024,1152]{1,0:T(8,128)(2,1)}) custom-call(bf16[1024,1152]{1,0:T(8,128)(2,1)} %get-tuple-element.405.mix_ref, bf16[1024,1152]{1,0:T(8,128)(2,1)} %bitcast.313, bf16[1024,16]{1,0:T(8,128)(2,1)} %copy.88.refs_8_.hot_ref.refs_10_, f32[1024,1]{1,0:T(8,128)} %copy.91.keep_ref.refs_11_, ...), custom_call_target="tpu_custom_call" | custom-call | flops 7247757312 | bytes 12054528 | tf_op jit(solution)/shard_map/join/pallas_call | solution.py:809
  243.1 14.6 %gate.1 = (bf16[1024,3072]{1,0:T(8,128)(2,1)}, bf16[1152,3072]{1,0:T(8,128)(2,1)}) custom-call(s32[4]{0:T(128)} %pad_add_fusion.refs_0_, bf16[4,2,48,1536]{3,2,1,0:T(8,128)(2,1)} %copy-done.8, bf16[4,2,48,1536]{3,2,1,0:T(8,128)(2,1)} %collective-permute-done.11.refs_2_, bf16[4,2,48,1536]{3,2,1,0:T(8,128)(2,1)} %copy-done.49, ...), custom_call_target="tpu_custom_call" | custom-call | flops 7247757312 | bytes 2359296 | tf_op jit(solution)/shard_map/gate/pallas_call | solution.py:171
  258.6 3.0 collective-permute-done.20.refs_2_
  265.8 16.6 %up.1 = (bf16[1024,3072]{1,0:T(8,128)(2,1)}, bf16[1024,3072]{1,0:T(8,128)(2,1)}, bf16[1152,3072]{1,0:T(8,128)(2,1)}) custom-call(s32[4]{0:T(128)} %pad_add_fusion.refs_0_, bf16[4,2,48,1536]{3,2,1,0:T(8,128)(2,1)} %all-to-all-done.5.refs_1_, bf16[4,2,48,1536]{3,2,1,0:T(8,128)(2,1)} %collective-permute-done.16.refs_2_, ...), custom_call_target="tpu_custom_call" | custom-call | flops 7247757312 | bytes 8650752 | tf_op jit(solution)/shard_map/up/pallas_call | solution.py:171
  282.4 11.4 %collective-permute-done.22.refs_3_ = bf16[4,2,128,640]{3,2,1,0:T(8,128)(2,1)} collective-permute-done((bf16[4,2,128,640]{3,2,1,0:T(8,128)(2,1)S(1)}, bf16[4,2,128,640]{3,2,1,0:T(8,128)(2,1)}, u32[]{:S(2)}, u32[]{:S(2)}) %collective-permute-start.22) | collective-permute-done | bytes 1310752 | tf_op jit(solution)/shard_map/ppermute | solution.py:210
  296.7 2.9 collective-permute-done.26.refs_6_
  300.7 17.5 %down.1 = (bf16[1024,1152]{1,0:T(8,128)(2,1)}, bf16[1024,1280]{1,0:T(8,128)(2,1)}, f32[16,1152]{1,0:T(8,128)}, bf16[3072,1280]{1,0:T(8,128)(2,1)}) custom-call(s32[4]{0:T(128)} %pad_add_fusion.refs_0_, bf16[4,2,128,640]{3,2,1,0:T(8,128)(2,1)} %copy-done.5, bf16[4,2,128,640]{3,2,1,0:T(8,128)(2,1)} %copy-done.33, ...), custom_call_target="tpu_custom_call" | custom-call | flops 8053063680 | bytes 13627392 | tf_op jit(solution)/shard_map/down/pallas_call | solution.py:171
  320.4 9.4 %convolution_convert_fusion.1 = bf16[3072,640]{1,0:T(8,128)(2,1)} fusion(bf16[1024,3072]{1,0:T(8,128)(2,1)} %get-tuple-element.447.refs_7_, bf16[1024,1280]{1,0:T(8,128)(2,1)S(1)} %copy-done.32, s32[]{:T(128)S(6)} %select_n.439), kind=kOutput, calls=%fused_computation.5 | convolution fusion | flops 4028497920 | bytes 11534340 | tf_op jit(solution)/shard_map/dot_general | solution.py:29
  330.1 18.6 %inner_back.1 = (bf16[1024,3072]{1,0:T(8,128)(2,1)}, bf16[1024,3072]{1,0:T(8,128)(2,1)}) custom-call(s32[1]{0:T(128)} %bitcast.1.core_ref, bf16[1024,1280]{1,0:T(8,128)(2,1)} %get-tuple-element.459.grad_ref, bf16[1024,3072]{1,0:T(8,128)(2,1)} %get-tuple-element.460.refs_8_.gate_ref, bf16[1024,3072]{1,0:T(8,128)(2,1)} %get-tuple-element.461.up_ref, ...), custom_call_target="tpu_custom_call" | custom-call | flops 8053063680 | bytes 23068672 | tf_op jit(solution)/shard_map/inner_back/pallas_call | solution.py:809
  348.7 9.9 %add_convert_fusion.1 = bf16[3072,640]{1,0:T(8,128)(2,1)} fusion(bf16[3072,640]{1,0:T(8,128)(2,1)S(1)} %collective-permute-done.27, bf16[1024,3072]{1,0:T(8,128)(2,1)} %get-tuple-element.447.refs_7_, bf16[1024,640]{1,0:T(8,128)(2,1)S(1)} %constant_dynamic-slice_fusion.3), kind=kOutput, calls=%fused_computation.4 | convolution fusion | flops 4032430080 | bytes 15466496 | tf_op jit(solution)/shard_map/dot_general | solution.py:29
  358.7 9.7 %convolution_convert_fusion = bf16[1152,3072]{1,0:T(8,128)(2,1)} fusion(bf16[1024,1152]{1,0:T(8,128)(2,1)S(1)} %copy-done.53, bf16[1024,3072]{1,0:T(8,128)(2,1)S(1)} %copy-done.55), kind=kOutput, calls=%fused_computation.1 | convolution fusion | flops 7251296256 | bytes 15728640 | tf_op jit(solution)/shard_map/dot_general | solution.py:29
  371.6 33.3 %middle_back.1 = (f32[1024,1152]{1,0:T(8,128)}, bf16[1024,1280]{1,0:T(8,128)(2,1)}, f32[16,3456]{1,0:T(8,128)}) custom-call(s32[1]{0:T(128)} %bitcast.1.core_ref, bf16[1024,3072]{1,0:T(8,128)(2,1)} %get-tuple-element.473.send_ref, bf16[1024,3072]{1,0:T(8,128)(2,1)} %get-tuple-element.484.mine_ref, f32[1024,1152]{1,0:T(8,128)} %get-tuple-element.475.refs_8_.mid_ref, ...), custom_call_target="tpu_custom_call" | custom-call | flops 14495514624 | bytes 36433920 | tf_op jit(solution)/shard_map/middle_back/pallas_call | solution.py:809
  404.9 3.6 constant_dynamic-slice_fusion.1
  408.6 11.8 %add_convert_fusion = bf16[1152,3072]{1,0:T(8,128)(2,1)S(1)} fusion(bf16[1152,3072]{1,0:T(8,128)(2,1)} %collective-permute-done.29, bf16[1024,1152]{1,0:T(8,128)(2,1)S(1)} %copy-done.54, bf16[1024,3072]{1,0:T(8,128)(2,1)} %get-tuple-element.484.mine_ref), kind=kOutput, calls=%fused_computation | convolution fusion | flops 7258374144 | bytes 22806528 | tf_op jit(solution)/shard_map/dot_general | solution.py:29
  426.4 12.7 %spread.1.do_ref = bf16[16,1024,128]{2,1,0:T(8,128)(2,1)} custom-call(bf16[1024,1280]{1,0:T(8,128)(2,1)} %get-tuple-element.492.ga_ref, bf16[1152,3072]{1,0:T(8,128)(2,1)} %get-tuple-element.407.w_ref.wt_ref, bf16[1024,1152]{1,0:T(8,128)(2,1)} %get-tuple-element.405.mix_ref), custom_call_target="tpu_custom_call" | custom-call | flops 2717908992 | bytes 12582912 | tf_op jit(solution)/shard_map/spread/pallas_call | solution.py:612
  439.1 4.5 convolution_convert_fusion.4
  444.2 8.7 %collective-permute-done.31 = bf16[2,2,48,3072]{3,2,1,0:T(8,128)(2,1)} collective-permute-done((bf16[2,2,48,3072]{3,2,1,0:T(8,128)(2,1)}, bf16[2,2,48,3072]{3,2,1,0:T(8,128)(2,1)}, u32[]{:S(2)}, u32[]{:S(2)}) %collective-permute-start.31) | collective-permute-done | bytes 1179680 | tf_op jit(solution)/shard_map/ppermute | solution.py:272
  455.8 4.0 all-to-all-start.7
  465.5 20.0 %attend_back.4 = (bf16[2,1024,896]{2,1,0:T(8,128)(2,1)}, f32[2,8,128]{2,1,0:T(8,128)}) custom-call(s32[1]{0:T(128)} %bitcast.1.core_ref, bf16[8,1024,128]{2,1,0:T(8,128)(2,1)} %get-tuple-element.500.q_ref, bf16[8,1024,128]{2,1,0:T(8,128)(2,1)} %get-tuple-element.389.refs_1_.k_ref, bf16[8,1024,128]{2,1,0:T(8,128)(2,1)} %get-tuple-element.390.refs_2_.v_ref, ...), custom_call_target="tpu_custom_call" | custom-call | flops 3355443200 | bytes 10485760 | tf_op jit(solution)/shard_map/attend_back/pallas_call | solution.py:716
  485.5 6.5 collective-permute-done.32
  495.0 4.0 fusion.7
  498.9 5.2 all-to-all-start.8
  505.6 20.2 %attend_back.5 = (bf16[2,1024,896]{2,1,0:T(8,128)(2,1)}, f32[2,8,128]{2,1,0:T(8,128)}) custom-call(s32[1]{0:T(128)} %bitcast.1.core_ref, bf16[8,1024,128]{2,1,0:T(8,128)(2,1)} %get-tuple-element.500.q_ref, bf16[8,1024,128]{2,1,0:T(8,128)(2,1)} %get-tuple-element.389.refs_1_.k_ref, ...), custom_call_target="tpu_custom_call", output_to_operand_aliasing={{0}: (10, {})} | custom-call | flops 3355443200 | bytes 10485760 | tf_op jit(solution)/shard_map/attend_back/pallas_call | solution.py:716
  525.8 5.6 convolution_convert_fusion.3
  531.4 4.5 fusion.5
  540.0 2.9 add_convert_fusion.2
  542.9 5.0 all-to-all-start.9
  548.7 20.5 %attend_back.6 = (bf16[2,1024,896]{2,1,0:T(8,128)(2,1)}, f32[2,8,128]{2,1,0:T(8,128)}) custom-call(s32[1]{0:T(128)} %bitcast.1.core_ref, bf16[8,1024,128]{2,1,0:T(8,128)(2,1)} %get-tuple-element.528.q_ref, bf16[8,1024,128]{2,1,0:T(8,128)(2,1)} %get-tuple-element.392.refs_4_.k_ref, bf16[8,1024,128]{2,1,0:T(8,128)(2,1)} %get-tuple-element.393.refs_5_.v_ref, ...), custom_call_target="tpu_custom_call" | custom-call | flops 3355443200 | bytes 10485760 | tf_op jit(solution)/shard_map/attend_back/pallas_call | solution.py:716
  569.3 4.3 fusion.1
  578.8 4.4 all-to-all-start.10
  585.4 20.3 %attend_back.7 = (bf16[2,1024,896]{2,1,0:T(8,128)(2,1)}, f32[2,8,128]{2,1,0:T(8,128)}) custom-call(s32[1]{0:T(128)} %bitcast.1.core_ref, bf16[8,1024,128]{2,1,0:T(8,128)(2,1)} %get-tuple-element.528.q_ref, bf16[8,1024,128]{2,1,0:T(8,128)(2,1)} %get-tuple-element.392.refs_4_.k_ref, ...), custom_call_target="tpu_custom_call", output_to_operand_aliasing={{0}: (10, {})} | custom-call | flops 3355443200 | bytes 10485760 | tf_op jit(solution)/shard_map/attend_back/pallas_call | solution.py:716
  608.3 4.0 convolution_convert_fusion.2
  626.4 4.7 all-to-all-start.11
  631.5 5.5 fusion.2
  639.9 21.5 %input_back.1 = (f32[1024,1152]{1,0:T(8,128)}, f32[16,2304]{1,0:T(8,128)}) custom-call(s32[1]{0:T(128)} %bitcast.1.core_ref, bf16[2,1024,896]{2,1,0:T(8,128)(2,1)} %get-tuple-element.555.one_ref, bf16[2,1024,896]{2,1,0:T(8,128)(2,1)} %get-tuple-element.556.two_ref, f32[1024,1152]{1,0:T(8,128)} %get-tuple-element.557.mid_ref, bf16[1024,1152]{1,0:T(8,128)(2,1)} %bitcast.314, ...), custom_call_target="tpu_custom_call" | custom-call | flops 11475615744 | bytes 25878528 | tf_op jit(solution)/shard_map/input_back/pallas_call | solution.py:809
  666.8 5.5 all-to-all-start.12
  678.7 2.6 collective-permute-start.45
  683.0 3.0 collective-permute-start.48
  686.0 3.3 collective-permute-done.48
  691.4 7.4 collective-permute-done.47
  705.5 4.2 all-to-all-start.13
  718.3 2.6 fusion.3
  720.8 6.4 all-to-all-done.13
  734.6 3.5 all-to-all-start.14
  (408 shorter events, 187.4 us)
Async XLA Ops:
  2.1 14.1 %all-to-all-start.1 = ((bf16[8,8,144]{2,1,0:T(8,128)(2,1)}), bf16[8,8,144]{2,1,0:T(8,128)(2,1)S(1)}, u32[]{:S(2)}, u32[]{:S(2)}) async-start(bf16[8,8,144]{2,1,0:T(8,128)(2,1)} %copy.84), calls=%async_computation.1 | async-start | bytes 65536 | tf_op jit(solution)/shard_map/all_to_all | solution.py:420
  17.1 22.1 %all-to-all-start = ((bf16[4,2,48,896]{3,2,1,0:T(8,128)(2,1)}), bf16[4,2,48,896]{3,2,1,0:T(8,128)(2,1)}, u32[]{:S(2)}, u32[]{:S(2)}) async-start(bf16[4,2,48,896]{3,2,1,0:T(8,128)(2,1)} %broadcast_in_dim.60), calls=%async_computation | async-start | bytes 1376256 | tf_op jit(solution)/shard_map/all_to_all | solution.py:89
  40.5 32.4 %all-to-all-start.2 = ((bf16[4,2,48,1536]{3,2,1,0:T(8,128)(2,1)}), bf16[4,2,48,1536]{3,2,1,0:T(8,128)(2,1)}, u32[]{:S(2)}, u32[]{:S(2)}) async-start(bf16[4,2,48,1536]{3,2,1,0:T(8,128)(2,1)} %broadcast_in_dim.61), calls=%async_computation.2 | async-start | bytes 2359296 | tf_op jit(solution)/shard_map/all_to_all | solution.py:89
  55.9 15.8 %collective-permute-start = (bf16[4,2,48,896]{3,2,1,0:T(8,128)(2,1)}, bf16[4,2,48,896]{3,2,1,0:T(8,128)(2,1)}, u32[]{:S(2)}, u32[]{:S(2)}) collective-permute-start(bf16[4,2,48,896]{3,2,1,0:T(8,128)(2,1)} %all-to-all-done.refs_1_), channel_id=1, source_target_pairs={{0,1},{1,0},{2,3},{3,2},{4,5},{5,4},{6,7},{7,6},{8,9},{9,8},{10,11... | collective-permute-start | bytes 2064392 | tf_op jit(solution)/shard_map/ppermute | solution.py:205
  72.8 24.6 %all-to-all-start.3 = ((bf16[8,8,6912]{2,1,0:T(8,128)(2,1)}), bf16[8,8,6912]{2,1,0:T(8,128)(2,1)S(1)}, u32[]{:S(2)}, u32[]{:S(2)}) async-start(bf16[8,8,6912]{2,1,0:T(8,128)(2,1)} %bitcast.20), calls=%async_computation.3 | async-start | bytes 1769472 | tf_op jit(solution)/shard_map/all_to_all | solution.py:426
  77.9 23.0 %collective-permute-start.4 = (bf16[4,2,48,896]{3,2,1,0:T(8,128)(2,1)}, bf16[4,2,48,896]{3,2,1,0:T(8,128)(2,1)}, u32[]{:S(2)}, u32[]{:S(2)}) collective-permute-start(bf16[4,2,48,896]{3,2,1,0:T(8,128)(2,1)} %all-to-all-done.refs_1_), channel_id=1, source_target_pairs={{0,8},{1,9},{2,10},{3,11},{4,12},{5,13},{6,14},{7,15},{8,0},{9,1},... | collective-permute-start | bytes 2064392 | tf_op jit(solution)/shard_map/ppermute | solution.py:215
  81.9 19.0 %collective-permute-start.3 = (bf16[4,2,48,896]{3,2,1,0:T(8,128)(2,1)}, bf16[4,2,48,896]{3,2,1,0:T(8,128)(2,1)}, u32[]{:S(2)}, u32[]{:S(2)}) collective-permute-start(bf16[4,2,48,896]{3,2,1,0:T(8,128)(2,1)} %collective-permute-done.refs_2_), channel_id=1, source_target_pairs={{0,8},{1,9},{2,10},{3,11},{4,12},{5,13},{6,14},{7,15},{8,0},{9,1},... | collective-permute-start | bytes 2064392 | tf_op jit(solution)/shard_map/ppermute | solution.py:215
  83.5 17.4 %collective-permute-start.2 = (bf16[4,2,48,896]{3,2,1,0:T(8,128)(2,1)}, bf16[4,2,48,896]{3,2,1,0:T(8,128)(2,1)}, u32[]{:S(2)}, u32[]{:S(2)}) collective-permute-start(bf16[4,2,48,896]{3,2,1,0:T(8,128)(2,1)} %pad_maximum_fusion.13), channel_id=1, source_target_pairs={{0,16},{1,17},{2,18},{3,19},{4,20},{5,21},{6,22},{7,23},{8,24},{9,... | collective-permute-start | bytes 2064392 | tf_op jit(solution)/shard_map/ppermute | solution.py:210
  84.7 31.9 %collective-permute-start.5 = (bf16[4,2,48,1536]{3,2,1,0:T(8,128)(2,1)}, bf16[4,2,48,1536]{3,2,1,0:T(8,128)(2,1)}, u32[]{:S(2)}, u32[]{:S(2)}) collective-permute-start(bf16[4,2,48,1536]{3,2,1,0:T(8,128)(2,1)} %all-to-all-done.2.refs_1_), channel_id=1, source_target_pairs={{0,1},{1,0},{2,3},{3,2},{4,5},{5,4},{6,7},{7,6},{8,9},{9,8},{10,11... | collective-permute-start | bytes 3538952 | tf_op jit(solution)/shard_map/ppermute | solution.py:205
  117.9 36.6 %all-to-all-start.4 = ((bf16[4,2,48,1536]{3,2,1,0:T(8,128)(2,1)}), bf16[4,2,48,1536]{3,2,1,0:T(8,128)(2,1)S(1)}, u32[]{:S(2)}, u32[]{:S(2)}) async-start(bf16[4,2,48,1536]{3,2,1,0:T(8,128)(2,1)} %broadcast_in_dim.65), calls=%async_computation.4 | async-start | bytes 2359296 | tf_op jit(solution)/shard_map/all_to_all | solution.py:89
  122.1 9.5 %collective-permute-start.10 = (bf16[4,2,48,896]{3,2,1,0:T(8,128)(2,1)}, bf16[4,2,48,896]{3,2,1,0:T(8,128)(2,1)}, u32[]{:S(2)}, u32[]{:S(2)}) collective-permute-start(bf16[4,2,48,896]{3,2,1,0:T(8,128)(2,1)} %collective-permute-done.2.refs_3_), channel_id=1, source_target_pairs={{0,8},{1,9},{2,10},{3,11},{4,12},{5,13},{6,14},{7,15},{8,0},{9,1},... | collective-permute-start | bytes 2064392 | tf_op jit(solution)/shard_map/ppermute | solution.py:215
  126.6 27.9 %collective-permute-start.7 = (bf16[4,2,48,1536]{3,2,1,0:T(8,128)(2,1)}, bf16[4,2,48,1536]{3,2,1,0:T(8,128)(2,1)}, u32[]{:S(2)}, u32[]{:S(2)}) collective-permute-start(bf16[4,2,48,1536]{3,2,1,0:T(8,128)(2,1)} %pad_maximum_fusion.7), channel_id=1, source_target_pairs={{0,16},{1,17},{2,18},{3,19},{4,20},{5,21},{6,22},{7,23},{8,24},{9,... | collective-permute-start | bytes 3538952 | tf_op jit(solution)/shard_map/ppermute | solution.py:210
  127.3 27.2 %collective-permute-start.9 = (bf16[4,2,48,1536]{3,2,1,0:T(8,128)(2,1)}, bf16[4,2,48,1536]{3,2,1,0:T(8,128)(2,1)}, u32[]{:S(2)}, u32[]{:S(2)}) collective-permute-start(bf16[4,2,48,1536]{3,2,1,0:T(8,128)(2,1)} %all-to-all-done.2.refs_1_), channel_id=1, source_target_pairs={{0,8},{1,9},{2,10},{3,11},{4,12},{5,13},{6,14},{7,15},{8,0},{9,1},... | collective-permute-start | bytes 3538952 | tf_op jit(solution)/shard_map/ppermute | solution.py:215
  127.6 26.9 %collective-permute-start.8 = (bf16[4,2,48,1536]{3,2,1,0:T(8,128)(2,1)}, bf16[4,2,48,1536]{3,2,1,0:T(8,128)(2,1)}, u32[]{:S(2)}, u32[]{:S(2)}) collective-permute-start(bf16[4,2,48,1536]{3,2,1,0:T(8,128)(2,1)} %collective-permute-done.5.refs_2_), channel_id=1, source_target_pairs={{0,8},{1,9},{2,10},{3,11},{4,12},{5,13},{6,14},{7,15},{8,0},{9,1},... | collective-permute-start | bytes 3538952 | tf_op jit(solution)/shard_map/ppermute | solution.py:215
  156.6 33.2 %all-to-all-start.5 = ((bf16[4,2,48,1536]{3,2,1,0:T(8,128)(2,1)}), bf16[4,2,48,1536]{3,2,1,0:T(8,128)(2,1)}, u32[]{:S(2)}, u32[]{:S(2)}) async-start(bf16[4,2,48,1536]{3,2,1,0:T(8,128)(2,1)} %broadcast_in_dim.68), calls=%async_computation.5 | async-start | bytes 2359296 | tf_op jit(solution)/shard_map/all_to_all | solution.py:89
  161.4 27.3 %collective-permute-start.11 = (bf16[4,2,48,1536]{3,2,1,0:T(8,128)(2,1)S(1)}, bf16[4,2,48,1536]{3,2,1,0:T(8,128)(2,1)}, u32[]{:S(2)}, u32[]{:S(2)}) collective-permute-start(bf16[4,2,48,1536]{3,2,1,0:T(8,128)(2,1)S(1)} %all-to-all-done.4.refs_1_), channel_id=1, source_target_pairs={{0,1},{1,0},{2,3},{3,2},{4,5},{5,4},{6,7},{7,6},{8,9},{9,8},{10,11... | collective-permute-start | bytes 3538952 | tf_op jit(solution)/shard_map/ppermute | solution.py:205
  191.2 34.3 %all-to-all-start.6 = ((bf16[4,2,128,640]{3,2,1,0:T(8,128)(2,1)}), bf16[4,2,128,640]{3,2,1,0:T(8,128)(2,1)S(1)}, u32[]{:S(2)}, u32[]{:S(2)}) async-start(bf16[4,2,128,640]{3,2,1,0:T(8,128)(2,1)} %broadcast_in_dim.69), calls=%async_computation.6 | async-start | bytes 2621440 | tf_op jit(solution)/shard_map/all_to_all | solution.py:89
  196.0 26.3 %collective-permute-start.13 = (bf16[4,2,48,1536]{3,2,1,0:T(8,128)(2,1)S(1)}, bf16[4,2,48,1536]{3,2,1,0:T(8,128)(2,1)S(1)}, u32[]{:S(2)}, u32[]{:S(2)}) collective-permute-start(bf16[4,2,48,1536]{3,2,1,0:T(8,128)(2,1)S(1)} %pad_maximum_fusion.8), channel_id=1, source_target_pairs={{0,16},{1,17},{2,18},{3,19},{4,20},{5,21},{6,22},{7,23},{8,24},{9,... | collective-permute-start | bytes 3538952 | tf_op jit(solution)/shard_map/ppermute | solution.py:210
  196.8 26.2 %collective-permute-start.16 = (bf16[4,2,48,1536]{3,2,1,0:T(8,128)(2,1)}, bf16[4,2,48,1536]{3,2,1,0:T(8,128)(2,1)}, u32[]{:S(2)}, u32[]{:S(2)}) collective-permute-start(bf16[4,2,48,1536]{3,2,1,0:T(8,128)(2,1)} %all-to-all-done.5.refs_1_), channel_id=1, source_target_pairs={{0,1},{1,0},{2,3},{3,2},{4,5},{5,4},{6,7},{7,6},{8,9},{9,8},{10,11... | collective-permute-start | bytes 3538952 | tf_op jit(solution)/shard_map/ppermute | solution.py:205
  196.8 26.2 %collective-permute-start.15 = (bf16[4,2,48,1536]{3,2,1,0:T(8,128)(2,1)S(1)}, bf16[4,2,48,1536]{3,2,1,0:T(8,128)(2,1)S(1)}, u32[]{:S(2)}, u32[]{:S(2)}) collective-permute-start(bf16[4,2,48,1536]{3,2,1,0:T(8,128)(2,1)S(1)} %copy-done.9), channel_id=1, source_target_pairs={{0,8},{1,9},{2,10},{3,11},{4,12},{5,13},{6,14},{7,15},{8,0},{9,1},... | collective-permute-start | bytes 3538952 | tf_op jit(solution)/shard_map/ppermute | solution.py:215
  198.7 25.7 %collective-permute-start.14 = (bf16[4,2,48,1536]{3,2,1,0:T(8,128)(2,1)}, bf16[4,2,48,1536]{3,2,1,0:T(8,128)(2,1)}, u32[]{:S(2)}, u32[]{:S(2)}) collective-permute-start(bf16[4,2,48,1536]{3,2,1,0:T(8,128)(2,1)} %collective-permute-done.11.refs_2_), channel_id=1, source_target_pairs={{0,8},{1,9},{2,10},{3,11},{4,12},{5,13},{6,14},{7,15},{8,0},{9,1},... | collective-permute-start | bytes 3538952 | tf_op jit(solution)/shard_map/ppermute | solution.py:215
  225.5 17.5 %collective-permute-start.21 = (bf16[4,2,48,1536]{3,2,1,0:T(8,128)(2,1)}, bf16[4,2,48,1536]{3,2,1,0:T(8,128)(2,1)}, u32[]{:S(2)}, u32[]{:S(2)}) collective-permute-start(bf16[4,2,48,1536]{3,2,1,0:T(8,128)(2,1)} %copy-done.49), channel_id=1, source_target_pairs={{0,8},{1,9},{2,10},{3,11},{4,12},{5,13},{6,14},{7,15},{8,0},{9,1},... | collective-permute-start | bytes 3538952 | tf_op jit(solution)/shard_map/ppermute | solution.py:215
  229.1 29.4 %collective-permute-start.19 = (bf16[4,2,48,1536]{3,2,1,0:T(8,128)(2,1)}, bf16[4,2,48,1536]{3,2,1,0:T(8,128)(2,1)S(1)}, u32[]{:S(2)}, u32[]{:S(2)}) collective-permute-start(bf16[4,2,48,1536]{3,2,1,0:T(8,128)(2,1)} %all-to-all-done.5.refs_1_), channel_id=1, source_target_pairs={{0,8},{1,9},{2,10},{3,11},{4,12},{5,13},{6,14},{7,15},{8,0},{9,1},... | collective-permute-start | bytes 3538952 | tf_op jit(solution)/shard_map/ppermute | solution.py:215
  230.5 28.1 %collective-permute-start.18 = (bf16[4,2,48,1536]{3,2,1,0:T(8,128)(2,1)}, bf16[4,2,48,1536]{3,2,1,0:T(8,128)(2,1)S(1)}, u32[]{:S(2)}, u32[]{:S(2)}) collective-permute-start(bf16[4,2,48,1536]{3,2,1,0:T(8,128)(2,1)} %collective-permute-done.16.refs_2_), channel_id=1, source_target_pairs={{0,8},{1,9},{2,10},{3,11},{4,12},{5,13},{6,14},{7,15},{8,0},{9,1},... | collective-permute-start | bytes 3538952 | tf_op jit(solution)/shard_map/ppermute | solution.py:215
  231.0 27.6 %collective-permute-start.17 = (bf16[4,2,48,1536]{3,2,1,0:T(8,128)(2,1)S(1)}, bf16[4,2,48,1536]{3,2,1,0:T(8,128)(2,1)}, u32[]{:S(2)}, u32[]{:S(2)}) collective-permute-start(bf16[4,2,48,1536]{3,2,1,0:T(8,128)(2,1)S(1)} %pad_maximum_fusion.9), channel_id=1, source_target_pairs={{0,16},{1,17},{2,18},{3,19},{4,20},{5,21},{6,22},{7,23},{8,24},{9,... | collective-permute-start | bytes 3538952 | tf_op jit(solution)/shard_map/ppermute | solution.py:210
  231.7 29.9 %collective-permute-start.20 = (bf16[4,2,128,640]{3,2,1,0:T(8,128)(2,1)S(1)}, bf16[4,2,128,640]{3,2,1,0:T(8,128)(2,1)S(1)}, u32[]{:S(2)}, u32[]{:S(2)}) collective-permute-start(bf16[4,2,128,640]{3,2,1,0:T(8,128)(2,1)S(1)} %all-to-all-done.6.refs_1_), channel_id=1, source_target_pairs={{0,1},{1,0},{2,3},{3,2},{4,5},{5,4},{6,7},{7,6},{8,9},{9,8},{10,11... | collective-permute-start | bytes 3932168 | tf_op jit(solution)/shard_map/ppermute | solution.py:205
  263.2 30.6 %collective-permute-start.22 = (bf16[4,2,128,640]{3,2,1,0:T(8,128)(2,1)S(1)}, bf16[4,2,128,640]{3,2,1,0:T(8,128)(2,1)}, u32[]{:S(2)}, u32[]{:S(2)}) collective-permute-start(bf16[4,2,128,640]{3,2,1,0:T(8,128)(2,1)S(1)} %pad_maximum_fusion.3), channel_id=1, source_target_pairs={{0,16},{1,17},{2,18},{3,19},{4,20},{5,21},{6,22},{7,23},{8,24},{9,... | collective-permute-start | bytes 3932168 | tf_op jit(solution)/shard_map/ppermute | solution.py:210
  264.1 29.7 %collective-permute-start.24 = (bf16[4,2,128,640]{3,2,1,0:T(8,128)(2,1)S(1)}, bf16[4,2,128,640]{3,2,1,0:T(8,128)(2,1)S(1)}, u32[]{:S(2)}, u32[]{:S(2)}) collective-permute-start(bf16[4,2,128,640]{3,2,1,0:T(8,128)(2,1)S(1)} %all-to-all-done.6.refs_1_), channel_id=1, source_target_pairs={{0,8},{1,9},{2,10},{3,11},{4,12},{5,13},{6,14},{7,15},{8,0},{9,1},... | collective-permute-start | bytes 3932168 | tf_op jit(solution)/shard_map/ppermute | solution.py:215
  264.4 29.4 %collective-permute-start.23 = (bf16[4,2,128,640]{3,2,1,0:T(8,128)(2,1)S(1)}, bf16[4,2,128,640]{3,2,1,0:T(8,128)(2,1)S(1)}, u32[]{:S(2)}, u32[]{:S(2)}) collective-permute-start(bf16[4,2,128,640]{3,2,1,0:T(8,128)(2,1)S(1)} %collective-permute-done.20.refs_2_), channel_id=1, source_target_pairs={{0,8},{1,9},{2,10},{3,11},{4,12},{5,13},{6,14},{7,15},{8,0},{9,1},... | collective-permute-start | bytes 3932168 | tf_op jit(solution)/shard_map/ppermute | solution.py:215
  329.7 19.0 %collective-permute-start.27 = (bf16[3072,640]{1,0:T(8,128)(2,1)}, bf16[3072,640]{1,0:T(8,128)(2,1)S(1)}, u32[]{:S(2)}, u32[]{:S(2)}) collective-permute-start(bf16[3072,640]{1,0:T(8,128)(2,1)} %convolution_convert_fusion.1), channel_id=1, source_target_pairs={{0,8},{1,9},{2,10},{3,11},{4,12},{5,13},{6,14},{7,15},{8,0},{9,1},... | collective-permute-start | bytes 11796488 | tf_op jit(solution)/shard_map/ppermute | solution.py:239
  368.4 40.2 %collective-permute-start.29 = (bf16[1152,3072]{1,0:T(8,128)(2,1)}, bf16[1152,3072]{1,0:T(8,128)(2,1)}, u32[]{:S(2)}, u32[]{:S(2)}) collective-permute-start(bf16[1152,3072]{1,0:T(8,128)(2,1)} %convolution_convert_fusion), channel_id=1, source_target_pairs={{0,8},{1,9},{2,10},{3,11},{4,12},{5,13},{6,14},{7,15},{8,0},{9,1},... | collective-permute-start | bytes 21233672 | tf_op jit(solution)/shard_map/ppermute | solution.py:239
  370.8 37.8 %collective-permute-start.28 = (bf16[4,2,128,640]{3,2,1,0:T(8,128)(2,1)S(1)}, bf16[4,2,128,640]{3,2,1,0:T(8,128)(2,1)S(1)}, u32[]{:S(2)}, u32[]{:S(2)}) collective-permute-start(bf16[4,2,128,640]{3,2,1,0:T(8,128)(2,1)S(1)} %dynamic-slice_bitcast_fusion), channel_id=1, source_target_pairs={{0,16},{1,17},{2,18},{3,19},{4,20},{5,21},{6,22},{7,23},{8,24},{9,... | collective-permute-start | bytes 3932168 | tf_op jit(solution)/shard_map/ppermute | solution.py:268
  422.1 30.8 %collective-permute-start.30 = (bf16[4,2,128,640]{3,2,1,0:T(8,128)(2,1)}, bf16[4,2,128,640]{3,2,1,0:T(8,128)(2,1)}, u32[]{:S(2)}, u32[]{:S(2)}) collective-permute-start(bf16[4,2,128,640]{3,2,1,0:T(8,128)(2,1)} %pad_maximum_fusion.4), channel_id=1, source_target_pairs={{0,1},{1,0},{2,3},{3,2},{4,5},{5,4},{6,7},{7,6},{8,9},{9,8},{10,11... | collective-permute-start | bytes 3932168 | tf_op jit(solution)/shard_map/ppermute | solution.py:302
  425.7 27.2 %collective-permute-start.31 = (bf16[2,2,48,3072]{3,2,1,0:T(8,128)(2,1)}, bf16[2,2,48,3072]{3,2,1,0:T(8,128)(2,1)}, u32[]{:S(2)}, u32[]{:S(2)}) collective-permute-start(bf16[2,2,48,3072]{3,2,1,0:T(8,128)(2,1)} %dynamic-slice_bitcast_fusion.3), channel_id=1, source_target_pairs={{0,16},{1,17},{2,18},{3,19},{4,20},{5,21},{6,22},{7,23},{8,24},{9,... | collective-permute-start | bytes 3538952 | tf_op jit(solution)/shard_map/ppermute | solution.py:272
  455.8 37.3 %all-to-all-start.7 = ((bf16[4,2,128,640]{3,2,1,0:T(8,128)(2,1)}), bf16[4,2,128,640]{3,2,1,0:T(8,128)(2,1)S(1)}, u32[]{:S(2)}, u32[]{:S(2)}) async-start(bf16[4,2,128,640]{3,2,1,0:T(8,128)(2,1)} %pad_maximum_fusion.5), calls=%async_computation.7 | async-start | bytes 2621440 | tf_op jit(solution)/shard_map/all_to_all | solution.py:89
  459.9 33.3 %collective-permute-start.34 = (bf16[1152,640]{1,0:T(8,128)(2,1)}, bf16[1152,640]{1,0:T(8,128)(2,1)}, u32[]{:S(2)}, u32[]{:S(2)}) collective-permute-start(bf16[1152,640]{1,0:T(8,128)(2,1)} %convolution_convert_fusion.4), channel_id=1, source_target_pairs={{0,8},{1,9},{2,10},{3,11},{4,12},{5,13},{6,14},{7,15},{8,0},{9,1},... | collective-permute-start | bytes 4423688 | tf_op jit(solution)/shard_map/ppermute | solution.py:239
  464.4 27.7 %collective-permute-start.32 = (bf16[4,48,3072]{2,1,0:T(8,128)(2,1)S(1)}, bf16[4,48,3072]{2,1,0:T(8,128)(2,1)S(1)}, u32[]{:S(2)}, u32[]{:S(2)}) collective-permute-start(bf16[4,48,3072]{2,1,0:T(8,128)(2,1)S(1)} %dynamic-slice_bitcast_fusion.2), channel_id=1, source_target_pairs={{0,1},{1,0},{2,3},{3,2},{4,5},{5,4},{6,7},{7,6},{8,9},{9,8},{10,11... | collective-permute-start | bytes 3538952 | tf_op jit(solution)/shard_map/ppermute | solution.py:291
  464.7 27.4 %collective-permute-start.33 = (bf16[2,2,48,3072]{3,2,1,0:T(8,128)(2,1)S(1)}, bf16[2,2,48,3072]{3,2,1,0:T(8,128)(2,1)S(1)}, u32[]{:S(2)}, u32[]{:S(2)}) collective-permute-start(bf16[2,2,48,3072]{3,2,1,0:T(8,128)(2,1)S(1)} %dynamic-slice_bitcast_fusion.1), channel_id=1, source_target_pairs={{0,16},{1,17},{2,18},{3,19},{4,20},{5,21},{6,22},{7,23},{8,24},{9,... | collective-permute-start | bytes 3538952 | tf_op jit(solution)/shard_map/ppermute | solution.py:272
  498.9 37.0 %all-to-all-start.8 = ((bf16[4,48,3072]{2,1,0:T(8,128)(2,1)}), bf16[4,48,3072]{2,1,0:T(8,128)(2,1)S(1)}, u32[]{:S(2)}, u32[]{:S(2)}) async-start(bf16[4,48,3072]{2,1,0:T(8,128)(2,1)} %get-tuple-element.616), calls=%async_computation.8 | async-start | bytes 2359296 | tf_op jit(solution)/shard_map/all_to_all | solution.py:89
  504.5 31.4 %collective-permute-start.35 = (bf16[2,128,640]{2,1,0:T(8,128)(2,1)S(1)}, bf16[2,128,640]{2,1,0:T(8,128)(2,1)S(1)}, u32[]{:S(2)}, u32[]{:S(2)}) collective-permute-start(bf16[2,128,640]{2,1,0:T(8,128)(2,1)S(1)} %reduce_sum.136), channel_id=1, source_target_pairs={{0,16},{1,17},{2,18},{3,19},{4,20},{5,21},{6,22},{7,23},{8,24},{9,... | collective-permute-start | bytes 983048 | tf_op jit(solution)/shard_map/ppermute | solution.py:354
  505.3 30.6 %collective-permute-start.36 = (bf16[4,48,3072]{2,1,0:T(8,128)(2,1)}, bf16[4,48,3072]{2,1,0:T(8,128)(2,1)S(1)}, u32[]{:S(2)}, u32[]{:S(2)}) collective-permute-start(bf16[4,48,3072]{2,1,0:T(8,128)(2,1)} %get-tuple-element.617), channel_id=1, source_target_pairs={{0,1},{1,0},{2,3},{3,2},{4,5},{5,4},{6,7},{7,6},{8,9},{9,8},{10,11... | collective-permute-start | bytes 3538952 | tf_op jit(solution)/shard_map/ppermute | solution.py:296
  536.0 33.4 %collective-permute-start.38 = (bf16[1152,896]{1,0:T(8,128)(2,1)}, bf16[1152,896]{1,0:T(8,128)(2,1)}, u32[]{:S(2)}, u32[]{:S(2)}) collective-permute-start(bf16[1152,896]{1,0:T(8,128)(2,1)} %convolution_convert_fusion.3), channel_id=1, source_target_pairs={{0,8},{1,9},{2,10},{3,11},{4,12},{5,13},{6,14},{7,15},{8,0},{9,1},... | collective-permute-start | bytes 6193160 | tf_op jit(solution)/shard_map/ppermute | solution.py:239
  542.9 33.2 %all-to-all-start.9 = ((bf16[4,48,3072]{2,1,0:T(8,128)(2,1)}), bf16[4,48,3072]{2,1,0:T(8,128)(2,1)}, u32[]{:S(2)}, u32[]{:S(2)}) async-start(bf16[4,48,3072]{2,1,0:T(8,128)(2,1)} %add_convert_fusion.2), calls=%async_computation.9 | async-start | bytes 2359296 | tf_op jit(solution)/shard_map/all_to_all | solution.py:89
  548.0 26.0 %collective-permute-start.37 = (bf16[384,640]{1,0:T(8,128)(2,1)S(1)}, bf16[384,640]{1,0:T(8,128)(2,1)}, u32[]{:S(2)}, u32[]{:S(2)}) collective-permute-start(bf16[384,640]{1,0:T(8,128)(2,1)S(1)} %pad_maximum_fusion.18), channel_id=1, source_target_pairs={{0,8},{1,9},{2,10},{3,11},{4,12},{5,13},{6,14},{7,15},{8,0},{9,1},... | collective-permute-start | bytes 1474568 | tf_op jit(solution)/shard_map/ppermute | solution.py:364
  578.8 33.5 %all-to-all-start.10 = ((bf16[8,8,4608]{2,1,0:T(8,128)(2,1)}), bf16[8,8,4608]{2,1,0:T(8,128)(2,1)}, u32[]{:S(2)}, u32[]{:S(2)}) async-start(bf16[8,8,4608]{2,1,0:T(8,128)(2,1)} %broadcast_in_dim.71), calls=%async_computation.10 | async-start | bytes 1179648 | tf_op jit(solution)/shard_map/all_to_all | solution.py:412
  583.3 29.0 %collective-permute-start.39 = (bf16[4,48,1536]{2,1,0:T(8,128)(2,1)}, bf16[4,48,1536]{2,1,0:T(8,128)(2,1)}, u32[]{:S(2)}, u32[]{:S(2)}) collective-permute-start(bf16[4,48,1536]{2,1,0:T(8,128)(2,1)} %dynamic-slice_bitcast_fusion.6), channel_id=1, source_target_pairs={{0,1},{1,0},{2,3},{3,2},{4,5},{5,4},{6,7},{7,6},{8,9},{9,8},{10,11... | collective-permute-start | bytes 1769480 | tf_op jit(solution)/shard_map/ppermute | solution.py:291
  584.7 27.6 %collective-permute-start.40 = (bf16[4,2,48,1536]{3,2,0,1:T(8,128)(2,1)}, bf16[4,2,48,1536]{3,2,0,1:T(8,128)(2,1)}, u32[]{:S(2)}, u32[]{:S(2)}) collective-permute-start(bf16[4,2,48,1536]{3,2,0,1:T(8,128)(2,1)} %copy_bitcast_fusion.1), channel_id=1, source_target_pairs={{0,16},{1,17},{2,18},{3,19},{4,20},{5,21},{6,22},{7,23},{8,24},{9,... | collective-permute-start | bytes 3538952 | tf_op jit(solution)/shard_map/ppermute | solution.py:268
  612.3 19.1 %collective-permute-start.43 = (bf16[1152,896]{1,0:T(8,128)(2,1)}, bf16[1152,896]{1,0:T(8,128)(2,1)}, u32[]{:S(2)}, u32[]{:S(2)}) collective-permute-start(bf16[1152,896]{1,0:T(8,128)(2,1)} %convolution_convert_fusion.2), channel_id=1, source_target_pairs={{0,8},{1,9},{2,10},{3,11},{4,12},{5,13},{6,14},{7,15},{8,0},{9,1},... | collective-permute-start | bytes 6193160 | tf_op jit(solution)/shard_map/ppermute | solution.py:239
  623.0 38.3 %collective-permute-start.41 = (bf16[2,48,3072]{2,1,0:T(8,128)(2,1)}, bf16[2,48,3072]{2,1,0:T(8,128)(2,1)}, u32[]{:S(2)}, u32[]{:S(2)}) collective-permute-start(bf16[2,48,3072]{2,1,0:T(8,128)(2,1)} %pad_maximum_fusion.17), channel_id=1, source_target_pairs={{0,16},{1,17},{2,18},{3,19},{4,20},{5,21},{6,22},{7,23},{8,24},{9,... | collective-permute-start | bytes 1769480 | tf_op jit(solution)/shard_map/ppermute | solution.py:354
  626.4 35.0 %all-to-all-start.11 = ((bf16[4,48,1536]{2,1,0:T(8,128)(2,1)}), bf16[4,48,1536]{2,1,0:T(8,128)(2,1)}, u32[]{:S(2)}, u32[]{:S(2)}) async-start(bf16[4,48,1536]{2,1,0:T(8,128)(2,1)} %get-tuple-element.620), calls=%async_computation.11 | async-start | bytes 1179648 | tf_op jit(solution)/shard_map/all_to_all | solution.py:89
  631.1 30.3 %collective-permute-start.42 = (bf16[4,48,1536]{2,1,0:T(8,128)(2,1)}, bf16[4,48,1536]{2,1,0:T(8,128)(2,1)}, u32[]{:S(2)}, u32[]{:S(2)}) collective-permute-start(bf16[4,48,1536]{2,1,0:T(8,128)(2,1)} %get-tuple-element.621), channel_id=1, source_target_pairs={{0,1},{1,0},{2,3},{3,2},{4,5},{5,4},{6,7},{7,6},{8,9},{9,8},{10,11... | collective-permute-start | bytes 1769480 | tf_op jit(solution)/shard_map/ppermute | solution.py:296
  639.2 22.2 %collective-permute-start.44 = (bf16[4,2,48,896]{3,2,1,0:T(8,128)(2,1)}, bf16[4,2,48,896]{3,2,1,0:T(8,128)(2,1)}, u32[]{:S(2)}, u32[]{:S(2)}) collective-permute-start(bf16[4,2,48,896]{3,2,1,0:T(8,128)(2,1)} %dynamic-slice_bitcast_fusion.4), channel_id=1, source_target_pairs={{0,16},{1,17},{2,18},{3,19},{4,20},{5,21},{6,22},{7,23},{8,24},{9,... | collective-permute-start | bytes 2064392 | tf_op jit(solution)/shard_map/ppermute | solution.py:268
  666.8 32.0 %all-to-all-start.12 = ((bf16[8,8,2560]{2,1,0:T(8,128)(2,1)}), bf16[8,8,2560]{2,1,0:T(8,128)(2,1)}, u32[]{:S(2)}, u32[]{:S(2)}) async-start(bf16[8,8,2560]{2,1,0:T(8,128)(2,1)} %broadcast_in_dim.73), calls=%async_computation.12 | async-start | bytes 655360 | tf_op jit(solution)/shard_map/all_to_all | solution.py:412
  674.6 24.2 %collective-permute-start.50 = (bf16[64,4608]{1,0:T(8,128)(2,1)}, bf16[64,4608]{1,0:T(8,128)(2,1)}, u32[]{:S(2)}, u32[]{:S(2)}) collective-permute-start(bf16[64,4608]{1,0:T(8,128)(2,1)} %bitcast.68), channel_id=1, source_target_pairs={{0,16},{1,17},{2,18},{3,19},{4,20},{5,21},{6,22},{7,23},{8,24},{9,... | collective-permute-start | bytes 1769480 | tf_op jit(solution)/shard_map/ppermute | solution.py:395
  676.3 22.5 %collective-permute-start.49 = (bf16[4,2,48,896]{3,2,1,0:T(8,128)(2,1)}, bf16[4,2,48,896]{3,2,1,0:T(8,128)(2,1)}, u32[]{:S(2)}, u32[]{:S(2)}) collective-permute-start(bf16[4,2,48,896]{3,2,1,0:T(8,128)(2,1)} %pad_maximum_fusion.14), channel_id=1, source_target_pairs={{0,1},{1,0},{2,3},{3,2},{4,5},{5,4},{6,7},{7,6},{8,9},{9,8},{10,11... | collective-permute-start | bytes 2064392 | tf_op jit(solution)/shard_map/ppermute | solution.py:302
  678.7 20.1 %collective-permute-start.45 = (bf16[144,3072]{1,0:T(8,128)(2,1)}, bf16[144,3072]{1,0:T(8,128)(2,1)}, u32[]{:S(2)}, u32[]{:S(2)}) collective-permute-start(bf16[144,3072]{1,0:T(8,128)(2,1)} %pad_maximum_fusion.12), channel_id=1, source_target_pairs={{0,8},{1,9},{2,10},{3,11},{4,12},{5,13},{6,14},{7,15},{8,0},{9,1},... | collective-permute-start | bytes 2654216 | tf_op jit(solution)/shard_map/ppermute | solution.py:364
  686.0 12.8 %collective-permute-start.47 = (bf16[48,1536]{1,0:T(8,128)(2,1)S(1)}, bf16[48,1536]{1,0:T(8,128)(2,1)S(1)}, u32[]{:S(2)}, u32[]{:S(2)}) collective-permute-start(bf16[48,1536]{1,0:T(8,128)(2,1)S(1)} %get-tuple-element.649), channel_id=1, source_target_pairs={{0,4},{1,5},{2,6},{3,7},{4,0},{5,1},{6,2},{7,3},{8,12},{9,13},{10,... | collective-permute-start | bytes 442376 | tf_op jit(solution)/shard_map/ppermute | solution.py:328
  689.4 9.4 %collective-permute-start.46 = (bf16[48,1536]{1,0:T(8,128)(2,1)S(1)}, bf16[48,1536]{1,0:T(8,128)(2,1)S(1)}, u32[]{:S(2)}, u32[]{:S(2)}) collective-permute-start(bf16[48,1536]{1,0:T(8,128)(2,1)S(1)} %get-tuple-element.650), channel_id=1, source_target_pairs={{0,2},{1,3},{2,4},{3,5},{4,6},{5,7},{6,0},{7,1},{8,10},{9,11},{10,... | collective-permute-start | bytes 442376 | tf_op jit(solution)/shard_map/ppermute | solution.py:328
  700.1 20.7 %collective-permute-start.51 = (bf16[2,48,1536]{2,1,0:T(8,128)(2,1)S(1)}, bf16[2,48,1536]{2,1,0:T(8,128)(2,1)}, u32[]{:S(2)}, u32[]{:S(2)}) collective-permute-start(bf16[2,48,1536]{2,1,0:T(8,128)(2,1)S(1)} %pad_maximum_fusion.24), channel_id=1, source_target_pairs={{0,16},{1,17},{2,18},{3,19},{4,20},{5,21},{6,22},{7,23},{8,24},{9,... | collective-permute-start | bytes 884744 | tf_op jit(solution)/shard_map/ppermute | solution.py:354
  700.9 20.0 %collective-permute-start.52 = (bf16[64,2560]{1,0:T(8,128)(2,1)}, bf16[64,2560]{1,0:T(8,128)(2,1)}, u32[]{:S(2)}, u32[]{:S(2)}) collective-permute-start(bf16[64,2560]{1,0:T(8,128)(2,1)} %bitcast.92), channel_id=1, source_target_pairs={{0,16},{1,17},{2,18},{3,19},{4,20},{5,21},{6,22},{7,23},{8,24},{9,... | collective-permute-start | bytes 983048 | tf_op jit(solution)/shard_map/ppermute | solution.py:395
  705.5 21.7 %all-to-all-start.13 = ((bf16[4,2,48,896]{3,2,1,0:T(8,128)(2,1)}), bf16[4,2,48,896]{3,2,1,0:T(8,128)(2,1)}, u32[]{:S(2)}, u32[]{:S(2)}) async-start(bf16[4,2,48,896]{3,2,1,0:T(8,128)(2,1)} %pad_maximum_fusion.15), calls=%async_computation.13 | async-start | bytes 1376256 | tf_op jit(solution)/shard_map/all_to_all | solution.py:89
  709.8 7.4 collective-permute-start.53
  730.0 9.6 %collective-permute-start.56 = (bf16[2,64,2560]{2,1,0:T(8,128)(2,1)}, bf16[2,64,2560]{2,1,0:T(8,128)(2,1)}, u32[]{:S(2)}, u32[]{:S(2)}) collective-permute-start(bf16[2,64,2560]{2,1,0:T(8,128)(2,1)} %pad_maximum_fusion.16), channel_id=1, source_target_pairs={{0,8},{1,9},{2,10},{3,11},{4,12},{5,13},{6,14},{7,15},{8,0},{9,1},... | collective-permute-start | bytes 1966088 | tf_op jit(solution)/shard_map/ppermute | solution.py:404
  734.6 10.3 %all-to-all-start.14 = ((bf16[8,8,144]{2,1,0:T(8,128)(2,1)}), bf16[8,8,144]{2,1,0:T(8,128)(2,1)S(1)}, u32[]{:S(2)}, u32[]{:S(2)}) async-start(bf16[8,8,144]{2,1,0:T(8,128)(2,1)} %bitcast.240), calls=%async_computation.14 | async-start | bytes 65536 | tf_op jit(solution)/shard_map/all_to_all | solution.py:1289
  (68 other events, 458.1 us)

commit v8 on v7

--- a/solution.py
+++ b/solution.py
@@ -1081,9 +1081,7 @@
     g_two.y()
     inputs_low = block_in[0]
     every_act = across_replicas(group_act, act_far)
-    modulation, tables, inputs_low, every_act = hold(
-        gathers, (modulation, tables, inputs_low, every_act)
-    )
+    every_act = hold(gathers[1:], every_act)
 
     g_one.core("both")
     g_two.x()

time: 763 us -> 758 us (level)
  waiting for transfers between devices: 114 us -> 95.6 us
  starting transfers between devices: 120 us -> 132 us
    ppermute x5, waiting for transfers between devices: 30.1 us -> 17.7 us  [y(): self.live['far'] = lax.ppermute(self.live['own'], AXES, TO_Y)]
    all_to_all x1, waiting for transfers between devices: 9.99 us -> 0.01 us  [sum_back(): got = lax.all_to_all(shaped, 'fsdp', 0, 0)]
  transfers between devices with their start and end apart: 73 -> 73, of which waited for: 25 -> 22; matrix products, arithmetic and copies ran while one was open for 18% -> 19% of each run, Pallas kernels for 36% -> 37%
where the time goes in v8:
time: 758 us; the launch traced here: 747 us
  Pallas kernels  293 us (39%)
  starting transfers between devices  132 us (17%)
  waiting for transfers between devices  95.6 us (13%)
  matrix products  77.3 us (10%)
  other arithmetic  76.8 us (10%)
  local copies, waits for them, and re-layouts  68.7 us (9%)
    pallas_call x5, Pallas kernels, call_placed(): pl.pallas_call(run, in_specs=[pl.BlockSpec(memory_space=pltpu.SMEM)] + [a...  90.5 us
    pallas_call x4, Pallas kernels, call_rows(): pl.pallas_call(kernel, in_specs=specs, out_specs=out_specs, out_shape=out...  84.7 us
    pallas_call x4, Pallas kernels, attend_back(): pl.pallas_call(partial(back_kernel, hd, c, score_scale, part), grid=(n //...  80.9 us
    dot_general x12, matrix products, dot_left(): lax.dot_general(left, right, (((0,), (0,)), ((), ())), preferred_element_...  72.2 us
    all_to_all x10, starting transfers between devices, over_z(): return lax.all_to_all(operand, 'fsdp', 0, 0, axis_index_groups=Z_GROUPS)  44.4 us
    ppermute x5, waiting for transfers between devices, x(): self.live['both'] = lax.ppermute(ends, AXES, TO_X)  23.4 us
    pallas_call x1, Pallas kernels, attend(): pl.pallas_call(partial(attend_kernel, hd, c), grid=(n // BLOCK,), in_spec...  22.7 us
    all_to_all x10, waiting for transfers between devices, over_z(): return lax.all_to_all(operand, 'fsdp', 0, 0, axis_index_groups=Z_GROUPS)  22.5 us
  transfers between devices with their start and end apart: 73, of which 22 were waited for; matrix products, arithmetic and copies ran while one was open for 19% of the time, Pallas kernels for 37%

profile of v8, /device:TPU:1, one launch (start us, length us, event | category | flops | bytes accessed | tf_op | source)
XLA Modules:
  0.0 747.3 jit_solution(5496555236271938301)
XLA Ops:
  2.1 6.4 all-to-all-start.1
  17.1 4.5 all-to-all-start
  25.1 2.7 fusion.60
  27.7 11.5 %all-to-all-done.refs_1_ = bf16[4,2,48,896]{3,2,1,0:T(8,128)(2,1)} async-done(((bf16[4,2,48,896]{3,2,1,0:T(8,128)(2,1)}), bf16[4,2,48,896]{3,2,1,0:T(8,128)(2,1)}, u32[]{:S(2)}, u32[]{:S(2)}) %all-to-all-start) | async-done | bytes 688160 | tf_op jit(solution)/shard_map/all_to_all | solution.py:89
  40.5 4.3 all-to-all-start.2
  44.7 5.4 multiply_cosine_fusion
  59.5 2.8 pad_maximum_fusion.2.refs_12_.rot_ref
  67.1 4.6 collective-permute-done.refs_2_
  76.4 3.6 all-to-all-start.4
  84.2 3.0 collective-permute-start.3
  90.2 7.3 collective-permute-done.7.refs_3_
  97.5 3.6 collective-permute-start.10
  101.1 5.1 collective-permute-done.2.refs_2_
  107.4 3.6 collective-permute-start.6
  116.2 4.6 all-to-all-start.3
  122.9 20.7 %prepare.2 = (bf16[1024,1152]{1,0:T(8,128)(2,1)}, bf16[8,1024,128]{2,1,0:T(8,128)(2,1)}, bf16[8,1024,128]{2,1,0:T(8,128)(2,1)}, bf16[8,1024,128]{2,1,0:T(8,128)(...) custom-call(s32[4]{0:T(128)} %pad_add_fusion.refs_0_, ...), custom_call_target="tpu_custom_call" | custom-call | flops 8153726976 | bytes 20971520 | tf_op jit(solution)/shard_map/prepare/pallas_call | solution.py:171
  143.7 4.7 collective-permute-done.4.refs_3_
  151.6 3.9 all-to-all-start.5
  156.7 21.0 %prepare.3 = (bf16[8,1024,128]{2,1,0:T(8,128)(2,1)}, bf16[8,1024,128]{2,1,0:T(8,128)(2,1)}, bf16[8,1024,128]{2,1,0:T(8,128)(2,1)}, bf16[8,1024,128]{2,1,0:T(8,12...) custom-call(s32[4]{0:T(128)} %pad_add_fusion.refs_0_, ...), custom_call_target="tpu_custom_call" | custom-call | flops 8153726976 | bytes 20971520 | tf_op jit(solution)/shard_map/prepare/pallas_call | solution.py:171
  177.8 5.4 collective-permute-done.11.refs_2_
  185.4 3.5 all-to-all-start.6
  196.0 22.7 %attend.1 = (bf16[1024,1152]{1,0:T(8,128)(2,1)}, bf16[8,1024,128]{2,1,0:T(8,128)(2,1)}, bf16[8,1024,128]{2,1,0:T(8,128)(2,1)}) custom-call(bf16[8,1024,128]{2,1,0:T(8,128)(2,1)} %get-tuple-element.364.refs_0_, bf16[8,1024,128]{2,1,0:T(8,128)(2,1)} %get-tuple-element.365.refs_1_.k_ref, bf16[8,1024,128]{2,1,0:T(8,128)(2,1)} %get-tuple-element.366.refs_2_.v_ref, ...), custom_call_target="tpu_custom_call" | custom-call | flops 5368709120 | bytes 20971520 | tf_op jit(solution)/shard_map/attend/pallas_call | solution.py:568
  227.7 11.3 %join.1 = (bf16[1024,1152]{1,0:T(8,128)(2,1)}, f32[1024,1152]{1,0:T(8,128)}, bf16[1024,1152]{1,0:T(8,128)(2,1)}) custom-call(bf16[1024,1152]{1,0:T(8,128)(2,1)} %get-tuple-element.381.mix_ref, bf16[1024,1152]{1,0:T(8,128)(2,1)} %bitcast.313, bf16[1024,16]{1,0:T(8,128)(2,1)} %copy.88.refs_8_.hot_ref.refs_10_, f32[1024,1]{1,0:T(8,128)} %copy.91.keep_ref.refs_11_, ...), custom_call_target="tpu_custom_call" | custom-call | flops 7247757312 | bytes 12054528 | tf_op jit(solution)/shard_map/join/pallas_call | solution.py:809
  239.0 14.6 %gate.1 = (bf16[1024,3072]{1,0:T(8,128)(2,1)}, bf16[1152,3072]{1,0:T(8,128)(2,1)}) custom-call(s32[4]{0:T(128)} %pad_add_fusion.refs_0_, bf16[4,2,48,1536]{3,2,1,0:T(8,128)(2,1)} %all-to-all-done.3.refs_1_, bf16[4,2,48,1536]{3,2,1,0:T(8,128)(2,1)} %collective-permute-done.11.refs_2_, bf16[4,2,48,1536]{3,2,1,0:T(8,128)(2,1)} %copy-done.51, ...), custom_call_target="tpu_custom_call" | custom-call | flops 7247757312 | bytes 2359296 | tf_op jit(solution)/shard_map/gate/pallas_call | solution.py:171
  253.7 2.6 collective-permute-done.20.refs_2_
  260.5 16.6 %up.1 = (bf16[1024,3072]{1,0:T(8,128)(2,1)}, bf16[1024,3072]{1,0:T(8,128)(2,1)}, bf16[1152,3072]{1,0:T(8,128)(2,1)}) custom-call(s32[4]{0:T(128)} %pad_add_fusion.refs_0_, bf16[4,2,48,1536]{3,2,1,0:T(8,128)(2,1)} %copy-done.8, bf16[4,2,48,1536]{3,2,1,0:T(8,128)(2,1)} %copy-done.34, bf16[4,2,48,1536]{3,2,1,0:T(8,128)(2,1)} %collective-permute-done.17.refs_3_, ...), custom_call_target="tpu_custom_call" | custom-call | flops 7247757312 | bytes 8650752 | tf_op jit(solution)/shard_map/up/pallas_call | solution.py:171
  277.1 11.3 %collective-permute-done.22.refs_3_ = bf16[4,2,128,640]{3,2,1,0:T(8,128)(2,1)S(1)} collective-permute-done((bf16[4,2,128,640]{3,2,1,0:T(8,128)(2,1)S(1)}, bf16[4,2,128,640]{3,2,1,0:T(8,128)(2,1)S(1)}, u32[]{:S(2)}, u32[]{:S(2)}) %collective-permute-start.22) | collective-permute-done | bytes 1310752 | tf_op jit(solution)/shard_map/ppermute | solution.py:210
  290.4 2.7 collective-permute-done.26.refs_6_
  294.1 17.5 %down.1 = (bf16[1024,1152]{1,0:T(8,128)(2,1)}, bf16[1024,1280]{1,0:T(8,128)(2,1)}, f32[16,1152]{1,0:T(8,128)}, bf16[3072,1280]{1,0:T(8,128)(2,1)}) custom-call(s32[4]{0:T(128)} %pad_add_fusion.refs_0_, bf16[4,2,128,640]{3,2,1,0:T(8,128)(2,1)} %copy-done.5, bf16[4,2,128,640]{3,2,1,0:T(8,128)(2,1)} %copy-done.33, bf16[4,2,128,640]{3,2,1,0:T(8,128)(2,1)} %copy-done.48, ...), custom_call_target="tpu_custom_call" | custom-call | flops 8053063680 | bytes 13627392 | tf_op jit(solution)/shard_map/down/pallas_call | solution.py:171
  313.8 9.4 %convolution_convert_fusion.1 = bf16[3072,640]{1,0:T(8,128)(2,1)} fusion(bf16[1024,3072]{1,0:T(8,128)(2,1)} %get-tuple-element.423.refs_7_, bf16[1024,1280]{1,0:T(8,128)(2,1)S(1)} %copy-done.32, s32[]{:T(128)S(6)} %select_n.439), kind=kOutput, calls=%fused_computation.5 | convolution fusion | flops 4028497920 | bytes 11534340 | tf_op jit(solution)/shard_map/dot_general | solution.py:29
  323.6 18.6 %inner_back.1 = (bf16[1024,3072]{1,0:T(8,128)(2,1)}, bf16[1024,3072]{1,0:T(8,128)(2,1)}) custom-call(s32[1]{0:T(128)} %bitcast.1.core_ref, bf16[1024,1280]{1,0:T(8,128)(2,1)} %get-tuple-element.435.grad_ref, bf16[1024,3072]{1,0:T(8,128)(2,1)} %get-tuple-element.436.refs_8_.gate_ref, bf16[1024,3072]{1,0:T(8,128)(2,1)} %get-tuple-element.437.up_ref, ...), custom_call_target="tpu_custom_call" | custom-call | flops 8053063680 | bytes 23068672 | tf_op jit(solution)/shard_map/inner_back/pallas_call | solution.py:809
  342.2 10.0 %add_convert_fusion.1 = bf16[3072,640]{1,0:T(8,128)(2,1)} fusion(bf16[3072,640]{1,0:T(8,128)(2,1)S(1)} %collective-permute-done.27, bf16[1024,3072]{1,0:T(8,128)(2,1)} %get-tuple-element.423.refs_7_, bf16[1024,640]{1,0:T(8,128)(2,1)S(1)} %constant_dynamic-slice_fusion.3), kind=kOutput, calls=%fused_computation.4 | convolution fusion | flops 4032430080 | bytes 15466496 | tf_op jit(solution)/shard_map/dot_general | solution.py:29
  352.2 9.7 %convolution_convert_fusion = bf16[1152,3072]{1,0:T(8,128)(2,1)} fusion(bf16[1024,1152]{1,0:T(8,128)(2,1)S(1)} %copy-done.53, bf16[1024,3072]{1,0:T(8,128)(2,1)S(1)} %copy-done.55), kind=kOutput, calls=%fused_computation.1 | convolution fusion | flops 7251296256 | bytes 15728640 | tf_op jit(solution)/shard_map/dot_general | solution.py:29
  365.4 33.3 %middle_back.1 = (f32[1024,1152]{1,0:T(8,128)}, bf16[1024,1280]{1,0:T(8,128)(2,1)}, f32[16,3456]{1,0:T(8,128)}) custom-call(s32[1]{0:T(128)} %bitcast.1.core_ref, bf16[1024,3072]{1,0:T(8,128)(2,1)} %get-tuple-element.449.send_ref, bf16[1024,3072]{1,0:T(8,128)(2,1)} %get-tuple-element.460.mine_ref, f32[1024,1152]{1,0:T(8,128)} %get-tuple-element.451.refs_8_.mid_ref, ...), custom_call_target="tpu_custom_call" | custom-call | flops 14495514624 | bytes 36433920 | tf_op jit(solution)/shard_map/middle_back/pallas_call | solution.py:809
  398.7 3.6 constant_dynamic-slice_fusion.1
  402.3 11.8 %add_convert_fusion = bf16[1152,3072]{1,0:T(8,128)(2,1)S(1)} fusion(bf16[1152,3072]{1,0:T(8,128)(2,1)} %collective-permute-done.29, bf16[1024,1152]{1,0:T(8,128)(2,1)S(1)} %copy-done.54, bf16[1024,3072]{1,0:T(8,128)(2,1)} %get-tuple-element.460.mine_ref), kind=kOutput, calls=%fused_computation | convolution fusion | flops 7258374144 | bytes 22806528 | tf_op jit(solution)/shard_map/dot_general | solution.py:29
  419.9 12.8 %spread.1.do_ref = bf16[16,1024,128]{2,1,0:T(8,128)(2,1)} custom-call(bf16[1024,1280]{1,0:T(8,128)(2,1)} %get-tuple-element.468.ga_ref, bf16[1152,3072]{1,0:T(8,128)(2,1)} %get-tuple-element.383.w_ref.wt_ref, bf16[1024,1152]{1,0:T(8,128)(2,1)} %get-tuple-element.381.mix_ref), custom_call_target="tpu_custom_call" | custom-call | flops 2717908992 | bytes 12582912 | tf_op jit(solution)/shard_map/spread/pallas_call | solution.py:612
  432.7 4.5 convolution_convert_fusion.4
  437.8 8.9 %collective-permute-done.31 = bf16[2,2,48,3072]{3,2,1,0:T(8,128)(2,1)} collective-permute-done((bf16[2,2,48,3072]{3,2,1,0:T(8,128)(2,1)}, bf16[2,2,48,3072]{3,2,1,0:T(8,128)(2,1)}, u32[]{:S(2)}, u32[]{:S(2)}) %collective-permute-start.31) | collective-permute-done | bytes 1179680 | tf_op jit(solution)/shard_map/ppermute | solution.py:272
  449.6 4.5 all-to-all-start.7
  460.2 20.0 %attend_back.4 = (bf16[2,1024,896]{2,1,0:T(8,128)(2,1)}, f32[2,8,128]{2,1,0:T(8,128)}) custom-call(s32[1]{0:T(128)} %bitcast.1.core_ref, bf16[8,1024,128]{2,1,0:T(8,128)(2,1)} %get-tuple-element.476.q_ref, bf16[8,1024,128]{2,1,0:T(8,128)(2,1)} %get-tuple-element.365.refs_1_.k_ref, bf16[8,1024,128]{2,1,0:T(8,128)(2,1)} %get-tuple-element.366.refs_2_.v_ref, ...), custom_call_target="tpu_custom_call" | custom-call | flops 3355443200 | bytes 10485760 | tf_op jit(solution)/shard_map/attend_back/pallas_call | solution.py:716
  480.2 6.0 collective-permute-done.32
  489.2 4.0 fusion.7
  493.1 5.2 all-to-all-start.8
  500.3 20.1 %attend_back.5 = (bf16[2,1024,896]{2,1,0:T(8,128)(2,1)}, f32[2,8,128]{2,1,0:T(8,128)}) custom-call(s32[1]{0:T(128)} %bitcast.1.core_ref, bf16[8,1024,128]{2,1,0:T(8,128)(2,1)} %get-tuple-element.476.q_ref, bf16[8,1024,128]{2,1,0:T(8,128)(2,1)} %get-tuple-element.365.refs_1_.k_ref, ...), custom_call_target="tpu_custom_call", output_to_operand_aliasing={{0}: (10, {})} | custom-call | flops 3355443200 | bytes 10485760 | tf_op jit(solution)/shard_map/attend_back/pallas_call | solution.py:716
  520.4 5.6 convolution_convert_fusion.3
  526.0 4.5 fusion.5
  534.5 2.9 add_convert_fusion.2
  537.4 5.0 all-to-all-start.9
  543.3 20.5 %attend_back.6 = (bf16[2,1024,896]{2,1,0:T(8,128)(2,1)}, f32[2,8,128]{2,1,0:T(8,128)}) custom-call(s32[1]{0:T(128)} %bitcast.1.core_ref, bf16[8,1024,128]{2,1,0:T(8,128)(2,1)} %get-tuple-element.504.q_ref, bf16[8,1024,128]{2,1,0:T(8,128)(2,1)} %get-tuple-element.368.refs_4_.k_ref, bf16[8,1024,128]{2,1,0:T(8,128)(2,1)} %get-tuple-element.369.refs_5_.v_ref, ...), custom_call_target="tpu_custom_call" | custom-call | flops 3355443200 | bytes 10485760 | tf_op jit(solution)/shard_map/attend_back/pallas_call | solution.py:716
  563.9 4.3 fusion.1
  573.4 4.4 all-to-all-start.10
  580.3 20.3 %attend_back.7 = (bf16[2,1024,896]{2,1,0:T(8,128)(2,1)}, f32[2,8,128]{2,1,0:T(8,128)}) custom-call(s32[1]{0:T(128)} %bitcast.1.core_ref, bf16[8,1024,128]{2,1,0:T(8,128)(2,1)} %get-tuple-element.504.q_ref, bf16[8,1024,128]{2,1,0:T(8,128)(2,1)} %get-tuple-element.368.refs_4_.k_ref, ...), custom_call_target="tpu_custom_call", output_to_operand_aliasing={{0}: (10, {})} | custom-call | flops 3355443200 | bytes 10485760 | tf_op jit(solution)/shard_map/attend_back/pallas_call | solution.py:716
  603.3 4.0 convolution_convert_fusion.2
  620.9 4.7 all-to-all-start.11
  626.0 5.5 fusion.2
  634.8 21.5 %input_back.1 = (f32[1024,1152]{1,0:T(8,128)}, f32[16,2304]{1,0:T(8,128)}) custom-call(s32[1]{0:T(128)} %bitcast.1.core_ref, bf16[2,1024,896]{2,1,0:T(8,128)(2,1)} %get-tuple-element.531.one_ref, bf16[2,1024,896]{2,1,0:T(8,128)(2,1)} %get-tuple-element.532.two_ref, f32[1024,1152]{1,0:T(8,128)} %get-tuple-element.533.mid_ref, bf16[1024,1152]{1,0:T(8,128)(2,1)} %bitcast.314, ...), custom_call_target="tpu_custom_call" | custom-call | flops 11475615744 | bytes 25878528 | tf_op jit(solution)/shard_map/input_back/pallas_call | solution.py:809
  661.7 5.5 all-to-all-start.12
  677.6 3.0 collective-permute-start.48
  680.6 3.3 collective-permute-done.48
  686.0 7.4 collective-permute-done.47
  700.1 4.2 all-to-all-start.13
  715.4 6.4 all-to-all-done.13
  729.1 3.5 all-to-all-start.14
  (408 shorter events, 193.4 us)
Async XLA Ops:
  2.1 14.1 %all-to-all-start.1 = ((bf16[8,8,144]{2,1,0:T(8,128)(2,1)}), bf16[8,8,144]{2,1,0:T(8,128)(2,1)S(1)}, u32[]{:S(2)}, u32[]{:S(2)}) async-start(bf16[8,8,144]{2,1,0:T(8,128)(2,1)} %copy.84), calls=%async_computation.1 | async-start | bytes 65536 | tf_op jit(solution)/shard_map/all_to_all | solution.py:420
  17.1 22.1 %all-to-all-start = ((bf16[4,2,48,896]{3,2,1,0:T(8,128)(2,1)}), bf16[4,2,48,896]{3,2,1,0:T(8,128)(2,1)}, u32[]{:S(2)}, u32[]{:S(2)}) async-start(bf16[4,2,48,896]{3,2,1,0:T(8,128)(2,1)} %broadcast_in_dim.60), calls=%async_computation | async-start | bytes 1376256 | tf_op jit(solution)/shard_map/all_to_all | solution.py:89
  40.5 32.4 %all-to-all-start.2 = ((bf16[4,2,48,1536]{3,2,1,0:T(8,128)(2,1)}), bf16[4,2,48,1536]{3,2,1,0:T(8,128)(2,1)}, u32[]{:S(2)}, u32[]{:S(2)}) async-start(bf16[4,2,48,1536]{3,2,1,0:T(8,128)(2,1)} %broadcast_in_dim.61), calls=%async_computation.2 | async-start | bytes 2359296 | tf_op jit(solution)/shard_map/all_to_all | solution.py:89
  55.9 15.8 %collective-permute-start = (bf16[4,2,48,896]{3,2,1,0:T(8,128)(2,1)}, bf16[4,2,48,896]{3,2,1,0:T(8,128)(2,1)}, u32[]{:S(2)}, u32[]{:S(2)}) collective-permute-start(bf16[4,2,48,896]{3,2,1,0:T(8,128)(2,1)} %all-to-all-done.refs_1_), channel_id=1, source_target_pairs={{0,1},{1,0},{2,3},{3,2},{4,5},{5,4},{6,7},{7,6},{8,9},{9,8},{10,11... | collective-permute-start | bytes 2064392 | tf_op jit(solution)/shard_map/ppermute | solution.py:205
  72.8 33.4 %collective-permute-start.2 = (bf16[4,2,48,1536]{3,2,1,0:T(8,128)(2,1)}, bf16[4,2,48,1536]{3,2,1,0:T(8,128)(2,1)}, u32[]{:S(2)}, u32[]{:S(2)}) collective-permute-start(bf16[4,2,48,1536]{3,2,1,0:T(8,128)(2,1)} %all-to-all-done.2.refs_1_), channel_id=1, source_target_pairs={{0,1},{1,0},{2,3},{3,2},{4,5},{5,4},{6,7},{7,6},{8,9},{9,8},{10,11... | collective-permute-start | bytes 3538952 | tf_op jit(solution)/shard_map/ppermute | solution.py:205
  76.4 37.7 %all-to-all-start.4 = ((bf16[8,8,6912]{2,1,0:T(8,128)(2,1)}), bf16[8,8,6912]{2,1,0:T(8,128)(2,1)S(1)}, u32[]{:S(2)}, u32[]{:S(2)}) async-start(bf16[8,8,6912]{2,1,0:T(8,128)(2,1)} %bitcast.27), calls=%async_computation.4 | async-start | bytes 1769472 | tf_op jit(solution)/shard_map/all_to_all | solution.py:426
  83.0 14.5 %collective-permute-start.7 = (bf16[4,2,48,896]{3,2,1,0:T(8,128)(2,1)}, bf16[4,2,48,896]{3,2,1,0:T(8,128)(2,1)}, u32[]{:S(2)}, u32[]{:S(2)}) collective-permute-start(bf16[4,2,48,896]{3,2,1,0:T(8,128)(2,1)} %pad_maximum_fusion.13), channel_id=1, source_target_pairs={{0,16},{1,17},{2,18},{3,19},{4,20},{5,21},{6,22},{7,23},{8,24},{9,... | collective-permute-start | bytes 2064392 | tf_op jit(solution)/shard_map/ppermute | solution.py:210
  87.8 33.1 %collective-permute-start.8 = (bf16[4,2,48,896]{3,2,1,0:T(8,128)(2,1)}, bf16[4,2,48,896]{3,2,1,0:T(8,128)(2,1)}, u32[]{:S(2)}, u32[]{:S(2)}) collective-permute-start(bf16[4,2,48,896]{3,2,1,0:T(8,128)(2,1)} %all-to-all-done.refs_1_), channel_id=1, source_target_pairs={{0,8},{1,9},{2,10},{3,11},{4,12},{5,13},{6,14},{7,15},{8,0},{9,1},... | collective-permute-start | bytes 2064392 | tf_op jit(solution)/shard_map/ppermute | solution.py:215
  87.9 35.1 %collective-permute-start.9 = (bf16[4,2,48,896]{3,2,1,0:T(8,128)(2,1)}, bf16[4,2,48,896]{3,2,1,0:T(8,128)(2,1)}, u32[]{:S(2)}, u32[]{:S(2)}) collective-permute-start(bf16[4,2,48,896]{3,2,1,0:T(8,128)(2,1)} %collective-permute-done.refs_2_), channel_id=1, source_target_pairs={{0,8},{1,9},{2,10},{3,11},{4,12},{5,13},{6,14},{7,15},{8,0},{9,1},... | collective-permute-start | bytes 2064392 | tf_op jit(solution)/shard_map/ppermute | solution.py:215
  97.5 25.4 %collective-permute-start.10 = (bf16[4,2,48,896]{3,2,1,0:T(8,128)(2,1)}, bf16[4,2,48,896]{3,2,1,0:T(8,128)(2,1)}, u32[]{:S(2)}, u32[]{:S(2)}) collective-permute-start(bf16[4,2,48,896]{3,2,1,0:T(8,128)(2,1)} %collective-permute-done.7.refs_3_), channel_id=1, source_target_pairs={{0,8},{1,9},{2,10},{3,11},{4,12},{5,13},{6,14},{7,15},{8,0},{9,1},... | collective-permute-start | bytes 2064392 | tf_op jit(solution)/shard_map/ppermute | solution.py:215
  107.4 41.0 %collective-permute-start.6 = (bf16[4,2,48,1536]{3,2,1,0:T(8,128)(2,1)}, bf16[4,2,48,1536]{3,2,1,0:T(8,128)(2,1)}, u32[]{:S(2)}, u32[]{:S(2)}) collective-permute-start(bf16[4,2,48,1536]{3,2,1,0:T(8,128)(2,1)} %all-to-all-done.2.refs_1_), channel_id=1, source_target_pairs={{0,8},{1,9},{2,10},{3,11},{4,12},{5,13},{6,14},{7,15},{8,0},{9,1},... | collective-permute-start | bytes 3538952 | tf_op jit(solution)/shard_map/ppermute | solution.py:215
  112.1 36.3 %collective-permute-start.5 = (bf16[4,2,48,1536]{3,2,1,0:T(8,128)(2,1)}, bf16[4,2,48,1536]{3,2,1,0:T(8,128)(2,1)}, u32[]{:S(2)}, u32[]{:S(2)}) collective-permute-start(bf16[4,2,48,1536]{3,2,1,0:T(8,128)(2,1)} %collective-permute-done.2.refs_2_), channel_id=1, source_target_pairs={{0,8},{1,9},{2,10},{3,11},{4,12},{5,13},{6,14},{7,15},{8,0},{9,1},... | collective-permute-start | bytes 3538952 | tf_op jit(solution)/shard_map/ppermute | solution.py:215
  116.2 32.8 %all-to-all-start.3 = ((bf16[4,2,48,1536]{3,2,1,0:T(8,128)(2,1)}), bf16[4,2,48,1536]{3,2,1,0:T(8,128)(2,1)}, u32[]{:S(2)}, u32[]{:S(2)}) async-start(bf16[4,2,48,1536]{3,2,1,0:T(8,128)(2,1)} %broadcast_in_dim.65), calls=%async_computation.3 | async-start | bytes 2359296 | tf_op jit(solution)/shard_map/all_to_all | solution.py:89
  121.0 27.4 %collective-permute-start.4 = (bf16[4,2,48,1536]{3,2,1,0:T(8,128)(2,1)}, bf16[4,2,48,1536]{3,2,1,0:T(8,128)(2,1)}, u32[]{:S(2)}, u32[]{:S(2)}) collective-permute-start(bf16[4,2,48,1536]{3,2,1,0:T(8,128)(2,1)} %pad_maximum_fusion.7), channel_id=1, source_target_pairs={{0,16},{1,17},{2,18},{3,19},{4,20},{5,21},{6,22},{7,23},{8,24},{9,... | collective-permute-start | bytes 3538952 | tf_op jit(solution)/shard_map/ppermute | solution.py:210
  149.1 7.6 %collective-permute-start.12 = (bf16[4,2,48,1536]{3,2,1,0:T(8,128)(2,1)}, bf16[4,2,48,1536]{3,2,1,0:T(8,128)(2,1)}, u32[]{:S(2)}, u32[]{:S(2)}) collective-permute-start(bf16[4,2,48,1536]{3,2,1,0:T(8,128)(2,1)} %collective-permute-done.4.refs_3_), channel_id=1, source_target_pairs={{0,8},{1,9},{2,10},{3,11},{4,12},{5,13},{6,14},{7,15},{8,0},{9,1},... | collective-permute-start | bytes 3538952 | tf_op jit(solution)/shard_map/ppermute | solution.py:215
  151.6 32.3 %all-to-all-start.5 = ((bf16[4,2,48,1536]{3,2,1,0:T(8,128)(2,1)}), bf16[4,2,48,1536]{3,2,1,0:T(8,128)(2,1)S(1)}, u32[]{:S(2)}, u32[]{:S(2)}) async-start(bf16[4,2,48,1536]{3,2,1,0:T(8,128)(2,1)} %broadcast_in_dim.68), calls=%async_computation.5 | async-start | bytes 2359296 | tf_op jit(solution)/shard_map/all_to_all | solution.py:89
  155.6 27.6 %collective-permute-start.11 = (bf16[4,2,48,1536]{3,2,1,0:T(8,128)(2,1)}, bf16[4,2,48,1536]{3,2,1,0:T(8,128)(2,1)}, u32[]{:S(2)}, u32[]{:S(2)}) collective-permute-start(bf16[4,2,48,1536]{3,2,1,0:T(8,128)(2,1)} %all-to-all-done.3.refs_1_), channel_id=1, source_target_pairs={{0,1},{1,0},{2,3},{3,2},{4,5},{5,4},{6,7},{7,6},{8,9},{9,8},{10,11... | collective-permute-start | bytes 3538952 | tf_op jit(solution)/shard_map/ppermute | solution.py:205
  185.4 35.7 %all-to-all-start.6 = ((bf16[4,2,128,640]{3,2,1,0:T(8,128)(2,1)}), bf16[4,2,128,640]{3,2,1,0:T(8,128)(2,1)S(1)}, u32[]{:S(2)}, u32[]{:S(2)}) async-start(bf16[4,2,128,640]{3,2,1,0:T(8,128)(2,1)} %broadcast_in_dim.69), calls=%async_computation.6 | async-start | bytes 2621440 | tf_op jit(solution)/shard_map/all_to_all | solution.py:89
  191.4 27.3 %collective-permute-start.13 = (bf16[4,2,48,1536]{3,2,1,0:T(8,128)(2,1)S(1)}, bf16[4,2,48,1536]{3,2,1,0:T(8,128)(2,1)S(1)}, u32[]{:S(2)}, u32[]{:S(2)}) collective-permute-start(bf16[4,2,48,1536]{3,2,1,0:T(8,128)(2,1)S(1)} %pad_maximum_fusion.8), channel_id=1, source_target_pairs={{0,16},{1,17},{2,18},{3,19},{4,20},{5,21},{6,22},{7,23},{8,24},{9,... | collective-permute-start | bytes 3538952 | tf_op jit(solution)/shard_map/ppermute | solution.py:210
  192.6 26.0 %collective-permute-start.16 = (bf16[4,2,48,1536]{3,2,1,0:T(8,128)(2,1)S(1)}, bf16[4,2,48,1536]{3,2,1,0:T(8,128)(2,1)S(1)}, u32[]{:S(2)}, u32[]{:S(2)}) collective-permute-start(bf16[4,2,48,1536]{3,2,1,0:T(8,128)(2,1)S(1)} %copy-done.9), channel_id=1, source_target_pairs={{0,1},{1,0},{2,3},{3,2},{4,5},{5,4},{6,7},{7,6},{8,9},{9,8},{10,11... | collective-permute-start | bytes 3538952 | tf_op jit(solution)/shard_map/ppermute | solution.py:205
  193.8 24.9 %collective-permute-start.15 = (bf16[4,2,48,1536]{3,2,1,0:T(8,128)(2,1)}, bf16[4,2,48,1536]{3,2,1,0:T(8,128)(2,1)S(1)}, u32[]{:S(2)}, u32[]{:S(2)}) collective-permute-start(bf16[4,2,48,1536]{3,2,1,0:T(8,128)(2,1)} %all-to-all-done.3.refs_1_), channel_id=1, source_target_pairs={{0,8},{1,9},{2,10},{3,11},{4,12},{5,13},{6,14},{7,15},{8,0},{9,1},... | collective-permute-start | bytes 3538952 | tf_op jit(solution)/shard_map/ppermute | solution.py:215
  196.0 25.1 %collective-permute-start.14 = (bf16[4,2,48,1536]{3,2,1,0:T(8,128)(2,1)}, bf16[4,2,48,1536]{3,2,1,0:T(8,128)(2,1)}, u32[]{:S(2)}, u32[]{:S(2)}) collective-permute-start(bf16[4,2,48,1536]{3,2,1,0:T(8,128)(2,1)} %collective-permute-done.11.refs_2_), channel_id=1, source_target_pairs={{0,8},{1,9},{2,10},{3,11},{4,12},{5,13},{6,14},{7,15},{8,0},{9,1},... | collective-permute-start | bytes 3538952 | tf_op jit(solution)/shard_map/ppermute | solution.py:215
  221.1 17.9 %collective-permute-start.21 = (bf16[4,2,48,1536]{3,2,1,0:T(8,128)(2,1)}, bf16[4,2,48,1536]{3,2,1,0:T(8,128)(2,1)}, u32[]{:S(2)}, u32[]{:S(2)}) collective-permute-start(bf16[4,2,48,1536]{3,2,1,0:T(8,128)(2,1)} %copy-done.51), channel_id=1, source_target_pairs={{0,8},{1,9},{2,10},{3,11},{4,12},{5,13},{6,14},{7,15},{8,0},{9,1},... | collective-permute-start | bytes 3538952 | tf_op jit(solution)/shard_map/ppermute | solution.py:215
  224.2 29.5 %collective-permute-start.19 = (bf16[4,2,48,1536]{3,2,1,0:T(8,128)(2,1)S(1)}, bf16[4,2,48,1536]{3,2,1,0:T(8,128)(2,1)}, u32[]{:S(2)}, u32[]{:S(2)}) collective-permute-start(bf16[4,2,48,1536]{3,2,1,0:T(8,128)(2,1)S(1)} %copy-done.9), channel_id=1, source_target_pairs={{0,8},{1,9},{2,10},{3,11},{4,12},{5,13},{6,14},{7,15},{8,0},{9,1},... | collective-permute-start | bytes 3538952 | tf_op jit(solution)/shard_map/ppermute | solution.py:215
  225.6 28.1 %collective-permute-start.18 = (bf16[4,2,48,1536]{3,2,1,0:T(8,128)(2,1)S(1)}, bf16[4,2,48,1536]{3,2,1,0:T(8,128)(2,1)}, u32[]{:S(2)}, u32[]{:S(2)}) collective-permute-start(bf16[4,2,48,1536]{3,2,1,0:T(8,128)(2,1)S(1)} %copy-done.35), channel_id=1, source_target_pairs={{0,8},{1,9},{2,10},{3,11},{4,12},{5,13},{6,14},{7,15},{8,0},{9,1},... | collective-permute-start | bytes 3538952 | tf_op jit(solution)/shard_map/ppermute | solution.py:215
  226.1 27.6 %collective-permute-start.17 = (bf16[4,2,48,1536]{3,2,1,0:T(8,128)(2,1)S(1)}, bf16[4,2,48,1536]{3,2,1,0:T(8,128)(2,1)}, u32[]{:S(2)}, u32[]{:S(2)}) collective-permute-start(bf16[4,2,48,1536]{3,2,1,0:T(8,128)(2,1)S(1)} %pad_maximum_fusion.9), channel_id=1, source_target_pairs={{0,16},{1,17},{2,18},{3,19},{4,20},{5,21},{6,22},{7,23},{8,24},{9,... | collective-permute-start | bytes 3538952 | tf_op jit(solution)/shard_map/ppermute | solution.py:210
  226.5 29.8 %collective-permute-start.20 = (bf16[4,2,128,640]{3,2,1,0:T(8,128)(2,1)S(1)}, bf16[4,2,128,640]{3,2,1,0:T(8,128)(2,1)S(1)}, u32[]{:S(2)}, u32[]{:S(2)}) collective-permute-start(bf16[4,2,128,640]{3,2,1,0:T(8,128)(2,1)S(1)} %all-to-all-done.6.refs_1_), channel_id=1, source_target_pairs={{0,1},{1,0},{2,3},{3,2},{4,5},{5,4},{6,7},{7,6},{8,9},{9,8},{10,11... | collective-permute-start | bytes 3932168 | tf_op jit(solution)/shard_map/ppermute | solution.py:205
  258.0 30.5 %collective-permute-start.22 = (bf16[4,2,128,640]{3,2,1,0:T(8,128)(2,1)S(1)}, bf16[4,2,128,640]{3,2,1,0:T(8,128)(2,1)S(1)}, u32[]{:S(2)}, u32[]{:S(2)}) collective-permute-start(bf16[4,2,128,640]{3,2,1,0:T(8,128)(2,1)S(1)} %pad_maximum_fusion.3), channel_id=1, source_target_pairs={{0,16},{1,17},{2,18},{3,19},{4,20},{5,21},{6,22},{7,23},{8,24},{9,... | collective-permute-start | bytes 3932168 | tf_op jit(solution)/shard_map/ppermute | solution.py:210
  259.1 29.3 %collective-permute-start.24 = (bf16[4,2,128,640]{3,2,1,0:T(8,128)(2,1)S(1)}, bf16[4,2,128,640]{3,2,1,0:T(8,128)(2,1)S(1)}, u32[]{:S(2)}, u32[]{:S(2)}) collective-permute-start(bf16[4,2,128,640]{3,2,1,0:T(8,128)(2,1)S(1)} %all-to-all-done.6.refs_1_), channel_id=1, source_target_pairs={{0,8},{1,9},{2,10},{3,11},{4,12},{5,13},{6,14},{7,15},{8,0},{9,1},... | collective-permute-start | bytes 3932168 | tf_op jit(solution)/shard_map/ppermute | solution.py:215
  259.4 29.0 %collective-permute-start.23 = (bf16[4,2,128,640]{3,2,1,0:T(8,128)(2,1)S(1)}, bf16[4,2,128,640]{3,2,1,0:T(8,128)(2,1)}, u32[]{:S(2)}, u32[]{:S(2)}) collective-permute-start(bf16[4,2,128,640]{3,2,1,0:T(8,128)(2,1)S(1)} %collective-permute-done.20.refs_2_), channel_id=1, source_target_pairs={{0,8},{1,9},{2,10},{3,11},{4,12},{5,13},{6,14},{7,15},{8,0},{9,1},... | collective-permute-start | bytes 3932168 | tf_op jit(solution)/shard_map/ppermute | solution.py:215
  323.2 19.0 %collective-permute-start.27 = (bf16[3072,640]{1,0:T(8,128)(2,1)}, bf16[3072,640]{1,0:T(8,128)(2,1)S(1)}, u32[]{:S(2)}, u32[]{:S(2)}) collective-permute-start(bf16[3072,640]{1,0:T(8,128)(2,1)} %convolution_convert_fusion.1), channel_id=1, source_target_pairs={{0,8},{1,9},{2,10},{3,11},{4,12},{5,13},{6,14},{7,15},{8,0},{9,1},... | collective-permute-start | bytes 11796488 | tf_op jit(solution)/shard_map/ppermute | solution.py:239
  361.9 40.4 %collective-permute-start.29 = (bf16[1152,3072]{1,0:T(8,128)(2,1)}, bf16[1152,3072]{1,0:T(8,128)(2,1)}, u32[]{:S(2)}, u32[]{:S(2)}) collective-permute-start(bf16[1152,3072]{1,0:T(8,128)(2,1)} %convolution_convert_fusion), channel_id=1, source_target_pairs={{0,8},{1,9},{2,10},{3,11},{4,12},{5,13},{6,14},{7,15},{8,0},{9,1},... | collective-permute-start | bytes 21233672 | tf_op jit(solution)/shard_map/ppermute | solution.py:239
  364.2 38.1 %collective-permute-start.28 = (bf16[4,2,128,640]{3,2,1,0:T(8,128)(2,1)S(1)}, bf16[4,2,128,640]{3,2,1,0:T(8,128)(2,1)S(1)}, u32[]{:S(2)}, u32[]{:S(2)}) collective-permute-start(bf16[4,2,128,640]{3,2,1,0:T(8,128)(2,1)S(1)} %dynamic-slice_bitcast_fusion), channel_id=1, source_target_pairs={{0,16},{1,17},{2,18},{3,19},{4,20},{5,21},{6,22},{7,23},{8,24},{9,... | collective-permute-start | bytes 3932168 | tf_op jit(solution)/shard_map/ppermute | solution.py:268
  415.8 30.8 %collective-permute-start.30 = (bf16[4,2,128,640]{3,2,1,0:T(8,128)(2,1)}, bf16[4,2,128,640]{3,2,1,0:T(8,128)(2,1)}, u32[]{:S(2)}, u32[]{:S(2)}) collective-permute-start(bf16[4,2,128,640]{3,2,1,0:T(8,128)(2,1)} %pad_maximum_fusion.4), channel_id=1, source_target_pairs={{0,1},{1,0},{2,3},{3,2},{4,5},{5,4},{6,7},{7,6},{8,9},{9,8},{10,11... | collective-permute-start | bytes 3932168 | tf_op jit(solution)/shard_map/ppermute | solution.py:302
  419.4 27.2 %collective-permute-start.31 = (bf16[2,2,48,3072]{3,2,1,0:T(8,128)(2,1)}, bf16[2,2,48,3072]{3,2,1,0:T(8,128)(2,1)}, u32[]{:S(2)}, u32[]{:S(2)}) collective-permute-start(bf16[2,2,48,3072]{3,2,1,0:T(8,128)(2,1)} %dynamic-slice_bitcast_fusion.3), channel_id=1, source_target_pairs={{0,16},{1,17},{2,18},{3,19},{4,20},{5,21},{6,22},{7,23},{8,24},{9,... | collective-permute-start | bytes 3538952 | tf_op jit(solution)/shard_map/ppermute | solution.py:272
  449.6 37.7 %all-to-all-start.7 = ((bf16[4,2,128,640]{3,2,1,0:T(8,128)(2,1)}), bf16[4,2,128,640]{3,2,1,0:T(8,128)(2,1)S(1)}, u32[]{:S(2)}, u32[]{:S(2)}) async-start(bf16[4,2,128,640]{3,2,1,0:T(8,128)(2,1)} %pad_maximum_fusion.5), calls=%async_computation.7 | async-start | bytes 2621440 | tf_op jit(solution)/shard_map/all_to_all | solution.py:89
  454.0 33.2 %collective-permute-start.34 = (bf16[1152,640]{1,0:T(8,128)(2,1)}, bf16[1152,640]{1,0:T(8,128)(2,1)}, u32[]{:S(2)}, u32[]{:S(2)}) collective-permute-start(bf16[1152,640]{1,0:T(8,128)(2,1)} %convolution_convert_fusion.4), channel_id=1, source_target_pairs={{0,8},{1,9},{2,10},{3,11},{4,12},{5,13},{6,14},{7,15},{8,0},{9,1},... | collective-permute-start | bytes 4423688 | tf_op jit(solution)/shard_map/ppermute | solution.py:239
  458.5 27.7 %collective-permute-start.32 = (bf16[4,48,3072]{2,1,0:T(8,128)(2,1)S(1)}, bf16[4,48,3072]{2,1,0:T(8,128)(2,1)S(1)}, u32[]{:S(2)}, u32[]{:S(2)}) collective-permute-start(bf16[4,48,3072]{2,1,0:T(8,128)(2,1)S(1)} %dynamic-slice_bitcast_fusion.2), channel_id=1, source_target_pairs={{0,1},{1,0},{2,3},{3,2},{4,5},{5,4},{6,7},{7,6},{8,9},{9,8},{10,11... | collective-permute-start | bytes 3538952 | tf_op jit(solution)/shard_map/ppermute | solution.py:291
  459.8 27.3 %collective-permute-start.33 = (bf16[2,2,48,3072]{3,2,1,0:T(8,128)(2,1)S(1)}, bf16[2,2,48,3072]{3,2,1,0:T(8,128)(2,1)S(1)}, u32[]{:S(2)}, u32[]{:S(2)}) collective-permute-start(bf16[2,2,48,3072]{3,2,1,0:T(8,128)(2,1)S(1)} %dynamic-slice_bitcast_fusion.1), channel_id=1, source_target_pairs={{0,16},{1,17},{2,18},{3,19},{4,20},{5,21},{6,22},{7,23},{8,24},{9,... | collective-permute-start | bytes 3538952 | tf_op jit(solution)/shard_map/ppermute | solution.py:272
  493.1 37.5 %all-to-all-start.8 = ((bf16[4,48,3072]{2,1,0:T(8,128)(2,1)}), bf16[4,48,3072]{2,1,0:T(8,128)(2,1)S(1)}, u32[]{:S(2)}, u32[]{:S(2)}) async-start(bf16[4,48,3072]{2,1,0:T(8,128)(2,1)} %get-tuple-element.592), calls=%async_computation.8 | async-start | bytes 2359296 | tf_op jit(solution)/shard_map/all_to_all | solution.py:89
  498.7 31.9 %collective-permute-start.35 = (bf16[2,128,640]{2,1,0:T(8,128)(2,1)S(1)}, bf16[2,128,640]{2,1,0:T(8,128)(2,1)S(1)}, u32[]{:S(2)}, u32[]{:S(2)}) collective-permute-start(bf16[2,128,640]{2,1,0:T(8,128)(2,1)S(1)} %reduce_sum.136), channel_id=1, source_target_pairs={{0,16},{1,17},{2,18},{3,19},{4,20},{5,21},{6,22},{7,23},{8,24},{9,... | collective-permute-start | bytes 983048 | tf_op jit(solution)/shard_map/ppermute | solution.py:354
  499.1 31.4 %collective-permute-start.36 = (bf16[4,48,3072]{2,1,0:T(8,128)(2,1)}, bf16[4,48,3072]{2,1,0:T(8,128)(2,1)S(1)}, u32[]{:S(2)}, u32[]{:S(2)}) collective-permute-start(bf16[4,48,3072]{2,1,0:T(8,128)(2,1)} %get-tuple-element.593), channel_id=1, source_target_pairs={{0,1},{1,0},{2,3},{3,2},{4,5},{5,4},{6,7},{7,6},{8,9},{9,8},{10,11... | collective-permute-start | bytes 3538952 | tf_op jit(solution)/shard_map/ppermute | solution.py:296
  530.6 33.3 %collective-permute-start.38 = (bf16[1152,896]{1,0:T(8,128)(2,1)}, bf16[1152,896]{1,0:T(8,128)(2,1)}, u32[]{:S(2)}, u32[]{:S(2)}) collective-permute-start(bf16[1152,896]{1,0:T(8,128)(2,1)} %convolution_convert_fusion.3), channel_id=1, source_target_pairs={{0,8},{1,9},{2,10},{3,11},{4,12},{5,13},{6,14},{7,15},{8,0},{9,1},... | collective-permute-start | bytes 6193160 | tf_op jit(solution)/shard_map/ppermute | solution.py:239
  537.4 33.2 %all-to-all-start.9 = ((bf16[4,48,3072]{2,1,0:T(8,128)(2,1)}), bf16[4,48,3072]{2,1,0:T(8,128)(2,1)}, u32[]{:S(2)}, u32[]{:S(2)}) async-start(bf16[4,48,3072]{2,1,0:T(8,128)(2,1)} %add_convert_fusion.2), calls=%async_computation.9 | async-start | bytes 2359296 | tf_op jit(solution)/shard_map/all_to_all | solution.py:89
  542.6 26.0 %collective-permute-start.37 = (bf16[384,640]{1,0:T(8,128)(2,1)S(1)}, bf16[384,640]{1,0:T(8,128)(2,1)}, u32[]{:S(2)}, u32[]{:S(2)}) collective-permute-start(bf16[384,640]{1,0:T(8,128)(2,1)S(1)} %pad_maximum_fusion.18), channel_id=1, source_target_pairs={{0,8},{1,9},{2,10},{3,11},{4,12},{5,13},{6,14},{7,15},{8,0},{9,1},... | collective-permute-start | bytes 1474568 | tf_op jit(solution)/shard_map/ppermute | solution.py:364
  573.4 33.8 %all-to-all-start.10 = ((bf16[8,8,4608]{2,1,0:T(8,128)(2,1)}), bf16[8,8,4608]{2,1,0:T(8,128)(2,1)}, u32[]{:S(2)}, u32[]{:S(2)}) async-start(bf16[8,8,4608]{2,1,0:T(8,128)(2,1)} %broadcast_in_dim.71), calls=%async_computation.10 | async-start | bytes 1179648 | tf_op jit(solution)/shard_map/all_to_all | solution.py:412
  577.8 29.4 %collective-permute-start.39 = (bf16[4,48,1536]{2,1,0:T(8,128)(2,1)}, bf16[4,48,1536]{2,1,0:T(8,128)(2,1)}, u32[]{:S(2)}, u32[]{:S(2)}) collective-permute-start(bf16[4,48,1536]{2,1,0:T(8,128)(2,1)} %dynamic-slice_bitcast_fusion.6), channel_id=1, source_target_pairs={{0,1},{1,0},{2,3},{3,2},{4,5},{5,4},{6,7},{7,6},{8,9},{9,8},{10,11... | collective-permute-start | bytes 1769480 | tf_op jit(solution)/shard_map/ppermute | solution.py:291
  579.3 28.0 %collective-permute-start.40 = (bf16[4,2,48,1536]{3,2,0,1:T(8,128)(2,1)}, bf16[4,2,48,1536]{3,2,0,1:T(8,128)(2,1)}, u32[]{:S(2)}, u32[]{:S(2)}) collective-permute-start(bf16[4,2,48,1536]{3,2,0,1:T(8,128)(2,1)} %copy_bitcast_fusion.1), channel_id=1, source_target_pairs={{0,16},{1,17},{2,18},{3,19},{4,20},{5,21},{6,22},{7,23},{8,24},{9,... | collective-permute-start | bytes 3538952 | tf_op jit(solution)/shard_map/ppermute | solution.py:268
  607.2 18.8 %collective-permute-start.43 = (bf16[1152,896]{1,0:T(8,128)(2,1)}, bf16[1152,896]{1,0:T(8,128)(2,1)}, u32[]{:S(2)}, u32[]{:S(2)}) collective-permute-start(bf16[1152,896]{1,0:T(8,128)(2,1)} %convolution_convert_fusion.2), channel_id=1, source_target_pairs={{0,8},{1,9},{2,10},{3,11},{4,12},{5,13},{6,14},{7,15},{8,0},{9,1},... | collective-permute-start | bytes 6193160 | tf_op jit(solution)/shard_map/ppermute | solution.py:239
  618.0 38.3 %collective-permute-start.41 = (bf16[2,48,3072]{2,1,0:T(8,128)(2,1)}, bf16[2,48,3072]{2,1,0:T(8,128)(2,1)}, u32[]{:S(2)}, u32[]{:S(2)}) collective-permute-start(bf16[2,48,3072]{2,1,0:T(8,128)(2,1)} %pad_maximum_fusion.17), channel_id=1, source_target_pairs={{0,16},{1,17},{2,18},{3,19},{4,20},{5,21},{6,22},{7,23},{8,24},{9,... | collective-permute-start | bytes 1769480 | tf_op jit(solution)/shard_map/ppermute | solution.py:354
  620.9 35.4 %all-to-all-start.11 = ((bf16[4,48,1536]{2,1,0:T(8,128)(2,1)}), bf16[4,48,1536]{2,1,0:T(8,128)(2,1)}, u32[]{:S(2)}, u32[]{:S(2)}) async-start(bf16[4,48,1536]{2,1,0:T(8,128)(2,1)} %get-tuple-element.596), calls=%async_computation.11 | async-start | bytes 1179648 | tf_op jit(solution)/shard_map/all_to_all | solution.py:89
  625.6 30.7 %collective-permute-start.42 = (bf16[4,48,1536]{2,1,0:T(8,128)(2,1)}, bf16[4,48,1536]{2,1,0:T(8,128)(2,1)}, u32[]{:S(2)}, u32[]{:S(2)}) collective-permute-start(bf16[4,48,1536]{2,1,0:T(8,128)(2,1)} %get-tuple-element.597), channel_id=1, source_target_pairs={{0,1},{1,0},{2,3},{3,2},{4,5},{5,4},{6,7},{7,6},{8,9},{9,8},{10,11... | collective-permute-start | bytes 1769480 | tf_op jit(solution)/shard_map/ppermute | solution.py:296
  633.7 22.6 %collective-permute-start.44 = (bf16[4,2,48,896]{3,2,1,0:T(8,128)(2,1)}, bf16[4,2,48,896]{3,2,1,0:T(8,128)(2,1)}, u32[]{:S(2)}, u32[]{:S(2)}) collective-permute-start(bf16[4,2,48,896]{3,2,1,0:T(8,128)(2,1)} %dynamic-slice_bitcast_fusion.4), channel_id=1, source_target_pairs={{0,16},{1,17},{2,18},{3,19},{4,20},{5,21},{6,22},{7,23},{8,24},{9,... | collective-permute-start | bytes 2064392 | tf_op jit(solution)/shard_map/ppermute | solution.py:268
  661.7 31.6 %all-to-all-start.12 = ((bf16[8,8,2560]{2,1,0:T(8,128)(2,1)}), bf16[8,8,2560]{2,1,0:T(8,128)(2,1)}, u32[]{:S(2)}, u32[]{:S(2)}) async-start(bf16[8,8,2560]{2,1,0:T(8,128)(2,1)} %broadcast_in_dim.73), calls=%async_computation.12 | async-start | bytes 655360 | tf_op jit(solution)/shard_map/all_to_all | solution.py:412
  669.5 23.9 %collective-permute-start.50 = (bf16[64,4608]{1,0:T(8,128)(2,1)}, bf16[64,4608]{1,0:T(8,128)(2,1)}, u32[]{:S(2)}, u32[]{:S(2)}) collective-permute-start(bf16[64,4608]{1,0:T(8,128)(2,1)} %bitcast.68), channel_id=1, source_target_pairs={{0,16},{1,17},{2,18},{3,19},{4,20},{5,21},{6,22},{7,23},{8,24},{9,... | collective-permute-start | bytes 1769480 | tf_op jit(solution)/shard_map/ppermute | solution.py:395
  670.9 22.5 %collective-permute-start.49 = (bf16[4,2,48,896]{3,2,1,0:T(8,128)(2,1)}, bf16[4,2,48,896]{3,2,1,0:T(8,128)(2,1)}, u32[]{:S(2)}, u32[]{:S(2)}) collective-permute-start(bf16[4,2,48,896]{3,2,1,0:T(8,128)(2,1)} %pad_maximum_fusion.14), channel_id=1, source_target_pairs={{0,1},{1,0},{2,3},{3,2},{4,5},{5,4},{6,7},{7,6},{8,9},{9,8},{10,11... | collective-permute-start | bytes 2064392 | tf_op jit(solution)/shard_map/ppermute | solution.py:302
  673.3 20.1 %collective-permute-start.45 = (bf16[144,3072]{1,0:T(8,128)(2,1)}, bf16[144,3072]{1,0:T(8,128)(2,1)}, u32[]{:S(2)}, u32[]{:S(2)}) collective-permute-start(bf16[144,3072]{1,0:T(8,128)(2,1)} %pad_maximum_fusion.12), channel_id=1, source_target_pairs={{0,8},{1,9},{2,10},{3,11},{4,12},{5,13},{6,14},{7,15},{8,0},{9,1},... | collective-permute-start | bytes 2654216 | tf_op jit(solution)/shard_map/ppermute | solution.py:364
  680.6 12.8 %collective-permute-start.47 = (bf16[48,1536]{1,0:T(8,128)(2,1)S(1)}, bf16[48,1536]{1,0:T(8,128)(2,1)S(1)}, u32[]{:S(2)}, u32[]{:S(2)}) collective-permute-start(bf16[48,1536]{1,0:T(8,128)(2,1)S(1)} %get-tuple-element.625), channel_id=1, source_target_pairs={{0,4},{1,5},{2,6},{3,7},{4,0},{5,1},{6,2},{7,3},{8,12},{9,13},{10,... | collective-permute-start | bytes 442376 | tf_op jit(solution)/shard_map/ppermute | solution.py:328
  683.9 9.4 %collective-permute-start.46 = (bf16[48,1536]{1,0:T(8,128)(2,1)S(1)}, bf16[48,1536]{1,0:T(8,128)(2,1)S(1)}, u32[]{:S(2)}, u32[]{:S(2)}) collective-permute-start(bf16[48,1536]{1,0:T(8,128)(2,1)S(1)} %get-tuple-element.626), channel_id=1, source_target_pairs={{0,2},{1,3},{2,4},{3,5},{4,6},{5,7},{6,0},{7,1},{8,10},{9,11},{10,... | collective-permute-start | bytes 442376 | tf_op jit(solution)/shard_map/ppermute | solution.py:328
  694.7 20.7 %collective-permute-start.51 = (bf16[2,48,1536]{2,1,0:T(8,128)(2,1)S(1)}, bf16[2,48,1536]{2,1,0:T(8,128)(2,1)}, u32[]{:S(2)}, u32[]{:S(2)}) collective-permute-start(bf16[2,48,1536]{2,1,0:T(8,128)(2,1)S(1)} %pad_maximum_fusion.24), channel_id=1, source_target_pairs={{0,16},{1,17},{2,18},{3,19},{4,20},{5,21},{6,22},{7,23},{8,24},{9,... | collective-permute-start | bytes 884744 | tf_op jit(solution)/shard_map/ppermute | solution.py:354
  695.8 19.6 %collective-permute-start.52 = (bf16[64,2560]{1,0:T(8,128)(2,1)}, bf16[64,2560]{1,0:T(8,128)(2,1)}, u32[]{:S(2)}, u32[]{:S(2)}) collective-permute-start(bf16[64,2560]{1,0:T(8,128)(2,1)} %bitcast.92), channel_id=1, source_target_pairs={{0,16},{1,17},{2,18},{3,19},{4,20},{5,21},{6,22},{7,23},{8,24},{9,... | collective-permute-start | bytes 983048 | tf_op jit(solution)/shard_map/ppermute | solution.py:395
  700.1 21.7 %all-to-all-start.13 = ((bf16[4,2,48,896]{3,2,1,0:T(8,128)(2,1)}), bf16[4,2,48,896]{3,2,1,0:T(8,128)(2,1)}, u32[]{:S(2)}, u32[]{:S(2)}) async-start(bf16[4,2,48,896]{3,2,1,0:T(8,128)(2,1)} %pad_maximum_fusion.15), calls=%async_computation.13 | async-start | bytes 1376256 | tf_op jit(solution)/shard_map/all_to_all | solution.py:89
  724.6 10.0 %collective-permute-start.56 = (bf16[2,64,2560]{2,1,0:T(8,128)(2,1)}, bf16[2,64,2560]{2,1,0:T(8,128)(2,1)}, u32[]{:S(2)}, u32[]{:S(2)}) collective-permute-start(bf16[2,64,2560]{2,1,0:T(8,128)(2,1)} %pad_maximum_fusion.16), channel_id=1, source_target_pairs={{0,8},{1,9},{2,10},{3,11},{4,12},{5,13},{6,14},{7,15},{8,0},{9,1},... | collective-permute-start | bytes 1966088 | tf_op jit(solution)/shard_map/ppermute | solution.py:404
  729.1 10.3 %all-to-all-start.14 = ((bf16[8,8,144]{2,1,0:T(8,128)(2,1)}), bf16[8,8,144]{2,1,0:T(8,128)(2,1)S(1)}, u32[]{:S(2)}, u32[]{:S(2)}) async-start(bf16[8,8,144]{2,1,0:T(8,128)(2,1)} %bitcast.240), calls=%async_computation.14 | async-start | bytes 65536 | tf_op jit(solution)/shard_map/all_to_all | solution.py:1287
  (68 other events, 459.6 us)
